TPU v7x, 256 devices: a whole 4x4x8 slice. The times are simulated.
256 devices in a mesh: dp: 2 (over y_lo), space: 16 (over z, y_hi), chan: 8 (over x, core).
Axes of the slice: x: 4, y: 4 (y_hi: 2, y_lo: 2; y = y_hi * 2 + y_lo), z: 8, core: 2. Of those that a mesh axis runs over, the one named last changes fastest.
Arguments:
- volumes: bfloat16 [2, 32, 512, 1024], P('dp', 'space', 'chan'), may hold values from -6 to 6
- kernel: bfloat16 [512, 13824], P('chan'), may hold values from -0.15625 to 0.15625
- bias: float32 [512], P('chan'), may hold values from -3 to 3
- act_grad: bfloat16 [2, 16, 512, 256], P('dp', 'space', 'chan'), may hold values from -6 to 6
Outputs:
- activation: bfloat16 [2, 16, 512, 256], P('dp', 'space', 'chan')
- grad_x: bfloat16 [2, 32, 512, 1024], P('dp', 'space', 'chan')
- grad_w: float32 [512, 13824], P('chan')
- grad_b: float32 [512], P('chan')
All inputs are finite; a program needn't handle non-finite values.
Results may differ from a plain program's by a relative error of at most 0.005.
Values may be sent and summed in bfloat16 or wider, within the bound.
No kernel may reach another device: no remote copies, remote signals or barrier semaphores. Data moves between devices by JAX's collectives and lax.ppermute only.
A program may use at most 64 MiB of HBM per device.

v0:
```python
import jax
import jax.numpy as jnp
import numpy as np
from jax import lax
from jax.experimental import pallas as pl
from jax.experimental.pallas import tpu as pltpu
from jax.sharding import PartitionSpec as P

BF = jnp.bfloat16
F32 = jnp.float32
DS = ("dp", "space")
Y_GROUPS = [[dp * 16 + z * 2 + yh for yh in range(2) for dp in range(2)] for z in range(8)]
Z_GROUPS = [[dp * 16 + z * 2 + yh for z in range(8)] for yh in range(2) for dp in range(2)]
X_GROUPS = [[2 * x + core for x in range(4)] for core in range(2)]
TAP_OF = {(0, 0): 1, (1, 0): 2, (1, 1): 0}
PARAMS = pltpu.CompilerParams(vmem_limit_bytes=48 * 1024 * 1024)


def split_matrix():
    matrix = np.zeros((512, 512), np.float32)
    for y in range(16):
        for z in range(32):
            matrix[y * 32 + z, (2 * (y % 2) + z % 2) * 128 + (y // 2) * 16 + z // 2] = 1
    return matrix


def class_shifts(c):
    py, pz = c // 2, c % 2
    return [(sy, sz) for sy in range(py + 1) for sz in range(pz + 1)]


def taps_of(c):
    py, pz = c // 2, c % 2
    return [(TAP_OF[py, sy] * 3 + TAP_OF[pz, sz], sy, sz) for sy, sz in class_shifts(c)]


def lanes(shape):
    return lax.broadcasted_iota(jnp.int32, shape, 1)


def later(a, sy, sz):
    lane = lanes(a.shape)
    if sy:
        a = jnp.where(lane < 16, 0.0, pltpu.roll(a, 16, 1))
    if sz:
        a = jnp.where(lane % 16 == 0, 0.0, pltpu.roll(a, 1, 1))
    return a


def earlier(a, sy, sz):
    lane = lanes(a.shape)
    if sy:
        a = jnp.where(lane >= 240, 0.0, pltpu.roll(a, 240, 1))
    if sz:
        a = jnp.where(lane % 16 == 15, 0.0, pltpu.roll(a, 255, 1))
    return a


def split_kernel(x_ref, m_ref, o_ref):
    for p in range(2):
        for h in range(2):
            r = jnp.dot(x_ref[p, :, h * 512 : (h + 1) * 512], m_ref[...], preferred_element_type=F32).astype(BF)
            for c in range(4):
                for copy in range(4):
                    o_ref[copy, p, c, :, h * 128 : (h + 1) * 128] = r[:, c * 128 : (c + 1) * 128]


def forward_kernel(core_ref, xo_ref, xp_ref, w_ref, xs_ref, own_ref, next_ref):
    core = core_ref[0]
    mine = pl.multiple_of(core * 64, 64)
    other = pl.multiple_of(64 - core * 64, 64)
    for p in range(2):
        for c in range(4):
            for x in range(4):
                xs_ref[p, c, pl.ds(x * 128 + mine, 64), :] = xo_ref[x, p, c]
                xs_ref[p, c, pl.ds(x * 128 + other, 64), :] = xp_ref[x, p, c]
    own = {}
    following = {}

    def add(table, key, value):
        table[key] = table[key] + value if key in table else value

    for c in range(4):
        taps = taps_of(c)
        for p, firsts in ((1, (0, 2)), (0, (1,))):
            rows = []
            for k1 in firsts:
                for tap, _, _ in taps:
                    at = (9 * k1 + tap) * 512
                    rows.append(w_ref[:, at : at + 512])
            r = jnp.dot(jnp.concatenate(rows, 0), xs_ref[p, c], preferred_element_type=F32)
            n = 0
            for k1 in firsts:
                for _, sy, sz in taps:
                    add(following if k1 == 0 else own, (sy, sz), r[64 * n : 64 * n + 64])
                    n += 1
    own_ref[...] = sum(later(v, *s) for s, v in own.items())
    next_ref[...] = sum(later(v, *s) for s, v in following.items())


def gelu_kernel(own_ref, from_ref, b_ref, g_ref, act_ref, dy_ref):
    u = own_ref[...] + from_ref[...] + b_ref[...]
    root = float(np.sqrt(2 / np.pi))
    t = jnp.tanh(root * (u + 0.044715 * (u * u * u)))
    act_ref[...] = (0.5 * u * (1.0 + t)).astype(BF)
    slope = 0.5 * (1.0 + t) + 0.5 * u * (1.0 - t * t) * (root * (1.0 + 3 * 0.044715 * (u * u)))
    dy_ref[...] = (g_ref[...].astype(F32) * slope).astype(BF)


def pair_block(total, shape):
    hi = total.astype(BF).astype(F32)
    lane = lanes(shape)
    return jnp.where(lane == 0, hi, jnp.where(lane == 1, total - hi, 0.0)).astype(BF)


def filter_grad_kernel(dy_ref, dn_ref, xs_ref, o_ref):
    now = dy_ref[...].astype(F32)
    nxt = dn_ref[...].astype(F32)
    shifted = {}
    for sy in range(2):
        for sz in range(2):
            shifted[0, sy, sz] = earlier(nxt, sy, sz).astype(BF)
            shifted[1, sy, sz] = earlier(now, sy, sz).astype(BF)
    for c in range(4):
        taps = taps_of(c)
        for p, firsts in ((0, (1,)), (1, (2, 0))):
            rows = [shifted[min(k1, 1), sy, sz] for k1 in firsts for _, sy, sz in taps]
            r = lax.dot_general(
                jnp.concatenate(rows, 0), xs_ref[p, c], (((1,), (1,)), ((), ())), preferred_element_type=F32
            ).astype(BF)
            n = 0
            for k1 in firsts:
                for tap, _, _ in taps:
                    h, at = divmod(9 * k1 + tap, 14)
                    for q in range(4):
                        for fb in range(4):
                            o_ref[q, fb * 2 + h, :, at * 128 : at * 128 + 128] = r[
                                64 * n + 16 * fb : 64 * n + 16 * fb + 16, q * 128 : q * 128 + 128
                            ]
                    n += 1
    block = pair_block(jnp.sum(now, 1, keepdims=True), (64, 128))
    for q in range(4):
        for fb in range(4):
            o_ref[q, fb * 2 + 1, :, 13 * 128 : 14 * 128] = block[16 * fb : 16 * fb + 16]


def sum_y_kernel(r_ref, o_ref):
    for z in range(8):
        for at in range(0, 1792, 256):
            total = sum(r_ref[s, z, :, at : at + 256].astype(F32) for s in range(4))
            o_ref[z, :, at : at + 256] = total.astype(BF)
            if z % 2 == 1 and at == 1536:
                bias_total = total[:, 128:129] + total[:, 129:130]
                o_ref[z, :, 1664:1792] = pair_block(bias_total, (16, 128))


def sum_z_kernel(odd_ref, r_ref, o_ref):
    for at in range(0, 1792, 256):
        total = sum(r_ref[s, :, at : at + 256].astype(F32) for s in range(8))
        out = total.astype(BF)
        for copy in range(8):
            o_ref[copy, :, at : at + 256] = out
        if at == 1536:

            @pl.when(odd_ref[0] == 1)
            def _():
                bias_total = total[:, 128:129] + total[:, 129:130]
                block = pair_block(bias_total, (16, 128))
                for copy in range(8):
                    o_ref[copy, :, 1664:1792] = block


def filter_out_kernel(r_ref, w_ref, b_ref):
    for tap in range(27):
        h, at = divmod(tap, 14)
        for q in range(4):
            for fb in range(4):
                w_ref[fb * 16 : fb * 16 + 16, tap * 512 + q * 128 : tap * 512 + q * 128 + 128] = (
                    r_ref[q, fb * 2 + h, :, at * 128 : at * 128 + 128].astype(F32) * 0.5
                )
    for fb in range(4):
        pair = r_ref[0, fb * 2 + 1, :, 1664:1792].astype(F32)
        b_ref[fb * 16 : fb * 16 + 16, :] = (pair[:, 0:1] + pair[:, 1:2]) * 0.5


def pack_kernel(x_ref, w_ref, *o_refs):
    for d in range(4):
        to = lax.rem(x_ref[0] + d, 4) * 128
        for tap in range(27):
            o_refs[d][:, tap * 128 : tap * 128 + 128] = w_ref[:, pl.ds(pl.multiple_of(tap * 512 + to, 128), 128)]


def input_grad_kernel(core_ref, *refs):
    w_refs, d_refs, (mine_ref, theirs_ref), (g_ref,) = refs[:4], refs[4:8], refs[8:10], refs[10:]
    shifted = {}
    for which in range(2):
        full = jnp.concatenate([d[which] for d in d_refs], 0).astype(F32)
        for sy in range(2):
            for sz in range(2):
                shifted[which, sy, sz] = earlier(full, sy, sz).astype(BF)
    mine = pl.multiple_of(core_ref[0] * 64, 64)
    other = pl.multiple_of(64 - core_ref[0] * 64, 64)
    for c in range(4):
        for p, firsts in ((0, (1,)), (1, (2, 0))):
            total = None
            for k1 in firsts:
                for tap, sy, sz in taps_of(c):
                    at = (9 * k1 + tap) * 128
                    w = jnp.concatenate([w[:, at : at + 128] for w in w_refs], 0)
                    r = lax.dot_general(
                        w, shifted[1 if k1 == 0 else 0, sy, sz], (((0,), (0,)), ((), ())), preferred_element_type=F32
                    )
                    total = r if total is None else total + r
            g_ref[...] = total
            mine_ref[p, c] = g_ref[pl.ds(mine, 64), :]
            theirs_ref[p, c] = g_ref[pl.ds(other, 64), :]


def join_kernel(a_ref, b_ref, m_ref, o_ref):
    for p in range(2):
        for h in range(2):
            at = slice(h * 128, h * 128 + 128)
            parts = [(a_ref[p, c, :, at] + b_ref[p, c, :, at]).astype(BF) for c in range(4)]
            r = lax.dot_general(
                jnp.concatenate(parts, 1), m_ref[...], (((1,), (1,)), ((), ())), preferred_element_type=F32
            )
            o_ref[p, :, h * 512 : (h + 1) * 512] = r.astype(BF)


VMEM = pl.BlockSpec(memory_space=pltpu.VMEM)
SMEM = pl.BlockSpec(memory_space=pltpu.SMEM)


def call(kernel, outs, *args, scalars=0, scratch=()):
    shapes = [jax.ShapeDtypeStruct(s, t) for s, t in outs]
    result = pl.pallas_call(
        kernel,
        out_shape=shapes,
        in_specs=[SMEM] * scalars + [VMEM] * (len(args) - scalars),
        out_specs=[VMEM] * len(outs),
        scratch_shapes=list(scratch),
        compiler_params=PARAMS,
    )(*args)
    return result


def shift_space(a, by):
    return lax.ppermute(a, "space", [(i, i + by) for i in range(16) if 0 <= i + by < 16])


def to_x(a, d):
    return lax.ppermute(a, "chan", [(i, (i + 2 * d) % 8) for i in range(8)])


def to_partner(a):
    return lax.ppermute(a, "chan", [(i, i ^ 1) for i in range(8)])


def per_device(volumes, kernel, bias, act_grad):
    chan = lax.axis_index("chan")
    core = (chan % 2).astype(jnp.int32).reshape(1)
    x = (chan // 2).astype(jnp.int32).reshape(1)
    z_odd = ((lax.axis_index("space") // 2) % 2).astype(jnp.int32).reshape(1)
    matrix = jnp.asarray(split_matrix(), BF)

    (copies,) = call(split_kernel, [((4, 2, 4, 64, 256), BF)], volumes.reshape(2, 64, 1024), matrix)
    x_own = lax.all_to_all(copies, "chan", 0, 0, axis_index_groups=X_GROUPS)
    x_partner = to_partner(x_own)
    xs, own, following = call(
        forward_kernel,
        [((2, 4, 512, 256), BF), ((64, 256), F32), ((64, 256), F32)],
        core,
        x_own,
        x_partner,
        kernel,
        scalars=1,
    )
    received = shift_space(following, 1)
    packed = call(pack_kernel, [((64, 3456), BF)] * 4, x, kernel, scalars=1)
    *packed, received = lax.optimization_barrier((*packed, received))
    weights = [packed[0]] + [to_x(packed[d], d) for d in range(1, 4)]
    activation, dy = call(
        gelu_kernel,
        [((64, 256), BF), ((64, 256), BF)],
        own,
        received,
        bias.reshape(64, 1),
        act_grad.reshape(64, 256),
    )
    dy_next = shift_space(dy, -1)
    (terms,) = call(filter_grad_kernel, [((4, 8, 16, 1792), BF)], dy, dy_next, xs)
    dys = jnp.stack([dy, dy_next])
    grads = [dys] + [to_x(dys, d) for d in range(1, 4)]

    terms = lax.all_to_all(terms, DS, 0, 0, axis_index_groups=Y_GROUPS)
    (terms,) = call(sum_y_kernel, [((8, 16, 1792), BF)], terms)
    terms = lax.all_to_all(terms, DS, 0, 0, axis_index_groups=Z_GROUPS)
    (terms,) = call(sum_z_kernel, [((8, 16, 1792), BF)], z_odd, terms, scalars=1)
    terms = lax.all_to_all(terms, DS, 0, 0, axis_index_groups=Z_GROUPS)
    terms = lax.all_to_all(jnp.broadcast_to(terms[None], (4, 8, 16, 1792)), DS, 0, 0, axis_index_groups=Y_GROUPS)
    grad_w, grad_b = call(filter_out_kernel, [((64, 13824), F32), ((64, 1), F32)], terms)

    mine, theirs = call(
        input_grad_kernel,
        [((2, 4, 64, 256), F32), ((2, 4, 64, 256), F32)],
        core,
        *weights,
        *grads,
        scalars=1,
        scratch=[pltpu.VMEM((128, 256), F32)],
    )
    (grad_x,) = call(join_kernel, [((2, 64, 1024), BF)], mine, to_partner(theirs), matrix)
    return (
        activation.reshape(1, 1, 64, 256),
        grad_x.reshape(1, 2, 64, 1024),
        grad_w,
        grad_b.reshape(64),
    )


def solution(mesh):
    in_specs = (
        P("dp", "space", "chan", None),
        P("chan", None),
        P("chan"),
        P("dp", "space", "chan", None),
    )
    out_specs = (
        P("dp", "space", "chan", None),
        P("dp", "space", "chan", None),
        P("chan", None),
        P("chan"),
    )
    return jax.shard_map(
        per_device, mesh=mesh, in_specs=in_specs, out_specs=out_specs, check_vma=False
    )
```

profile of v0, /device:TPU:1, one launch (start us, length us, event | category | flops | bytes accessed | tf_op | source)
XLA Modules:
  0.0 149.7 jit_solution(15560701618389404047)
XLA Ops:
  0.6 0.0 copy-start.1
  0.6 1.0 copy-done.1
  1.7 0.9 copy-done.5
  2.6 0.5 shard_map.84
  3.2 18.8 %all_to_all.25.xo_ref = bf16[4,2,4,64,256]{4,3,2,1,0:T(8,128)(2,1)S(1)} all-to-all(bf16[4,2,4,64,256]{4,3,2,1,0:T(8,128)(2,1)S(1)} %shard_map.84), channel_id=1, replica_groups={{0,2,4,6},{1,3,5,7},{8,10,12,14},{9,11,13,15},{16,18,20,22},{17,19,21,2..., dimensions={0} | all-to-all | bytes 2097152 | tf_op jit(solution)/shard_map/all_to_all | solution.py:267
  21.9 1.9 %collective-permute-start = (bf16[4,2,4,64,256]{4,3,2,1,0:T(8,128)(2,1)S(1)}, bf16[4,2,4,64,256]{4,3,2,1,0:T(8,128)(2,1)}, u32[]{:S(2)}, u32[]{:S(2)}) collective-permute-start(bf16[4,2,4,64,256]{4,3,2,1,0:T(8,128)(2,1)S(1)} %all_to_all.25.xo_ref), channel_id=1, source_target_pairs={{0,1},{1,0},{2,3},{3,2},{4,5},{5,4},{6,7},{7,6},{8,9},{9,8},{10,11... | collective-permute-start | bytes 3145736 | tf_op jit(solution)/shard_map/ppermute | solution.py:256
  23.9 2.4 %collective-permute-done.xp_ref = bf16[4,2,4,64,256]{4,3,2,1,0:T(8,128)(2,1)} collective-permute-done((bf16[4,2,4,64,256]{4,3,2,1,0:T(8,128)(2,1)S(1)}, bf16[4,2,4,64,256]{4,3,2,1,0:T(8,128)(2,1)}, u32[]{:S(2)}, u32[]{:S(2)}) %collective-permute-start) | collective-permute-done | bytes 1048608 | tf_op jit(solution)/shard_map/ppermute | solution.py:256
  26.3 2.2 %shard_map.85 = (bf16[2,4,512,256]{3,2,1,0:T(8,128)(2,1)S(1)}, f32[64,256]{1,0:T(8,128)S(1)}, f32[64,256]{1,0:T(8,128)S(1)}) custom-call(s32[1]{0:T(128)} %bitcast.core_ref, bf16[4,2,4,64,256]{4,3,2,1,0:T(8,128)(2,1)S(1)} %all_to_all.25.xo_ref, bf16[4,2,4,64,256]{4,3,2,1,0:T(8,128)(2,1)} %collective-permute-done.xp_ref, bf16[64,13824]{1,0:T(8,128)(2,1)S(1)} %copy-done), custom_call_target="tpu_custom_call" | custom-call | tf_op jit(solution)/shard_map/pallas_call | solution.py:236
  28.5 0.0 copy-start.3
  28.5 1.3 copy-done.3
  29.8 4.9 %collective-permute-start.1 = (f32[64,256]{1,0:T(8,128)S(1)}, f32[64,256]{1,0:T(8,128)S(1)}, u32[]{:S(2)}, u32[]{:S(2)}) collective-permute-start(f32[64,256]{1,0:T(8,128)S(1)} %get-tuple-element.27), channel_id=1, source_target_pairs={{0,8},{8,16},{16,24},{24,32},{32,40},{40,48},{48,56},{56,64},{64,7... | collective-permute-start | bytes 196616 | tf_op jit(solution)/shard_map/ppermute | solution.py:248
  34.8 0.4 shard_map.86
  35.2 0.8 copy-done.7
  35.9 0.1 copy.10.b_ref
  36.0 0.0 collective-permute-done.1.from_ref
  36.1 0.7 shard_map.87
  36.8 1.3 collective-permute-start.5
  38.1 5.2 %collective-permute-done.5.dn_ref = bf16[64,256]{1,0:T(8,128)(2,1)S(1)} collective-permute-done((bf16[64,256]{1,0:T(8,128)(2,1)S(1)}, bf16[64,256]{1,0:T(8,128)(2,1)S(1)}, u32[]{:S(2)}, u32[]{:S(2)}) %collective-permute-start.5) | collective-permute-done | bytes 32800 | tf_op jit(solution)/shard_map/ppermute | solution.py:248
  43.3 1.6 %copy-done.4 = bf16[2,4,512,256]{3,2,1,0:T(8,128)(2,1)S(1)} copy-done((bf16[2,4,512,256]{3,2,1,0:T(8,128)(2,1)S(1)}, bf16[2,4,512,256]{3,2,1,0:T(8,128)(2,1)}, u32[]{:S(2)}) %copy-start.4) | copy-done | bytes 2097176
  44.9 0.9 shard_map.90
  45.8 25.5 %all_to_all.26.r_ref = bf16[4,8,16,1792]{3,2,1,0:T(8,128)(2,1)S(1)} all-to-all(bf16[4,8,16,1792]{3,2,1,0:T(8,128)(2,1)S(1)} %shard_map.90), channel_id=1, replica_groups={{0,128,8,136},{16,144,24,152},{32,160,40,168},{48,176,56,184},{64,192,7..., dimensions={0} | all-to-all | bytes 3670016 | tf_op jit(solution)/shard_map/all_to_all | solution.py:295
  71.2 1.1 shard_map.91
  72.3 8.2 %all-to-all-start.2 = ((bf16[8,16,1792]{2,1,0:T(8,128)(2,1)}), bf16[8,16,1792]{2,1,0:T(8,128)(2,1)S(1)}, u32[]{:S(2)}, u32[]{:S(2)}) async-start(bf16[8,16,1792]{2,1,0:T(8,128)(2,1)} %shard_map.91), calls=%async_computation.2 | async-start | bytes 917504 | tf_op jit(solution)/shard_map/all_to_all | solution.py:297
  80.5 11.1 %all-to-all-done.2.r_ref = bf16[8,16,1792]{2,1,0:T(8,128)(2,1)S(1)} async-done(((bf16[8,16,1792]{2,1,0:T(8,128)(2,1)}), bf16[8,16,1792]{2,1,0:T(8,128)(2,1)S(1)}, u32[]{:S(2)}, u32[]{:S(2)}) %all-to-all-start.2) | async-done | bytes 458784 | tf_op jit(solution)/shard_map/all_to_all | solution.py:297
  91.6 0.1 shard_map.92
  91.7 15.6 %all_to_all.27 = bf16[8,16,1792]{2,1,0:T(8,128)(2,1)S(1)} all-to-all(bf16[8,16,1792]{2,1,0:T(8,128)(2,1)S(1)} %shard_map.92), channel_id=1, replica_groups={{0,16,32,48,64,80,96,112},{128,144,160,176,192,208,224,240},{8,24,40,56..., dimensions={0} | all-to-all | bytes 917504 | tf_op jit(solution)/shard_map/all_to_all | solution.py:299
  107.3 1.4 broadcast_in_dim.2
  108.6 3.6 %all-to-all-start.4 = ((bf16[4,8,16,1792]{3,2,1,0:T(8,128)(2,1)}), bf16[4,8,16,1792]{3,2,1,0:T(8,128)(2,1)S(1)}, u32[]{:S(2)}, u32[]{:S(2)}) async-start(bf16[4,8,16,1792]{3,2,1,0:T(8,128)(2,1)} %broadcast_in_dim.2), calls=%async_computation.4 | async-start | bytes 3670016 | tf_op jit(solution)/shard_map/all_to_all | solution.py:300
  112.2 0.0 copy-start.2
  112.3 0.3 collective-permute-start.2
  112.6 1.8 %collective-permute-start.3 = (bf16[64,3456]{1,0:T(8,128)(2,1)S(1)}, bf16[64,3456]{1,0:T(8,128)(2,1)S(1)}, u32[]{:S(2)}, u32[]{:S(2)}) collective-permute-start(bf16[64,3456]{1,0:T(8,128)(2,1)S(1)} %get-tuple-element.32), channel_id=1, source_target_pairs={{0,4},{1,5},{2,6},{3,7},{4,0},{5,1},{6,2},{7,3},{8,12},{9,13},{10,... | collective-permute-start | bytes 1327112 | tf_op jit(solution)/shard_map/ppermute | solution.py:252
  114.4 0.7 collective-permute-start.4
  115.1 0.9 collective-permute-start.6
  116.0 1.6 %collective-permute-start.7 = (bf16[2,64,256]{2,1,0:T(8,128)(2,1)S(1)}, bf16[2,64,256]{2,1,0:T(8,128)(2,1)S(1)}, u32[]{:S(2)}, u32[]{:S(2)}) collective-permute-start(bf16[2,64,256]{2,1,0:T(8,128)(2,1)S(1)} %pad_maximum_fusion.refs_4_), channel_id=1, source_target_pairs={{0,4},{1,5},{2,6},{3,7},{4,0},{5,1},{6,2},{7,3},{8,12},{9,13},{10,... | collective-permute-start | bytes 196616 | tf_op jit(solution)/shard_map/ppermute | solution.py:252
  117.6 10.2 %collective-permute-done.6.refs_5_ = bf16[2,64,256]{2,1,0:T(8,128)(2,1)S(1)} collective-permute-done((bf16[2,64,256]{2,1,0:T(8,128)(2,1)S(1)}, bf16[2,64,256]{2,1,0:T(8,128)(2,1)S(1)}, u32[]{:S(2)}, u32[]{:S(2)}) %collective-permute-start.6) | collective-permute-done | bytes 65568 | tf_op jit(solution)/shard_map/ppermute | solution.py:252
  127.7 2.8 %collective-permute-start.8 = (bf16[2,64,256]{2,1,0:T(8,128)(2,1)S(1)}, bf16[2,64,256]{2,1,0:T(8,128)(2,1)S(1)}, u32[]{:S(2)}, u32[]{:S(2)}) collective-permute-start(bf16[2,64,256]{2,1,0:T(8,128)(2,1)S(1)} %pad_maximum_fusion.refs_4_), channel_id=1, source_target_pairs={{0,6},{1,7},{2,0},{3,1},{4,2},{5,3},{6,4},{7,5},{8,14},{9,15},{10,... | collective-permute-start | bytes 196616 | tf_op jit(solution)/shard_map/ppermute | solution.py:252
  130.6 1.1 collective-permute-done.7.refs_6_
  131.7 3.3 %collective-permute-done.8.refs_7_ = bf16[2,64,256]{2,1,0:T(8,128)(2,1)S(1)} collective-permute-done((bf16[2,64,256]{2,1,0:T(8,128)(2,1)S(1)}, bf16[2,64,256]{2,1,0:T(8,128)(2,1)S(1)}, u32[]{:S(2)}, u32[]{:S(2)}) %collective-permute-start.8) | collective-permute-done | bytes 65568 | tf_op jit(solution)/shard_map/ppermute | solution.py:252
  135.0 0.0 collective-permute-done.2.refs_1_
  135.0 0.0 collective-permute-done.3.refs_2_
  135.0 0.0 collective-permute-done.4.refs_3_
  135.0 1.0 shard_map.88
  136.0 8.0 %collective-permute-start.9 = (f32[2,4,64,256]{3,2,1,0:T(8,128)S(1)}, f32[2,4,64,256]{3,2,1,0:T(8,128)S(1)}, u32[]{:S(2)}, u32[]{:S(2)}) collective-permute-start(f32[2,4,64,256]{3,2,1,0:T(8,128)S(1)} %get-tuple-element.36), channel_id=1, source_target_pairs={{0,1},{1,0},{2,3},{3,2},{4,5},{5,4},{6,7},{7,6},{8,9},{9,8},{10,11... | collective-permute-start | bytes 1572872 | tf_op jit(solution)/shard_map/ppermute | solution.py:256
  144.0 1.5 %collective-permute-done.9.b_ref = f32[2,4,64,256]{3,2,1,0:T(8,128)S(1)} collective-permute-done((f32[2,4,64,256]{3,2,1,0:T(8,128)S(1)}, f32[2,4,64,256]{3,2,1,0:T(8,128)S(1)}, u32[]{:S(2)}, u32[]{:S(2)}) %collective-permute-start.9) | collective-permute-done | bytes 524320 | tf_op jit(solution)/shard_map/ppermute | solution.py:256
  145.5 1.5 shard_map.89
  147.0 0.0 all-to-all-done.4.r_ref
  147.0 2.0 %shard_map.93 = (f32[64,13824]{1,0:T(8,128)}, f32[64,1]{1,0:T(8,128)S(1)}) custom-call(bf16[4,8,16,1792]{3,2,1,0:T(8,128)(2,1)S(1)} %all-to-all-done.4.r_ref), custom_call_target="tpu_custom_call" | custom-call | tf_op jit(solution)/shard_map/pallas_call | solution.py:236
  149.0 0.6 reduce
  (11 shorter events, 0.0 us)
Async XLA Ops:
  0.6 1.0 copy-start.1
  1.7 0.9 copy-start.5
  2.6 23.7 %copy-start = (bf16[64,13824]{1,0:T(8,128)(2,1)S(1)}, bf16[64,13824]{1,0:T(8,128)(2,1)}, u32[]{:S(2)}) copy-start(bf16[64,13824]{1,0:T(8,128)(2,1)} %w_ref.3) | copy-start | bytes 5308420
  21.9 4.4 %collective-permute-start = (bf16[4,2,4,64,256]{4,3,2,1,0:T(8,128)(2,1)S(1)}, bf16[4,2,4,64,256]{4,3,2,1,0:T(8,128)(2,1)}, u32[]{:S(2)}, u32[]{:S(2)}) collective-permute-start(bf16[4,2,4,64,256]{4,3,2,1,0:T(8,128)(2,1)S(1)} %all_to_all.25.xo_ref), channel_id=1, source_target_pairs={{0,1},{1,0},{2,3},{3,2},{4,5},{5,4},{6,7},{7,6},{8,9},{9,8},{10,11... | collective-permute-start | bytes 3145736 | tf_op jit(solution)/shard_map/ppermute | solution.py:256
  26.3 9.6 %copy-start.8 = (f32[64]{0:T(128)S(1)}, f32[64]{0:T(128)}, u32[]{:S(2)}) copy-start(f32[64]{0:T(128)} %param.7) | copy-start | bytes 772
  28.5 1.3 copy-start.3
  29.8 6.3 %copy-start.6 = (bf16[1,1,64,256]{3,2,1,0:T(8,128)(2,1)S(1)}, bf16[1,1,64,256]{3,2,1,0:T(8,128)(2,1)}, u32[]{:S(2)}) copy-start(bf16[1,1,64,256]{3,2,1,0:T(8,128)(2,1)} %param.8) | copy-start | bytes 98308
  29.8 6.3 %collective-permute-start.1 = (f32[64,256]{1,0:T(8,128)S(1)}, f32[64,256]{1,0:T(8,128)S(1)}, u32[]{:S(2)}, u32[]{:S(2)}) collective-permute-start(f32[64,256]{1,0:T(8,128)S(1)} %get-tuple-element.27), channel_id=1, source_target_pairs={{0,8},{8,16},{16,24},{24,32},{32,40},{40,48},{48,56},{56,64},{64,7... | collective-permute-start | bytes 196616 | tf_op jit(solution)/shard_map/ppermute | solution.py:248
  35.2 0.8 copy-start.7
  36.8 6.5 %collective-permute-start.5 = (bf16[64,256]{1,0:T(8,128)(2,1)S(1)}, bf16[64,256]{1,0:T(8,128)(2,1)S(1)}, u32[]{:S(2)}, u32[]{:S(2)}) collective-permute-start(bf16[64,256]{1,0:T(8,128)(2,1)S(1)} %get-tuple-element.34.dy_ref), channel_id=1, source_target_pairs={{8,0},{16,8},{24,16},{32,24},{40,32},{48,40},{56,48},{64,56},{72,6... | collective-permute-start | bytes 98312 | tf_op jit(solution)/shard_map/ppermute | solution.py:248
  43.3 1.6 %copy-start.4 = (bf16[2,4,512,256]{3,2,1,0:T(8,128)(2,1)S(1)}, bf16[2,4,512,256]{3,2,1,0:T(8,128)(2,1)}, u32[]{:S(2)}) copy-start(bf16[2,4,512,256]{3,2,1,0:T(8,128)(2,1)} %copy-done.3) | copy-start | bytes 6291460
  72.3 19.3 %all-to-all-start.2 = ((bf16[8,16,1792]{2,1,0:T(8,128)(2,1)}), bf16[8,16,1792]{2,1,0:T(8,128)(2,1)S(1)}, u32[]{:S(2)}, u32[]{:S(2)}) async-start(bf16[8,16,1792]{2,1,0:T(8,128)(2,1)} %shard_map.91), calls=%async_computation.2 | async-start | bytes 917504 | tf_op jit(solution)/shard_map/all_to_all | solution.py:297
  108.6 38.4 %all-to-all-start.4 = ((bf16[4,8,16,1792]{3,2,1,0:T(8,128)(2,1)}), bf16[4,8,16,1792]{3,2,1,0:T(8,128)(2,1)S(1)}, u32[]{:S(2)}, u32[]{:S(2)}) async-start(bf16[4,8,16,1792]{3,2,1,0:T(8,128)(2,1)} %broadcast_in_dim.2), calls=%async_computation.4 | async-start | bytes 3670016 | tf_op jit(solution)/shard_map/all_to_all | solution.py:300
  112.2 33.3 %copy-start.2 = (bf16[512,512]{1,0:T(8,128)(2,1)S(1)}, bf16[512,512]{1,0:T(8,128)(2,1)}, u32[]{:S(2)}) copy-start(bf16[512,512]{1,0:T(8,128)(2,1)} %constant.46.clone.m_ref) | copy-start | bytes 1572868
  112.3 22.7 %collective-permute-start.2 = (bf16[64,3456]{1,0:T(8,128)(2,1)}, bf16[64,3456]{1,0:T(8,128)(2,1)S(1)}, u32[]{:S(2)}, u32[]{:S(2)}) collective-permute-start(bf16[64,3456]{1,0:T(8,128)(2,1)} %copy-done.7), channel_id=1, source_target_pairs={{0,2},{1,3},{2,4},{3,5},{4,6},{5,7},{6,0},{7,1},{8,10},{9,11},{10,... | collective-permute-start | bytes 1327112 | tf_op jit(solution)/shard_map/ppermute | solution.py:252
  112.6 22.4 %collective-permute-start.3 = (bf16[64,3456]{1,0:T(8,128)(2,1)S(1)}, bf16[64,3456]{1,0:T(8,128)(2,1)S(1)}, u32[]{:S(2)}, u32[]{:S(2)}) collective-permute-start(bf16[64,3456]{1,0:T(8,128)(2,1)S(1)} %get-tuple-element.32), channel_id=1, source_target_pairs={{0,4},{1,5},{2,6},{3,7},{4,0},{5,1},{6,2},{7,3},{8,12},{9,13},{10,... | collective-permute-start | bytes 1327112 | tf_op jit(solution)/shard_map/ppermute | solution.py:252
  114.4 20.6 %collective-permute-start.4 = (bf16[64,3456]{1,0:T(8,128)(2,1)S(1)}, bf16[64,3456]{1,0:T(8,128)(2,1)S(1)}, u32[]{:S(2)}, u32[]{:S(2)}) collective-permute-start(bf16[64,3456]{1,0:T(8,128)(2,1)S(1)} %get-tuple-element.33), channel_id=1, source_target_pairs={{0,6},{1,7},{2,0},{3,1},{4,2},{5,3},{6,4},{7,5},{8,14},{9,15},{10,... | collective-permute-start | bytes 1327112 | tf_op jit(solution)/shard_map/ppermute | solution.py:252
  115.1 12.6 %collective-permute-start.6 = (bf16[2,64,256]{2,1,0:T(8,128)(2,1)S(1)}, bf16[2,64,256]{2,1,0:T(8,128)(2,1)S(1)}, u32[]{:S(2)}, u32[]{:S(2)}) collective-permute-start(bf16[2,64,256]{2,1,0:T(8,128)(2,1)S(1)} %pad_maximum_fusion.refs_4_), channel_id=1, source_target_pairs={{0,2},{1,3},{2,4},{3,5},{4,6},{5,7},{6,0},{7,1},{8,10},{9,11},{10,... | collective-permute-start | bytes 196616 | tf_op jit(solution)/shard_map/ppermute | solution.py:252
  116.0 15.8 %collective-permute-start.7 = (bf16[2,64,256]{2,1,0:T(8,128)(2,1)S(1)}, bf16[2,64,256]{2,1,0:T(8,128)(2,1)S(1)}, u32[]{:S(2)}, u32[]{:S(2)}) collective-permute-start(bf16[2,64,256]{2,1,0:T(8,128)(2,1)S(1)} %pad_maximum_fusion.refs_4_), channel_id=1, source_target_pairs={{0,4},{1,5},{2,6},{3,7},{4,0},{5,1},{6,2},{7,3},{8,12},{9,13},{10,... | collective-permute-start | bytes 196616 | tf_op jit(solution)/shard_map/ppermute | solution.py:252
  127.7 7.2 %collective-permute-start.8 = (bf16[2,64,256]{2,1,0:T(8,128)(2,1)S(1)}, bf16[2,64,256]{2,1,0:T(8,128)(2,1)S(1)}, u32[]{:S(2)}, u32[]{:S(2)}) collective-permute-start(bf16[2,64,256]{2,1,0:T(8,128)(2,1)S(1)} %pad_maximum_fusion.refs_4_), channel_id=1, source_target_pairs={{0,6},{1,7},{2,0},{3,1},{4,2},{5,3},{6,4},{7,5},{8,14},{9,15},{10,... | collective-permute-start | bytes 196616 | tf_op jit(solution)/shard_map/ppermute | solution.py:252
  136.0 9.6 %collective-permute-start.9 = (f32[2,4,64,256]{3,2,1,0:T(8,128)S(1)}, f32[2,4,64,256]{3,2,1,0:T(8,128)S(1)}, u32[]{:S(2)}, u32[]{:S(2)}) collective-permute-start(f32[2,4,64,256]{3,2,1,0:T(8,128)S(1)} %get-tuple-element.36), channel_id=1, source_target_pairs={{0,1},{1,0},{2,3},{3,2},{4,5},{5,4},{6,7},{7,6},{8,9},{9,8},{10,11... | collective-permute-start | bytes 1572872 | tf_op jit(solution)/shard_map/ppermute | solution.py:256
where the time goes:
time: 150 us
  blocking collectives  59.8 us (40%)
  starting transfers between devices  36.1 us (24%)
  waiting for transfers between devices  34.9 us (23%)
  Pallas kernels  10.3 us (7%)
  local copies, waits for them, and re-layouts  7.14 us (5%)
    all_to_all x1, blocking collectives, per_device(): terms = lax.all_to_all(terms, DS, 0, 0, axis_index_groups=Y_GROUPS)  25.5 us
    all_to_all x1, blocking collectives, per_device(): x_own = lax.all_to_all(copies, 'chan', 0, 0, axis_index_groups=X_GROUPS)  18.8 us
    all_to_all x1, blocking collectives, per_device(): terms = lax.all_to_all(terms, DS, 0, 0, axis_index_groups=Z_GROUPS)  15.6 us
    ppermute x6, waiting for transfers between devices, to_x(): return lax.ppermute(a, 'chan', [(i, (i + 2 * d) % 8) for i in range(8)])  14.6 us
    all_to_all x1, waiting for transfers between devices, per_device(): terms = lax.all_to_all(terms, DS, 0, 0, axis_index_groups=Z_GROUPS)  11.1 us
    pallas_call x10, Pallas kernels, call(): pl.pallas_call(kernel, out_shape=shapes, in_specs=[SMEM] * scalars + [VME...  10.3 us
    ppermute x2, starting transfers between devices, to_partner(): return lax.ppermute(a, 'chan', [(i, i ^ 1) for i in range(8)])  9.96 us
    all_to_all x1, starting transfers between devices, per_device(): terms = lax.all_to_all(terms, DS, 0, 0, axis_index_groups=Z_GROUPS)  8.19 us
  transfers between devices with their start and end apart: 12, of which 7 were waited for; matrix products, arithmetic and copies ran while one was open for 0% of the time, Pallas kernels for 2%

commit v1 on v0

--- a/solution.py
+++ b/solution.py
@@ -49,10 +49,11 @@
 
 def earlier(a, sy, sz):
     lane = lanes(a.shape)
+    width = a.shape[1]
     if sy:
-        a = jnp.where(lane >= 240, 0.0, pltpu.roll(a, 240, 1))
+        a = jnp.where(lane % 256 >= 240, 0.0, pltpu.roll(a, width - 16, 1))
     if sz:
-        a = jnp.where(lane % 16 == 15, 0.0, pltpu.roll(a, 255, 1))
+        a = jnp.where(lane % 16 == 15, 0.0, pltpu.roll(a, width - 1, 1))
     return a
 
 
@@ -65,7 +66,7 @@
                     o_ref[copy, p, c, :, h * 128 : (h + 1) * 128] = r[:, c * 128 : (c + 1) * 128]
 
 
-def forward_kernel(core_ref, xo_ref, xp_ref, w_ref, xs_ref, own_ref, next_ref):
+def forward_kernel(core_ref, xo_ref, xp_ref, w_ref, own_ref, next_ref, xs_ref):
     core = core_ref[0]
     mine = pl.multiple_of(core * 64, 64)
     other = pl.multiple_of(64 - core * 64, 64)
@@ -104,7 +105,9 @@
     t = jnp.tanh(root * (u + 0.044715 * (u * u * u)))
     act_ref[...] = (0.5 * u * (1.0 + t)).astype(BF)
     slope = 0.5 * (1.0 + t) + 0.5 * u * (1.0 - t * t) * (root * (1.0 + 3 * 0.044715 * (u * u)))
-    dy_ref[...] = (g_ref[...].astype(F32) * slope).astype(BF)
+    dy = (g_ref[...].astype(F32) * slope).astype(BF)
+    for copy in range(4):
+        dy_ref[copy] = dy
 
 
 def pair_block(total, shape):
@@ -113,45 +116,44 @@
     return jnp.where(lane == 0, hi, jnp.where(lane == 1, total - hi, 0.0)).astype(BF)
 
 
-def filter_grad_kernel(dy_ref, dn_ref, xs_ref, o_ref):
-    now = dy_ref[...].astype(F32)
-    nxt = dn_ref[...].astype(F32)
-    shifted = {}
-    for sy in range(2):
-        for sz in range(2):
-            shifted[0, sy, sz] = earlier(nxt, sy, sz).astype(BF)
-            shifted[1, sy, sz] = earlier(now, sy, sz).astype(BF)
+def filter_grad_kernel(where_ref, dy_ref, dn_ref, xo_ref, xp_ref, o_ref, both_ref, xs_ref):
+    mine = pl.multiple_of(where_ref[0] * 64, 64)
+    other = pl.multiple_of(64 - where_ref[0] * 64, 64)
+    for c in range(4):
+        for p in range(2):
+            for y in range(4):
+                xs_ref[c, pl.ds(p * 128 + mine, 64), y * 256 : y * 256 + 256] = xo_ref[y, p, c]
+                xs_ref[c, pl.ds(p * 128 + other, 64), y * 256 : y * 256 + 256] = xp_ref[y, p, c]
+    q = where_ref[1]
+    both_ref[0] = dy_ref[q]
+
+    @pl.when(q < 2)
+    def _():
+        both_ref[1] = dy_ref[lax.rem(q + 2, 4)]
+
+    @pl.when(q >= 2)
+    def _():
+        both_ref[1] = dn_ref[lax.rem(q, 2)]
+
+    now = jnp.concatenate([dy_ref[y] for y in range(4)], 1).astype(F32)
+    nxt = jnp.concatenate([dy_ref[2], dy_ref[3], dn_ref[0], dn_ref[1]], 1).astype(F32)
     for c in range(4):
         taps = taps_of(c)
-        for p, firsts in ((0, (1,)), (1, (2, 0))):
-            rows = [shifted[min(k1, 1), sy, sz] for k1 in firsts for _, sy, sz in taps]
+        for grads, firsts, rows in ((now, (1, 2), slice(0, 256)), (nxt, (0,), slice(128, 256))):
+            left = jnp.concatenate([earlier(grads, sy, sz).astype(BF) for _, sy, sz in taps], 0)
             r = lax.dot_general(
-                jnp.concatenate(rows, 0), xs_ref[p, c], (((1,), (1,)), ((), ())), preferred_element_type=F32
+                left, xs_ref[c, rows, :], (((1,), (1,)), ((), ())), preferred_element_type=F32
             ).astype(BF)
-            n = 0
-            for k1 in firsts:
-                for tap, _, _ in taps:
+            for n, (tap, _, _) in enumerate(taps):
+                for m, k1 in enumerate(firsts):
                     h, at = divmod(9 * k1 + tap, 14)
-                    for q in range(4):
-                        for fb in range(4):
-                            o_ref[q, fb * 2 + h, :, at * 128 : at * 128 + 128] = r[
-                                64 * n + 16 * fb : 64 * n + 16 * fb + 16, q * 128 : q * 128 + 128
-                            ]
-                    n += 1
+                    for fb in range(4):
+                        o_ref[fb * 2 + h, :, at * 128 : at * 128 + 128] = r[
+                            64 * n + 16 * fb : 64 * n + 16 * fb + 16, m * 128 : m * 128 + 128
+                        ]
     block = pair_block(jnp.sum(now, 1, keepdims=True), (64, 128))
-    for q in range(4):
-        for fb in range(4):
-            o_ref[q, fb * 2 + 1, :, 13 * 128 : 14 * 128] = block[16 * fb : 16 * fb + 16]
-
-
-def sum_y_kernel(r_ref, o_ref):
-    for z in range(8):
-        for at in range(0, 1792, 256):
-            total = sum(r_ref[s, z, :, at : at + 256].astype(F32) for s in range(4))
-            o_ref[z, :, at : at + 256] = total.astype(BF)
-            if z % 2 == 1 and at == 1536:
-                bias_total = total[:, 128:129] + total[:, 129:130]
-                o_ref[z, :, 1664:1792] = pair_block(bias_total, (16, 128))
+    for fb in range(4):
+        o_ref[fb * 2 + 1, :, 13 * 128 : 14 * 128] = block[16 * fb : 16 * fb + 16]
 
 
 def sum_z_kernel(odd_ref, r_ref, o_ref):
@@ -263,53 +265,68 @@
     z_odd = ((lax.axis_index("space") // 2) % 2).astype(jnp.int32).reshape(1)
     matrix = jnp.asarray(split_matrix(), BF)
 
+    q = ((lax.axis_index("space") % 2) * 2 + lax.axis_index("dp")).astype(jnp.int32)
+    where = jnp.stack([core[0], q])
+
     (copies,) = call(split_kernel, [((4, 2, 4, 64, 256), BF)], volumes.reshape(2, 64, 1024), matrix)
     x_own = lax.all_to_all(copies, "chan", 0, 0, axis_index_groups=X_GROUPS)
     x_partner = to_partner(x_own)
-    xs, own, following = call(
+    ring_own = lax.all_to_all(x_own, DS, 0, 0, axis_index_groups=Y_GROUPS)
+    ring_partner = to_partner(ring_own)
+    own, following = call(
         forward_kernel,
-        [((2, 4, 512, 256), BF), ((64, 256), F32), ((64, 256), F32)],
+        [((64, 256), F32), ((64, 256), F32)],
         core,
         x_own,
         x_partner,
         kernel,
         scalars=1,
+        scratch=[pltpu.VMEM((2, 4, 512, 256), BF)],
     )
     received = shift_space(following, 1)
     packed = call(pack_kernel, [((64, 3456), BF)] * 4, x, kernel, scalars=1)
     *packed, received = lax.optimization_barrier((*packed, received))
     weights = [packed[0]] + [to_x(packed[d], d) for d in range(1, 4)]
-    activation, dy = call(
+    activation, dy_copies = call(
         gelu_kernel,
-        [((64, 256), BF), ((64, 256), BF)],
+        [((64, 256), BF), ((4, 64, 256), BF)],
         own,
         received,
         bias.reshape(64, 1),
         act_grad.reshape(64, 256),
     )
-    dy_next = shift_space(dy, -1)
-    (terms,) = call(filter_grad_kernel, [((4, 8, 16, 1792), BF)], dy, dy_next, xs)
-    dys = jnp.stack([dy, dy_next])
-    grads = [dys] + [to_x(dys, d) for d in range(1, 4)]
-
-    terms = lax.all_to_all(terms, DS, 0, 0, axis_index_groups=Y_GROUPS)
-    (terms,) = call(sum_y_kernel, [((8, 16, 1792), BF)], terms)
+    dy = lax.all_to_all(dy_copies, DS, 0, 0, axis_index_groups=Y_GROUPS)
+    dy_next = shift_space(dy[:2], -2)
+    terms, both = call(
+        filter_grad_kernel,
+        [((8, 16, 1792), BF), ((2, 64, 256), BF)],
+        where,
+        dy,
+        dy_next,
+        ring_own,
+        ring_partner,
+        scalars=1,
+        scratch=[pltpu.VMEM((4, 256, 1024), BF)],
+    )
+    grads = [both] + [to_x(both, d) for d in range(1, 4)]
+
     terms = lax.all_to_all(terms, DS, 0, 0, axis_index_groups=Z_GROUPS)
+    *inputs, terms = lax.optimization_barrier((*weights, *grads, terms))
     (terms,) = call(sum_z_kernel, [((8, 16, 1792), BF)], z_odd, terms, scalars=1)
-    terms = lax.all_to_all(terms, DS, 0, 0, axis_index_groups=Z_GROUPS)
-    terms = lax.all_to_all(jnp.broadcast_to(terms[None], (4, 8, 16, 1792)), DS, 0, 0, axis_index_groups=Y_GROUPS)
-    grad_w, grad_b = call(filter_out_kernel, [((64, 13824), F32), ((64, 1), F32)], terms)
-
     mine, theirs = call(
         input_grad_kernel,
         [((2, 4, 64, 256), F32), ((2, 4, 64, 256), F32)],
         core,
-        *weights,
-        *grads,
+        *inputs,
         scalars=1,
         scratch=[pltpu.VMEM((128, 256), F32)],
     )
-    (grad_x,) = call(join_kernel, [((2, 64, 1024), BF)], mine, to_partner(theirs), matrix)
+    terms = lax.all_to_all(terms, DS, 0, 0, axis_index_groups=Z_GROUPS)
+    theirs = to_partner(theirs)
+    mine, theirs, terms = lax.optimization_barrier((mine, theirs, terms))
+    terms = lax.all_to_all(jnp.broadcast_to(terms[None], (4, 8, 16, 1792)), DS, 0, 0, axis_index_groups=Y_GROUPS)
+    grad_w, grad_b = call(filter_out_kernel, [((64, 13824), F32), ((64, 1), F32)], terms)
+    (grad_x,) = call(join_kernel, [((2, 64, 1024), BF)], mine, theirs, matrix)
     return (
         activation.reshape(1, 1, 64, 256),
         grad_x.reshape(1, 2, 64, 1024),

time: 150 us -> 156 us (1.040)
  the two profiles are of different devices: /device:TPU:1 before, /device:TPU:6 now
where the time goes in v1:
time: 156 us; the launch traced here: 155 us
  waiting for transfers between devices  73.7 us (47%)
  starting transfers between devices  45 us (29%)
  blocking collectives  17.8 us (11%)
  Pallas kernels  13.6 us (9%)
  local copies, waits for them, and re-layouts  3.54 us (2%)
    all_to_all x1, waiting for transfers between devices, per_device(): lax.all_to_all(jnp.broadcast_to(terms[None], (4, 8, 16, 1792)), DS, 0, 0,...  18.2 us
    all_to_all x1, blocking collectives, per_device(): x_own = lax.all_to_all(copies, 'chan', 0, 0, axis_index_groups=X_GROUPS)  17.8 us
    all_to_all x2, starting transfers between devices, per_device(): terms = lax.all_to_all(terms, DS, 0, 0, axis_index_groups=Z_GROUPS)  16.7 us
    ppermute x6, waiting for transfers between devices, to_x(): return lax.ppermute(a, 'chan', [(i, (i + 2 * d) % 8) for i in range(8)])  15.8 us
    all_to_all x1, waiting for transfers between devices, per_device(): ring_own = lax.all_to_all(x_own, DS, 0, 0, axis_index_groups=Y_GROUPS)  13.9 us
    pallas_call x9, Pallas kernels, call(): pl.pallas_call(kernel, out_shape=shapes, in_specs=[SMEM] * scalars + [VME...  13.6 us
    all_to_all x2, waiting for transfers between devices, per_device(): terms = lax.all_to_all(terms, DS, 0, 0, axis_index_groups=Z_GROUPS)  10.7 us
    ppermute x6, starting transfers between devices, to_x(): return lax.ppermute(a, 'chan', [(i, (i + 2 * d) % 8) for i in range(8)])  10.4 us
  transfers between devices with their start and end apart: 16, of which 10 were waited for; matrix products, arithmetic and copies ran while one was open for 0% of the time, Pallas kernels for 4%

profile of v1, /device:TPU:6, one launch (start us, length us, event | category | flops | bytes accessed | tf_op | source)
XLA Modules:
  0.0 155.2 jit_solution(16922693978674404829)
XLA Ops:
  0.6 0.0 copy-start.1
  0.6 1.0 copy-done.1
  1.7 0.9 copy-done.3
  2.6 0.5 shard_map.84
  3.2 0.0 copy-start
  3.2 17.8 %all_to_all.30.xo_ref = bf16[4,2,4,64,256]{4,3,2,1,0:T(8,128)(2,1)} all-to-all(bf16[4,2,4,64,256]{4,3,2,1,0:T(8,128)(2,1)S(1)} %shard_map.84), channel_id=1, replica_groups={{0,2,4,6},{1,3,5,7},{8,10,12,14},{9,11,13,15},{16,18,20,22},{17,19,21,2..., dimensions={0} | all-to-all | bytes 2097152 | tf_op jit(solution)/shard_map/all_to_all | solution.py:272
  21.0 4.5 %all-to-all-start.2 = ((bf16[4,2,4,64,256]{4,3,2,1,0:T(8,128)(2,1)}), bf16[4,2,4,64,256]{4,3,2,1,0:T(8,128)(2,1)S(1)}, u32[]{:S(2)}, u32[]{:S(2)}) async-start(bf16[4,2,4,64,256]{4,3,2,1,0:T(8,128)(2,1)} %all_to_all.30.xo_ref), calls=%async_computation.2 | async-start | bytes 2097152 | tf_op jit(solution)/shard_map/all_to_all | solution.py:274
  25.5 13.9 %all-to-all-done.2.xo_ref = bf16[4,2,4,64,256]{4,3,2,1,0:T(8,128)(2,1)S(1)} async-done(((bf16[4,2,4,64,256]{4,3,2,1,0:T(8,128)(2,1)}), bf16[4,2,4,64,256]{4,3,2,1,0:T(8,128)(2,1)S(1)}, u32[]{:S(2)}, u32[]{:S(2)}) %all-to-all-start.2) | async-done | bytes 1048608 | tf_op jit(solution)/shard_map/all_to_all | solution.py:274
  39.4 0.0 copy-start.7
  39.4 2.5 %shard_map.85 = (f32[64,256]{1,0:T(8,128)S(1)}, f32[64,256]{1,0:T(8,128)S(1)}) custom-call(s32[1]{0:T(128)} %bitcast.core_ref, bf16[4,2,4,64,256]{4,3,2,1,0:T(8,128)(2,1)} %all_to_all.30.xo_ref, bf16[4,2,4,64,256]{4,3,2,1,0:T(8,128)(2,1)} %collective-permute-done.xp_ref, bf16[64,13824]{1,0:T(8,128)(2,1)S(1)} %copy-done), custom_call_target="tpu_custom_call" | custom-call | tf_op jit(solution)/shard_map/pallas_call | solution.py:238
  41.9 0.0 copy-start.4
  41.9 2.5 %collective-permute-start.1 = (f32[64,256]{1,0:T(8,128)S(1)}, f32[64,256]{1,0:T(8,128)S(1)}, u32[]{:S(2)}, u32[]{:S(2)}) collective-permute-start(f32[64,256]{1,0:T(8,128)S(1)} %get-tuple-element.40), channel_id=1, source_target_pairs={{0,8},{8,16},{16,24},{24,32},{32,40},{40,48},{48,56},{56,64},{64,7... | collective-permute-start | bytes 196616 | tf_op jit(solution)/shard_map/ppermute | solution.py:250
  44.4 0.1 copy.10.b_ref
  44.5 1.1 shard_map.86
  45.7 0.7 collective-permute-done.1.from_ref
  46.4 0.0 copy-done.6
  46.4 0.8 shard_map.87
  47.2 5.8 %all-to-all-start.1 = ((bf16[4,64,256]{2,1,0:T(8,128)(2,1)}), bf16[4,64,256]{2,1,0:T(8,128)(2,1)S(1)}, u32[]{:S(2)}, u32[]{:S(2)}) async-start(bf16[4,64,256]{2,1,0:T(8,128)(2,1)} %get-tuple-element.47), calls=%async_computation.1 | async-start | bytes 262144 | tf_op jit(solution)/shard_map/all_to_all | solution.py:298
  53.1 6.0 %all-to-all-done.1.dy_ref = bf16[4,64,256]{2,1,0:T(8,128)(2,1)S(1)} async-done(((bf16[4,64,256]{2,1,0:T(8,128)(2,1)}), bf16[4,64,256]{2,1,0:T(8,128)(2,1)S(1)}, u32[]{:S(2)}, u32[]{:S(2)}) %all-to-all-start.1) | async-done | bytes 131104 | tf_op jit(solution)/shard_map/all_to_all | solution.py:298
  59.0 1.3 collective-permute-start.5
  60.3 0.1 pad_add_fusion.where_ref
  60.4 6.4 %collective-permute-done.5.dn_ref = bf16[2,64,256]{2,1,0:T(8,128)(2,1)S(1)} collective-permute-done((bf16[2,64,256]{2,1,0:T(8,128)(2,1)S(1)}, bf16[2,64,256]{2,1,0:T(8,128)(2,1)S(1)}, u32[]{:S(2)}, u32[]{:S(2)}) %collective-permute-start.5) | collective-permute-done | bytes 65568 | tf_op jit(solution)/shard_map/ppermute | solution.py:250
  66.8 0.0 collective-permute-done.6.xp_ref
  66.8 3.4 %shard_map.88 = (bf16[8,16,1792]{2,1,0:T(8,128)(2,1)}, bf16[2,64,256]{2,1,0:T(8,128)(2,1)S(1)}) custom-call(s32[2]{0:T(128)S(1)} %pad_add_fusion.where_ref, bf16[4,64,256]{2,1,0:T(8,128)(2,1)S(1)} %all-to-all-done.1.dy_ref, bf16[2,64,256]{2,1,0:T(8,128)(2,1)S(1)} %collective-permute-done.5.dn_ref, bf16[4,2,4,64,256]{4,3,2,1,0:T(8,128)(2,1)S(1)} %all-to-all-done.2.xo_ref, ...), custom_call_target="tpu_custom_call" | custom-call | tf_op jit(solution)/shard_map/pallas_call | solution.py:238
  70.2 9.8 %all-to-all-start.3 = ((bf16[8,16,1792]{2,1,0:T(8,128)(2,1)}), bf16[8,16,1792]{2,1,0:T(8,128)(2,1)S(1)}, u32[]{:S(2)}, u32[]{:S(2)}) async-start(bf16[8,16,1792]{2,1,0:T(8,128)(2,1)} %get-tuple-element.49), calls=%async_computation.3 | async-start | bytes 917504 | tf_op jit(solution)/shard_map/all_to_all | solution.py:313
  80.0 2.1 %collective-permute-start.2 = (bf16[64,3456]{1,0:T(8,128)(2,1)}, bf16[64,3456]{1,0:T(8,128)(2,1)S(1)}, u32[]{:S(2)}, u32[]{:S(2)}) collective-permute-start(bf16[64,3456]{1,0:T(8,128)(2,1)} %get-tuple-element.44), channel_id=1, source_target_pairs={{0,2},{1,3},{2,4},{3,5},{4,6},{5,7},{6,0},{7,1},{8,10},{9,11},{10,... | collective-permute-start | bytes 1327112 | tf_op jit(solution)/shard_map/ppermute | solution.py:254
  82.1 0.1 collective-permute-start.3
  82.2 1.3 collective-permute-start.4
  83.5 2.1 %collective-permute-start.9 = (bf16[2,64,256]{2,1,0:T(8,128)(2,1)S(1)}, bf16[2,64,256]{2,1,0:T(8,128)(2,1)S(1)}, u32[]{:S(2)}, u32[]{:S(2)}) collective-permute-start(bf16[2,64,256]{2,1,0:T(8,128)(2,1)S(1)} %get-tuple-element.54.refs_4_), channel_id=1, source_target_pairs={{0,6},{1,7},{2,0},{3,1},{4,2},{5,3},{6,4},{7,5},{8,14},{9,15},{10,... | collective-permute-start | bytes 196616 | tf_op jit(solution)/shard_map/ppermute | solution.py:254
  85.6 1.3 collective-permute-start.8
  86.9 13.9 %collective-permute-done.2.refs_1_ = bf16[64,3456]{1,0:T(8,128)(2,1)S(1)} collective-permute-done((bf16[64,3456]{1,0:T(8,128)(2,1)}, bf16[64,3456]{1,0:T(8,128)(2,1)S(1)}, u32[]{:S(2)}, u32[]{:S(2)}) %collective-permute-start.2) | collective-permute-done | bytes 442400 | tf_op jit(solution)/shard_map/ppermute | solution.py:254
  100.7 3.6 %collective-permute-start.7 = (bf16[2,64,256]{2,1,0:T(8,128)(2,1)S(1)}, bf16[2,64,256]{2,1,0:T(8,128)(2,1)S(1)}, u32[]{:S(2)}, u32[]{:S(2)}) collective-permute-start(bf16[2,64,256]{2,1,0:T(8,128)(2,1)S(1)} %get-tuple-element.54.refs_4_), channel_id=1, source_target_pairs={{0,2},{1,3},{2,4},{3,5},{4,6},{5,7},{6,0},{7,1},{8,10},{9,11},{10,... | collective-permute-start | bytes 196616 | tf_op jit(solution)/shard_map/ppermute | solution.py:254
  104.3 0.0 collective-permute-done.3.refs_2_
  104.3 0.0 collective-permute-done.4.refs_3_
  104.3 0.7 collective-permute-done.8.refs_6_
  105.0 1.1 collective-permute-done.7.refs_5_
  106.2 0.8 shard_map.90
  107.0 6.9 %all-to-all-start.4 = ((bf16[8,16,1792]{2,1,0:T(8,128)(2,1)}), bf16[8,16,1792]{2,1,0:T(8,128)(2,1)S(1)}, u32[]{:S(2)}, u32[]{:S(2)}) async-start(bf16[8,16,1792]{2,1,0:T(8,128)(2,1)} %shard_map.90), calls=%async_computation.4 | async-start | bytes 917504 | tf_op jit(solution)/shard_map/all_to_all | solution.py:324
  114.0 1.0 shard_map.89
  115.0 0.1 collective-permute-start.10
  115.1 1.9 %collective-permute-done.10.b_ref = f32[2,4,64,256]{3,2,1,0:T(8,128)S(1)} collective-permute-done((f32[2,4,64,256]{3,2,1,0:T(8,128)S(1)}, f32[2,4,64,256]{3,2,1,0:T(8,128)S(1)}, u32[]{:S(2)}, u32[]{:S(2)}) %collective-permute-start.10) | collective-permute-done | bytes 524320 | tf_op jit(solution)/shard_map/ppermute | solution.py:258
  117.0 10.7 %all-to-all-done.4 = bf16[8,16,1792]{2,1,0:T(8,128)(2,1)S(1)} async-done(((bf16[8,16,1792]{2,1,0:T(8,128)(2,1)}), bf16[8,16,1792]{2,1,0:T(8,128)(2,1)S(1)}, u32[]{:S(2)}, u32[]{:S(2)}) %all-to-all-start.4) | async-done | bytes 458784 | tf_op jit(solution)/shard_map/all_to_all | solution.py:324
  127.7 1.4 broadcast_in_dim.2
  129.1 3.7 %all-to-all-start.5 = ((bf16[4,8,16,1792]{3,2,1,0:T(8,128)(2,1)}), bf16[4,8,16,1792]{3,2,1,0:T(8,128)(2,1)S(1)}, u32[]{:S(2)}, u32[]{:S(2)}) async-start(bf16[4,8,16,1792]{3,2,1,0:T(8,128)(2,1)} %broadcast_in_dim.2), calls=%async_computation.5 | async-start | bytes 3670016 | tf_op jit(solution)/shard_map/all_to_all | solution.py:327
  132.8 1.5 shard_map.91
  134.3 18.2 %all-to-all-done.5.r_ref = bf16[4,8,16,1792]{3,2,1,0:T(8,128)(2,1)S(1)} async-done(((bf16[4,8,16,1792]{3,2,1,0:T(8,128)(2,1)}), bf16[4,8,16,1792]{3,2,1,0:T(8,128)(2,1)S(1)}, u32[]{:S(2)}, u32[]{:S(2)}) %all-to-all-start.5) | async-done | bytes 1835040 | tf_op jit(solution)/shard_map/all_to_all | solution.py:327
  152.5 2.0 %shard_map.92 = (f32[64,13824]{1,0:T(8,128)}, f32[64,1]{1,0:T(8,128)S(1)}) custom-call(bf16[4,8,16,1792]{3,2,1,0:T(8,128)(2,1)S(1)} %all-to-all-done.5.r_ref), custom_call_target="tpu_custom_call" | custom-call | tf_op jit(solution)/shard_map/pallas_call | solution.py:238
  154.5 0.6 reduce
  (15 shorter events, 0.0 us)
Async XLA Ops:
  0.6 1.0 copy-start.1
  1.7 0.9 copy-start.3
  3.2 36.2 %copy-start = (bf16[64,13824]{1,0:T(8,128)(2,1)S(1)}, bf16[64,13824]{1,0:T(8,128)(2,1)}, u32[]{:S(2)}) copy-start(bf16[64,13824]{1,0:T(8,128)(2,1)} %w_ref.3) | copy-start | bytes 5308420
  21.0 18.4 %all-to-all-start.2 = ((bf16[4,2,4,64,256]{4,3,2,1,0:T(8,128)(2,1)}), bf16[4,2,4,64,256]{4,3,2,1,0:T(8,128)(2,1)S(1)}, u32[]{:S(2)}, u32[]{:S(2)}) async-start(bf16[4,2,4,64,256]{4,3,2,1,0:T(8,128)(2,1)} %all_to_all.30.xo_ref), calls=%async_computation.2 | async-start | bytes 2097152 | tf_op jit(solution)/shard_map/all_to_all | solution.py:274
  25.5 13.9 %collective-permute-start = (bf16[4,2,4,64,256]{4,3,2,1,0:T(8,128)(2,1)}, bf16[4,2,4,64,256]{4,3,2,1,0:T(8,128)(2,1)}, u32[]{:S(2)}, u32[]{:S(2)}) collective-permute-start(bf16[4,2,4,64,256]{4,3,2,1,0:T(8,128)(2,1)} %all_to_all.30.xo_ref), channel_id=1, source_target_pairs={{0,1},{1,0},{2,3},{3,2},{4,5},{5,4},{6,7},{7,6},{8,9},{9,8},{10,11... | collective-permute-start | bytes 3145736 | tf_op jit(solution)/shard_map/ppermute | solution.py:258
  39.4 27.5 %collective-permute-start.6 = (bf16[4,2,4,64,256]{4,3,2,1,0:T(8,128)(2,1)S(1)}, bf16[4,2,4,64,256]{4,3,2,1,0:T(8,128)(2,1)}, u32[]{:S(2)}, u32[]{:S(2)}) collective-permute-start(bf16[4,2,4,64,256]{4,3,2,1,0:T(8,128)(2,1)S(1)} %all-to-all-done.2.xo_ref), channel_id=1, source_target_pairs={{0,1},{1,0},{2,3},{3,2},{4,5},{5,4},{6,7},{7,6},{8,9},{9,8},{10,11... | collective-permute-start | bytes 3145736 | tf_op jit(solution)/shard_map/ppermute | solution.py:258
  39.4 5.0 %copy-start.7 = (f32[64]{0:T(128)S(1)}, f32[64]{0:T(128)}, u32[]{:S(2)}) copy-start(f32[64]{0:T(128)} %param.7) | copy-start | bytes 772
  41.9 4.5 %copy-start.4 = (bf16[1,1,64,256]{3,2,1,0:T(8,128)(2,1)S(1)}, bf16[1,1,64,256]{3,2,1,0:T(8,128)(2,1)}, u32[]{:S(2)}) copy-start(bf16[1,1,64,256]{3,2,1,0:T(8,128)(2,1)} %param.8) | copy-start | bytes 98308
  41.9 4.5 %collective-permute-start.1 = (f32[64,256]{1,0:T(8,128)S(1)}, f32[64,256]{1,0:T(8,128)S(1)}, u32[]{:S(2)}, u32[]{:S(2)}) collective-permute-start(f32[64,256]{1,0:T(8,128)S(1)} %get-tuple-element.40), channel_id=1, source_target_pairs={{0,8},{8,16},{16,24},{24,32},{32,40},{40,48},{48,56},{56,64},{64,7... | collective-permute-start | bytes 196616 | tf_op jit(solution)/shard_map/ppermute | solution.py:250
  45.7 0.8 copy-start.6
  45.7 1.6 %copy-start.5 = (bf16[64,3456]{1,0:T(8,128)(2,1)}, bf16[64,3456]{1,0:T(8,128)(2,1)S(1)}, u32[]{:S(2)}) copy-start(bf16[64,3456]{1,0:T(8,128)(2,1)S(1)} %get-tuple-element.46) | copy-start | bytes 1327108
  47.2 11.8 %all-to-all-start.1 = ((bf16[4,64,256]{2,1,0:T(8,128)(2,1)}), bf16[4,64,256]{2,1,0:T(8,128)(2,1)S(1)}, u32[]{:S(2)}, u32[]{:S(2)}) async-start(bf16[4,64,256]{2,1,0:T(8,128)(2,1)} %get-tuple-element.47), calls=%async_computation.1 | async-start | bytes 262144 | tf_op jit(solution)/shard_map/all_to_all | solution.py:298
  59.0 7.8 %collective-permute-start.5 = (bf16[2,64,256]{2,1,0:T(8,128)(2,1)S(1)}, bf16[2,64,256]{2,1,0:T(8,128)(2,1)S(1)}, u32[]{:S(2)}, u32[]{:S(2)}) collective-permute-start(bf16[2,64,256]{2,1,0:T(8,128)(2,1)S(1)} %slice.4), channel_id=1, source_target_pairs={{16,0},{24,8},{32,16},{40,24},{48,32},{56,40},{64,48},{72,56},{80,... | collective-permute-start | bytes 196616 | tf_op jit(solution)/shard_map/ppermute | solution.py:250
  70.2 36.0 %all-to-all-start.3 = ((bf16[8,16,1792]{2,1,0:T(8,128)(2,1)}), bf16[8,16,1792]{2,1,0:T(8,128)(2,1)S(1)}, u32[]{:S(2)}, u32[]{:S(2)}) async-start(bf16[8,16,1792]{2,1,0:T(8,128)(2,1)} %get-tuple-element.49), calls=%async_computation.3 | async-start | bytes 917504 | tf_op jit(solution)/shard_map/all_to_all | solution.py:313
  80.0 20.7 %collective-permute-start.2 = (bf16[64,3456]{1,0:T(8,128)(2,1)}, bf16[64,3456]{1,0:T(8,128)(2,1)S(1)}, u32[]{:S(2)}, u32[]{:S(2)}) collective-permute-start(bf16[64,3456]{1,0:T(8,128)(2,1)} %get-tuple-element.44), channel_id=1, source_target_pairs={{0,2},{1,3},{2,4},{3,5},{4,6},{5,7},{6,0},{7,1},{8,10},{9,11},{10,... | collective-permute-start | bytes 1327112 | tf_op jit(solution)/shard_map/ppermute | solution.py:254
  82.1 22.2 %collective-permute-start.3 = (bf16[64,3456]{1,0:T(8,128)(2,1)}, bf16[64,3456]{1,0:T(8,128)(2,1)S(1)}, u32[]{:S(2)}, u32[]{:S(2)}) collective-permute-start(bf16[64,3456]{1,0:T(8,128)(2,1)} %copy-done.6), channel_id=1, source_target_pairs={{0,4},{1,5},{2,6},{3,7},{4,0},{5,1},{6,2},{7,3},{8,12},{9,13},{10,... | collective-permute-start | bytes 1327112 | tf_op jit(solution)/shard_map/ppermute | solution.py:254
  82.2 22.1 %collective-permute-start.4 = (bf16[64,3456]{1,0:T(8,128)(2,1)}, bf16[64,3456]{1,0:T(8,128)(2,1)S(1)}, u32[]{:S(2)}, u32[]{:S(2)}) collective-permute-start(bf16[64,3456]{1,0:T(8,128)(2,1)} %copy-done.5), channel_id=1, source_target_pairs={{0,6},{1,7},{2,0},{3,1},{4,2},{5,3},{6,4},{7,5},{8,14},{9,15},{10,... | collective-permute-start | bytes 1327112 | tf_op jit(solution)/shard_map/ppermute | solution.py:254
  83.5 20.8 %collective-permute-start.9 = (bf16[2,64,256]{2,1,0:T(8,128)(2,1)S(1)}, bf16[2,64,256]{2,1,0:T(8,128)(2,1)S(1)}, u32[]{:S(2)}, u32[]{:S(2)}) collective-permute-start(bf16[2,64,256]{2,1,0:T(8,128)(2,1)S(1)} %get-tuple-element.54.refs_4_), channel_id=1, source_target_pairs={{0,6},{1,7},{2,0},{3,1},{4,2},{5,3},{6,4},{7,5},{8,14},{9,15},{10,... | collective-permute-start | bytes 196616 | tf_op jit(solution)/shard_map/ppermute | solution.py:254
  85.6 19.5 %collective-permute-start.8 = (bf16[2,64,256]{2,1,0:T(8,128)(2,1)S(1)}, bf16[2,64,256]{2,1,0:T(8,128)(2,1)S(1)}, u32[]{:S(2)}, u32[]{:S(2)}) collective-permute-start(bf16[2,64,256]{2,1,0:T(8,128)(2,1)S(1)} %get-tuple-element.54.refs_4_), channel_id=1, source_target_pairs={{0,4},{1,5},{2,6},{3,7},{4,0},{5,1},{6,2},{7,3},{8,12},{9,13},{10,... | collective-permute-start | bytes 196616 | tf_op jit(solution)/shard_map/ppermute | solution.py:254
  100.7 5.5 %collective-permute-start.7 = (bf16[2,64,256]{2,1,0:T(8,128)(2,1)S(1)}, bf16[2,64,256]{2,1,0:T(8,128)(2,1)S(1)}, u32[]{:S(2)}, u32[]{:S(2)}) collective-permute-start(bf16[2,64,256]{2,1,0:T(8,128)(2,1)S(1)} %get-tuple-element.54.refs_4_), channel_id=1, source_target_pairs={{0,2},{1,3},{2,4},{3,5},{4,6},{5,7},{6,0},{7,1},{8,10},{9,11},{10,... | collective-permute-start | bytes 196616 | tf_op jit(solution)/shard_map/ppermute | solution.py:254
  107.0 20.7 %all-to-all-start.4 = ((bf16[8,16,1792]{2,1,0:T(8,128)(2,1)}), bf16[8,16,1792]{2,1,0:T(8,128)(2,1)S(1)}, u32[]{:S(2)}, u32[]{:S(2)}) async-start(bf16[8,16,1792]{2,1,0:T(8,128)(2,1)} %shard_map.90), calls=%async_computation.4 | async-start | bytes 917504 | tf_op jit(solution)/shard_map/all_to_all | solution.py:324
  115.0 2.0 %collective-permute-start.10 = (f32[2,4,64,256]{3,2,1,0:T(8,128)S(1)}, f32[2,4,64,256]{3,2,1,0:T(8,128)S(1)}, u32[]{:S(2)}, u32[]{:S(2)}) collective-permute-start(f32[2,4,64,256]{3,2,1,0:T(8,128)S(1)} %get-tuple-element.59), channel_id=1, source_target_pairs={{0,1},{1,0},{2,3},{3,2},{4,5},{5,4},{6,7},{7,6},{8,9},{9,8},{10,11... | collective-permute-start | bytes 1572872 | tf_op jit(solution)/shard_map/ppermute | solution.py:258
  129.1 3.7 %copy-start.2 = (bf16[512,512]{1,0:T(8,128)(2,1)S(1)}, bf16[512,512]{1,0:T(8,128)(2,1)}, u32[]{:S(2)}) copy-start(bf16[512,512]{1,0:T(8,128)(2,1)} %constant.55.clone.m_ref) | copy-start | bytes 1572868
  129.1 23.4 %all-to-all-start.5 = ((bf16[4,8,16,1792]{3,2,1,0:T(8,128)(2,1)}), bf16[4,8,16,1792]{3,2,1,0:T(8,128)(2,1)S(1)}, u32[]{:S(2)}, u32[]{:S(2)}) async-start(bf16[4,8,16,1792]{3,2,1,0:T(8,128)(2,1)} %broadcast_in_dim.2), calls=%async_computation.5 | async-start | bytes 3670016 | tf_op jit(solution)/shard_map/all_to_all | solution.py:327

commit v2 on v1

--- a/solution.py
+++ b/solution.py
@@ -116,42 +116,34 @@
     return jnp.where(lane == 0, hi, jnp.where(lane == 1, total - hi, 0.0)).astype(BF)
 
 
-def filter_grad_kernel(where_ref, dy_ref, dn_ref, xo_ref, xp_ref, o_ref, both_ref, xs_ref):
-    mine = pl.multiple_of(where_ref[0] * 64, 64)
-    other = pl.multiple_of(64 - where_ref[0] * 64, 64)
-    for c in range(4):
-        for p in range(2):
+def filter_grad_kernel(core_ref, dy_ref, xo_ref, xp_ref, e_ref, o_ref, xs_ref):
+    mine = pl.multiple_of(core_ref[0] * 64, 64)
+    other = pl.multiple_of(64 - core_ref[0] * 64, 64)
+    for at, x_ref, side in ((mine, xo_ref, 0), (other, xp_ref, 1)):
+        for c in range(4):
             for y in range(4):
-                xs_ref[c, pl.ds(p * 128 + mine, 64), y * 256 : y * 256 + 256] = xo_ref[y, p, c]
-                xs_ref[c, pl.ds(p * 128 + other, 64), y * 256 : y * 256 + 256] = xp_ref[y, p, c]
-    q = where_ref[1]
-    both_ref[0] = dy_ref[q]
-
-    @pl.when(q < 2)
-    def _():
-        both_ref[1] = dy_ref[lax.rem(q + 2, 4)]
-
-    @pl.when(q >= 2)
-    def _():
-        both_ref[1] = dn_ref[lax.rem(q, 2)]
-
-    now = jnp.concatenate([dy_ref[y] for y in range(4)], 1).astype(F32)
-    nxt = jnp.concatenate([dy_ref[2], dy_ref[3], dn_ref[0], dn_ref[1]], 1).astype(F32)
+                cells = slice(y * 256, y * 256 + 256)
+                xs_ref[c, pl.ds(at, 64), cells] = e_ref[side, y, c] if y < 2 else x_ref[y - 2, 1, c]
+                xs_ref[c, pl.ds(128 + at, 64), cells] = x_ref[y, 0, c]
+                xs_ref[c, pl.ds(256 + at, 64), cells] = x_ref[y, 1, c]
+    grads = jnp.concatenate([dy_ref[y] for y in range(4)], 1).astype(F32)
+    shifted = {(sy, sz): earlier(grads, sy, sz).astype(BF) for sy in range(2) for sz in range(2)}
     for c in range(4):
         taps = taps_of(c)
-        for grads, firsts, rows in ((now, (1, 2), slice(0, 256)), (nxt, (0,), slice(128, 256))):
-            left = jnp.concatenate([earlier(grads, sy, sz).astype(BF) for _, sy, sz in taps], 0)
-            r = lax.dot_general(
-                left, xs_ref[c, rows, :], (((1,), (1,)), ((), ())), preferred_element_type=F32
-            ).astype(BF)
-            for n, (tap, _, _) in enumerate(taps):
-                for m, k1 in enumerate(firsts):
-                    h, at = divmod(9 * k1 + tap, 14)
-                    for fb in range(4):
-                        o_ref[fb * 2 + h, :, at * 128 : at * 128 + 128] = r[
-                            64 * n + 16 * fb : 64 * n + 16 * fb + 16, m * 128 : m * 128 + 128
-                        ]
-    block = pair_block(jnp.sum(now, 1, keepdims=True), (64, 128))
+        r = lax.dot_general(
+            jnp.concatenate([shifted[sy, sz] for _, sy, sz in taps], 0),
+            xs_ref[c],
+            (((1,), (1,)), ((), ())),
+            preferred_element_type=F32,
+        ).astype(BF)
+        for n, (tap, _, _) in enumerate(taps):
+            for k1 in range(3):
+                h, at = divmod(9 * k1 + tap, 14)
+                for fb in range(4):
+                    o_ref[fb * 2 + h, :, at * 128 : at * 128 + 128] = r[
+                        64 * n + 16 * fb : 64 * n + 16 * fb + 16, k1 * 128 : k1 * 128 + 128
+                    ]
+    block = pair_block(jnp.sum(grads, 1, keepdims=True), (64, 128))
     for fb in range(4):
         o_ref[fb * 2 + 1, :, 13 * 128 : 14 * 128] = block[16 * fb : 16 * fb + 16]
 
@@ -218,6 +210,11 @@
             theirs_ref[p, c] = g_ref[pl.ds(other, 64), :]
 
 
+def edge_kernel(o_in, p_in, o_ref):
+    o_ref[0] = o_in[...]
+    o_ref[1] = p_in[...]
+
+
 def join_kernel(a_ref, b_ref, m_ref, o_ref):
     for p in range(2):
         for h in range(2):
@@ -265,14 +262,13 @@
     z_odd = ((lax.axis_index("space") // 2) % 2).astype(jnp.int32).reshape(1)
     matrix = jnp.asarray(split_matrix(), BF)
 
-    q = ((lax.axis_index("space") % 2) * 2 + lax.axis_index("dp")).astype(jnp.int32)
-    where = jnp.stack([core[0], q])
-
     (copies,) = call(split_kernel, [((4, 2, 4, 64, 256), BF)], volumes.reshape(2, 64, 1024), matrix)
     x_own = lax.all_to_all(copies, "chan", 0, 0, axis_index_groups=X_GROUPS)
+    packed = call(pack_kernel, [((64, 3456), BF)] * 4, x, kernel, scalars=1)
+    *packed, x_own = lax.optimization_barrier((*packed, x_own))
+    ring_own = lax.all_to_all(x_own, DS, 0, 0, axis_index_groups=Y_GROUPS)
     x_partner = to_partner(x_own)
-    ring_own = lax.all_to_all(x_own, DS, 0, 0, axis_index_groups=Y_GROUPS)
-    ring_partner = to_partner(ring_own)
+    near = [to_x(packed[1], 1), to_x(packed[3], 3)]
     own, following = call(
         forward_kernel,
         [((64, 256), F32), ((64, 256), F32)],
@@ -284,9 +280,9 @@
         scratch=[pltpu.VMEM((2, 4, 512, 256), BF)],
     )
     received = shift_space(following, 1)
-    packed = call(pack_kernel, [((64, 3456), BF)] * 4, x, kernel, scalars=1)
-    *packed, received = lax.optimization_barrier((*packed, received))
-    weights = [packed[0]] + [to_x(packed[d], d) for d in range(1, 4)]
+    ring_own, _, *near = lax.optimization_barrier((ring_own, received, *near))
+    far = to_x(packed[2], 2)
+    ring_partner = to_partner(ring_own)
     activation, dy_copies = call(
         gelu_kernel,
         [((64, 256), BF), ((4, 64, 256), BF)],
@@ -295,29 +291,42 @@
         bias.reshape(64, 1),
         act_grad.reshape(64, 256),
     )
+    piece = pl.BlockSpec((2, None, 4, 64, 256), lambda i: (1, 1, 0, 0, 0))
+    edge = pl.pallas_call(
+        edge_kernel,
+        grid=(1,),
+        out_shape=jax.ShapeDtypeStruct((2, 2, 4, 64, 256), BF),
+        in_specs=[piece, piece],
+        out_specs=pl.BlockSpec((2, 2, 4, 64, 256), lambda i: (0, 0, 0, 0, 0)),
+        compiler_params=PARAMS,
+    )(ring_own, ring_partner)
+    edge = shift_space(edge, 2)
     dy = lax.all_to_all(dy_copies, DS, 0, 0, axis_index_groups=Y_GROUPS)
-    dy_next = shift_space(dy[:2], -2)
-    terms, both = call(
+    dy_next = shift_space(dy_copies[0], -1)
+    (terms,) = call(
         filter_grad_kernel,
-        [((8, 16, 1792), BF), ((2, 64, 256), BF)],
-        where,
+        [((8, 16, 1792), BF)],
+        core,
         dy,
-        dy_next,
         ring_own,
         ring_partner,
+        edge,
         scalars=1,
-        scratch=[pltpu.VMEM((4, 256, 1024), BF)],
-    )
+        scratch=[pltpu.VMEM((4, 384, 1024), BF)],
+    )
+    terms, far, dy_next = lax.optimization_barrier((terms, far, dy_next))
+    terms = lax.all_to_all(terms, DS, 0, 0, axis_index_groups=Z_GROUPS)
+    both = jnp.stack([dy_copies[0], dy_next])
     grads = [both] + [to_x(both, d) for d in range(1, 4)]
-
-    terms = lax.all_to_all(terms, DS, 0, 0, axis_index_groups=Z_GROUPS)
-    *inputs, terms = lax.optimization_barrier((*weights, *grads, terms))
+    weights = [packed[0], near[0], far, near[1]]
+    *grads, terms = lax.optimization_barrier((*grads, terms))
     (terms,) = call(sum_z_kernel, [((8, 16, 1792), BF)], z_odd, terms, scalars=1)
     mine, theirs = call(
         input_grad_kernel,
         [((2, 4, 64, 256), F32), ((2, 4, 64, 256), F32)],
         core,
-        *inputs,
+        *weights,
+        *grads,
         scalars=1,
         scratch=[pltpu.VMEM((128, 256), F32)],
     )

time: 156 us -> 139 us (0.89)
  the two profiles are of different devices: /device:TPU:6 before, /device:TPU:32 now
where the time goes in v2:
time: 139 us; the launch traced here: 137 us
  waiting for transfers between devices  61.7 us (44%)
  starting transfers between devices  51.7 us (37%)
  Pallas kernels  14.1 us (10%)
  local copies, waits for them, and re-layouts  8.07 us (6%)
    all_to_all x1, waiting for transfers between devices, per_device(): lax.all_to_all(jnp.broadcast_to(terms[None], (4, 8, 16, 1792)), DS, 0, 0,...  18.3 us
    all_to_all x2, waiting for transfers between devices, per_device(): terms = lax.all_to_all(terms, DS, 0, 0, axis_index_groups=Z_GROUPS)  15.2 us
    all_to_all x2, starting transfers between devices, per_device(): terms = lax.all_to_all(terms, DS, 0, 0, axis_index_groups=Z_GROUPS)  14.6 us
    ppermute x3, starting transfers between devices, shift_space(): lax.ppermute(a, 'space', [(i, i + by) for i in range(16) if 0 <= i + by <...  14.2 us
    pallas_call x9, Pallas kernels, call(): pl.pallas_call(kernel, out_shape=shapes, in_specs=[SMEM] * scalars + [VME...  14 us
    all_to_all x1, waiting for transfers between devices, per_device(): x_own = lax.all_to_all(copies, 'chan', 0, 0, axis_index_groups=X_GROUPS)  12 us
    ppermute x6, waiting for transfers between devices, to_x(): return lax.ppermute(a, 'chan', [(i, (i + 2 * d) % 8) for i in range(8)])  7.64 us
    ppermute x6, starting transfers between devices, to_x(): return lax.ppermute(a, 'chan', [(i, (i + 2 * d) % 8) for i in range(8)])  6.95 us
  transfers between devices with their start and end apart: 18, of which 13 were waited for; matrix products, arithmetic and copies ran while one was open for 1% of the time, Pallas kernels for 7%

profile of v2, /device:TPU:32, one launch (start us, length us, event | category | flops | bytes accessed | tf_op | source)
XLA Modules:
  0.0 137.0 jit_solution(12530801884047547846)
XLA Ops:
  0.6 1.0 copy-done.1
  1.7 0.9 copy-done.7
  2.6 1.5 %shard_map.85 = bf16[4,2,4,64,256]{4,3,2,1,0:T(8,128)(2,1)} custom-call(bf16[2,64,1024]{2,1,0:T(8,128)(2,1)S(1)} %bitcast.11, bf16[512,512]{1,0:T(8,128)(2,1)S(1)} %copy-done.1), custom_call_target="tpu_custom_call" | custom-call | tf_op jit(solution)/shard_map/pallas_call | solution.py:235
  4.1 4.3 %all-to-all-start = ((bf16[4,2,4,64,256]{4,3,2,1,0:T(8,128)(2,1)}), bf16[4,2,4,64,256]{4,3,2,1,0:T(8,128)(2,1)}, u32[]{:S(2)}, u32[]{:S(2)}) async-start(bf16[4,2,4,64,256]{4,3,2,1,0:T(8,128)(2,1)} %shard_map.85), calls=%async_computation | async-start | bytes 2097152 | tf_op jit(solution)/shard_map/all_to_all | solution.py:266
  8.4 0.4 shard_map.84
  8.8 0.8 copy-done.3
  9.6 0.7 copy-done.9
  10.4 0.8 copy-done.10
  11.1 0.8 copy-done.11
  11.9 12.0 %all-to-all-done.xo_ref = bf16[4,2,4,64,256]{4,3,2,1,0:T(8,128)(2,1)} async-done(((bf16[4,2,4,64,256]{4,3,2,1,0:T(8,128)(2,1)}), bf16[4,2,4,64,256]{4,3,2,1,0:T(8,128)(2,1)}, u32[]{:S(2)}, u32[]{:S(2)}) %all-to-all-start) | async-done | bytes 1048608 | tf_op jit(solution)/shard_map/all_to_all | solution.py:266
  23.8 4.5 %all-to-all-start.1 = ((bf16[4,2,4,64,256]{4,3,2,1,0:T(8,128)(2,1)}), bf16[4,2,4,64,256]{4,3,2,1,0:T(8,128)(2,1)S(1)}, u32[]{:S(2)}, u32[]{:S(2)}) async-start(bf16[4,2,4,64,256]{4,3,2,1,0:T(8,128)(2,1)} %all-to-all-done.xo_ref), calls=%async_computation.1 | async-start | bytes 2097152 | tf_op jit(solution)/shard_map/all_to_all | solution.py:269
  28.3 0.6 collective-permute-start.2
  28.9 2.7 %collective-permute-start.3 = (bf16[64,3456]{1,0:T(8,128)(2,1)}, bf16[64,3456]{1,0:T(8,128)(2,1)}, u32[]{:S(2)}, u32[]{:S(2)}) collective-permute-start(bf16[64,3456]{1,0:T(8,128)(2,1)} %copy-done.10), channel_id=1, source_target_pairs={{0,6},{1,7},{2,0},{3,1},{4,2},{5,3},{6,4},{7,5},{8,14},{9,15},{10,... | collective-permute-start | bytes 1327112 | tf_op jit(solution)/shard_map/ppermute | solution.py:251
  31.5 2.5 %shard_map.86 = (f32[64,256]{1,0:T(8,128)S(1)}, f32[64,256]{1,0:T(8,128)S(1)}) custom-call(s32[1]{0:T(128)} %bitcast.core_ref, bf16[4,2,4,64,256]{4,3,2,1,0:T(8,128)(2,1)} %all-to-all-done.xo_ref, bf16[4,2,4,64,256]{4,3,2,1,0:T(8,128)(2,1)} %collective-permute-done.xp_ref, bf16[64,13824]{1,0:T(8,128)(2,1)S(1)} %copy-done), custom_call_target="tpu_custom_call" | custom-call | tf_op jit(solution)/shard_map/pallas_call | solution.py:235
  34.1 5.4 %collective-permute-start.1 = (f32[64,256]{1,0:T(8,128)S(1)}, f32[64,256]{1,0:T(8,128)S(1)}, u32[]{:S(2)}, u32[]{:S(2)}) collective-permute-start(f32[64,256]{1,0:T(8,128)S(1)} %get-tuple-element.41), channel_id=1, source_target_pairs={{0,8},{8,16},{16,24},{24,32},{32,40},{40,48},{48,56},{56,64},{64,7... | collective-permute-start | bytes 196616 | tf_op jit(solution)/shard_map/ppermute | solution.py:247
  39.5 2.5 %collective-permute-done.2.refs_1_ = bf16[64,3456]{1,0:T(8,128)(2,1)S(1)} collective-permute-done((bf16[64,3456]{1,0:T(8,128)(2,1)}, bf16[64,3456]{1,0:T(8,128)(2,1)S(1)}, u32[]{:S(2)}, u32[]{:S(2)}) %collective-permute-start.2) | collective-permute-done | bytes 442400 | tf_op jit(solution)/shard_map/ppermute | solution.py:251
  42.0 0.8 copy-done.5
  42.8 2.7 %all-to-all-done.1.o_in.xo_ref = bf16[4,2,4,64,256]{4,3,2,1,0:T(8,128)(2,1)S(1)} async-done(((bf16[4,2,4,64,256]{4,3,2,1,0:T(8,128)(2,1)}), bf16[4,2,4,64,256]{4,3,2,1,0:T(8,128)(2,1)S(1)}, u32[]{:S(2)}, u32[]{:S(2)}) %all-to-all-start.1) | async-done | bytes 1048608 | tf_op jit(solution)/shard_map/all_to_all | solution.py:269
  45.5 2.7 %collective-permute-done.4.p_in.xp_ref = bf16[4,2,4,64,256]{4,3,2,1,0:T(8,128)(2,1)S(1)} collective-permute-done((bf16[4,2,4,64,256]{4,3,2,1,0:T(8,128)(2,1)S(1)}, bf16[4,2,4,64,256]{4,3,2,1,0:T(8,128)(2,1)S(1)}, u32[]{:S(2)}, u32[]{:S(2)}) %collective-permute-start.4) | collective-permute-done | bytes 1048608 | tf_op jit(solution)/shard_map/ppermute | solution.py:255
  48.2 3.8 %collective-permute-start.5 = (bf16[2,2,4,64,256]{4,3,2,1,0:T(8,128)(2,1)S(1)}, bf16[2,2,4,64,256]{4,3,2,1,0:T(8,128)(2,1)S(1)}, u32[]{:S(2)}, u32[]{:S(2)}) collective-permute-start(bf16[2,2,4,64,256]{4,3,2,1,0:T(8,128)(2,1)S(1)} %shard_map.88), channel_id=1, source_target_pairs={{0,16},{8,24},{16,32},{24,40},{32,48},{40,56},{48,64},{56,72},{64,... | collective-permute-start | bytes 1572872 | tf_op jit(solution)/shard_map/ppermute | solution.py:247
  52.0 0.6 collective-permute-start.6
  52.7 0.1 copy.10.b_ref
  52.8 0.8 shard_map.87
  53.6 3.3 %all-to-all-start.2 = ((bf16[4,64,256]{2,1,0:T(8,128)(2,1)}), bf16[4,64,256]{2,1,0:T(8,128)(2,1)S(1)}, u32[]{:S(2)}, u32[]{:S(2)}) async-start(bf16[4,64,256]{2,1,0:T(8,128)(2,1)} %get-tuple-element.47), calls=%async_computation.2 | async-start | bytes 262144 | tf_op jit(solution)/shard_map/all_to_all | solution.py:304
  56.9 0.8 fusion
  57.6 5.0 %collective-permute-start.7 = (bf16[64,256]{1,0:T(8,128)(2,1)S(1)}, bf16[64,256]{1,0:T(8,128)(2,1)S(1)}, u32[]{:S(2)}, u32[]{:S(2)}) collective-permute-start(bf16[64,256]{1,0:T(8,128)(2,1)S(1)} %get-tuple-element.67), channel_id=1, source_target_pairs={{8,0},{16,8},{24,16},{32,24},{40,32},{48,40},{56,48},{64,56},{72,6... | collective-permute-start | bytes 98312 | tf_op jit(solution)/shard_map/ppermute | solution.py:247
  62.6 0.2 all-to-all-done.2.dy_ref
  62.8 1.2 collective-permute-done.5.e_ref
  64.0 2.3 %shard_map.89 = bf16[8,16,1792]{2,1,0:T(8,128)(2,1)} custom-call(s32[1]{0:T(128)} %bitcast.core_ref, bf16[4,64,256]{2,1,0:T(8,128)(2,1)S(1)} %all-to-all-done.2.dy_ref, bf16[4,2,4,64,256]{4,3,2,1,0:T(8,128)(2,1)S(1)} %all-to-all-done.1.o_in.xo_ref, bf16[4,2,4,64,256]{4,3,2,1,0:T(8,128)(2,1)S(1)} %collective-permute-done.4.p_in.xp_ref, ...), custom_call_target="tpu_custom_call" | custom-call | tf_op jit(solution)/shard_map/pallas_call | solution.py:235
  66.3 9.9 %all-to-all-start.3 = ((bf16[8,16,1792]{2,1,0:T(8,128)(2,1)}), bf16[8,16,1792]{2,1,0:T(8,128)(2,1)S(1)}, u32[]{:S(2)}, u32[]{:S(2)}) async-start(bf16[8,16,1792]{2,1,0:T(8,128)(2,1)} %shard_map.89), calls=%async_computation.3 | async-start | bytes 917504 | tf_op jit(solution)/shard_map/all_to_all | solution.py:318
  76.3 1.4 collective-permute-start.10
  77.6 1.3 collective-permute-start.9
  79.0 0.4 collective-permute-start.8
  79.3 1.3 collective-permute-done.10.refs_7_
  80.6 2.8 %collective-permute-done.9.refs_6_ = bf16[2,64,256]{2,1,0:T(8,128)(2,1)S(1)} collective-permute-done((bf16[2,64,256]{2,1,0:T(8,128)(2,1)S(1)}, bf16[2,64,256]{2,1,0:T(8,128)(2,1)S(1)}, u32[]{:S(2)}, u32[]{:S(2)}) %collective-permute-start.9) | collective-permute-done | bytes 65568 | tf_op jit(solution)/shard_map/ppermute | solution.py:251
  83.4 1.1 collective-permute-done.8.refs_5_
  84.4 6.0 %all-to-all-done.3.r_ref = bf16[8,16,1792]{2,1,0:T(8,128)(2,1)S(1)} async-done(((bf16[8,16,1792]{2,1,0:T(8,128)(2,1)}), bf16[8,16,1792]{2,1,0:T(8,128)(2,1)S(1)}, u32[]{:S(2)}, u32[]{:S(2)}) %all-to-all-start.3) | async-done | bytes 458784 | tf_op jit(solution)/shard_map/all_to_all | solution.py:318
  90.5 1.0 shard_map.91
  91.4 4.7 %all-to-all-start.4 = ((bf16[8,16,1792]{2,1,0:T(8,128)(2,1)}), bf16[8,16,1792]{2,1,0:T(8,128)(2,1)S(1)}, u32[]{:S(2)}, u32[]{:S(2)}) async-start(bf16[8,16,1792]{2,1,0:T(8,128)(2,1)} %shard_map.91), calls=%async_computation.4 | async-start | bytes 917504 | tf_op jit(solution)/shard_map/all_to_all | solution.py:333
  96.1 2.1 %shard_map.90 = (f32[2,4,64,256]{3,2,1,0:T(8,128)S(1)}, f32[2,4,64,256]{3,2,1,0:T(8,128)S(1)}) custom-call(s32[1]{0:T(128)} %bitcast.core_ref, bf16[64,3456]{1,0:T(8,128)(2,1)S(1)} %copy-done.4, bf16[64,3456]{1,0:T(8,128)(2,1)S(1)} %copy-done.6, bf16[64,3456]{1,0:T(8,128)(2,1)} %collective-permute-done.6.refs_2_, ...), custom_call_target="tpu_custom_call" | custom-call | tf_op jit(solution)/shard_map/pallas_call | solution.py:235
  98.4 1.9 %collective-permute-done.11.b_ref = f32[2,4,64,256]{3,2,1,0:T(8,128)S(1)} collective-permute-done((f32[2,4,64,256]{3,2,1,0:T(8,128)S(1)}, f32[2,4,64,256]{3,2,1,0:T(8,128)S(1)}, u32[]{:S(2)}, u32[]{:S(2)}) %collective-permute-start.11) | collective-permute-done | bytes 524320 | tf_op jit(solution)/shard_map/ppermute | solution.py:255
  100.3 9.2 %all-to-all-done.4 = bf16[8,16,1792]{2,1,0:T(8,128)(2,1)S(1)} async-done(((bf16[8,16,1792]{2,1,0:T(8,128)(2,1)}), bf16[8,16,1792]{2,1,0:T(8,128)(2,1)S(1)}, u32[]{:S(2)}, u32[]{:S(2)}) %all-to-all-start.4) | async-done | bytes 458784 | tf_op jit(solution)/shard_map/all_to_all | solution.py:333
  109.5 1.4 %broadcast_in_dim.2 = bf16[4,8,16,1792]{3,2,1,0:T(8,128)(2,1)} broadcast(bf16[8,16,1792]{2,1,0:T(8,128)(2,1)S(1)} %all-to-all-done.4), dimensions={1,2,3} | broadcast | bytes 2293760 | tf_op jit(solution)/shard_map/broadcast_in_dim | solution.py:336
  110.9 3.7 %all-to-all-start.5 = ((bf16[4,8,16,1792]{3,2,1,0:T(8,128)(2,1)}), bf16[4,8,16,1792]{3,2,1,0:T(8,128)(2,1)S(1)}, u32[]{:S(2)}, u32[]{:S(2)}) async-start(bf16[4,8,16,1792]{3,2,1,0:T(8,128)(2,1)} %broadcast_in_dim.2), calls=%async_computation.5 | async-start | bytes 3670016 | tf_op jit(solution)/shard_map/all_to_all | solution.py:336
  114.6 1.5 %shard_map.92 = bf16[2,64,1024]{2,1,0:T(8,128)(2,1)} custom-call(f32[2,4,64,256]{3,2,1,0:T(8,128)S(1)} %get-tuple-element.61.a_ref, f32[2,4,64,256]{3,2,1,0:T(8,128)S(1)} %collective-permute-done.11.b_ref, bf16[512,512]{1,0:T(8,128)(2,1)S(1)} %copy-done.2), custom_call_target="tpu_custom_call" | custom-call | tf_op jit(solution)/shard_map/pallas_call | solution.py:235
  116.1 18.3 %all-to-all-done.5.r_ref = bf16[4,8,16,1792]{3,2,1,0:T(8,128)(2,1)S(1)} async-done(((bf16[4,8,16,1792]{3,2,1,0:T(8,128)(2,1)}), bf16[4,8,16,1792]{3,2,1,0:T(8,128)(2,1)S(1)}, u32[]{:S(2)}, u32[]{:S(2)}) %all-to-all-start.5) | async-done | bytes 1835040 | tf_op jit(solution)/shard_map/all_to_all | solution.py:336
  134.3 2.0 %shard_map.93 = (f32[64,13824]{1,0:T(8,128)}, f32[64,1]{1,0:T(8,128)S(1)}) custom-call(bf16[4,8,16,1792]{3,2,1,0:T(8,128)(2,1)S(1)} %all-to-all-done.5.r_ref), custom_call_target="tpu_custom_call" | custom-call | tf_op jit(solution)/shard_map/pallas_call | solution.py:235
  136.3 0.6 reduce
  (29 shorter events, 0.2 us)
Async XLA Ops:
  0.6 1.0 copy-start.1
  1.7 0.9 copy-start.7
  2.6 5.8 %copy-start = (bf16[64,13824]{1,0:T(8,128)(2,1)S(1)}, bf16[64,13824]{1,0:T(8,128)(2,1)}, u32[]{:S(2)}) copy-start(bf16[64,13824]{1,0:T(8,128)(2,1)} %w_ref.3) | copy-start | bytes 5308420
  4.1 19.7 %all-to-all-start = ((bf16[4,2,4,64,256]{4,3,2,1,0:T(8,128)(2,1)}), bf16[4,2,4,64,256]{4,3,2,1,0:T(8,128)(2,1)}, u32[]{:S(2)}, u32[]{:S(2)}) async-start(bf16[4,2,4,64,256]{4,3,2,1,0:T(8,128)(2,1)} %shard_map.85), calls=%async_computation | async-start | bytes 2097152 | tf_op jit(solution)/shard_map/all_to_all | solution.py:266
  8.8 0.8 copy-start.3
  9.6 0.8 copy-start.9
  10.4 0.8 copy-start.10
  11.1 0.8 copy-start.11
  23.8 7.7 %collective-permute-start = (bf16[4,2,4,64,256]{4,3,2,1,0:T(8,128)(2,1)}, bf16[4,2,4,64,256]{4,3,2,1,0:T(8,128)(2,1)}, u32[]{:S(2)}, u32[]{:S(2)}) collective-permute-start(bf16[4,2,4,64,256]{4,3,2,1,0:T(8,128)(2,1)} %all-to-all-done.xo_ref), channel_id=1, source_target_pairs={{0,1},{1,0},{2,3},{3,2},{4,5},{5,4},{6,7},{7,6},{8,9},{9,8},{10,11... | collective-permute-start | bytes 3145736 | tf_op jit(solution)/shard_map/ppermute | solution.py:255
  23.8 21.6 %all-to-all-start.1 = ((bf16[4,2,4,64,256]{4,3,2,1,0:T(8,128)(2,1)}), bf16[4,2,4,64,256]{4,3,2,1,0:T(8,128)(2,1)S(1)}, u32[]{:S(2)}, u32[]{:S(2)}) async-start(bf16[4,2,4,64,256]{4,3,2,1,0:T(8,128)(2,1)} %all-to-all-done.xo_ref), calls=%async_computation.1 | async-start | bytes 2097152 | tf_op jit(solution)/shard_map/all_to_all | solution.py:269
  28.3 13.7 %collective-permute-start.2 = (bf16[64,3456]{1,0:T(8,128)(2,1)}, bf16[64,3456]{1,0:T(8,128)(2,1)S(1)}, u32[]{:S(2)}, u32[]{:S(2)}) collective-permute-start(bf16[64,3456]{1,0:T(8,128)(2,1)} %copy-done.11), channel_id=1, source_target_pairs={{0,2},{1,3},{2,4},{3,5},{4,6},{5,7},{6,0},{7,1},{8,10},{9,11},{10,... | collective-permute-start | bytes 1327112 | tf_op jit(solution)/shard_map/ppermute | solution.py:251
  28.9 13.9 %collective-permute-start.3 = (bf16[64,3456]{1,0:T(8,128)(2,1)}, bf16[64,3456]{1,0:T(8,128)(2,1)}, u32[]{:S(2)}, u32[]{:S(2)}) collective-permute-start(bf16[64,3456]{1,0:T(8,128)(2,1)} %copy-done.10), channel_id=1, source_target_pairs={{0,6},{1,7},{2,0},{3,1},{4,2},{5,3},{6,4},{7,5},{8,14},{9,15},{10,... | collective-permute-start | bytes 1327112 | tf_op jit(solution)/shard_map/ppermute | solution.py:251
  34.0 18.6 %copy-start.12 = (f32[64]{0:T(128)S(1)}, f32[64]{0:T(128)}, u32[]{:S(2)}) copy-start(f32[64]{0:T(128)} %param.7) | copy-start | bytes 772
  34.1 18.7 %copy-start.8 = (bf16[1,1,64,256]{3,2,1,0:T(8,128)(2,1)S(1)}, bf16[1,1,64,256]{3,2,1,0:T(8,128)(2,1)}, u32[]{:S(2)}) copy-start(bf16[1,1,64,256]{3,2,1,0:T(8,128)(2,1)} %param.8) | copy-start | bytes 98308
  34.1 11.4 %collective-permute-start.1 = (f32[64,256]{1,0:T(8,128)S(1)}, f32[64,256]{1,0:T(8,128)S(1)}, u32[]{:S(2)}, u32[]{:S(2)}) collective-permute-start(f32[64,256]{1,0:T(8,128)S(1)} %get-tuple-element.41), channel_id=1, source_target_pairs={{0,8},{8,16},{16,24},{24,32},{32,40},{40,48},{48,56},{56,64},{64,7... | collective-permute-start | bytes 196616 | tf_op jit(solution)/shard_map/ppermute | solution.py:247
  42.0 0.8 copy-start.5
  45.5 2.7 %collective-permute-start.4 = (bf16[4,2,4,64,256]{4,3,2,1,0:T(8,128)(2,1)S(1)}, bf16[4,2,4,64,256]{4,3,2,1,0:T(8,128)(2,1)S(1)}, u32[]{:S(2)}, u32[]{:S(2)}) collective-permute-start(bf16[4,2,4,64,256]{4,3,2,1,0:T(8,128)(2,1)S(1)} %all-to-all-done.1.o_in.xo_ref), channel_id=1, source_target_pairs={{0,1},{1,0},{2,3},{3,2},{4,5},{5,4},{6,7},{7,6},{8,9},{9,8},{10,11... | collective-permute-start | bytes 3145736 | tf_op jit(solution)/shard_map/ppermute | solution.py:255
  48.2 15.9 %collective-permute-start.5 = (bf16[2,2,4,64,256]{4,3,2,1,0:T(8,128)(2,1)S(1)}, bf16[2,2,4,64,256]{4,3,2,1,0:T(8,128)(2,1)S(1)}, u32[]{:S(2)}, u32[]{:S(2)}) collective-permute-start(bf16[2,2,4,64,256]{4,3,2,1,0:T(8,128)(2,1)S(1)} %shard_map.88), channel_id=1, source_target_pairs={{0,16},{8,24},{16,32},{24,40},{32,48},{40,56},{48,64},{56,72},{64,... | collective-permute-start | bytes 1572872 | tf_op jit(solution)/shard_map/ppermute | solution.py:247
  52.0 14.3 %collective-permute-start.6 = (bf16[64,3456]{1,0:T(8,128)(2,1)}, bf16[64,3456]{1,0:T(8,128)(2,1)}, u32[]{:S(2)}, u32[]{:S(2)}) collective-permute-start(bf16[64,3456]{1,0:T(8,128)(2,1)} %copy-done.9), channel_id=1, source_target_pairs={{0,4},{1,5},{2,6},{3,7},{4,0},{5,1},{6,2},{7,3},{8,12},{9,13},{10,... | collective-permute-start | bytes 1327112 | tf_op jit(solution)/shard_map/ppermute | solution.py:251
  53.6 9.3 %all-to-all-start.2 = ((bf16[4,64,256]{2,1,0:T(8,128)(2,1)}), bf16[4,64,256]{2,1,0:T(8,128)(2,1)S(1)}, u32[]{:S(2)}, u32[]{:S(2)}) async-start(bf16[4,64,256]{2,1,0:T(8,128)(2,1)} %get-tuple-element.47), calls=%async_computation.2 | async-start | bytes 262144 | tf_op jit(solution)/shard_map/all_to_all | solution.py:304
  57.6 8.7 %collective-permute-start.7 = (bf16[64,256]{1,0:T(8,128)(2,1)S(1)}, bf16[64,256]{1,0:T(8,128)(2,1)S(1)}, u32[]{:S(2)}, u32[]{:S(2)}) collective-permute-start(bf16[64,256]{1,0:T(8,128)(2,1)S(1)} %get-tuple-element.67), channel_id=1, source_target_pairs={{8,0},{16,8},{24,16},{32,24},{40,32},{48,40},{56,48},{64,56},{72,6... | collective-permute-start | bytes 98312 | tf_op jit(solution)/shard_map/ppermute | solution.py:247
  66.3 29.8 %copy-start.4 = (bf16[64,3456]{1,0:T(8,128)(2,1)S(1)}, bf16[64,3456]{1,0:T(8,128)(2,1)}, u32[]{:S(2)}) copy-start(bf16[64,3456]{1,0:T(8,128)(2,1)} %copy-done.3) | copy-start | bytes 1327108
  66.3 29.8 %copy-start.6 = (bf16[64,3456]{1,0:T(8,128)(2,1)S(1)}, bf16[64,3456]{1,0:T(8,128)(2,1)}, u32[]{:S(2)}) copy-start(bf16[64,3456]{1,0:T(8,128)(2,1)} %copy-done.5) | copy-start | bytes 1327108
  66.3 24.1 %all-to-all-start.3 = ((bf16[8,16,1792]{2,1,0:T(8,128)(2,1)}), bf16[8,16,1792]{2,1,0:T(8,128)(2,1)S(1)}, u32[]{:S(2)}, u32[]{:S(2)}) async-start(bf16[8,16,1792]{2,1,0:T(8,128)(2,1)} %shard_map.89), calls=%async_computation.3 | async-start | bytes 917504 | tf_op jit(solution)/shard_map/all_to_all | solution.py:318
  76.3 4.3 %collective-permute-start.10 = (bf16[2,64,256]{2,1,0:T(8,128)(2,1)S(1)}, bf16[2,64,256]{2,1,0:T(8,128)(2,1)S(1)}, u32[]{:S(2)}, u32[]{:S(2)}) collective-permute-start(bf16[2,64,256]{2,1,0:T(8,128)(2,1)S(1)} %pad_maximum_fusion.refs_4_), channel_id=1, source_target_pairs={{0,6},{1,7},{2,0},{3,1},{4,2},{5,3},{6,4},{7,5},{8,14},{9,15},{10,... | collective-permute-start | bytes 196616 | tf_op jit(solution)/shard_map/ppermute | solution.py:251
  77.6 5.8 %collective-permute-start.9 = (bf16[2,64,256]{2,1,0:T(8,128)(2,1)S(1)}, bf16[2,64,256]{2,1,0:T(8,128)(2,1)S(1)}, u32[]{:S(2)}, u32[]{:S(2)}) collective-permute-start(bf16[2,64,256]{2,1,0:T(8,128)(2,1)S(1)} %pad_maximum_fusion.refs_4_), channel_id=1, source_target_pairs={{0,4},{1,5},{2,6},{3,7},{4,0},{5,1},{6,2},{7,3},{8,12},{9,13},{10,... | collective-permute-start | bytes 196616 | tf_op jit(solution)/shard_map/ppermute | solution.py:251
  79.0 5.5 %collective-permute-start.8 = (bf16[2,64,256]{2,1,0:T(8,128)(2,1)S(1)}, bf16[2,64,256]{2,1,0:T(8,128)(2,1)S(1)}, u32[]{:S(2)}, u32[]{:S(2)}) collective-permute-start(bf16[2,64,256]{2,1,0:T(8,128)(2,1)S(1)} %pad_maximum_fusion.refs_4_), channel_id=1, source_target_pairs={{0,2},{1,3},{2,4},{3,5},{4,6},{5,7},{6,0},{7,1},{8,10},{9,11},{10,... | collective-permute-start | bytes 196616 | tf_op jit(solution)/shard_map/ppermute | solution.py:251
  91.4 18.0 %all-to-all-start.4 = ((bf16[8,16,1792]{2,1,0:T(8,128)(2,1)}), bf16[8,16,1792]{2,1,0:T(8,128)(2,1)S(1)}, u32[]{:S(2)}, u32[]{:S(2)}) async-start(bf16[8,16,1792]{2,1,0:T(8,128)(2,1)} %shard_map.91), calls=%async_computation.4 | async-start | bytes 917504 | tf_op jit(solution)/shard_map/all_to_all | solution.py:333
  98.3 2.0 %collective-permute-start.11 = (f32[2,4,64,256]{3,2,1,0:T(8,128)S(1)}, f32[2,4,64,256]{3,2,1,0:T(8,128)S(1)}, u32[]{:S(2)}, u32[]{:S(2)}) collective-permute-start(f32[2,4,64,256]{3,2,1,0:T(8,128)S(1)} %get-tuple-element.59), channel_id=1, source_target_pairs={{0,1},{1,0},{2,3},{3,2},{4,5},{5,4},{6,7},{7,6},{8,9},{9,8},{10,11... | collective-permute-start | bytes 1572872 | tf_op jit(solution)/shard_map/ppermute | solution.py:255
  110.9 3.7 %copy-start.2 = (bf16[512,512]{1,0:T(8,128)(2,1)S(1)}, bf16[512,512]{1,0:T(8,128)(2,1)}, u32[]{:S(2)}) copy-start(bf16[512,512]{1,0:T(8,128)(2,1)} %constant.46.clone.m_ref) | copy-start | bytes 1572868
  110.9 23.5 %all-to-all-start.5 = ((bf16[4,8,16,1792]{3,2,1,0:T(8,128)(2,1)}), bf16[4,8,16,1792]{3,2,1,0:T(8,128)(2,1)S(1)}, u32[]{:S(2)}, u32[]{:S(2)}) async-start(bf16[4,8,16,1792]{3,2,1,0:T(8,128)(2,1)} %broadcast_in_dim.2), calls=%async_computation.5 | async-start | bytes 3670016 | tf_op jit(solution)/shard_map/all_to_all | solution.py:336

commit v3 on v2

v3 whole, which is shorter than its diff:
```python
import jax
import jax.numpy as jnp
import numpy as np
from jax import lax
from jax.experimental import pallas as pl
from jax.experimental.pallas import tpu as pltpu
from jax.sharding import PartitionSpec as P

BF = jnp.bfloat16
F32 = jnp.float32
DS = ("dp", "space")
ALL = ("dp", "space", "chan")
Y_GROUPS = [[dp * 16 + z * 2 + yh for yh in range(2) for dp in range(2)] for z in range(8)]
Z_GROUPS = [[dp * 16 + z * 2 + yh for z in range(8)] for yh in range(2) for dp in range(2)]
YC_GROUPS = [
    [((dp * 16 + z * 2 + yh) * 8 + 2 * x + core) for yh in range(2) for dp in range(2) for core in range(2)]
    for z in range(8)
    for x in range(4)
]
ZC_GROUPS = [
    [((dp * 16 + z * 2 + yh) * 8 + 2 * x + core) for z in range(8) for core in range(2)]
    for yh in range(2)
    for dp in range(2)
    for x in range(4)
]
X_GROUPS = [[2 * x + core for x in range(4)] for core in range(2)]
TAP_OF = {(0, 0): 1, (1, 0): 2, (1, 1): 0}
PARAMS = pltpu.CompilerParams(vmem_limit_bytes=48 * 1024 * 1024)


def split_matrix():
    matrix = np.zeros((512, 512), np.float32)
    for y in range(16):
        for z in range(32):
            matrix[y * 32 + z, (2 * (y % 2) + z % 2) * 128 + (y // 2) * 16 + z // 2] = 1
    return matrix


def class_shifts(c):
    py, pz = c // 2, c % 2
    return [(sy, sz) for sy in range(py + 1) for sz in range(pz + 1)]


def taps_of(c):
    py, pz = c // 2, c % 2
    return [(TAP_OF[py, sy] * 3 + TAP_OF[pz, sz], sy, sz) for sy, sz in class_shifts(c)]


def lanes(shape):
    return lax.broadcasted_iota(jnp.int32, shape, 1)


def later(a, sy, sz):
    lane = lanes(a.shape)
    if sy:
        a = jnp.where(lane < 16, 0.0, pltpu.roll(a, 16, 1))
    if sz:
        a = jnp.where(lane % 16 == 0, 0.0, pltpu.roll(a, 1, 1))
    return a


def earlier(a, sy, sz):
    lane = lanes(a.shape)
    width = a.shape[1]
    if sy:
        a = jnp.where(lane % 256 >= 240, 0.0, pltpu.roll(a, width - 16, 1))
    if sz:
        a = jnp.where(lane % 16 == 15, 0.0, pltpu.roll(a, width - 1, 1))
    return a


def split_kernel(x_ref, m_ref, o_ref):
    for p in range(2):
        for h in range(2):
            r = jnp.dot(x_ref[p, :, h * 512 : (h + 1) * 512], m_ref[...], preferred_element_type=F32).astype(BF)
            for c in range(4):
                for copy in range(4):
                    o_ref[copy, p, c, :, h * 128 : (h + 1) * 128] = r[:, c * 128 : (c + 1) * 128]


def halves(a, b):
    low = lanes(a.shape) < 64
    return jnp.where(low, a, pltpu.roll(b, 64, 1)), jnp.where(low, pltpu.roll(a, 64, 1), b)


def core_pack_kernel(core_ref, w_ref, keep_ref, send_ref):
    first = core_ref[0] == 0
    for tap in range(27):
        for pair in range(2):
            at = tap * 512 + pair * 256
            low, high = halves(w_ref[:, at : at + 128].astype(F32), w_ref[:, at + 128 : at + 256].astype(F32))
            to = tap * 256 + pair * 128
            keep_ref[:, to : to + 128] = jnp.where(first, low, high).astype(BF)
            send_ref[:, to : to + 128] = jnp.where(first, high, low).astype(BF)


def forward_kernel(x_ref, w_ref, v_ref, mine_ref, theirs_ref, next_ref, next_theirs_ref):
    own = {}
    following = {}

    def add(table, key, value):
        table[key] = table[key] + value if key in table else value

    for c in range(4):
        taps = taps_of(c)
        for p, firsts in ((1, (0, 2)), (0, (1,))):
            rows = []
            for k1 in firsts:
                for tap, _, _ in taps:
                    at = (9 * k1 + tap) * 256
                    rows += [w_ref[:, at : at + 256], v_ref[:, at : at + 256]]
            cells = jnp.concatenate([x_ref[x, p, c] for x in range(4)], 0)
            r = jnp.dot(jnp.concatenate(rows, 0), cells, preferred_element_type=F32)
            n = 0
            for k1 in firsts:
                for _, sy, sz in taps:
                    add(following if k1 == 0 else own, (sy, sz), r[128 * n : 128 * n + 128])
                    n += 1
    total = sum(later(v, *s) for s, v in own.items())
    mine_ref[...] = total[:64]
    theirs_ref[...] = total[64:]
    total = sum(later(v, *s) for s, v in following.items())
    next_ref[...] = total[:64]
    next_theirs_ref[...] = total[64:]


def gelu_kernel(a_ref, b_ref, c_ref, d_ref, bias_ref, g_ref, act_ref, dy_ref):
    u = ((a_ref[...] + b_ref[...]) + (c_ref[...] + d_ref[...])) + bias_ref[...]
    root = float(np.sqrt(2 / np.pi))
    t = jnp.tanh(root * (u + 0.044715 * (u * u * u)))
    act_ref[...] = (0.5 * u * (1.0 + t)).astype(BF)
    slope = 0.5 * (1.0 + t) + 0.5 * u * (1.0 - t * t) * (root * (1.0 + 3 * 0.044715 * (u * u)))
    dy = (g_ref[...].astype(F32) * slope).astype(BF)
    for copy in range(8):
        dy_ref[copy] = dy


def with_pair(block, total):
    hi = total.astype(BF).astype(F32)
    lane = lanes(block.shape)
    pair = jnp.where(lane == 64, hi, jnp.where(lane == 65, total - hi, 0.0))
    return jnp.where(lane < 64, block, pair).astype(BF)


def filter_grad_kernel(dy_ref, x_ref, e_ref, o_ref, xs_ref):
    for c in range(4):
        for y in range(4):
            cells = slice(y * 256, y * 256 + 256)
            xs_ref[c, 0:64, cells] = x_ref[y, 0, c]
            xs_ref[c, 64:128, cells] = x_ref[y, 1, c]
            xs_ref[c, 128:192, cells] = e_ref[y, c] if y < 2 else x_ref[y - 2, 1, c]
    grads = jnp.concatenate(
        [jnp.concatenate([dy_ref[2 * y + core] for y in range(4)], 1) for core in range(2)], 0
    ).astype(F32)
    shifted = {(sy, sz): earlier(grads, sy, sz).astype(BF) for sy in range(2) for sz in range(2)}

    def put(n, block):
        h, at = divmod(n, 7)
        for core in range(2):
            for fb in range(4):
                row = core * 64 + fb * 16
                o_ref[4 * fb + 2 * h + core, :, at * 128 : at * 128 + 128] = block[row : row + 16]

    firsts = {}
    for c in range(4):
        taps = taps_of(c)
        r = lax.dot_general(
            jnp.concatenate([shifted[sy, sz] for _, sy, sz in taps], 0),
            xs_ref[c],
            (((1,), (1,)), ((), ())),
            preferred_element_type=F32,
        )
        for n, (tap, _, _) in enumerate(taps):
            put(tap, r[128 * n : 128 * n + 128, 0:128].astype(BF))
            firsts[tap] = r[128 * n : 128 * n + 128, 128:192]
    for j in range(4):
        put(9 + j, jnp.concatenate([firsts[2 * j], firsts[2 * j + 1]], 1).astype(BF))
    last = jnp.concatenate([firsts[8], jnp.zeros((128, 64), F32)], 1)
    put(13, with_pair(last, jnp.sum(grads, 1, keepdims=True)))


def sum_z_kernel(odd_ref, r_ref, o_ref):
    for core in range(2):
        for at in range(0, 896, 128):
            total = sum(r_ref[2 * s + core, :, at : at + 128].astype(F32) for s in range(8))
            out = total.astype(BF)
            if at == 768:
                both = total[:, 64:65] + total[:, 65:66]
                out = jnp.where(odd_ref[0] == 1, with_pair(total, both).astype(F32), out.astype(F32)).astype(BF)
            for copy in range(8):
                o_ref[copy, core, :, at : at + 128] = out


def filter_out_kernel(q_ref, own_ref, back_ref, ahead_ref, c_ref, d_ref, w_ref, b_ref):
    q = q_ref[0]
    for source, refs in ((0, (own_ref,)), (3, (back_ref,)), (1, (ahead_ref,)), (2, (c_ref, d_ref))):
        to = lax.rem(q + source, 4) * 128
        for fb in range(4):
            rows = slice(fb * 16, fb * 16 + 16)
            for n in range(14):
                h, at = divmod(n, 7)
                z = 2 * fb + h
                ref = refs[0] if len(refs) == 1 or z < 4 else refs[1]
                z = z if len(refs) == 1 else z % 4
                a = ref[z, 0, :, at * 128 : at * 128 + 128].astype(F32) * 0.5
                b = ref[z, 1, :, at * 128 : at * 128 + 128].astype(F32) * 0.5
                low, high = halves(a, b)
                taps = (9 + n, 18 + n) if n < 9 else (2 * n - 18, 2 * n - 17)
                w_ref[rows, pl.ds(pl.multiple_of(taps[0] * 512 + to, 128), 128)] = low
                if n < 13:
                    w_ref[rows, pl.ds(pl.multiple_of(taps[1] * 512 + to, 128), 128)] = high
                elif source == 0:
                    b_ref[rows, :] = a[:, 64:65] + a[:, 65:66]


def pack_kernel(x_ref, w_ref, *o_refs):
    for d in range(4):
        to = lax.rem(x_ref[0] + d, 4) * 128
        for tap in range(27):
            o_refs[d][:, tap * 128 : tap * 128 + 128] = w_ref[:, pl.ds(pl.multiple_of(tap * 512 + to, 128), 128)]


def input_grad_kernel(core_ref, *refs):
    w_refs, d_refs, (mine_ref, theirs_ref), (g_ref,) = refs[:4], refs[4:8], refs[8:10], refs[10:]
    shifted = {}
    for which in range(2):
        full = jnp.concatenate([d[which] for d in d_refs], 0).astype(F32)
        for sy in range(2):
            for sz in range(2):
                shifted[which, sy, sz] = earlier(full, sy, sz).astype(BF)
    mine = pl.multiple_of(core_ref[0] * 64, 64)
    other = pl.multiple_of(64 - core_ref[0] * 64, 64)
    for c in range(4):
        for p, firsts in ((0, (1,)), (1, (2, 0))):
            total = None
            for k1 in firsts:
                for tap, sy, sz in taps_of(c):
                    at = (9 * k1 + tap) * 128
                    w = jnp.concatenate([w[:, at : at + 128] for w in w_refs], 0)
                    r = lax.dot_general(
                        w, shifted[1 if k1 == 0 else 0, sy, sz], (((0,), (0,)), ((), ())), preferred_element_type=F32
                    )
                    total = r if total is None else total + r
            g_ref[...] = total
            mine_ref[p, c] = g_ref[pl.ds(mine, 64), :]
            theirs_ref[p, c] = g_ref[pl.ds(other, 64), :]


def join_kernel(a_ref, b_ref, m_ref, o_ref):
    for p in range(2):
        for h in range(2):
            at = slice(h * 128, h * 128 + 128)
            parts = [(a_ref[p, c, :, at] + b_ref[p, c, :, at]).astype(BF) for c in range(4)]
            r = lax.dot_general(
                jnp.concatenate(parts, 1), m_ref[...], (((1,), (1,)), ((), ())), preferred_element_type=F32
            )
            o_ref[p, :, h * 512 : (h + 1) * 512] = r.astype(BF)


VMEM = pl.BlockSpec(memory_space=pltpu.VMEM)
SMEM = pl.BlockSpec(memory_space=pltpu.SMEM)


def call(kernel, outs, *args, scalars=0, scratch=()):
    shapes = [jax.ShapeDtypeStruct(s, t) for s, t in outs]
    result = pl.pallas_call(
        kernel,
        out_shape=shapes,
        in_specs=[SMEM] * scalars + [VMEM] * (len(args) - scalars),
        out_specs=[VMEM] * len(outs),
        scratch_shapes=list(scratch),
        compiler_params=PARAMS,
    )(*args)
    return result


def shift_space(a, by):
    return lax.ppermute(a, "space", [(i, i + by) for i in range(16) if 0 <= i + by < 16])


def to_x(a, d):
    return lax.ppermute(a, "chan", [(i, (i + 2 * d) % 8) for i in range(8)])


def over_y(a, by):
    pairs = []
    for i in range(32):
        dp, z, yh = i // 16, i % 16 // 2, i % 2
        y = (2 * yh + dp + by) % 4
        pairs.append((i, y % 2 * 16 + 2 * z + y // 2))
    return lax.ppermute(a, DS, pairs)


def next_partner(a):
    pairs = []
    for i in range(256):
        chan, space, dp = i % 8, i // 8 % 16, i // 128
        if space < 15:
            pairs.append((i, (dp * 16 + space + 1) * 8 + (chan ^ 1)))
    return lax.ppermute(a, ALL, pairs)


def to_partner(a):
    return lax.ppermute(a, "chan", [(i, i ^ 1) for i in range(8)])


def per_device(volumes, kernel, bias, act_grad):
    chan = lax.axis_index("chan")
    core = (chan % 2).astype(jnp.int32).reshape(1)
    x = (chan // 2).astype(jnp.int32).reshape(1)
    z_odd = ((lax.axis_index("space") // 2) % 2).astype(jnp.int32).reshape(1)
    matrix = jnp.asarray(split_matrix(), BF)

    q = ((lax.axis_index("space") % 2) * 2 + lax.axis_index("dp")).astype(jnp.int32).reshape(1)

    (copies,) = call(split_kernel, [((4, 2, 4, 64, 256), BF)], volumes.reshape(2, 64, 1024), matrix)
    w_keep, w_send = call(core_pack_kernel, [((64, 6912), BF)] * 2, core, kernel, scalars=1)
    w_other = to_partner(w_send)
    x_own = lax.all_to_all(copies, "chan", 0, 0, axis_index_groups=X_GROUPS)
    packed = call(pack_kernel, [((64, 3456), BF)] * 4, x, kernel, scalars=1)
    *packed, x_own = lax.optimization_barrier((*packed, x_own))
    ring = lax.all_to_all(x_own, DS, 0, 0, axis_index_groups=Y_GROUPS)
    far = [to_x(packed[d], d) for d in range(1, 4)]
    mine, theirs, following, following_theirs = call(
        forward_kernel, [((64, 256), F32)] * 4, x_own, w_keep, w_other
    )
    parts = (mine, to_partner(theirs), shift_space(following, 1), next_partner(following_theirs))
    activation, dy_copies = call(
        gelu_kernel,
        [((64, 256), BF), ((8, 64, 256), BF)],
        *parts,
        bias.reshape(64, 1),
        act_grad.reshape(64, 256),
    )
    ring, _ = lax.optimization_barrier((ring, parts[2]))
    edge = shift_space(ring[2:, 1], 2)
    dy = lax.all_to_all(dy_copies, ALL, 0, 0, axis_index_groups=YC_GROUPS)
    dy_next = shift_space(dy_copies[0], -1)
    (terms,) = call(
        filter_grad_kernel, [((16, 16, 896), BF)], dy, ring, edge, scratch=[pltpu.VMEM((4, 192, 1024), BF)]
    )
    *far, terms, dy_next = lax.optimization_barrier((*far, terms, dy_next))
    terms = lax.all_to_all(terms, ALL, 0, 0, axis_index_groups=ZC_GROUPS)
    both = jnp.stack([dy_copies[0], dy_next])
    grads = [both] + [to_x(both, d) for d in range(1, 4)]
    *grads, terms = lax.optimization_barrier((*grads, terms))
    (terms,) = call(sum_z_kernel, [((8, 2, 16, 896), BF)], z_odd, terms, scalars=1)
    mine, theirs = call(
        input_grad_kernel,
        [((2, 4, 64, 256), F32), ((2, 4, 64, 256), F32)],
        core,
        packed[0],
        *far,
        *grads,
        scalars=1,
        scratch=[pltpu.VMEM((128, 256), F32)],
    )
    terms = lax.all_to_all(terms, DS, 0, 0, axis_index_groups=Z_GROUPS)
    theirs = to_partner(theirs)
    mine, theirs, terms = lax.optimization_barrier((mine, theirs, terms))
    back, ahead = over_y(terms, 1), over_y(terms, -1)
    (grad_x,) = call(join_kernel, [((2, 64, 1024), BF)], mine, theirs, matrix)
    grad_w, grad_b = call(
        filter_out_kernel,
        [((64, 13824), F32), ((64, 1), F32)],
        q,
        terms,
        back,
        ahead,
        over_y(back[:4], 1),
        over_y(ahead[4:], -1),
        scalars=1,
    )
    return (
        activation.reshape(1, 1, 64, 256),
        grad_x.reshape(1, 2, 64, 1024),
        grad_w,
        grad_b.reshape(64),
    )


def solution(mesh):
    in_specs = (
        P("dp", "space", "chan", None),
        P("chan", None),
        P("chan"),
        P("dp", "space", "chan", None),
    )
    out_specs = (
        P("dp", "space", "chan", None),
        P("dp", "space", "chan", None),
        P("chan", None),
        P("chan"),
    )
    return jax.shard_map(
        per_device, mesh=mesh, in_specs=in_specs, out_specs=out_specs, check_vma=False
    )
```

time: 139 us -> 138 us (level)
  the two profiles are of different devices: /device:TPU:32 before, /device:TPU:24 now
where the time goes in v3:
time: 138 us; the launch traced here: 137 us
  waiting for transfers between devices  57.5 us (42%)
  starting transfers between devices  52.9 us (38%)
  Pallas kernels  15.6 us (11%)
  local copies, waits for them, and re-layouts  9.23 us (7%)
    ppermute x4, waiting for transfers between devices, over_y(): return lax.ppermute(a, DS, pairs)  16.6 us
    pallas_call x10, Pallas kernels, call(): pl.pallas_call(kernel, out_shape=shapes, in_specs=[SMEM] * scalars + [VME...  15.6 us
    ppermute x3, starting transfers between devices, shift_space(): lax.ppermute(a, 'space', [(i, i + by) for i in range(16) if 0 <= i + by <...  12.2 us
    all_to_all x1, waiting for transfers between devices, per_device(): terms = lax.all_to_all(terms, DS, 0, 0, axis_index_groups=Z_GROUPS)  11.7 us
    all_to_all x1, waiting for transfers between devices, per_device(): x_own = lax.all_to_all(copies, 'chan', 0, 0, axis_index_groups=X_GROUPS)  10.2 us
    all_to_all x1, starting transfers between devices, per_device(): terms = lax.all_to_all(terms, ALL, 0, 0, axis_index_groups=ZC_GROUPS)  8.58 us
    ppermute x6, starting transfers between devices, to_x(): return lax.ppermute(a, 'chan', [(i, (i + 2 * d) % 8) for i in range(8)])  7.58 us
    all_to_all x1, waiting for transfers between devices, per_device(): terms = lax.all_to_all(terms, ALL, 0, 0, axis_index_groups=ZC_GROUPS)  7.09 us
  transfers between devices with their start and end apart: 22, of which 13 were waited for; matrix products, arithmetic and copies ran while one was open for 2% of the time, Pallas kernels for 7%

profile of v3, /device:TPU:24, one launch (start us, length us, event | category | flops | bytes accessed | tf_op | source)
XLA Modules:
  0.0 136.7 jit_solution(531325590186057965)
XLA Ops:
  0.7 1.2 copy-done.1
  1.8 0.9 copy-done.7
  2.8 1.5 %shard_map.85 = bf16[4,2,4,64,256]{4,3,2,1,0:T(8,128)(2,1)} custom-call(bf16[2,64,1024]{2,1,0:T(8,128)(2,1)S(1)} %bitcast.14, bf16[512,512]{1,0:T(8,128)(2,1)S(1)} %copy-done.1), custom_call_target="tpu_custom_call" | custom-call | tf_op jit(solution)/shard_map/pallas_call | solution.py:266
  4.3 4.3 %all-to-all-start = ((bf16[4,2,4,64,256]{4,3,2,1,0:T(8,128)(2,1)}), bf16[4,2,4,64,256]{4,3,2,1,0:T(8,128)(2,1)}, u32[]{:S(2)}, u32[]{:S(2)}) async-start(bf16[4,2,4,64,256]{4,3,2,1,0:T(8,128)(2,1)} %shard_map.85), calls=%async_computation | async-start | bytes 2097152 | tf_op jit(solution)/shard_map/all_to_all | solution.py:319
  8.6 1.7 %shard_map.86 = (bf16[64,6912]{1,0:T(8,128)(2,1)S(1)}, bf16[64,6912]{1,0:T(8,128)(2,1)}) custom-call(s32[1]{0:T(128)} %bitcast.2.core_ref, bf16[64,13824]{1,0:T(8,128)(2,1)S(1)} %copy-done), custom_call_target="tpu_custom_call" | custom-call | tf_op jit(solution)/shard_map/pallas_call | solution.py:266
  10.7 0.8 copy-done.3
  11.5 0.8 copy-done.9
  12.3 0.8 copy-done.10
  13.0 0.8 copy-done.11
  13.8 10.2 %all-to-all-done.x_ref = bf16[4,2,4,64,256]{4,3,2,1,0:T(8,128)(2,1)} async-done(((bf16[4,2,4,64,256]{4,3,2,1,0:T(8,128)(2,1)}), bf16[4,2,4,64,256]{4,3,2,1,0:T(8,128)(2,1)}, u32[]{:S(2)}, u32[]{:S(2)}) %all-to-all-start) | async-done | bytes 1048608 | tf_op jit(solution)/shard_map/all_to_all | solution.py:319
  24.0 4.7 %all-to-all-start.2 = ((bf16[4,2,4,64,256]{4,3,2,1,0:T(8,128)(2,1)}), bf16[4,2,4,64,256]{4,3,2,1,0:T(8,128)(2,1)S(1)}, u32[]{:S(2)}, u32[]{:S(2)}) async-start(bf16[4,2,4,64,256]{4,3,2,1,0:T(8,128)(2,1)} %all-to-all-done.x_ref), calls=%async_computation.2 | async-start | bytes 2097152 | tf_op jit(solution)/shard_map/all_to_all | solution.py:322
  28.6 2.1 %shard_map.87 = (f32[64,256]{1,0:T(8,128)S(1)}, f32[64,256]{1,0:T(8,128)S(1)}, f32[64,256]{1,0:T(8,128)S(1)}, f32[64,256]{1,0:T(8,128)S(1)}) custom-call(bf16[4,2,4,64,256]{4,3,2,1,0:T(8,128)(2,1)} %all-to-all-done.x_ref, bf16[64,6912]{1,0:T(8,128)(2,1)S(1)} %get-tuple-element.44.w_ref, bf16[64,6912]{1,0:T(8,128)(2,1)S(1)} %collective-permute-done.v_ref), custom_call_target="tpu_custom_call" | custom-call | tf_op jit(solution)/shard_map/pallas_call | solution.py:266
  30.7 4.9 %collective-permute-start.2 = (f32[64,256]{1,0:T(8,128)S(1)}, f32[64,256]{1,0:T(8,128)S(1)}, u32[]{:S(2)}, u32[]{:S(2)}) collective-permute-start(f32[64,256]{1,0:T(8,128)S(1)} %get-tuple-element.48), channel_id=1, source_target_pairs={{0,8},{8,16},{16,24},{24,32},{32,40},{40,48},{48,56},{56,64},{64,7... | collective-permute-start | bytes 196616 | tf_op jit(solution)/shard_map/ppermute | solution.py:278
  36.2 2.1 %collective-permute-start.5 = (bf16[64,3456]{1,0:T(8,128)(2,1)}, bf16[64,3456]{1,0:T(8,128)(2,1)S(1)}, u32[]{:S(2)}, u32[]{:S(2)}) collective-permute-start(bf16[64,3456]{1,0:T(8,128)(2,1)} %copy-done.10), channel_id=1, source_target_pairs={{0,4},{1,5},{2,6},{3,7},{4,0},{5,1},{6,2},{7,3},{8,12},{9,13},{10,... | collective-permute-start | bytes 1327112 | tf_op jit(solution)/shard_map/ppermute | solution.py:282
  38.3 0.7 collective-permute-start.6
  39.0 3.1 %collective-permute-done.2.c_ref = f32[64,256]{1,0:T(8,128)S(1)} collective-permute-done((f32[64,256]{1,0:T(8,128)S(1)}, f32[64,256]{1,0:T(8,128)S(1)}, u32[]{:S(2)}, u32[]{:S(2)}) %collective-permute-start.2) | collective-permute-done | bytes 65568 | tf_op jit(solution)/shard_map/ppermute | solution.py:278
  42.1 1.9 %collective-permute-start.3 = (f32[64,256]{1,0:T(8,128)S(1)}, f32[64,256]{1,0:T(8,128)S(1)}, u32[]{:S(2)}, u32[]{:S(2)}) collective-permute-start(f32[64,256]{1,0:T(8,128)S(1)} %get-tuple-element.49), channel_id=1, source_target_pairs={{0,9},{1,8},{2,11},{3,10},{4,13},{5,12},{6,15},{7,14},{8,17},{9,16... | collective-permute-start | bytes 196616 | tf_op jit(solution)/shard_map/ppermute | solution.py:300
  44.0 0.7 slice_bitcast_fusion
  44.7 3.8 %collective-permute-start.7 = (bf16[2,4,64,256]{3,2,1,0:T(8,128)(2,1)}, bf16[2,4,64,256]{3,2,1,0:T(8,128)(2,1)S(1)}, u32[]{:S(2)}, u32[]{:S(2)}) collective-permute-start(bf16[2,4,64,256]{3,2,1,0:T(8,128)(2,1)} %slice_bitcast_fusion), channel_id=1, source_target_pairs={{0,16},{8,24},{16,32},{24,40},{32,48},{40,56},{48,64},{56,72},{64,... | collective-permute-start | bytes 786440 | tf_op jit(solution)/shard_map/ppermute | solution.py:278
  49.2 0.8 shard_map.88
  50.0 4.5 %all-to-all-start.1 = ((bf16[8,64,256]{2,1,0:T(8,128)(2,1)}), bf16[8,64,256]{2,1,0:T(8,128)(2,1)S(1)}, u32[]{:S(2)}, u32[]{:S(2)}) async-start(bf16[8,64,256]{2,1,0:T(8,128)(2,1)} %get-tuple-element.55), calls=%async_computation.1 | async-start | bytes 524288 | tf_op jit(solution)/shard_map/all_to_all | solution.py:337
  54.5 0.8 fusion
  55.3 3.5 %collective-permute-start.8 = (bf16[64,256]{1,0:T(8,128)(2,1)S(1)}, bf16[64,256]{1,0:T(8,128)(2,1)S(1)}, u32[]{:S(2)}, u32[]{:S(2)}) collective-permute-start(bf16[64,256]{1,0:T(8,128)(2,1)S(1)} %get-tuple-element.75), channel_id=1, source_target_pairs={{8,0},{16,8},{24,16},{32,24},{40,32},{48,40},{56,48},{64,56},{72,6... | collective-permute-start | bytes 98312 | tf_op jit(solution)/shard_map/ppermute | solution.py:278
  58.8 1.3 all-to-all-done.1.dy_ref
  60.1 1.6 %shard_map.89 = bf16[16,16,896]{2,1,0:T(8,128)(2,1)} custom-call(bf16[8,64,256]{2,1,0:T(8,128)(2,1)S(1)} %all-to-all-done.1.dy_ref, bf16[4,2,4,64,256]{4,3,2,1,0:T(8,128)(2,1)S(1)} %all-to-all-done.2.x_ref, bf16[2,4,64,256]{3,2,1,0:T(8,128)(2,1)S(1)} %collective-permute-done.7.e_ref), custom_call_target="tpu_custom_call" | custom-call | tf_op jit(solution)/shard_map/pallas_call | solution.py:266
  61.7 1.9 %collective-permute-done.8 = bf16[64,256]{1,0:T(8,128)(2,1)S(1)} collective-permute-done((bf16[64,256]{1,0:T(8,128)(2,1)S(1)}, bf16[64,256]{1,0:T(8,128)(2,1)S(1)}, u32[]{:S(2)}, u32[]{:S(2)}) %collective-permute-start.8) | collective-permute-done | bytes 32800 | tf_op jit(solution)/shard_map/ppermute | solution.py:278
  63.7 8.6 %all-to-all-start.3 = ((bf16[16,16,896]{2,1,0:T(8,128)(2,1)}), bf16[16,16,896]{2,1,0:T(8,128)(2,1)S(1)}, u32[]{:S(2)}, u32[]{:S(2)}) async-start(bf16[16,16,896]{2,1,0:T(8,128)(2,1)} %shard_map.89), calls=%async_computation.3 | async-start | bytes 917504 | tf_op jit(solution)/shard_map/all_to_all | solution.py:343
  72.3 0.7 collective-permute-start.9
  72.9 2.2 %collective-permute-start.10 = (bf16[2,64,256]{2,1,0:T(8,128)(2,1)S(1)}, bf16[2,64,256]{2,1,0:T(8,128)(2,1)S(1)}, u32[]{:S(2)}, u32[]{:S(2)}) collective-permute-start(bf16[2,64,256]{2,1,0:T(8,128)(2,1)S(1)} %pad_maximum_fusion.refs_4_), channel_id=1, source_target_pairs={{0,4},{1,5},{2,6},{3,7},{4,0},{5,1},{6,2},{7,3},{8,12},{9,13},{10,... | collective-permute-start | bytes 196616 | tf_op jit(solution)/shard_map/ppermute | solution.py:282
  75.1 1.3 collective-permute-start.11
  76.4 3.0 %collective-permute-done.9.refs_5_ = bf16[2,64,256]{2,1,0:T(8,128)(2,1)S(1)} collective-permute-done((bf16[2,64,256]{2,1,0:T(8,128)(2,1)S(1)}, bf16[2,64,256]{2,1,0:T(8,128)(2,1)S(1)}, u32[]{:S(2)}, u32[]{:S(2)}) %collective-permute-start.9) | collective-permute-done | bytes 65568 | tf_op jit(solution)/shard_map/ppermute | solution.py:282
  80.0 7.1 %all-to-all-done.3.r_ref = bf16[16,16,896]{2,1,0:T(8,128)(2,1)S(1)} async-done(((bf16[16,16,896]{2,1,0:T(8,128)(2,1)}), bf16[16,16,896]{2,1,0:T(8,128)(2,1)S(1)}, u32[]{:S(2)}, u32[]{:S(2)}) %all-to-all-start.3) | async-done | bytes 458784 | tf_op jit(solution)/shard_map/all_to_all | solution.py:343
  87.1 0.9 shard_map.91
  88.0 3.9 %all-to-all-start.4 = ((bf16[8,2,16,896]{3,2,1,0:T(8,128)(2,1)}), bf16[8,2,16,896]{3,2,1,0:T(8,128)(2,1)S(1)}, u32[]{:S(2)}, u32[]{:S(2)}) async-start(bf16[8,2,16,896]{3,2,1,0:T(8,128)(2,1)} %shard_map.91), calls=%async_computation.4 | async-start | bytes 917504 | tf_op jit(solution)/shard_map/all_to_all | solution.py:358
  91.9 1.0 copy-done.6
  92.9 2.0 %shard_map.90 = (f32[2,4,64,256]{3,2,1,0:T(8,128)S(1)}, f32[2,4,64,256]{3,2,1,0:T(8,128)S(1)}) custom-call(s32[1]{0:T(128)} %bitcast.2.core_ref, bf16[64,3456]{1,0:T(8,128)(2,1)S(1)} %copy-done.4, bf16[64,3456]{1,0:T(8,128)(2,1)S(1)} %collective-permute-done.4.refs_1_, bf16[64,3456]{1,0:T(8,128)(2,1)S(1)} %copy-done.6, ...), custom_call_target="tpu_custom_call" | custom-call | tf_op jit(solution)/shard_map/pallas_call | solution.py:266
  94.9 1.2 collective-permute-start.12
  96.2 1.5 %collective-permute-done.12.b_ref = f32[2,4,64,256]{3,2,1,0:T(8,128)S(1)} collective-permute-done((f32[2,4,64,256]{3,2,1,0:T(8,128)S(1)}, f32[2,4,64,256]{3,2,1,0:T(8,128)S(1)}, u32[]{:S(2)}, u32[]{:S(2)}) %collective-permute-start.12) | collective-permute-done | bytes 524320 | tf_op jit(solution)/shard_map/ppermute | solution.py:304
  97.7 11.7 %all-to-all-done.4.own_ref = bf16[8,2,16,896]{3,2,1,0:T(8,128)(2,1)S(1)} async-done(((bf16[8,2,16,896]{3,2,1,0:T(8,128)(2,1)}), bf16[8,2,16,896]{3,2,1,0:T(8,128)(2,1)S(1)}, u32[]{:S(2)}, u32[]{:S(2)}) %all-to-all-start.4) | async-done | bytes 458784 | tf_op jit(solution)/shard_map/all_to_all | solution.py:358
  109.6 1.9 %collective-permute-start.14 = (bf16[8,2,16,896]{3,2,1,0:T(8,128)(2,1)S(1)}, bf16[8,2,16,896]{3,2,1,0:T(8,128)(2,1)S(1)}, u32[]{:S(2)}, u32[]{:S(2)}) collective-permute-start(bf16[8,2,16,896]{3,2,1,0:T(8,128)(2,1)S(1)} %all-to-all-done.4.own_ref), channel_id=1, source_target_pairs={{0,136},{8,128},{16,152},{24,144},{32,168},{40,160},{48,184},{56,1... | collective-permute-start | bytes 1376264 | tf_op jit(solution)/shard_map/ppermute | solution.py:291
  111.5 10.5 %collective-permute-done.13.back_ref = bf16[8,2,16,896]{3,2,1,0:T(8,128)(2,1)S(1)} collective-permute-done((bf16[8,2,16,896]{3,2,1,0:T(8,128)(2,1)S(1)}, bf16[8,2,16,896]{3,2,1,0:T(8,128)(2,1)S(1)}, u32[]{:S(2)}, u32[]{:S(2)}) %collective-permute-start.13) | collective-permute-done | bytes 458784 | tf_op jit(solution)/shard_map/ppermute | solution.py:291
  122.0 0.7 slice.18
  122.7 1.5 %collective-permute-start.15 = (bf16[4,2,16,896]{3,2,1,0:T(8,128)(2,1)}, bf16[4,2,16,896]{3,2,1,0:T(8,128)(2,1)S(1)}, u32[]{:S(2)}, u32[]{:S(2)}) collective-permute-start(bf16[4,2,16,896]{3,2,1,0:T(8,128)(2,1)} %slice.18), channel_id=1, source_target_pairs={{0,128},{8,136},{16,144},{24,152},{32,160},{40,168},{48,176},{56,1... | collective-permute-start | bytes 688136 | tf_op jit(solution)/shard_map/ppermute | solution.py:291
  124.2 0.7 slice.19
  125.4 1.5 %shard_map.92 = bf16[2,64,1024]{2,1,0:T(8,128)(2,1)} custom-call(f32[2,4,64,256]{3,2,1,0:T(8,128)S(1)} %get-tuple-element.69.a_ref, f32[2,4,64,256]{3,2,1,0:T(8,128)S(1)} %collective-permute-done.12.b_ref, bf16[512,512]{1,0:T(8,128)(2,1)S(1)} %copy-done.2), custom_call_target="tpu_custom_call" | custom-call | tf_op jit(solution)/shard_map/pallas_call | solution.py:266
  126.9 2.8 %collective-permute-done.15.c_ref = bf16[4,2,16,896]{3,2,1,0:T(8,128)(2,1)S(1)} collective-permute-done((bf16[4,2,16,896]{3,2,1,0:T(8,128)(2,1)}, bf16[4,2,16,896]{3,2,1,0:T(8,128)(2,1)S(1)}, u32[]{:S(2)}, u32[]{:S(2)}) %collective-permute-start.15) | collective-permute-done | bytes 229408 | tf_op jit(solution)/shard_map/ppermute | solution.py:291
  129.7 3.3 %collective-permute-done.16.d_ref = bf16[4,2,16,896]{3,2,1,0:T(8,128)(2,1)S(1)} collective-permute-done((bf16[4,2,16,896]{3,2,1,0:T(8,128)(2,1)}, bf16[4,2,16,896]{3,2,1,0:T(8,128)(2,1)S(1)}, u32[]{:S(2)}, u32[]{:S(2)}) %collective-permute-start.16) | collective-permute-done | bytes 229408 | tf_op jit(solution)/shard_map/ppermute | solution.py:291
  133.0 3.0 %shard_map.93 = (f32[64,13824]{1,0:T(8,128)}, f32[64,1]{1,0:T(8,128)S(1)}) custom-call(s32[1]{0:T(128)} %bitcast.11.q_ref, bf16[8,2,16,896]{3,2,1,0:T(8,128)(2,1)S(1)} %all-to-all-done.4.own_ref, bf16[8,2,16,896]{3,2,1,0:T(8,128)(2,1)S(1)} %collective-permute-done.13.back_ref, bf16[8,2,16,896]{3,2,1,0:T(8,128)(2,1)S(1)} %collective-permute-done.14.ahead_ref, ...), custom_call_target="tpu_custom_call" | custom-call | tf_op jit(solution)/shard_map/pallas_call | solution.py:266
  (39 shorter events, 3.5 us)
Async XLA Ops:
  0.6 7.9 %copy-start = (bf16[64,13824]{1,0:T(8,128)(2,1)S(1)}, bf16[64,13824]{1,0:T(8,128)(2,1)}, u32[]{:S(2)}) copy-start(bf16[64,13824]{1,0:T(8,128)(2,1)} %w_ref.3) | copy-start | bytes 5308420
  0.6 1.2 copy-start.1
  1.8 0.9 copy-start.7
  4.3 19.7 %all-to-all-start = ((bf16[4,2,4,64,256]{4,3,2,1,0:T(8,128)(2,1)}), bf16[4,2,4,64,256]{4,3,2,1,0:T(8,128)(2,1)}, u32[]{:S(2)}, u32[]{:S(2)}) async-start(bf16[4,2,4,64,256]{4,3,2,1,0:T(8,128)(2,1)} %shard_map.85), calls=%async_computation | async-start | bytes 2097152 | tf_op jit(solution)/shard_map/all_to_all | solution.py:319
  10.3 18.3 %collective-permute-start = (bf16[64,6912]{1,0:T(8,128)(2,1)}, bf16[64,6912]{1,0:T(8,128)(2,1)S(1)}, u32[]{:S(2)}, u32[]{:S(2)}) collective-permute-start(bf16[64,6912]{1,0:T(8,128)(2,1)} %get-tuple-element.45), channel_id=1, source_target_pairs={{0,1},{1,0},{2,3},{3,2},{4,5},{5,4},{6,7},{7,6},{8,9},{9,8},{10,11... | collective-permute-start | bytes 2654216 | tf_op jit(solution)/shard_map/ppermute | solution.py:304
  10.3 38.3 %copy-start.12 = (f32[64]{0:T(128)S(1)}, f32[64]{0:T(128)}, u32[]{:S(2)}) copy-start(f32[64]{0:T(128)} %param.7) | copy-start | bytes 772
  10.7 0.8 copy-start.3
  11.5 0.8 copy-start.9
  12.3 0.8 copy-start.10
  13.0 0.8 copy-start.11
  13.8 35.4 %copy-start.8 = (bf16[1,1,64,256]{3,2,1,0:T(8,128)(2,1)S(1)}, bf16[1,1,64,256]{3,2,1,0:T(8,128)(2,1)}, u32[]{:S(2)}) copy-start(bf16[1,1,64,256]{3,2,1,0:T(8,128)(2,1)} %param.8) | copy-start | bytes 98308
  24.0 20.1 %all-to-all-start.2 = ((bf16[4,2,4,64,256]{4,3,2,1,0:T(8,128)(2,1)}), bf16[4,2,4,64,256]{4,3,2,1,0:T(8,128)(2,1)S(1)}, u32[]{:S(2)}, u32[]{:S(2)}) async-start(bf16[4,2,4,64,256]{4,3,2,1,0:T(8,128)(2,1)} %all-to-all-done.x_ref), calls=%async_computation.2 | async-start | bytes 2097152 | tf_op jit(solution)/shard_map/all_to_all | solution.py:322
  30.7 61.2 %copy-start.4 = (bf16[64,3456]{1,0:T(8,128)(2,1)S(1)}, bf16[64,3456]{1,0:T(8,128)(2,1)}, u32[]{:S(2)}) copy-start(bf16[64,3456]{1,0:T(8,128)(2,1)} %copy-done.3) | copy-start | bytes 1327108
  30.7 11.4 %collective-permute-start.2 = (f32[64,256]{1,0:T(8,128)S(1)}, f32[64,256]{1,0:T(8,128)S(1)}, u32[]{:S(2)}, u32[]{:S(2)}) collective-permute-start(f32[64,256]{1,0:T(8,128)S(1)} %get-tuple-element.48), channel_id=1, source_target_pairs={{0,8},{8,16},{16,24},{24,32},{32,40},{40,48},{48,56},{56,64},{64,7... | collective-permute-start | bytes 196616 | tf_op jit(solution)/shard_map/ppermute | solution.py:278
  35.6 28.1 %collective-permute-start.4 = (bf16[64,3456]{1,0:T(8,128)(2,1)}, bf16[64,3456]{1,0:T(8,128)(2,1)S(1)}, u32[]{:S(2)}, u32[]{:S(2)}) collective-permute-start(bf16[64,3456]{1,0:T(8,128)(2,1)} %copy-done.11), channel_id=1, source_target_pairs={{0,2},{1,3},{2,4},{3,5},{4,6},{5,7},{6,0},{7,1},{8,10},{9,11},{10,... | collective-permute-start | bytes 1327112 | tf_op jit(solution)/shard_map/ppermute | solution.py:282
  36.2 27.4 %collective-permute-start.5 = (bf16[64,3456]{1,0:T(8,128)(2,1)}, bf16[64,3456]{1,0:T(8,128)(2,1)S(1)}, u32[]{:S(2)}, u32[]{:S(2)}) collective-permute-start(bf16[64,3456]{1,0:T(8,128)(2,1)} %copy-done.10), channel_id=1, source_target_pairs={{0,4},{1,5},{2,6},{3,7},{4,0},{5,1},{6,2},{7,3},{8,12},{9,13},{10,... | collective-permute-start | bytes 1327112 | tf_op jit(solution)/shard_map/ppermute | solution.py:282
  38.3 25.4 %collective-permute-start.6 = (bf16[64,3456]{1,0:T(8,128)(2,1)}, bf16[64,3456]{1,0:T(8,128)(2,1)}, u32[]{:S(2)}, u32[]{:S(2)}) collective-permute-start(bf16[64,3456]{1,0:T(8,128)(2,1)} %copy-done.9), channel_id=1, source_target_pairs={{0,6},{1,7},{2,0},{3,1},{4,2},{5,3},{6,4},{7,5},{8,14},{9,15},{10,... | collective-permute-start | bytes 1327112 | tf_op jit(solution)/shard_map/ppermute | solution.py:282
  39.0 5.7 %collective-permute-start.1 = (f32[64,256]{1,0:T(8,128)S(1)}, f32[64,256]{1,0:T(8,128)S(1)}, u32[]{:S(2)}, u32[]{:S(2)}) collective-permute-start(f32[64,256]{1,0:T(8,128)S(1)} %get-tuple-element.47), channel_id=1, source_target_pairs={{0,1},{1,0},{2,3},{3,2},{4,5},{5,4},{6,7},{7,6},{8,9},{9,8},{10,11... | collective-permute-start | bytes 196616 | tf_op jit(solution)/shard_map/ppermute | solution.py:304
  42.1 7.1 %collective-permute-start.3 = (f32[64,256]{1,0:T(8,128)S(1)}, f32[64,256]{1,0:T(8,128)S(1)}, u32[]{:S(2)}, u32[]{:S(2)}) collective-permute-start(f32[64,256]{1,0:T(8,128)S(1)} %get-tuple-element.49), channel_id=1, source_target_pairs={{0,9},{1,8},{2,11},{3,10},{4,13},{5,12},{6,15},{7,14},{8,17},{9,16... | collective-permute-start | bytes 196616 | tf_op jit(solution)/shard_map/ppermute | solution.py:300
  44.7 15.3 %collective-permute-start.7 = (bf16[2,4,64,256]{3,2,1,0:T(8,128)(2,1)}, bf16[2,4,64,256]{3,2,1,0:T(8,128)(2,1)S(1)}, u32[]{:S(2)}, u32[]{:S(2)}) collective-permute-start(bf16[2,4,64,256]{3,2,1,0:T(8,128)(2,1)} %slice_bitcast_fusion), channel_id=1, source_target_pairs={{0,16},{8,24},{16,32},{24,40},{32,48},{40,56},{48,64},{56,72},{64,... | collective-permute-start | bytes 786440 | tf_op jit(solution)/shard_map/ppermute | solution.py:278
  50.0 10.1 %all-to-all-start.1 = ((bf16[8,64,256]{2,1,0:T(8,128)(2,1)}), bf16[8,64,256]{2,1,0:T(8,128)(2,1)S(1)}, u32[]{:S(2)}, u32[]{:S(2)}) async-start(bf16[8,64,256]{2,1,0:T(8,128)(2,1)} %get-tuple-element.55), calls=%async_computation.1 | async-start | bytes 524288 | tf_op jit(solution)/shard_map/all_to_all | solution.py:337
  55.3 70.1 %copy-start.2 = (bf16[512,512]{1,0:T(8,128)(2,1)S(1)}, bf16[512,512]{1,0:T(8,128)(2,1)}, u32[]{:S(2)}) copy-start(bf16[512,512]{1,0:T(8,128)(2,1)} %constant.55.clone.m_ref) | copy-start | bytes 1572868
  55.3 8.3 %collective-permute-start.8 = (bf16[64,256]{1,0:T(8,128)(2,1)S(1)}, bf16[64,256]{1,0:T(8,128)(2,1)S(1)}, u32[]{:S(2)}, u32[]{:S(2)}) collective-permute-start(bf16[64,256]{1,0:T(8,128)(2,1)S(1)} %get-tuple-element.75), channel_id=1, source_target_pairs={{8,0},{16,8},{24,16},{32,24},{40,32},{48,40},{56,48},{64,56},{72,6... | collective-permute-start | bytes 98312 | tf_op jit(solution)/shard_map/ppermute | solution.py:278
  63.7 24.3 %copy-start.5 = (bf16[64,3456]{1,0:T(8,128)(2,1)}, bf16[64,3456]{1,0:T(8,128)(2,1)S(1)}, u32[]{:S(2)}) copy-start(bf16[64,3456]{1,0:T(8,128)(2,1)S(1)} %collective-permute-done.5.refs_2_) | copy-start | bytes 1327108
  63.7 23.4 %all-to-all-start.3 = ((bf16[16,16,896]{2,1,0:T(8,128)(2,1)}), bf16[16,16,896]{2,1,0:T(8,128)(2,1)S(1)}, u32[]{:S(2)}, u32[]{:S(2)}) async-start(bf16[16,16,896]{2,1,0:T(8,128)(2,1)} %shard_map.89), calls=%async_computation.3 | async-start | bytes 917504 | tf_op jit(solution)/shard_map/all_to_all | solution.py:343
  72.3 7.1 %collective-permute-start.9 = (bf16[2,64,256]{2,1,0:T(8,128)(2,1)S(1)}, bf16[2,64,256]{2,1,0:T(8,128)(2,1)S(1)}, u32[]{:S(2)}, u32[]{:S(2)}) collective-permute-start(bf16[2,64,256]{2,1,0:T(8,128)(2,1)S(1)} %pad_maximum_fusion.refs_4_), channel_id=1, source_target_pairs={{0,2},{1,3},{2,4},{3,5},{4,6},{5,7},{6,0},{7,1},{8,10},{9,11},{10,... | collective-permute-start | bytes 196616 | tf_op jit(solution)/shard_map/ppermute | solution.py:282
  72.9 6.5 %collective-permute-start.10 = (bf16[2,64,256]{2,1,0:T(8,128)(2,1)S(1)}, bf16[2,64,256]{2,1,0:T(8,128)(2,1)S(1)}, u32[]{:S(2)}, u32[]{:S(2)}) collective-permute-start(bf16[2,64,256]{2,1,0:T(8,128)(2,1)S(1)} %pad_maximum_fusion.refs_4_), channel_id=1, source_target_pairs={{0,4},{1,5},{2,6},{3,7},{4,0},{5,1},{6,2},{7,3},{8,12},{9,13},{10,... | collective-permute-start | bytes 196616 | tf_op jit(solution)/shard_map/ppermute | solution.py:282
  75.1 4.9 %collective-permute-start.11 = (bf16[2,64,256]{2,1,0:T(8,128)(2,1)S(1)}, bf16[2,64,256]{2,1,0:T(8,128)(2,1)S(1)}, u32[]{:S(2)}, u32[]{:S(2)}) collective-permute-start(bf16[2,64,256]{2,1,0:T(8,128)(2,1)S(1)} %pad_maximum_fusion.refs_4_), channel_id=1, source_target_pairs={{0,6},{1,7},{2,0},{3,1},{4,2},{5,3},{6,4},{7,5},{8,14},{9,15},{10,... | collective-permute-start | bytes 196616 | tf_op jit(solution)/shard_map/ppermute | solution.py:282
  88.0 21.4 %all-to-all-start.4 = ((bf16[8,2,16,896]{3,2,1,0:T(8,128)(2,1)}), bf16[8,2,16,896]{3,2,1,0:T(8,128)(2,1)S(1)}, u32[]{:S(2)}, u32[]{:S(2)}) async-start(bf16[8,2,16,896]{3,2,1,0:T(8,128)(2,1)} %shard_map.91), calls=%async_computation.4 | async-start | bytes 917504 | tf_op jit(solution)/shard_map/all_to_all | solution.py:358
  91.9 1.0 copy-start.6
  94.9 2.8 %collective-permute-start.12 = (f32[2,4,64,256]{3,2,1,0:T(8,128)S(1)}, f32[2,4,64,256]{3,2,1,0:T(8,128)S(1)}, u32[]{:S(2)}, u32[]{:S(2)}) collective-permute-start(f32[2,4,64,256]{3,2,1,0:T(8,128)S(1)} %get-tuple-element.67), channel_id=1, source_target_pairs={{0,1},{1,0},{2,3},{3,2},{4,5},{5,4},{6,7},{7,6},{8,9},{9,8},{10,11... | collective-permute-start | bytes 1572872 | tf_op jit(solution)/shard_map/ppermute | solution.py:304
  109.4 12.5 %collective-permute-start.13 = (bf16[8,2,16,896]{3,2,1,0:T(8,128)(2,1)S(1)}, bf16[8,2,16,896]{3,2,1,0:T(8,128)(2,1)S(1)}, u32[]{:S(2)}, u32[]{:S(2)}) collective-permute-start(bf16[8,2,16,896]{3,2,1,0:T(8,128)(2,1)S(1)} %all-to-all-done.4.own_ref), channel_id=1, source_target_pairs={{0,128},{8,136},{16,144},{24,152},{32,160},{40,168},{48,176},{56,1... | collective-permute-start | bytes 1376264 | tf_op jit(solution)/shard_map/ppermute | solution.py:291
  109.6 14.6 %collective-permute-start.14 = (bf16[8,2,16,896]{3,2,1,0:T(8,128)(2,1)S(1)}, bf16[8,2,16,896]{3,2,1,0:T(8,128)(2,1)S(1)}, u32[]{:S(2)}, u32[]{:S(2)}) collective-permute-start(bf16[8,2,16,896]{3,2,1,0:T(8,128)(2,1)S(1)} %all-to-all-done.4.own_ref), channel_id=1, source_target_pairs={{0,136},{8,128},{16,152},{24,144},{32,168},{40,160},{48,184},{56,1... | collective-permute-start | bytes 1376264 | tf_op jit(solution)/shard_map/ppermute | solution.py:291
  122.7 7.0 %collective-permute-start.15 = (bf16[4,2,16,896]{3,2,1,0:T(8,128)(2,1)}, bf16[4,2,16,896]{3,2,1,0:T(8,128)(2,1)S(1)}, u32[]{:S(2)}, u32[]{:S(2)}) collective-permute-start(bf16[4,2,16,896]{3,2,1,0:T(8,128)(2,1)} %slice.18), channel_id=1, source_target_pairs={{0,128},{8,136},{16,144},{24,152},{32,160},{40,168},{48,176},{56,1... | collective-permute-start | bytes 688136 | tf_op jit(solution)/shard_map/ppermute | solution.py:291
  124.9 8.1 %collective-permute-start.16 = (bf16[4,2,16,896]{3,2,1,0:T(8,128)(2,1)}, bf16[4,2,16,896]{3,2,1,0:T(8,128)(2,1)S(1)}, u32[]{:S(2)}, u32[]{:S(2)}) collective-permute-start(bf16[4,2,16,896]{3,2,1,0:T(8,128)(2,1)} %slice.19), channel_id=1, source_target_pairs={{0,136},{8,128},{16,152},{24,144},{32,168},{40,160},{48,184},{56,1... | collective-permute-start | bytes 688136 | tf_op jit(solution)/shard_map/ppermute | solution.py:291

commit v4 on v3

--- a/solution.py
+++ b/solution.py
@@ -1,3 +1,5 @@
+import functools
+
 import jax
 import jax.numpy as jnp
 import numpy as np
@@ -94,43 +96,33 @@
             send_ref[:, to : to + 128] = jnp.where(first, high, low).astype(BF)
 
 
-def forward_kernel(x_ref, w_ref, v_ref, mine_ref, theirs_ref, next_ref, next_theirs_ref):
-    own = {}
-    following = {}
-
-    def add(table, key, value):
-        table[key] = table[key] + value if key in table else value
-
+def forward_kernel(choice, x_ref, w_ref, v_ref, mine_ref, theirs_ref):
+    sums = {}
     for c in range(4):
         taps = taps_of(c)
-        for p, firsts in ((1, (0, 2)), (0, (1,))):
+        for p, k1 in choice:
             rows = []
-            for k1 in firsts:
-                for tap, _, _ in taps:
-                    at = (9 * k1 + tap) * 256
-                    rows += [w_ref[:, at : at + 256], v_ref[:, at : at + 256]]
+            for tap, _, _ in taps:
+                at = (9 * k1 + tap) * 256
+                rows += [w_ref[:, at : at + 256], v_ref[:, at : at + 256]]
             cells = jnp.concatenate([x_ref[x, p, c] for x in range(4)], 0)
             r = jnp.dot(jnp.concatenate(rows, 0), cells, preferred_element_type=F32)
-            n = 0
-            for k1 in firsts:
-                for _, sy, sz in taps:
-                    add(following if k1 == 0 else own, (sy, sz), r[128 * n : 128 * n + 128])
-                    n += 1
-    total = sum(later(v, *s) for s, v in own.items())
+            for n, (_, sy, sz) in enumerate(taps):
+                value = r[128 * n : 128 * n + 128]
+                sums[sy, sz] = sums[sy, sz] + value if (sy, sz) in sums else value
+    total = sum(later(v, *s) for s, v in sums.items())
     mine_ref[...] = total[:64]
     theirs_ref[...] = total[64:]
-    total = sum(later(v, *s) for s, v in following.items())
-    next_ref[...] = total[:64]
-    next_theirs_ref[...] = total[64:]
-
-
-def gelu_kernel(a_ref, b_ref, c_ref, d_ref, bias_ref, g_ref, act_ref, dy_ref):
-    u = ((a_ref[...] + b_ref[...]) + (c_ref[...] + d_ref[...])) + bias_ref[...]
+
+
+def gelu_kernel(a_ref, b_ref, c_ref, bias_ref, g_ref, act_ref, one_ref, dy_ref):
+    u = ((a_ref[...] + b_ref[...]) + c_ref[...]) + bias_ref[...]
     root = float(np.sqrt(2 / np.pi))
     t = jnp.tanh(root * (u + 0.044715 * (u * u * u)))
     act_ref[...] = (0.5 * u * (1.0 + t)).astype(BF)
     slope = 0.5 * (1.0 + t) + 0.5 * u * (1.0 - t * t) * (root * (1.0 + 3 * 0.044715 * (u * u)))
     dy = (g_ref[...].astype(F32) * slope).astype(BF)
+    one_ref[...] = dy
     for copy in range(8):
         dy_ref[copy] = dy
 
@@ -191,26 +183,62 @@
                 o_ref[copy, core, :, at : at + 128] = out
 
 
-def filter_out_kernel(q_ref, own_ref, back_ref, ahead_ref, c_ref, d_ref, w_ref, b_ref):
-    q = q_ref[0]
-    for source, refs in ((0, (own_ref,)), (3, (back_ref,)), (1, (ahead_ref,)), (2, (c_ref, d_ref))):
-        to = lax.rem(q + source, 4) * 128
-        for fb in range(4):
-            rows = slice(fb * 16, fb * 16 + 16)
-            for n in range(14):
-                h, at = divmod(n, 7)
-                z = 2 * fb + h
-                ref = refs[0] if len(refs) == 1 or z < 4 else refs[1]
-                z = z if len(refs) == 1 else z % 4
-                a = ref[z, 0, :, at * 128 : at * 128 + 128].astype(F32) * 0.5
-                b = ref[z, 1, :, at * 128 : at * 128 + 128].astype(F32) * 0.5
-                low, high = halves(a, b)
-                taps = (9 + n, 18 + n) if n < 9 else (2 * n - 18, 2 * n - 17)
-                w_ref[rows, pl.ds(pl.multiple_of(taps[0] * 512 + to, 128), 128)] = low
-                if n < 13:
-                    w_ref[rows, pl.ds(pl.multiple_of(taps[1] * 512 + to, 128), 128)] = high
-                elif source == 0:
-                    b_ref[rows, :] = a[:, 64:65] + a[:, 65:66]
+def cut_kernel(r_ref, a_ref, b_ref):
+    a_ref[...] = r_ref[:4]
+    b_ref[...] = r_ref[4:]
+
+
+def place(first, second, store, bias):
+    for z in range(8):
+        fb, h = divmod(z, 2)
+        ref = first if z < 4 else second
+        rows = slice(fb * 16, fb * 16 + 16)
+        for at in range(7):
+            n = 7 * h + at
+            a = ref[z % 4, 0, :, at * 128 : at * 128 + 128].astype(F32) * 0.5
+            b = ref[z % 4, 1, :, at * 128 : at * 128 + 128].astype(F32) * 0.5
+            low, high = halves(a, b)
+            taps = (9 + n, 18 + n) if n < 9 else (2 * n - 18, 2 * n - 17)
+            store(rows, taps[0], low)
+            if n < 13:
+                store(rows, taps[1], high)
+            elif bias is not None:
+                bias[rows, :] = a[:, 64:65] + a[:, 65:66]
+
+
+def filter_out_kernel(q_ref, o0, o1, a0, a1, b0, b1, w_ref, b_ref):
+    def at(tap, source):
+        to = lax.rem(q_ref[0] + source, 4) * 128
+        return pl.ds(pl.multiple_of(tap * 512 + to, 128), 128)
+
+    for source, first, second in ((0, o0, o1), (3, a0, a1), (1, b0, b1)):
+
+        def store(rows, tap, value, source=source):
+            w_ref[rows, at(tap, source)] = value
+
+        place(first, second, store, b_ref if source == 0 else None)
+    for tap in range(27):
+        w_ref[:, at(tap, 2)] = jnp.zeros((64, 128), F32)
+
+
+def filter_last_kernel(q_ref, c_ref, d_ref, w_in, w_ref, s_ref, sems):
+    def store(rows, tap, value):
+        s_ref[rows, tap * 128 : tap * 128 + 128] = value
+
+    place(c_ref, d_ref, store, None)
+    to = lax.rem(q_ref[0] + 2, 4) * 128
+    copies = []
+    for tap in range(27):
+        copies.append(
+            pltpu.make_async_copy(
+                s_ref.at[:, pl.ds(tap * 128, 128)],
+                w_ref.at[:, pl.ds(pl.multiple_of(tap * 512 + to, 128), 128)],
+                sems.at[tap],
+            )
+        )
+        copies[-1].start()
+    for copy in copies:
+        copy.wait()
 
 
 def pack_kernel(x_ref, w_ref, *o_refs):
@@ -291,15 +319,6 @@
     return lax.ppermute(a, DS, pairs)
 
 
-def next_partner(a):
-    pairs = []
-    for i in range(256):
-        chan, space, dp = i % 8, i // 8 % 16, i // 128
-        if space < 15:
-            pairs.append((i, (dp * 16 + space + 1) * 8 + (chan ^ 1)))
-    return lax.ppermute(a, ALL, pairs)
-
-
 def to_partner(a):
     return lax.ppermute(a, "chan", [(i, i ^ 1) for i in range(8)])
 
@@ -320,30 +339,32 @@
     packed = call(pack_kernel, [((64, 3456), BF)] * 4, x, kernel, scalars=1)
     *packed, x_own = lax.optimization_barrier((*packed, x_own))
     ring = lax.all_to_all(x_own, DS, 0, 0, axis_index_groups=Y_GROUPS)
-    far = [to_x(packed[d], d) for d in range(1, 4)]
-    mine, theirs, following, following_theirs = call(
-        forward_kernel, [((64, 256), F32)] * 4, x_own, w_keep, w_other
-    )
-    parts = (mine, to_partner(theirs), shift_space(following, 1), next_partner(following_theirs))
-    activation, dy_copies = call(
+    far = to_x(packed[2], 2)
+    outs = [((64, 256), F32)] * 2
+    following, theirs = call(functools.partial(forward_kernel, ((1, 0),)), outs, x_own, w_keep, w_other)
+    following = shift_space(following + to_partner(theirs), 1)
+    mine, theirs = call(functools.partial(forward_kernel, ((0, 1), (1, 2))), outs, x_own, w_keep, w_other)
+    parts = (mine, to_partner(theirs), following)
+    activation, dy_own, dy_copies = call(
         gelu_kernel,
-        [((64, 256), BF), ((8, 64, 256), BF)],
+        [((64, 256), BF), ((64, 256), BF), ((8, 64, 256), BF)],
         *parts,
         bias.reshape(64, 1),
         act_grad.reshape(64, 256),
     )
-    ring, _ = lax.optimization_barrier((ring, parts[2]))
+    ring, dy_own = lax.optimization_barrier((ring, dy_own))
+    dy = lax.all_to_all(dy_copies, ALL, 0, 0, axis_index_groups=YC_GROUPS)
     edge = shift_space(ring[2:, 1], 2)
-    dy = lax.all_to_all(dy_copies, ALL, 0, 0, axis_index_groups=YC_GROUPS)
-    dy_next = shift_space(dy_copies[0], -1)
+    dy_next = shift_space(dy_own, -1)
     (terms,) = call(
         filter_grad_kernel, [((16, 16, 896), BF)], dy, ring, edge, scratch=[pltpu.VMEM((4, 192, 1024), BF)]
     )
-    *far, terms, dy_next = lax.optimization_barrier((*far, terms, dy_next))
+    far, dy_next, terms, *packed = lax.optimization_barrier((far, dy_next, terms, *packed))
+    far = [to_x(packed[1], 1), far, to_x(packed[3], 3)]
     terms = lax.all_to_all(terms, ALL, 0, 0, axis_index_groups=ZC_GROUPS)
-    both = jnp.stack([dy_copies[0], dy_next])
+    both = jnp.stack([dy_own, dy_next])
     grads = [both] + [to_x(both, d) for d in range(1, 4)]
-    *grads, terms = lax.optimization_barrier((*grads, terms))
+    *far, terms = lax.optimization_barrier((*far, terms))
     (terms,) = call(sum_z_kernel, [((8, 2, 16, 896), BF)], z_odd, terms, scalars=1)
     mine, theirs = call(
         input_grad_kernel,
@@ -358,19 +379,23 @@
     terms = lax.all_to_all(terms, DS, 0, 0, axis_index_groups=Z_GROUPS)
     theirs = to_partner(theirs)
     mine, theirs, terms = lax.optimization_barrier((mine, theirs, terms))
-    back, ahead = over_y(terms, 1), over_y(terms, -1)
+    half = call(cut_kernel, [((4, 2, 16, 896), BF)] * 2, terms)
+    back = [over_y(half[0], 1), over_y(half[1], 1)]
+    ahead = [over_y(half[0], -1), over_y(half[1], -1)]
+    across = [over_y(back[0], 1), over_y(ahead[1], -1)]
     (grad_x,) = call(join_kernel, [((2, 64, 1024), BF)], mine, theirs, matrix)
     grad_w, grad_b = call(
-        filter_out_kernel,
-        [((64, 13824), F32), ((64, 1), F32)],
-        q,
-        terms,
-        back,
-        ahead,
-        over_y(back[:4], 1),
-        over_y(ahead[4:], -1),
-        scalars=1,
-    )
+        filter_out_kernel, [((64, 13824), F32), ((64, 1), F32)], q, *half, *back, *ahead, scalars=1
+    )
+    grad_w = pl.pallas_call(
+        filter_last_kernel,
+        out_shape=jax.ShapeDtypeStruct((64, 13824), F32),
+        in_specs=[SMEM, VMEM, VMEM, pl.BlockSpec(memory_space=pl.ANY)],
+        out_specs=pl.BlockSpec(memory_space=pl.ANY),
+        scratch_shapes=[pltpu.VMEM((64, 3456), F32), pltpu.SemaphoreType.DMA((27,))],
+        input_output_aliases={3: 0},
+        compiler_params=PARAMS,
+    )(q, *across, grad_w)
     return (
         activation.reshape(1, 1, 64, 256),
         grad_x.reshape(1, 2, 64, 1024),

time: 138 us -> 126 us (0.913)
  the two profiles are of different devices: /device:TPU:24 before, /device:TPU:32 now
where the time goes in v4:
time: 126 us; the launch traced here: 124 us
  starting transfers between devices  59.3 us (47%)
  waiting for transfers between devices  39.8 us (32%)
  Pallas kernels  17.4 us (14%)
  local copies, waits for them, and re-layouts  6.33 us (5%)
    pallas_call x12, Pallas kernels, call(): pl.pallas_call(kernel, out_shape=shapes, in_specs=[SMEM] * scalars + [VME...  16 us
    ppermute x6, waiting for transfers between devices, to_x(): return lax.ppermute(a, 'chan', [(i, (i + 2 * d) % 8) for i in range(8)])  15.6 us
    ppermute x3, starting transfers between devices, shift_space(): lax.ppermute(a, 'space', [(i, i + by) for i in range(16) if 0 <= i + by <...  14.3 us
    all_to_all x1, waiting for transfers between devices, per_device(): x_own = lax.all_to_all(copies, 'chan', 0, 0, axis_index_groups=X_GROUPS)  10.2 us
    ppermute x6, starting transfers between devices, over_y(): return lax.ppermute(a, DS, pairs)  9.17 us
    ppermute x6, starting transfers between devices, to_x(): return lax.ppermute(a, 'chan', [(i, (i + 2 * d) % 8) for i in range(8)])  7.82 us
    all_to_all x1, starting transfers between devices, per_device(): terms = lax.all_to_all(terms, ALL, 0, 0, axis_index_groups=ZC_GROUPS)  7.69 us
    all_to_all x1, starting transfers between devices, per_device(): terms = lax.all_to_all(terms, DS, 0, 0, axis_index_groups=Z_GROUPS)  7.21 us
  transfers between devices with their start and end apart: 24, of which 13 were waited for; matrix products, arithmetic and copies ran while one was open for 1% of the time, Pallas kernels for 11%

profile of v4, /device:TPU:32, one launch (start us, length us, event | category | flops | bytes accessed | tf_op | source)
XLA Modules:
  0.0 124.4 jit_solution(1699735261815645620)
XLA Ops:
  0.7 1.2 copy-done.1
  1.8 0.9 copy-done.7
  2.8 1.5 %shard_map.85 = bf16[4,2,4,64,256]{4,3,2,1,0:T(8,128)(2,1)} custom-call(bf16[2,64,1024]{2,1,0:T(8,128)(2,1)S(1)} %bitcast.13, bf16[512,512]{1,0:T(8,128)(2,1)S(1)} %copy-done.1), custom_call_target="tpu_custom_call" | custom-call | tf_op jit(solution)/shard_map/pallas_call | solution.py:294
  4.3 4.3 %all-to-all-start = ((bf16[4,2,4,64,256]{4,3,2,1,0:T(8,128)(2,1)}), bf16[4,2,4,64,256]{4,3,2,1,0:T(8,128)(2,1)}, u32[]{:S(2)}, u32[]{:S(2)}) async-start(bf16[4,2,4,64,256]{4,3,2,1,0:T(8,128)(2,1)} %shard_map.85), calls=%async_computation | async-start | bytes 2097152 | tf_op jit(solution)/shard_map/all_to_all | solution.py:338
  8.6 1.7 %shard_map.86 = (bf16[64,6912]{1,0:T(8,128)(2,1)S(1)}, bf16[64,6912]{1,0:T(8,128)(2,1)}) custom-call(s32[1]{0:T(128)} %bitcast.2.core_ref, bf16[64,13824]{1,0:T(8,128)(2,1)S(1)} %copy-done), custom_call_target="tpu_custom_call" | custom-call | tf_op jit(solution)/shard_map/pallas_call | solution.py:294
  10.7 0.8 copy-done.3
  11.5 0.8 copy-done.9
  12.3 0.8 copy-done.10
  13.0 0.8 copy-done.11
  13.8 10.2 %all-to-all-done.x_ref = bf16[4,2,4,64,256]{4,3,2,1,0:T(8,128)(2,1)} async-done(((bf16[4,2,4,64,256]{4,3,2,1,0:T(8,128)(2,1)}), bf16[4,2,4,64,256]{4,3,2,1,0:T(8,128)(2,1)}, u32[]{:S(2)}, u32[]{:S(2)}) %all-to-all-start) | async-done | bytes 1048608 | tf_op jit(solution)/shard_map/all_to_all | solution.py:338
  24.0 4.6 %all-to-all-start.1 = ((bf16[4,2,4,64,256]{4,3,2,1,0:T(8,128)(2,1)}), bf16[4,2,4,64,256]{4,3,2,1,0:T(8,128)(2,1)S(1)}, u32[]{:S(2)}, u32[]{:S(2)}) async-start(bf16[4,2,4,64,256]{4,3,2,1,0:T(8,128)(2,1)} %all-to-all-done.x_ref), calls=%async_computation.1 | async-start | bytes 2097152 | tf_op jit(solution)/shard_map/all_to_all | solution.py:341
  28.6 1.7 %shard_map.88 = (f32[64,256]{1,0:T(8,128)S(1)}, f32[64,256]{1,0:T(8,128)S(1)}) custom-call(bf16[4,2,4,64,256]{4,3,2,1,0:T(8,128)(2,1)} %all-to-all-done.x_ref, bf16[64,6912]{1,0:T(8,128)(2,1)S(1)} %get-tuple-element.48.w_ref, bf16[64,6912]{1,0:T(8,128)(2,1)S(1)} %collective-permute-done.v_ref), custom_call_target="tpu_custom_call" | custom-call | tf_op jit(solution)/shard_map/pallas_call | solution.py:294
  30.4 1.9 %shard_map.87 = (f32[64,256]{1,0:T(8,128)S(1)}, f32[64,256]{1,0:T(8,128)S(1)}) custom-call(bf16[4,2,4,64,256]{4,3,2,1,0:T(8,128)(2,1)} %all-to-all-done.x_ref, bf16[64,6912]{1,0:T(8,128)(2,1)S(1)} %get-tuple-element.48.w_ref, bf16[64,6912]{1,0:T(8,128)(2,1)S(1)} %collective-permute-done.v_ref), custom_call_target="tpu_custom_call" | custom-call | tf_op jit(solution)/shard_map/pallas_call | solution.py:294
  32.3 0.6 collective-permute-start.1
  32.9 5.4 %collective-permute-start.3 = (f32[64,256]{1,0:T(8,128)S(1)}, f32[64,256]{1,0:T(8,128)S(1)}, u32[]{:S(2)}, u32[]{:S(2)}) collective-permute-start(f32[64,256]{1,0:T(8,128)S(1)} %add.19), channel_id=1, source_target_pairs={{0,8},{8,16},{16,24},{24,32},{32,40},{40,48},{48,56},{56,64},{64,7... | collective-permute-start | bytes 196616 | tf_op jit(solution)/shard_map/ppermute | solution.py:306
  38.4 0.6 collective-permute-start.4
  39.0 2.4 %collective-permute-done.3.c_ref = f32[64,256]{1,0:T(8,128)S(1)} collective-permute-done((f32[64,256]{1,0:T(8,128)S(1)}, f32[64,256]{1,0:T(8,128)S(1)}, u32[]{:S(2)}, u32[]{:S(2)}) %collective-permute-start.3) | collective-permute-done | bytes 65568 | tf_op jit(solution)/shard_map/ppermute | solution.py:306
  41.4 0.8 shard_map.89
  42.3 1.8 %all-to-all-done.1.x_ref = bf16[4,2,4,64,256]{4,3,2,1,0:T(8,128)(2,1)S(1)} async-done(((bf16[4,2,4,64,256]{4,3,2,1,0:T(8,128)(2,1)}), bf16[4,2,4,64,256]{4,3,2,1,0:T(8,128)(2,1)S(1)}, u32[]{:S(2)}, u32[]{:S(2)}) %all-to-all-start.1) | async-done | bytes 1048608 | tf_op jit(solution)/shard_map/all_to_all | solution.py:341
  44.1 3.8 %collective-permute-start.6 = (bf16[2,4,64,256]{3,2,1,0:T(8,128)(2,1)S(1)}, bf16[2,4,64,256]{3,2,1,0:T(8,128)(2,1)S(1)}, u32[]{:S(2)}, u32[]{:S(2)}) collective-permute-start(bf16[2,4,64,256]{3,2,1,0:T(8,128)(2,1)S(1)} %slice_bitcast_fusion), channel_id=1, source_target_pairs={{0,16},{8,24},{16,32},{24,40},{32,48},{40,56},{48,64},{56,72},{64,... | collective-permute-start | bytes 786440 | tf_op jit(solution)/shard_map/ppermute | solution.py:306
  48.0 3.4 %all-to-all-start.2 = ((bf16[8,64,256]{2,1,0:T(8,128)(2,1)}), bf16[8,64,256]{2,1,0:T(8,128)(2,1)S(1)}, u32[]{:S(2)}, u32[]{:S(2)}) async-start(bf16[8,64,256]{2,1,0:T(8,128)(2,1)} %get-tuple-element.58), calls=%async_computation.2 | async-start | bytes 524288 | tf_op jit(solution)/shard_map/all_to_all | solution.py:356
  51.4 5.0 %collective-permute-start.5 = (bf16[64,256]{1,0:T(8,128)(2,1)S(1)}, bf16[64,256]{1,0:T(8,128)(2,1)S(1)}, u32[]{:S(2)}, u32[]{:S(2)}) collective-permute-start(bf16[64,256]{1,0:T(8,128)(2,1)S(1)} %get-tuple-element.57), channel_id=1, source_target_pairs={{8,0},{16,8},{24,16},{32,24},{40,32},{48,40},{56,48},{64,56},{72,6... | collective-permute-start | bytes 98312 | tf_op jit(solution)/shard_map/ppermute | solution.py:306
  56.4 2.8 %all-to-all-done.2.dy_ref = bf16[8,64,256]{2,1,0:T(8,128)(2,1)S(1)} async-done(((bf16[8,64,256]{2,1,0:T(8,128)(2,1)}), bf16[8,64,256]{2,1,0:T(8,128)(2,1)S(1)}, u32[]{:S(2)}, u32[]{:S(2)}) %all-to-all-start.2) | async-done | bytes 262176 | tf_op jit(solution)/shard_map/all_to_all | solution.py:356
  59.2 1.6 %shard_map.90 = bf16[16,16,896]{2,1,0:T(8,128)(2,1)} custom-call(bf16[8,64,256]{2,1,0:T(8,128)(2,1)S(1)} %all-to-all-done.2.dy_ref, bf16[4,2,4,64,256]{4,3,2,1,0:T(8,128)(2,1)S(1)} %all-to-all-done.1.x_ref, bf16[2,4,64,256]{3,2,1,0:T(8,128)(2,1)S(1)} %collective-permute-done.6.e_ref), custom_call_target="tpu_custom_call" | custom-call | tf_op jit(solution)/shard_map/pallas_call | solution.py:294
  60.9 7.7 %all-to-all-start.3 = ((bf16[16,16,896]{2,1,0:T(8,128)(2,1)}), bf16[16,16,896]{2,1,0:T(8,128)(2,1)S(1)}, u32[]{:S(2)}, u32[]{:S(2)}) async-start(bf16[16,16,896]{2,1,0:T(8,128)(2,1)} %shard_map.90), calls=%async_computation.3 | async-start | bytes 917504 | tf_op jit(solution)/shard_map/all_to_all | solution.py:364
  68.5 0.6 collective-permute-start.7
  69.1 2.7 %collective-permute-start.8 = (bf16[64,3456]{1,0:T(8,128)(2,1)}, bf16[64,3456]{1,0:T(8,128)(2,1)S(1)}, u32[]{:S(2)}, u32[]{:S(2)}) collective-permute-start(bf16[64,3456]{1,0:T(8,128)(2,1)} %copy-done.9), channel_id=1, source_target_pairs={{0,6},{1,7},{2,0},{3,1},{4,2},{5,3},{6,4},{7,5},{8,14},{9,15},{10,... | collective-permute-start | bytes 1327112 | tf_op jit(solution)/shard_map/ppermute | solution.py:310
  71.8 10.4 %collective-permute-done.7.refs_1_ = bf16[64,3456]{1,0:T(8,128)(2,1)S(1)} collective-permute-done((bf16[64,3456]{1,0:T(8,128)(2,1)}, bf16[64,3456]{1,0:T(8,128)(2,1)S(1)}, u32[]{:S(2)}, u32[]{:S(2)}) %collective-permute-start.7) | collective-permute-done | bytes 442400 | tf_op jit(solution)/shard_map/ppermute | solution.py:310
  82.2 0.9 shard_map.92
  83.1 7.2 %all-to-all-start.4 = ((bf16[8,2,16,896]{3,2,1,0:T(8,128)(2,1)}), bf16[8,2,16,896]{3,2,1,0:T(8,128)(2,1)S(1)}, u32[]{:S(2)}, u32[]{:S(2)}) async-start(bf16[8,2,16,896]{3,2,1,0:T(8,128)(2,1)} %shard_map.92), calls=%async_computation.4 | async-start | bytes 917504 | tf_op jit(solution)/shard_map/all_to_all | solution.py:379
  90.4 3.0 %collective-permute-start.11 = (bf16[2,64,256]{2,1,0:T(8,128)(2,1)S(1)}, bf16[2,64,256]{2,1,0:T(8,128)(2,1)S(1)}, u32[]{:S(2)}, u32[]{:S(2)}) collective-permute-start(bf16[2,64,256]{2,1,0:T(8,128)(2,1)S(1)} %pad_maximum_fusion.refs_4_), channel_id=1, source_target_pairs={{0,6},{1,7},{2,0},{3,1},{4,2},{5,3},{6,4},{7,5},{8,14},{9,15},{10,... | collective-permute-start | bytes 196616 | tf_op jit(solution)/shard_map/ppermute | solution.py:310
  93.4 1.0 collective-permute-start.9
  94.3 1.6 %collective-permute-done.11.refs_7_ = bf16[2,64,256]{2,1,0:T(8,128)(2,1)S(1)} collective-permute-done((bf16[2,64,256]{2,1,0:T(8,128)(2,1)S(1)}, bf16[2,64,256]{2,1,0:T(8,128)(2,1)S(1)}, u32[]{:S(2)}, u32[]{:S(2)}) %collective-permute-start.11) | collective-permute-done | bytes 65568 | tf_op jit(solution)/shard_map/ppermute | solution.py:310
  95.9 3.4 %collective-permute-done.10.refs_6_ = bf16[2,64,256]{2,1,0:T(8,128)(2,1)S(1)} collective-permute-done((bf16[2,64,256]{2,1,0:T(8,128)(2,1)S(1)}, bf16[2,64,256]{2,1,0:T(8,128)(2,1)S(1)}, u32[]{:S(2)}, u32[]{:S(2)}) %collective-permute-start.10) | collective-permute-done | bytes 65568 | tf_op jit(solution)/shard_map/ppermute | solution.py:310
  99.6 1.0 copy-done.6
  100.6 1.0 shard_map.91
  101.7 1.9 %collective-permute-done.12.b_ref = f32[2,4,64,256]{3,2,1,0:T(8,128)S(1)} collective-permute-done((f32[2,4,64,256]{3,2,1,0:T(8,128)S(1)}, f32[2,4,64,256]{3,2,1,0:T(8,128)S(1)}, u32[]{:S(2)}, u32[]{:S(2)}) %collective-permute-start.12) | collective-permute-done | bytes 524320 | tf_op jit(solution)/shard_map/ppermute | solution.py:323
  103.6 0.8 all-to-all-done.4.r_ref
  104.5 0.5 collective-permute-start.13
  105.0 3.0 %collective-permute-start.15 = (bf16[4,2,16,896]{3,2,1,0:T(8,128)(2,1)S(1)}, bf16[4,2,16,896]{3,2,1,0:T(8,128)(2,1)S(1)}, u32[]{:S(2)}, u32[]{:S(2)}) collective-permute-start(bf16[4,2,16,896]{3,2,1,0:T(8,128)(2,1)S(1)} %get-tuple-element.79.o1), channel_id=1, source_target_pairs={{0,136},{8,128},{16,152},{24,144},{32,168},{40,160},{48,184},{56,1... | collective-permute-start | bytes 688136 | tf_op jit(solution)/shard_map/ppermute | solution.py:319
  108.0 1.6 %collective-permute-start.18 = (bf16[4,2,16,896]{3,2,1,0:T(8,128)(2,1)S(1)}, bf16[4,2,16,896]{3,2,1,0:T(8,128)(2,1)S(1)}, u32[]{:S(2)}, u32[]{:S(2)}) collective-permute-start(bf16[4,2,16,896]{3,2,1,0:T(8,128)(2,1)S(1)} %get-tuple-element.78.o0), channel_id=1, source_target_pairs={{0,136},{8,128},{16,152},{24,144},{32,168},{40,160},{48,184},{56,1... | collective-permute-start | bytes 688136 | tf_op jit(solution)/shard_map/ppermute | solution.py:319
  110.0 3.6 %collective-permute-done.13.a0 = bf16[4,2,16,896]{3,2,1,0:T(8,128)(2,1)S(1)} collective-permute-done((bf16[4,2,16,896]{3,2,1,0:T(8,128)(2,1)S(1)}, bf16[4,2,16,896]{3,2,1,0:T(8,128)(2,1)S(1)}, u32[]{:S(2)}, u32[]{:S(2)}) %collective-permute-start.13) | collective-permute-done | bytes 229408 | tf_op jit(solution)/shard_map/ppermute | solution.py:319
  113.9 0.5 collective-permute-done.15.b1
  114.3 3.4 %collective-permute-start.16 = (bf16[4,2,16,896]{3,2,1,0:T(8,128)(2,1)S(1)}, bf16[4,2,16,896]{3,2,1,0:T(8,128)(2,1)S(1)}, u32[]{:S(2)}, u32[]{:S(2)}) collective-permute-start(bf16[4,2,16,896]{3,2,1,0:T(8,128)(2,1)S(1)} %collective-permute-done.15.b1), channel_id=1, source_target_pairs={{0,136},{8,128},{16,152},{24,144},{32,168},{40,160},{48,184},{56,1... | collective-permute-start | bytes 688136 | tf_op jit(solution)/shard_map/ppermute | solution.py:319
  117.7 1.5 %shard_map.93 = bf16[2,64,1024]{2,1,0:T(8,128)(2,1)} custom-call(f32[2,4,64,256]{3,2,1,0:T(8,128)S(1)} %get-tuple-element.75.a_ref, f32[2,4,64,256]{3,2,1,0:T(8,128)S(1)} %collective-permute-done.12.b_ref, bf16[512,512]{1,0:T(8,128)(2,1)S(1)} %copy-done.2), custom_call_target="tpu_custom_call" | custom-call | tf_op jit(solution)/shard_map/pallas_call | solution.py:294
  119.3 2.8 %shard_map.95 = (f32[64,13824]{1,0:T(8,128)}, f32[64,1]{1,0:T(8,128)S(1)}) custom-call(s32[1]{0:T(128)} %bitcast.11.q_ref, bf16[4,2,16,896]{3,2,1,0:T(8,128)(2,1)S(1)} %get-tuple-element.78.o0, bf16[4,2,16,896]{3,2,1,0:T(8,128)(2,1)S(1)} %get-tuple-element.79.o1, bf16[4,2,16,896]{3,2,1,0:T(8,128)(2,1)S(1)} %collective-permute-done.13.a0, ...), custom_call_target="tpu_custom_call" | custom-call | tf_op jit(solution)/shard_map/pallas_call | solution.py:294
  122.2 0.6 reduce
  122.8 1.4 %shard_map.96 = f32[64,13824]{1,0:T(8,128)} custom-call(s32[1]{0:T(128)} %bitcast.11.q_ref, bf16[4,2,16,896]{3,2,1,0:T(8,128)(2,1)S(1)} %collective-permute-done.14.c_ref, bf16[4,2,16,896]{3,2,1,0:T(8,128)(2,1)S(1)} %collective-permute-done.16.d_ref, f32[64,13824]{1,0:T(8,128)} %get-tuple-element.80.w_in), custom_call_target="tpu_custom_call", output_to_operand_aliasing={{}: (3, {})} | custom-call | tf_op jit(solution)/shard_map/pallas_call | solution.py:390
  (44 shorter events, 1.9 us)
Async XLA Ops:
  0.6 7.9 %copy-start = (bf16[64,13824]{1,0:T(8,128)(2,1)S(1)}, bf16[64,13824]{1,0:T(8,128)(2,1)}, u32[]{:S(2)}) copy-start(bf16[64,13824]{1,0:T(8,128)(2,1)} %w_ref.3) | copy-start | bytes 5308420
  0.6 1.2 copy-start.1
  1.8 0.9 copy-start.7
  4.3 19.7 %all-to-all-start = ((bf16[4,2,4,64,256]{4,3,2,1,0:T(8,128)(2,1)}), bf16[4,2,4,64,256]{4,3,2,1,0:T(8,128)(2,1)}, u32[]{:S(2)}, u32[]{:S(2)}) async-start(bf16[4,2,4,64,256]{4,3,2,1,0:T(8,128)(2,1)} %shard_map.85), calls=%async_computation | async-start | bytes 2097152 | tf_op jit(solution)/shard_map/all_to_all | solution.py:338
  10.3 18.3 %collective-permute-start = (bf16[64,6912]{1,0:T(8,128)(2,1)}, bf16[64,6912]{1,0:T(8,128)(2,1)S(1)}, u32[]{:S(2)}, u32[]{:S(2)}) collective-permute-start(bf16[64,6912]{1,0:T(8,128)(2,1)} %get-tuple-element.49), channel_id=1, source_target_pairs={{0,1},{1,0},{2,3},{3,2},{4,5},{5,4},{6,7},{7,6},{8,9},{9,8},{10,11... | collective-permute-start | bytes 2654216 | tf_op jit(solution)/shard_map/ppermute | solution.py:323
  10.7 0.8 copy-start.3
  11.5 0.8 copy-start.9
  12.2 0.8 copy-start.10
  13.0 0.8 copy-start.11
  24.0 14.3 %copy-start.12 = (f32[64]{0:T(128)S(1)}, f32[64]{0:T(128)}, u32[]{:S(2)}) copy-start(f32[64]{0:T(128)} %param.7) | copy-start | bytes 772
  24.0 17.5 %copy-start.8 = (bf16[1,1,64,256]{3,2,1,0:T(8,128)(2,1)S(1)}, bf16[1,1,64,256]{3,2,1,0:T(8,128)(2,1)}, u32[]{:S(2)}) copy-start(bf16[1,1,64,256]{3,2,1,0:T(8,128)(2,1)} %param.8) | copy-start | bytes 98308
  24.0 20.1 %all-to-all-start.1 = ((bf16[4,2,4,64,256]{4,3,2,1,0:T(8,128)(2,1)}), bf16[4,2,4,64,256]{4,3,2,1,0:T(8,128)(2,1)S(1)}, u32[]{:S(2)}, u32[]{:S(2)}) async-start(bf16[4,2,4,64,256]{4,3,2,1,0:T(8,128)(2,1)} %all-to-all-done.x_ref), calls=%async_computation.1 | async-start | bytes 2097152 | tf_op jit(solution)/shard_map/all_to_all | solution.py:341
  30.3 2.6 %collective-permute-start.2 = (f32[64,256]{1,0:T(8,128)S(1)}, f32[64,256]{1,0:T(8,128)S(1)}, u32[]{:S(2)}, u32[]{:S(2)}) collective-permute-start(f32[64,256]{1,0:T(8,128)S(1)} %get-tuple-element.53), channel_id=1, source_target_pairs={{0,1},{1,0},{2,3},{3,2},{4,5},{5,4},{6,7},{7,6},{8,9},{9,8},{10,11... | collective-permute-start | bytes 196616 | tf_op jit(solution)/shard_map/ppermute | solution.py:323
  32.3 67.3 %copy-start.4 = (bf16[64,3456]{1,0:T(8,128)(2,1)S(1)}, bf16[64,3456]{1,0:T(8,128)(2,1)}, u32[]{:S(2)}) copy-start(bf16[64,3456]{1,0:T(8,128)(2,1)} %copy-done.3) | copy-start | bytes 1327108
  32.3 6.8 %collective-permute-start.1 = (f32[64,256]{1,0:T(8,128)S(1)}, f32[64,256]{1,0:T(8,128)S(1)}, u32[]{:S(2)}, u32[]{:S(2)}) collective-permute-start(f32[64,256]{1,0:T(8,128)S(1)} %get-tuple-element.51), channel_id=1, source_target_pairs={{0,1},{1,0},{2,3},{3,2},{4,5},{5,4},{6,7},{7,6},{8,9},{9,8},{10,11... | collective-permute-start | bytes 196616 | tf_op jit(solution)/shard_map/ppermute | solution.py:323
  32.9 8.6 %collective-permute-start.3 = (f32[64,256]{1,0:T(8,128)S(1)}, f32[64,256]{1,0:T(8,128)S(1)}, u32[]{:S(2)}, u32[]{:S(2)}) collective-permute-start(f32[64,256]{1,0:T(8,128)S(1)} %add.19), channel_id=1, source_target_pairs={{0,8},{8,16},{16,24},{24,32},{32,40},{40,48},{48,56},{56,64},{64,7... | collective-permute-start | bytes 196616 | tf_op jit(solution)/shard_map/ppermute | solution.py:306
  38.4 22.4 %collective-permute-start.4 = (bf16[64,3456]{1,0:T(8,128)(2,1)}, bf16[64,3456]{1,0:T(8,128)(2,1)S(1)}, u32[]{:S(2)}, u32[]{:S(2)}) collective-permute-start(bf16[64,3456]{1,0:T(8,128)(2,1)} %copy-done.11), channel_id=1, source_target_pairs={{0,4},{1,5},{2,6},{3,7},{4,0},{5,1},{6,2},{7,3},{8,12},{9,13},{10,... | collective-permute-start | bytes 1327112 | tf_op jit(solution)/shard_map/ppermute | solution.py:310
  44.1 15.1 %collective-permute-start.6 = (bf16[2,4,64,256]{3,2,1,0:T(8,128)(2,1)S(1)}, bf16[2,4,64,256]{3,2,1,0:T(8,128)(2,1)S(1)}, u32[]{:S(2)}, u32[]{:S(2)}) collective-permute-start(bf16[2,4,64,256]{3,2,1,0:T(8,128)(2,1)S(1)} %slice_bitcast_fusion), channel_id=1, source_target_pairs={{0,16},{8,24},{16,32},{24,40},{32,48},{40,56},{48,64},{56,72},{64,... | collective-permute-start | bytes 786440 | tf_op jit(solution)/shard_map/ppermute | solution.py:306
  48.0 11.2 %all-to-all-start.2 = ((bf16[8,64,256]{2,1,0:T(8,128)(2,1)}), bf16[8,64,256]{2,1,0:T(8,128)(2,1)S(1)}, u32[]{:S(2)}, u32[]{:S(2)}) async-start(bf16[8,64,256]{2,1,0:T(8,128)(2,1)} %get-tuple-element.58), calls=%async_computation.2 | async-start | bytes 524288 | tf_op jit(solution)/shard_map/all_to_all | solution.py:356
  51.4 66.3 %copy-start.2 = (bf16[512,512]{1,0:T(8,128)(2,1)S(1)}, bf16[512,512]{1,0:T(8,128)(2,1)}, u32[]{:S(2)}) copy-start(bf16[512,512]{1,0:T(8,128)(2,1)} %constant.55.clone.m_ref) | copy-start | bytes 1572868
  51.4 9.4 %collective-permute-start.5 = (bf16[64,256]{1,0:T(8,128)(2,1)S(1)}, bf16[64,256]{1,0:T(8,128)(2,1)S(1)}, u32[]{:S(2)}, u32[]{:S(2)}) collective-permute-start(bf16[64,256]{1,0:T(8,128)(2,1)S(1)} %get-tuple-element.57), channel_id=1, source_target_pairs={{8,0},{16,8},{24,16},{32,24},{40,32},{48,40},{56,48},{64,56},{72,6... | collective-permute-start | bytes 98312 | tf_op jit(solution)/shard_map/ppermute | solution.py:306
  60.9 21.3 %all-to-all-start.3 = ((bf16[16,16,896]{2,1,0:T(8,128)(2,1)}), bf16[16,16,896]{2,1,0:T(8,128)(2,1)S(1)}, u32[]{:S(2)}, u32[]{:S(2)}) async-start(bf16[16,16,896]{2,1,0:T(8,128)(2,1)} %shard_map.90), calls=%async_computation.3 | async-start | bytes 917504 | tf_op jit(solution)/shard_map/all_to_all | solution.py:364
  68.5 13.6 %collective-permute-start.7 = (bf16[64,3456]{1,0:T(8,128)(2,1)}, bf16[64,3456]{1,0:T(8,128)(2,1)S(1)}, u32[]{:S(2)}, u32[]{:S(2)}) collective-permute-start(bf16[64,3456]{1,0:T(8,128)(2,1)} %copy-done.10), channel_id=1, source_target_pairs={{0,2},{1,3},{2,4},{3,5},{4,6},{5,7},{6,0},{7,1},{8,10},{9,11},{10,... | collective-permute-start | bytes 1327112 | tf_op jit(solution)/shard_map/ppermute | solution.py:310
  69.1 13.1 %collective-permute-start.8 = (bf16[64,3456]{1,0:T(8,128)(2,1)}, bf16[64,3456]{1,0:T(8,128)(2,1)S(1)}, u32[]{:S(2)}, u32[]{:S(2)}) collective-permute-start(bf16[64,3456]{1,0:T(8,128)(2,1)} %copy-done.9), channel_id=1, source_target_pairs={{0,6},{1,7},{2,0},{3,1},{4,2},{5,3},{6,4},{7,5},{8,14},{9,15},{10,... | collective-permute-start | bytes 1327112 | tf_op jit(solution)/shard_map/ppermute | solution.py:310
  82.2 17.1 %copy-start.5 = (bf16[64,3456]{1,0:T(8,128)(2,1)}, bf16[64,3456]{1,0:T(8,128)(2,1)S(1)}, u32[]{:S(2)}) copy-start(bf16[64,3456]{1,0:T(8,128)(2,1)S(1)} %collective-permute-done.8.refs_3_) | copy-start | bytes 1327108
  83.1 21.3 %all-to-all-start.4 = ((bf16[8,2,16,896]{3,2,1,0:T(8,128)(2,1)}), bf16[8,2,16,896]{3,2,1,0:T(8,128)(2,1)S(1)}, u32[]{:S(2)}, u32[]{:S(2)}) async-start(bf16[8,2,16,896]{3,2,1,0:T(8,128)(2,1)} %shard_map.92), calls=%async_computation.4 | async-start | bytes 917504 | tf_op jit(solution)/shard_map/all_to_all | solution.py:379
  90.4 5.5 %collective-permute-start.11 = (bf16[2,64,256]{2,1,0:T(8,128)(2,1)S(1)}, bf16[2,64,256]{2,1,0:T(8,128)(2,1)S(1)}, u32[]{:S(2)}, u32[]{:S(2)}) collective-permute-start(bf16[2,64,256]{2,1,0:T(8,128)(2,1)S(1)} %pad_maximum_fusion.refs_4_), channel_id=1, source_target_pairs={{0,6},{1,7},{2,0},{3,1},{4,2},{5,3},{6,4},{7,5},{8,14},{9,15},{10,... | collective-permute-start | bytes 196616 | tf_op jit(solution)/shard_map/ppermute | solution.py:310
  93.4 5.9 %collective-permute-start.10 = (bf16[2,64,256]{2,1,0:T(8,128)(2,1)S(1)}, bf16[2,64,256]{2,1,0:T(8,128)(2,1)S(1)}, u32[]{:S(2)}, u32[]{:S(2)}) collective-permute-start(bf16[2,64,256]{2,1,0:T(8,128)(2,1)S(1)} %pad_maximum_fusion.refs_4_), channel_id=1, source_target_pairs={{0,4},{1,5},{2,6},{3,7},{4,0},{5,1},{6,2},{7,3},{8,12},{9,13},{10,... | collective-permute-start | bytes 196616 | tf_op jit(solution)/shard_map/ppermute | solution.py:310
  93.4 6.2 %collective-permute-start.9 = (bf16[2,64,256]{2,1,0:T(8,128)(2,1)S(1)}, bf16[2,64,256]{2,1,0:T(8,128)(2,1)S(1)}, u32[]{:S(2)}, u32[]{:S(2)}) collective-permute-start(bf16[2,64,256]{2,1,0:T(8,128)(2,1)S(1)} %pad_maximum_fusion.refs_4_), channel_id=1, source_target_pairs={{0,2},{1,3},{2,4},{3,5},{4,6},{5,7},{6,0},{7,1},{8,10},{9,11},{10,... | collective-permute-start | bytes 196616 | tf_op jit(solution)/shard_map/ppermute | solution.py:310
  99.6 1.0 copy-start.6
  101.6 2.0 %collective-permute-start.12 = (f32[2,4,64,256]{3,2,1,0:T(8,128)S(1)}, f32[2,4,64,256]{3,2,1,0:T(8,128)S(1)}, u32[]{:S(2)}, u32[]{:S(2)}) collective-permute-start(f32[2,4,64,256]{3,2,1,0:T(8,128)S(1)} %get-tuple-element.73), channel_id=1, source_target_pairs={{0,1},{1,0},{2,3},{3,2},{4,5},{5,4},{6,7},{7,6},{8,9},{9,8},{10,11... | collective-permute-start | bytes 1572872 | tf_op jit(solution)/shard_map/ppermute | solution.py:323
  104.5 9.1 %collective-permute-start.13 = (bf16[4,2,16,896]{3,2,1,0:T(8,128)(2,1)S(1)}, bf16[4,2,16,896]{3,2,1,0:T(8,128)(2,1)S(1)}, u32[]{:S(2)}, u32[]{:S(2)}) collective-permute-start(bf16[4,2,16,896]{3,2,1,0:T(8,128)(2,1)S(1)} %get-tuple-element.78.o0), channel_id=1, source_target_pairs={{0,128},{8,136},{16,144},{24,152},{32,160},{40,168},{48,176},{56,1... | collective-permute-start | bytes 688136 | tf_op jit(solution)/shard_map/ppermute | solution.py:319
  105.0 9.3 %collective-permute-start.15 = (bf16[4,2,16,896]{3,2,1,0:T(8,128)(2,1)S(1)}, bf16[4,2,16,896]{3,2,1,0:T(8,128)(2,1)S(1)}, u32[]{:S(2)}, u32[]{:S(2)}) collective-permute-start(bf16[4,2,16,896]{3,2,1,0:T(8,128)(2,1)S(1)} %get-tuple-element.79.o1), channel_id=1, source_target_pairs={{0,136},{8,128},{16,152},{24,144},{32,168},{40,160},{48,184},{56,1... | collective-permute-start | bytes 688136 | tf_op jit(solution)/shard_map/ppermute | solution.py:319
  108.0 11.2 %collective-permute-start.18 = (bf16[4,2,16,896]{3,2,1,0:T(8,128)(2,1)S(1)}, bf16[4,2,16,896]{3,2,1,0:T(8,128)(2,1)S(1)}, u32[]{:S(2)}, u32[]{:S(2)}) collective-permute-start(bf16[4,2,16,896]{3,2,1,0:T(8,128)(2,1)S(1)} %get-tuple-element.78.o0), channel_id=1, source_target_pairs={{0,136},{8,128},{16,152},{24,144},{32,168},{40,160},{48,184},{56,1... | collective-permute-start | bytes 688136 | tf_op jit(solution)/shard_map/ppermute | solution.py:319
  109.6 9.8 %collective-permute-start.17 = (bf16[4,2,16,896]{3,2,1,0:T(8,128)(2,1)S(1)}, bf16[4,2,16,896]{3,2,1,0:T(8,128)(2,1)S(1)}, u32[]{:S(2)}, u32[]{:S(2)}) collective-permute-start(bf16[4,2,16,896]{3,2,1,0:T(8,128)(2,1)S(1)} %get-tuple-element.79.o1), channel_id=1, source_target_pairs={{0,128},{8,136},{16,144},{24,152},{32,160},{40,168},{48,176},{56,1... | collective-permute-start | bytes 688136 | tf_op jit(solution)/shard_map/ppermute | solution.py:319
  113.6 9.2 %collective-permute-start.14 = (bf16[4,2,16,896]{3,2,1,0:T(8,128)(2,1)S(1)}, bf16[4,2,16,896]{3,2,1,0:T(8,128)(2,1)S(1)}, u32[]{:S(2)}, u32[]{:S(2)}) collective-permute-start(bf16[4,2,16,896]{3,2,1,0:T(8,128)(2,1)S(1)} %collective-permute-done.13.a0), channel_id=1, source_target_pairs={{0,128},{8,136},{16,144},{24,152},{32,160},{40,168},{48,176},{56,1... | collective-permute-start | bytes 688136 | tf_op jit(solution)/shard_map/ppermute | solution.py:319
  114.3 8.5 %collective-permute-start.16 = (bf16[4,2,16,896]{3,2,1,0:T(8,128)(2,1)S(1)}, bf16[4,2,16,896]{3,2,1,0:T(8,128)(2,1)S(1)}, u32[]{:S(2)}, u32[]{:S(2)}) collective-permute-start(bf16[4,2,16,896]{3,2,1,0:T(8,128)(2,1)S(1)} %collective-permute-done.15.b1), channel_id=1, source_target_pairs={{0,136},{8,128},{16,152},{24,144},{32,168},{40,160},{48,184},{56,1... | collective-permute-start | bytes 688136 | tf_op jit(solution)/shard_map/ppermute | solution.py:319

commit v5 on v4

--- a/solution.py
+++ b/solution.py
@@ -31,11 +31,10 @@
 
 
 def split_matrix():
-    matrix = np.zeros((512, 512), np.float32)
-    for y in range(16):
-        for z in range(32):
-            matrix[y * 32 + z, (2 * (y % 2) + z % 2) * 128 + (y // 2) * 16 + z // 2] = 1
-    return matrix
+    cell = lax.broadcasted_iota(jnp.int32, (512, 512), 0)
+    lane = lax.broadcasted_iota(jnp.int32, (512, 512), 1)
+    to = ((cell >> 5) & 1) * 256 + (cell & 1) * 128 + (cell >> 6) * 16 + ((cell & 31) >> 1)
+    return jnp.where(lane == to, 1.0, 0.0).astype(BF)
 
 
 def class_shifts(c):
@@ -71,13 +70,13 @@
     return a
 
 
-def split_kernel(x_ref, m_ref, o_ref):
+def split_kernel(x_ref, o_ref):
+    matrix = split_matrix()
     for p in range(2):
         for h in range(2):
-            r = jnp.dot(x_ref[p, :, h * 512 : (h + 1) * 512], m_ref[...], preferred_element_type=F32).astype(BF)
+            r = jnp.dot(x_ref[p, :, h * 512 : (h + 1) * 512], matrix, preferred_element_type=F32).astype(BF)
             for c in range(4):
-                for copy in range(4):
-                    o_ref[copy, p, c, :, h * 128 : (h + 1) * 128] = r[:, c * 128 : (c + 1) * 128]
+                o_ref[p, c, :, h * 128 : (h + 1) * 128] = r[:, c * 128 : (c + 1) * 128]
 
 
 def halves(a, b):
@@ -85,34 +84,63 @@
     return jnp.where(low, a, pltpu.roll(b, 64, 1)), jnp.where(low, pltpu.roll(a, 64, 1), b)
 
 
-def core_pack_kernel(core_ref, w_ref, keep_ref, send_ref):
-    first = core_ref[0] == 0
+STEPS = (0, 3, 2, 1)
+
+
+def core_pack_kernel(where_ref, w_ref, keep_ref, send_ref):
+    first = where_ref[0] == 0
+    starts = [lax.rem(where_ref[1] + step, 4) * 128 for step in STEPS]
+
+    def block(tap, k):
+        return w_ref[:, pl.ds(pl.multiple_of(tap * 512 + starts[k], 128), 128)].astype(F32)
+
     for tap in range(27):
         for pair in range(2):
-            at = tap * 512 + pair * 256
-            low, high = halves(w_ref[:, at : at + 128].astype(F32), w_ref[:, at + 128 : at + 256].astype(F32))
+            low, high = halves(block(tap, 2 * pair), block(tap, 2 * pair + 1))
             to = tap * 256 + pair * 128
             keep_ref[:, to : to + 128] = jnp.where(first, low, high).astype(BF)
             send_ref[:, to : to + 128] = jnp.where(first, high, low).astype(BF)
 
 
-def forward_kernel(choice, x_ref, w_ref, v_ref, mine_ref, theirs_ref):
-    sums = {}
-    for c in range(4):
-        taps = taps_of(c)
-        for p, k1 in choice:
-            rows = []
-            for tap, _, _ in taps:
-                at = (9 * k1 + tap) * 256
-                rows += [w_ref[:, at : at + 256], v_ref[:, at : at + 256]]
-            cells = jnp.concatenate([x_ref[x, p, c] for x in range(4)], 0)
-            r = jnp.dot(jnp.concatenate(rows, 0), cells, preferred_element_type=F32)
-            for n, (_, sy, sz) in enumerate(taps):
-                value = r[128 * n : 128 * n + 128]
-                sums[sy, sz] = sums[sy, sz] + value if (sy, sz) in sums else value
+def in_order_kernel(x_ref, own_ref, back_ref, ahead_ref, across_0, across_1, o_ref):
+    for step, ref in ((0, own_ref), (3, back_ref), (1, ahead_ref)):
+        o_ref[lax.rem(x_ref[0] + step, 4)] = ref[...]
+    for p, ref in enumerate((across_0, across_1)):
+        o_ref[lax.rem(x_ref[0] + 2, 4), p] = ref[...]
+
+
+def accumulate(sums, c, k1, w_ref, v_ref, cells):
+    taps = taps_of(c)
+    rows = []
+    for tap, _, _ in taps:
+        at = (9 * k1 + tap) * 256
+        rows += [w_ref[:, at : at + 256], v_ref[:, at : at + 256]]
+    r = jnp.dot(jnp.concatenate(rows, 0), jnp.concatenate(cells, 0), preferred_element_type=F32)
+    for m, (_, sy, sz) in enumerate(taps):
+        value = r[128 * m : 128 * m + 128]
+        sums[sy, sz] = sums[sy, sz] + value if (sy, sz) in sums else value
+
+
+def finish(sums, mine_ref, theirs_ref):
     total = sum(later(v, *s) for s, v in sums.items())
     mine_ref[...] = total[:64]
     theirs_ref[...] = total[64:]
+
+
+def next_kernel(own_ref, back_ref, across_ref, ahead_ref, w_ref, v_ref, mine_ref, theirs_ref):
+    sums = {}
+    for c in range(4):
+        accumulate(sums, c, 0, w_ref, v_ref, [own_ref[1, c], back_ref[1, c], across_ref[c], ahead_ref[1, c]])
+    finish(sums, mine_ref, theirs_ref)
+
+
+def forward_kernel(x_ref, all_ref, w_ref, v_ref, mine_ref, theirs_ref):
+    sums = {}
+    at = [lax.rem(x_ref[0] + step, 4) for step in STEPS]
+    for c in range(4):
+        for p in range(2):
+            accumulate(sums, c, p + 1, w_ref, v_ref, [all_ref[i, p, c] for i in at])
+    finish(sums, mine_ref, theirs_ref)
 
 
 def gelu_kernel(a_ref, b_ref, c_ref, bias_ref, g_ref, act_ref, one_ref, dy_ref):
@@ -206,39 +234,49 @@
                 bias[rows, :] = a[:, 64:65] + a[:, 65:66]
 
 
-def filter_out_kernel(q_ref, o0, o1, a0, a1, b0, b1, w_ref, b_ref):
-    def at(tap, source):
+def filter_out_kernel(sources, has_bias, q_ref, *refs):
+    n = 2 * len(sources)
+    ins = refs[:n]
+    if has_bias:
+        w_ref, b_ref, s_ref, sems = refs[n:]
+    else:
+        _, w_ref, s_ref, sems = refs[n:]
+        b_ref = None
+    copies = []
+    for k, source in enumerate(sources):
+
+        def store(rows, tap, value, k=k):
+            s_ref[k, rows, tap * 128 : tap * 128 + 128] = value
+
+        place(ins[2 * k], ins[2 * k + 1], store, b_ref)
         to = lax.rem(q_ref[0] + source, 4) * 128
-        return pl.ds(pl.multiple_of(tap * 512 + to, 128), 128)
-
-    for source, first, second in ((0, o0, o1), (3, a0, a1), (1, b0, b1)):
-
-        def store(rows, tap, value, source=source):
-            w_ref[rows, at(tap, source)] = value
-
-        place(first, second, store, b_ref if source == 0 else None)
-    for tap in range(27):
-        w_ref[:, at(tap, 2)] = jnp.zeros((64, 128), F32)
-
-
-def filter_last_kernel(q_ref, c_ref, d_ref, w_in, w_ref, s_ref, sems):
-    def store(rows, tap, value):
-        s_ref[rows, tap * 128 : tap * 128 + 128] = value
-
-    place(c_ref, d_ref, store, None)
-    to = lax.rem(q_ref[0] + 2, 4) * 128
-    copies = []
-    for tap in range(27):
-        copies.append(
-            pltpu.make_async_copy(
-                s_ref.at[:, pl.ds(tap * 128, 128)],
-                w_ref.at[:, pl.ds(pl.multiple_of(tap * 512 + to, 128), 128)],
-                sems.at[tap],
+        for tap in range(27):
+            copies.append(
+                pltpu.make_async_copy(
+                    s_ref.at[k, :, pl.ds(tap * 128, 128)],
+                    w_ref.at[:, pl.ds(pl.multiple_of(tap * 512 + to, 128), 128)],
+                    sems.at[k * 27 + tap],
+                )
             )
-        )
-        copies[-1].start()
+            copies[-1].start()
     for copy in copies:
         copy.wait()
+
+
+def filter_out(sources, q, pieces, so_far=None):
+    n = len(sources)
+    anywhere = pl.BlockSpec(memory_space=pl.ANY)
+    first = so_far is None
+    shape = jax.ShapeDtypeStruct((64, 13824), F32)
+    return pl.pallas_call(
+        functools.partial(filter_out_kernel, sources, first),
+        out_shape=[shape, jax.ShapeDtypeStruct((64, 1), F32)] if first else shape,
+        in_specs=[SMEM] + [VMEM] * (2 * n) + ([] if first else [anywhere]),
+        out_specs=[anywhere, VMEM] if first else anywhere,
+        scratch_shapes=[pltpu.VMEM((n, 64, 3456), F32), pltpu.SemaphoreType.DMA((27 * n,))],
+        input_output_aliases={} if first else {2 * n + 1: 0},
+        compiler_params=PARAMS,
+    )(q, *pieces, *([] if first else [so_far]))
 
 
 def pack_kernel(x_ref, w_ref, *o_refs):
@@ -274,13 +312,14 @@
             theirs_ref[p, c] = g_ref[pl.ds(other, 64), :]
 
 
-def join_kernel(a_ref, b_ref, m_ref, o_ref):
+def join_kernel(a_ref, b_ref, o_ref):
+    matrix = split_matrix()
     for p in range(2):
         for h in range(2):
             at = slice(h * 128, h * 128 + 128)
             parts = [(a_ref[p, c, :, at] + b_ref[p, c, :, at]).astype(BF) for c in range(4)]
             r = lax.dot_general(
-                jnp.concatenate(parts, 1), m_ref[...], (((1,), (1,)), ((), ())), preferred_element_type=F32
+                jnp.concatenate(parts, 1), matrix, (((1,), (1,)), ((), ())), preferred_element_type=F32
             )
             o_ref[p, :, h * 512 : (h + 1) * 512] = r.astype(BF)
 
@@ -328,22 +367,25 @@
     core = (chan % 2).astype(jnp.int32).reshape(1)
     x = (chan // 2).astype(jnp.int32).reshape(1)
     z_odd = ((lax.axis_index("space") // 2) % 2).astype(jnp.int32).reshape(1)
-    matrix = jnp.asarray(split_matrix(), BF)
 
     q = ((lax.axis_index("space") % 2) * 2 + lax.axis_index("dp")).astype(jnp.int32).reshape(1)
 
-    (copies,) = call(split_kernel, [((4, 2, 4, 64, 256), BF)], volumes.reshape(2, 64, 1024), matrix)
-    w_keep, w_send = call(core_pack_kernel, [((64, 6912), BF)] * 2, core, kernel, scalars=1)
+    (cells,) = call(split_kernel, [((2, 4, 64, 256), BF)], volumes.reshape(2, 64, 1024))
+    w_keep, w_send = call(
+        core_pack_kernel, [((64, 6912), BF)] * 2, jnp.concatenate([core, x]), kernel, scalars=1
+    )
+    back, ahead = to_x(cells, 1), to_x(cells, 3)
+    across = to_x(ahead[0], 3), to_x(back[1], 1)
     w_other = to_partner(w_send)
-    x_own = lax.all_to_all(copies, "chan", 0, 0, axis_index_groups=X_GROUPS)
+    outs = [((64, 256), F32)] * 2
+    following, theirs = call(next_kernel, outs, cells, back, across[1], ahead, w_keep, w_other)
+    following = shift_space(following + to_partner(theirs), 1)
+    (x_own,) = call(in_order_kernel, [((4, 2, 4, 64, 256), BF)], x, cells, back, ahead, *across, scalars=1)
     packed = call(pack_kernel, [((64, 3456), BF)] * 4, x, kernel, scalars=1)
     *packed, x_own = lax.optimization_barrier((*packed, x_own))
     ring = lax.all_to_all(x_own, DS, 0, 0, axis_index_groups=Y_GROUPS)
     far = to_x(packed[2], 2)
-    outs = [((64, 256), F32)] * 2
-    following, theirs = call(functools.partial(forward_kernel, ((1, 0),)), outs, x_own, w_keep, w_other)
-    following = shift_space(following + to_partner(theirs), 1)
-    mine, theirs = call(functools.partial(forward_kernel, ((0, 1), (1, 2))), outs, x_own, w_keep, w_other)
+    mine, theirs = call(forward_kernel, outs, x, x_own, w_keep, w_other, scalars=1)
     parts = (mine, to_partner(theirs), following)
     activation, dy_own, dy_copies = call(
         gelu_kernel,
@@ -383,19 +425,10 @@
     back = [over_y(half[0], 1), over_y(half[1], 1)]
     ahead = [over_y(half[0], -1), over_y(half[1], -1)]
     across = [over_y(back[0], 1), over_y(ahead[1], -1)]
-    (grad_x,) = call(join_kernel, [((2, 64, 1024), BF)], mine, theirs, matrix)
-    grad_w, grad_b = call(
-        filter_out_kernel, [((64, 13824), F32), ((64, 1), F32)], q, *half, *back, *ahead, scalars=1
-    )
-    grad_w = pl.pallas_call(
-        filter_last_kernel,
-        out_shape=jax.ShapeDtypeStruct((64, 13824), F32),
-        in_specs=[SMEM, VMEM, VMEM, pl.BlockSpec(memory_space=pl.ANY)],
-        out_specs=pl.BlockSpec(memory_space=pl.ANY),
-        scratch_shapes=[pltpu.VMEM((64, 3456), F32), pltpu.SemaphoreType.DMA((27,))],
-        input_output_aliases={3: 0},
-        compiler_params=PARAMS,
-    )(q, *across, grad_w)
+    (grad_x,) = call(join_kernel, [((2, 64, 1024), BF)], mine, theirs)
+    grad_w, grad_b = filter_out((0,), q, half)
+    grad_w = filter_out((3, 1), q, back + ahead, grad_w)
+    grad_w = filter_out((2,), q, across, grad_w)
     return (
         activation.reshape(1, 1, 64, 256),
         grad_x.reshape(1, 2, 64, 1024),

time: 126 us -> 123 us (0.976)
  waiting for transfers between devices: 39.8 us -> 35.8 us
  starting transfers between devices: 59.3 us -> 61.8 us
  local copies, waits for them, and re-layouts: 6.33 us -> 4.29 us
    all_to_all x1 -> x0, waiting for transfers between devices: 10.2 us -> none  [per_device(): x_own = lax.all_to_all(copies, 'chan', 0, 0, axis_index_groups=X_GROUPS)]
    ppermute x6 -> x10, waiting for transfers between devices: 15.6 us -> 22.3 us  [to_x(): return lax.ppermute(a, 'chan', [(i, (i + 2 * d) % 8) for i in range(8)])]
    ppermute x6 -> x10, starting transfers between devices: 7.82 us -> 14.1 us  [to_x(): return lax.ppermute(a, 'chan', [(i, (i + 2 * d) % 8) for i in range(8)])]
    all_to_all x1 -> x0, starting transfers between devices: 4.29 us -> none  [per_device(): x_own = lax.all_to_all(copies, 'chan', 0, 0, axis_index_groups=X_GROUPS)]
    pallas_call x1 -> x3, Pallas kernels: 1.43 us -> 5 us  [filter_out(): pl.pallas_call(functools.partial(filter_out_kernel, sources, first), out_...]
    pallas_call x12, Pallas kernels: 16 us -> 12.6 us  [call(): pl.pallas_call(kernel, out_shape=shapes, in_specs=[SMEM] * scalars + [VME...]
    unnamed x26 -> x22, local copies, waits for them, and re-layouts: 6.21 us -> 4.16 us
  transfers between devices with their start and end apart: 24 -> 27, of which waited for: 13 -> 14; matrix products, arithmetic and copies ran while one was open for 1% -> 1% of each run, Pallas kernels for 11% -> 12%
where the time goes in v5:
time: 123 us; the launch traced here: 121 us
  starting transfers between devices  61.8 us (50%)
  waiting for transfers between devices  35.8 us (29%)
  Pallas kernels  17.6 us (14%)
  local copies, waits for them, and re-layouts  4.29 us (3%)
    ppermute x10, waiting for transfers between devices, to_x(): return lax.ppermute(a, 'chan', [(i, (i + 2 * d) % 8) for i in range(8)])  22.3 us
    ppermute x3, starting transfers between devices, shift_space(): lax.ppermute(a, 'space', [(i, i + by) for i in range(16) if 0 <= i + by <...  14.2 us
    ppermute x10, starting transfers between devices, to_x(): return lax.ppermute(a, 'chan', [(i, (i + 2 * d) % 8) for i in range(8)])  14.1 us
    pallas_call x12, Pallas kernels, call(): pl.pallas_call(kernel, out_shape=shapes, in_specs=[SMEM] * scalars + [VME...  12.6 us
    ppermute x6, starting transfers between devices, over_y(): return lax.ppermute(a, DS, pairs)  9.89 us
    all_to_all x1, starting transfers between devices, per_device(): terms = lax.all_to_all(terms, ALL, 0, 0, axis_index_groups=ZC_GROUPS)  7.7 us
    all_to_all x1, starting transfers between devices, per_device(): terms = lax.all_to_all(terms, DS, 0, 0, axis_index_groups=Z_GROUPS)  7.21 us
    pallas_call x3, Pallas kernels, filter_out(): pl.pallas_call(functools.partial(filter_out_kernel, sources, first), out_...  5 us
  transfers between devices with their start and end apart: 27, of which 14 were waited for; matrix products, arithmetic and copies ran while one was open for 1% of the time, Pallas kernels for 12%

profile of v5, /device:TPU:32, one launch (start us, length us, event | category | flops | bytes accessed | tf_op | source)
XLA Modules:
  0.0 121.2 jit_solution(13002898355689830691)
XLA Ops:
  0.6 0.9 copy-done.5
  1.6 0.6 shard_map.76.own_ref
  2.2 2.8 %collective-permute-start.1 = (bf16[2,4,64,256]{3,2,1,0:T(8,128)(2,1)S(1)}, bf16[2,4,64,256]{3,2,1,0:T(8,128)(2,1)S(1)}, u32[]{:S(2)}, u32[]{:S(2)}) collective-permute-start(bf16[2,4,64,256]{3,2,1,0:T(8,128)(2,1)S(1)} %shard_map.76.own_ref), channel_id=1, source_target_pairs={{0,6},{1,7},{2,0},{3,1},{4,2},{5,3},{6,4},{7,5},{8,14},{9,15},{10,... | collective-permute-start | bytes 786440 | tf_op jit(solution)/shard_map/ppermute | solution.py:349
  5.1 1.5 %copy-done = bf16[64,13824]{1,0:T(8,128)(2,1)S(1)} copy-done((bf16[64,13824]{1,0:T(8,128)(2,1)S(1)}, bf16[64,13824]{1,0:T(8,128)(2,1)}, u32[]{:S(2)}) %copy-start) | copy-done | bytes 1769496
  6.6 2.3 %shard_map.78 = (bf16[64,6912]{1,0:T(8,128)(2,1)S(1)}, bf16[64,6912]{1,0:T(8,128)(2,1)}) custom-call(s32[2]{0:T(128)S(1)} %pad_add_fusion.where_ref, bf16[64,13824]{1,0:T(8,128)(2,1)S(1)} %copy-done), custom_call_target="tpu_custom_call" | custom-call | tf_op jit(solution)/shard_map/pallas_call | solution.py:333
  8.9 1.7 %collective-permute-done.1.ahead_ref = bf16[2,4,64,256]{3,2,1,0:T(8,128)(2,1)S(1)} collective-permute-done((bf16[2,4,64,256]{3,2,1,0:T(8,128)(2,1)S(1)}, bf16[2,4,64,256]{3,2,1,0:T(8,128)(2,1)S(1)}, u32[]{:S(2)}, u32[]{:S(2)}) %collective-permute-start.1) | collective-permute-done | bytes 262176 | tf_op jit(solution)/shard_map/ppermute | solution.py:349
  10.6 3.8 %collective-permute-start.2 = (bf16[4,64,256]{2,1,0:T(8,128)(2,1)S(1)}, bf16[4,64,256]{2,1,0:T(8,128)(2,1)S(1)}, u32[]{:S(2)}, u32[]{:S(2)}) collective-permute-start(bf16[4,64,256]{2,1,0:T(8,128)(2,1)S(1)} %slice_bitcast_fusion.2), channel_id=1, source_target_pairs={{0,6},{1,7},{2,0},{3,1},{4,2},{5,3},{6,4},{7,5},{8,14},{9,15},{10,... | collective-permute-start | bytes 393224 | tf_op jit(solution)/shard_map/ppermute | solution.py:349
  14.9 0.8 copy-done.3
  15.6 1.2 %collective-permute-done.2.across_0 = bf16[4,64,256]{2,1,0:T(8,128)(2,1)S(1)} collective-permute-done((bf16[4,64,256]{2,1,0:T(8,128)(2,1)S(1)}, bf16[4,64,256]{2,1,0:T(8,128)(2,1)S(1)}, u32[]{:S(2)}, u32[]{:S(2)}) %collective-permute-start.2) | collective-permute-done | bytes 131104 | tf_op jit(solution)/shard_map/ppermute | solution.py:349
  16.9 3.8 %collective-permute-done.3.across_1.across_ref = bf16[4,64,256]{2,1,0:T(8,128)(2,1)S(1)} collective-permute-done((bf16[4,64,256]{2,1,0:T(8,128)(2,1)S(1)}, bf16[4,64,256]{2,1,0:T(8,128)(2,1)S(1)}, u32[]{:S(2)}, u32[]{:S(2)}) %collective-permute-start.3) | collective-permute-done | bytes 131104 | tf_op jit(solution)/shard_map/ppermute | solution.py:349
  20.7 1.0 shard_map.77.all_ref
  21.7 4.5 %all-to-all-start = ((bf16[4,2,4,64,256]{4,3,2,1,0:T(8,128)(2,1)}), bf16[4,2,4,64,256]{4,3,2,1,0:T(8,128)(2,1)S(1)}, u32[]{:S(2)}, u32[]{:S(2)}) async-start(bf16[4,2,4,64,256]{4,3,2,1,0:T(8,128)(2,1)} %shard_map.77.all_ref), calls=%async_computation | async-start | bytes 2097152 | tf_op jit(solution)/shard_map/all_to_all | solution.py:386
  26.2 0.9 copy-done.2
  27.2 0.4 shard_map.80
  27.7 1.9 %shard_map.79 = (f32[64,256]{1,0:T(8,128)S(1)}, f32[64,256]{1,0:T(8,128)S(1)}) custom-call(s32[1]{0:T(128)} %bitcast.x_ref, bf16[4,2,4,64,256]{4,3,2,1,0:T(8,128)(2,1)} %shard_map.77.all_ref, bf16[64,6912]{1,0:T(8,128)(2,1)S(1)} %get-tuple-element.48.w_ref, bf16[64,6912]{1,0:T(8,128)(2,1)S(1)} %collective-permute-done.4.v_ref), custom_call_target="tpu_custom_call" | custom-call | tf_op jit(solution)/shard_map/pallas_call | solution.py:333
  29.6 0.6 collective-permute-start.5
  30.2 5.4 %collective-permute-start.7 = (f32[64,256]{1,0:T(8,128)S(1)}, f32[64,256]{1,0:T(8,128)S(1)}, u32[]{:S(2)}, u32[]{:S(2)}) collective-permute-start(f32[64,256]{1,0:T(8,128)S(1)} %add.19), channel_id=1, source_target_pairs={{0,8},{8,16},{16,24},{24,32},{32,40},{40,48},{48,56},{56,64},{64,7... | collective-permute-start | bytes 196616 | tf_op jit(solution)/shard_map/ppermute | solution.py:345
  35.8 2.9 %collective-permute-done.7.c_ref = f32[64,256]{1,0:T(8,128)S(1)} collective-permute-done((f32[64,256]{1,0:T(8,128)S(1)}, f32[64,256]{1,0:T(8,128)S(1)}, u32[]{:S(2)}, u32[]{:S(2)}) %collective-permute-start.7) | collective-permute-done | bytes 65568 | tf_op jit(solution)/shard_map/ppermute | solution.py:345
  38.8 0.8 shard_map.81
  39.6 0.8 all-to-all-done.x_ref
  40.4 3.8 %collective-permute-start.10 = (bf16[2,4,64,256]{3,2,1,0:T(8,128)(2,1)S(1)}, bf16[2,4,64,256]{3,2,1,0:T(8,128)(2,1)S(1)}, u32[]{:S(2)}, u32[]{:S(2)}) collective-permute-start(bf16[2,4,64,256]{3,2,1,0:T(8,128)(2,1)S(1)} %slice_bitcast_fusion), channel_id=1, source_target_pairs={{0,16},{8,24},{16,32},{24,40},{32,48},{40,56},{48,64},{56,72},{64,... | collective-permute-start | bytes 786440 | tf_op jit(solution)/shard_map/ppermute | solution.py:345
  44.3 3.4 %all-to-all-start.1 = ((bf16[8,64,256]{2,1,0:T(8,128)(2,1)}), bf16[8,64,256]{2,1,0:T(8,128)(2,1)S(1)}, u32[]{:S(2)}, u32[]{:S(2)}) async-start(bf16[8,64,256]{2,1,0:T(8,128)(2,1)} %get-tuple-element.58), calls=%async_computation.1 | async-start | bytes 524288 | tf_op jit(solution)/shard_map/all_to_all | solution.py:398
  47.7 4.9 %collective-permute-start.9 = (bf16[64,256]{1,0:T(8,128)(2,1)S(1)}, bf16[64,256]{1,0:T(8,128)(2,1)S(1)}, u32[]{:S(2)}, u32[]{:S(2)}) collective-permute-start(bf16[64,256]{1,0:T(8,128)(2,1)S(1)} %get-tuple-element.57), channel_id=1, source_target_pairs={{8,0},{16,8},{24,16},{32,24},{40,32},{48,40},{56,48},{64,56},{72,6... | collective-permute-start | bytes 98312 | tf_op jit(solution)/shard_map/ppermute | solution.py:345
  52.6 2.9 %all-to-all-done.1.dy_ref = bf16[8,64,256]{2,1,0:T(8,128)(2,1)S(1)} async-done(((bf16[8,64,256]{2,1,0:T(8,128)(2,1)}), bf16[8,64,256]{2,1,0:T(8,128)(2,1)S(1)}, u32[]{:S(2)}, u32[]{:S(2)}) %all-to-all-start.1) | async-done | bytes 262176 | tf_op jit(solution)/shard_map/all_to_all | solution.py:398
  55.5 1.6 %shard_map.82 = bf16[16,16,896]{2,1,0:T(8,128)(2,1)} custom-call(bf16[8,64,256]{2,1,0:T(8,128)(2,1)S(1)} %all-to-all-done.1.dy_ref, bf16[4,2,4,64,256]{4,3,2,1,0:T(8,128)(2,1)S(1)} %all-to-all-done.x_ref, bf16[2,4,64,256]{3,2,1,0:T(8,128)(2,1)S(1)} %collective-permute-done.10.e_ref), custom_call_target="tpu_custom_call" | custom-call | tf_op jit(solution)/shard_map/pallas_call | solution.py:333
  57.1 7.7 %all-to-all-start.2 = ((bf16[16,16,896]{2,1,0:T(8,128)(2,1)}), bf16[16,16,896]{2,1,0:T(8,128)(2,1)S(1)}, u32[]{:S(2)}, u32[]{:S(2)}) async-start(bf16[16,16,896]{2,1,0:T(8,128)(2,1)} %shard_map.82), calls=%async_computation.2 | async-start | bytes 917504 | tf_op jit(solution)/shard_map/all_to_all | solution.py:406
  64.8 3.2 %collective-permute-start.12 = (bf16[64,3456]{1,0:T(8,128)(2,1)}, bf16[64,3456]{1,0:T(8,128)(2,1)S(1)}, u32[]{:S(2)}, u32[]{:S(2)}) collective-permute-start(bf16[64,3456]{1,0:T(8,128)(2,1)} %copy-done.7), channel_id=1, source_target_pairs={{0,6},{1,7},{2,0},{3,1},{4,2},{5,3},{6,4},{7,5},{8,14},{9,15},{10,... | collective-permute-start | bytes 1327112 | tf_op jit(solution)/shard_map/ppermute | solution.py:349
  68.1 10.4 %collective-permute-done.11.refs_1_ = bf16[64,3456]{1,0:T(8,128)(2,1)S(1)} collective-permute-done((bf16[64,3456]{1,0:T(8,128)(2,1)}, bf16[64,3456]{1,0:T(8,128)(2,1)S(1)}, u32[]{:S(2)}, u32[]{:S(2)}) %collective-permute-start.11) | collective-permute-done | bytes 442400 | tf_op jit(solution)/shard_map/ppermute | solution.py:349
  78.5 0.9 shard_map.84
  79.4 7.2 %all-to-all-start.3 = ((bf16[8,2,16,896]{3,2,1,0:T(8,128)(2,1)}), bf16[8,2,16,896]{3,2,1,0:T(8,128)(2,1)S(1)}, u32[]{:S(2)}, u32[]{:S(2)}) async-start(bf16[8,2,16,896]{3,2,1,0:T(8,128)(2,1)} %shard_map.84), calls=%async_computation.3 | async-start | bytes 917504 | tf_op jit(solution)/shard_map/all_to_all | solution.py:421
  86.6 3.2 %collective-permute-start.15 = (bf16[2,64,256]{2,1,0:T(8,128)(2,1)S(1)}, bf16[2,64,256]{2,1,0:T(8,128)(2,1)S(1)}, u32[]{:S(2)}, u32[]{:S(2)}) collective-permute-start(bf16[2,64,256]{2,1,0:T(8,128)(2,1)S(1)} %pad_maximum_fusion.refs_4_), channel_id=1, source_target_pairs={{0,6},{1,7},{2,0},{3,1},{4,2},{5,3},{6,4},{7,5},{8,14},{9,15},{10,... | collective-permute-start | bytes 196616 | tf_op jit(solution)/shard_map/ppermute | solution.py:349
  89.8 1.0 collective-permute-start.13
  90.8 1.6 %collective-permute-done.15.refs_7_ = bf16[2,64,256]{2,1,0:T(8,128)(2,1)S(1)} collective-permute-done((bf16[2,64,256]{2,1,0:T(8,128)(2,1)S(1)}, bf16[2,64,256]{2,1,0:T(8,128)(2,1)S(1)}, u32[]{:S(2)}, u32[]{:S(2)}) %collective-permute-start.15) | collective-permute-done | bytes 65568 | tf_op jit(solution)/shard_map/ppermute | solution.py:349
  92.4 3.4 %collective-permute-done.14.refs_6_ = bf16[2,64,256]{2,1,0:T(8,128)(2,1)S(1)} collective-permute-done((bf16[2,64,256]{2,1,0:T(8,128)(2,1)S(1)}, bf16[2,64,256]{2,1,0:T(8,128)(2,1)S(1)}, u32[]{:S(2)}, u32[]{:S(2)}) %collective-permute-start.14) | collective-permute-done | bytes 65568 | tf_op jit(solution)/shard_map/ppermute | solution.py:349
  96.0 1.0 shard_map.83
  97.1 1.9 %collective-permute-done.16.b_ref = f32[2,4,64,256]{3,2,1,0:T(8,128)S(1)} collective-permute-done((f32[2,4,64,256]{3,2,1,0:T(8,128)S(1)}, f32[2,4,64,256]{3,2,1,0:T(8,128)S(1)}, u32[]{:S(2)}, u32[]{:S(2)}) %collective-permute-start.16) | collective-permute-done | bytes 524320 | tf_op jit(solution)/shard_map/ppermute | solution.py:362
  99.0 1.7 %all-to-all-done.3.r_ref = bf16[8,2,16,896]{3,2,1,0:T(8,128)(2,1)S(1)} async-done(((bf16[8,2,16,896]{3,2,1,0:T(8,128)(2,1)}), bf16[8,2,16,896]{3,2,1,0:T(8,128)(2,1)S(1)}, u32[]{:S(2)}, u32[]{:S(2)}) %all-to-all-start.3) | async-done | bytes 458784 | tf_op jit(solution)/shard_map/all_to_all | solution.py:421
  101.1 3.0 %collective-permute-start.19 = (bf16[4,2,16,896]{3,2,1,0:T(8,128)(2,1)S(1)}, bf16[4,2,16,896]{3,2,1,0:T(8,128)(2,1)S(1)}, u32[]{:S(2)}, u32[]{:S(2)}) collective-permute-start(bf16[4,2,16,896]{3,2,1,0:T(8,128)(2,1)S(1)} %get-tuple-element.79.refs_1_), channel_id=1, source_target_pairs={{0,136},{8,128},{16,152},{24,144},{32,168},{40,160},{48,184},{56,1... | collective-permute-start | bytes 688136 | tf_op jit(solution)/shard_map/ppermute | solution.py:358
  104.1 1.9 %collective-permute-start.22 = (bf16[4,2,16,896]{3,2,1,0:T(8,128)(2,1)S(1)}, bf16[4,2,16,896]{3,2,1,0:T(8,128)(2,1)S(1)}, u32[]{:S(2)}, u32[]{:S(2)}) collective-permute-start(bf16[4,2,16,896]{3,2,1,0:T(8,128)(2,1)S(1)} %get-tuple-element.78.refs_0_), channel_id=1, source_target_pairs={{0,136},{8,128},{16,152},{24,144},{32,168},{40,160},{48,184},{56,1... | collective-permute-start | bytes 688136 | tf_op jit(solution)/shard_map/ppermute | solution.py:358
  106.1 2.7 %collective-permute-done.17.refs_0_ = bf16[4,2,16,896]{3,2,1,0:T(8,128)(2,1)S(1)} collective-permute-done((bf16[4,2,16,896]{3,2,1,0:T(8,128)(2,1)S(1)}, bf16[4,2,16,896]{3,2,1,0:T(8,128)(2,1)S(1)}, u32[]{:S(2)}, u32[]{:S(2)}) %collective-permute-start.17) | collective-permute-done | bytes 229408 | tf_op jit(solution)/shard_map/ppermute | solution.py:358
  108.8 1.4 %collective-permute-start.18 = (bf16[4,2,16,896]{3,2,1,0:T(8,128)(2,1)S(1)}, bf16[4,2,16,896]{3,2,1,0:T(8,128)(2,1)S(1)}, u32[]{:S(2)}, u32[]{:S(2)}) collective-permute-start(bf16[4,2,16,896]{3,2,1,0:T(8,128)(2,1)S(1)} %collective-permute-done.17.refs_0_), channel_id=1, source_target_pairs={{0,128},{8,136},{16,144},{24,152},{32,160},{40,168},{48,176},{56,1... | collective-permute-start | bytes 688136 | tf_op jit(solution)/shard_map/ppermute | solution.py:358
  110.2 0.5 collective-permute-done.19.refs_3_
  110.7 3.2 %collective-permute-start.20 = (bf16[4,2,16,896]{3,2,1,0:T(8,128)(2,1)S(1)}, bf16[4,2,16,896]{3,2,1,0:T(8,128)(2,1)S(1)}, u32[]{:S(2)}, u32[]{:S(2)}) collective-permute-start(bf16[4,2,16,896]{3,2,1,0:T(8,128)(2,1)S(1)} %collective-permute-done.19.refs_3_), channel_id=1, source_target_pairs={{0,136},{8,128},{16,152},{24,144},{32,168},{40,160},{48,184},{56,1... | collective-permute-start | bytes 688136 | tf_op jit(solution)/shard_map/ppermute | solution.py:358
  113.8 1.6 %shard_map.87 = (f32[64,13824]{1,0:T(8,128)}, f32[64,1]{1,0:T(8,128)S(1)}) custom-call(s32[1]{0:T(128)} %bitcast.13.q_ref, bf16[4,2,16,896]{3,2,1,0:T(8,128)(2,1)S(1)} %get-tuple-element.78.refs_0_, bf16[4,2,16,896]{3,2,1,0:T(8,128)(2,1)S(1)} %get-tuple-element.79.refs_1_), custom_call_target="tpu_custom_call" | custom-call | tf_op jit(solution)/shard_map/pallas_call | solution.py:271
  115.5 1.5 %shard_map.85 = bf16[2,64,1024]{2,1,0:T(8,128)(2,1)} custom-call(f32[2,4,64,256]{3,2,1,0:T(8,128)S(1)} %get-tuple-element.75.a_ref, f32[2,4,64,256]{3,2,1,0:T(8,128)S(1)} %collective-permute-done.16.b_ref), custom_call_target="tpu_custom_call" | custom-call | tf_op jit(solution)/shard_map/pallas_call | solution.py:333
  117.0 0.6 reduce
  117.7 2.0 %shard_map.88.refs_2_ = f32[64,13824]{1,0:T(8,128)} custom-call(s32[1]{0:T(128)} %bitcast.13.q_ref, bf16[4,2,16,896]{3,2,1,0:T(8,128)(2,1)S(1)} %collective-permute-done.17.refs_0_, bf16[4,2,16,896]{3,2,1,0:T(8,128)(2,1)S(1)} %collective-permute-done.21.refs_1_, ...), custom_call_target="tpu_custom_call", output_to_operand_aliasing={{}: (5, {})} | custom-call | tf_op jit(solution)/shard_map/pallas_call | solution.py:271
  119.6 1.4 %shard_map.89 = f32[64,13824]{1,0:T(8,128)} custom-call(s32[1]{0:T(128)} %bitcast.13.q_ref, bf16[4,2,16,896]{3,2,1,0:T(8,128)(2,1)S(1)} %collective-permute-done.18.refs_0_, bf16[4,2,16,896]{3,2,1,0:T(8,128)(2,1)S(1)} %collective-permute-done.20.refs_1_, f32[64,13824]{1,0:T(8,128)} %shard_map.88.refs_2_), custom_call_target="tpu_custom_call", output_to_operand_aliasing={{}: (3, {})} | custom-call | tf_op jit(solution)/shard_map/pallas_call | solution.py:271
  (51 shorter events, 1.8 us)
Async XLA Ops:
  0.6 1.0 copy-start.5
  2.2 8.4 %collective-permute-start.1 = (bf16[2,4,64,256]{3,2,1,0:T(8,128)(2,1)S(1)}, bf16[2,4,64,256]{3,2,1,0:T(8,128)(2,1)S(1)}, u32[]{:S(2)}, u32[]{:S(2)}) collective-permute-start(bf16[2,4,64,256]{3,2,1,0:T(8,128)(2,1)S(1)} %shard_map.76.own_ref), channel_id=1, source_target_pairs={{0,6},{1,7},{2,0},{3,1},{4,2},{5,3},{6,4},{7,5},{8,14},{9,15},{10,... | collective-permute-start | bytes 786440 | tf_op jit(solution)/shard_map/ppermute | solution.py:349
  5.0 9.3 %collective-permute-start = (bf16[2,4,64,256]{3,2,1,0:T(8,128)(2,1)S(1)}, bf16[2,4,64,256]{3,2,1,0:T(8,128)(2,1)S(1)}, u32[]{:S(2)}, u32[]{:S(2)}) collective-permute-start(bf16[2,4,64,256]{3,2,1,0:T(8,128)(2,1)S(1)} %shard_map.76.own_ref), channel_id=1, source_target_pairs={{0,2},{1,3},{2,4},{3,5},{4,6},{5,7},{6,0},{7,1},{8,10},{9,11},{10,... | collective-permute-start | bytes 786440 | tf_op jit(solution)/shard_map/ppermute | solution.py:349
  5.1 1.5 %copy-start = (bf16[64,13824]{1,0:T(8,128)(2,1)S(1)}, bf16[64,13824]{1,0:T(8,128)(2,1)}, u32[]{:S(2)}) copy-start(bf16[64,13824]{1,0:T(8,128)(2,1)} %w_ref.3) | copy-start | bytes 5308420
  8.9 17.3 %collective-permute-start.4 = (bf16[64,6912]{1,0:T(8,128)(2,1)}, bf16[64,6912]{1,0:T(8,128)(2,1)S(1)}, u32[]{:S(2)}, u32[]{:S(2)}) collective-permute-start(bf16[64,6912]{1,0:T(8,128)(2,1)} %get-tuple-element.49), channel_id=1, source_target_pairs={{0,1},{1,0},{2,3},{3,2},{4,5},{5,4},{6,7},{7,6},{8,9},{9,8},{10,11... | collective-permute-start | bytes 2654216 | tf_op jit(solution)/shard_map/ppermute | solution.py:362
  10.6 6.3 %collective-permute-start.2 = (bf16[4,64,256]{2,1,0:T(8,128)(2,1)S(1)}, bf16[4,64,256]{2,1,0:T(8,128)(2,1)S(1)}, u32[]{:S(2)}, u32[]{:S(2)}) collective-permute-start(bf16[4,64,256]{2,1,0:T(8,128)(2,1)S(1)} %slice_bitcast_fusion.2), channel_id=1, source_target_pairs={{0,6},{1,7},{2,0},{3,1},{4,2},{5,3},{6,4},{7,5},{8,14},{9,15},{10,... | collective-permute-start | bytes 393224 | tf_op jit(solution)/shard_map/ppermute | solution.py:349
  14.4 7.3 %copy-start.1 = (bf16[2,4,64,256]{3,2,1,0:T(8,128)(2,1)}, bf16[2,4,64,256]{3,2,1,0:T(8,128)(2,1)S(1)}, u32[]{:S(2)}) copy-start(bf16[2,4,64,256]{3,2,1,0:T(8,128)(2,1)S(1)} %collective-permute-done.back_ref) | copy-start | bytes 786436
  14.4 6.3 %collective-permute-start.3 = (bf16[4,64,256]{2,1,0:T(8,128)(2,1)S(1)}, bf16[4,64,256]{2,1,0:T(8,128)(2,1)S(1)}, u32[]{:S(2)}, u32[]{:S(2)}) collective-permute-start(bf16[4,64,256]{2,1,0:T(8,128)(2,1)S(1)} %slice_bitcast_fusion.1), channel_id=1, source_target_pairs={{0,2},{1,3},{2,4},{3,5},{4,6},{5,7},{6,0},{7,1},{8,10},{9,11},{10,... | collective-permute-start | bytes 393224 | tf_op jit(solution)/shard_map/ppermute | solution.py:349
  14.9 0.8 copy-start.3
  15.6 6.1 %copy-start.8 = (bf16[64,3456]{1,0:T(8,128)(2,1)}, bf16[64,3456]{1,0:T(8,128)(2,1)S(1)}, u32[]{:S(2)}) copy-start(bf16[64,3456]{1,0:T(8,128)(2,1)S(1)} %get-tuple-element.64) | copy-start | bytes 1327108
  15.6 6.1 %copy-start.9 = (bf16[64,3456]{1,0:T(8,128)(2,1)}, bf16[64,3456]{1,0:T(8,128)(2,1)S(1)}, u32[]{:S(2)}) copy-start(bf16[64,3456]{1,0:T(8,128)(2,1)S(1)} %get-tuple-element.55) | copy-start | bytes 1327108
  15.6 6.1 %copy-start.7 = (bf16[64,3456]{1,0:T(8,128)(2,1)}, bf16[64,3456]{1,0:T(8,128)(2,1)S(1)}, u32[]{:S(2)}) copy-start(bf16[64,3456]{1,0:T(8,128)(2,1)S(1)} %get-tuple-element.66) | copy-start | bytes 1327108
  21.7 13.9 %copy-start.10 = (f32[64]{0:T(128)S(1)}, f32[64]{0:T(128)}, u32[]{:S(2)}) copy-start(f32[64]{0:T(128)} %param.6) | copy-start | bytes 772
  21.7 17.1 %copy-start.6 = (bf16[1,1,64,256]{3,2,1,0:T(8,128)(2,1)S(1)}, bf16[1,1,64,256]{3,2,1,0:T(8,128)(2,1)}, u32[]{:S(2)}) copy-start(bf16[1,1,64,256]{3,2,1,0:T(8,128)(2,1)} %param.7) | copy-start | bytes 98308
  21.7 18.7 %all-to-all-start = ((bf16[4,2,4,64,256]{4,3,2,1,0:T(8,128)(2,1)}), bf16[4,2,4,64,256]{4,3,2,1,0:T(8,128)(2,1)S(1)}, u32[]{:S(2)}, u32[]{:S(2)}) async-start(bf16[4,2,4,64,256]{4,3,2,1,0:T(8,128)(2,1)} %shard_map.77.all_ref), calls=%async_computation | async-start | bytes 2097152 | tf_op jit(solution)/shard_map/all_to_all | solution.py:386
  26.2 1.0 copy-start.2
  27.6 2.6 %collective-permute-start.6 = (f32[64,256]{1,0:T(8,128)S(1)}, f32[64,256]{1,0:T(8,128)S(1)}, u32[]{:S(2)}, u32[]{:S(2)}) collective-permute-start(f32[64,256]{1,0:T(8,128)S(1)} %get-tuple-element.53), channel_id=1, source_target_pairs={{0,1},{1,0},{2,3},{3,2},{4,5},{5,4},{6,7},{7,6},{8,9},{9,8},{10,11... | collective-permute-start | bytes 196616 | tf_op jit(solution)/shard_map/ppermute | solution.py:362
  29.6 66.4 %copy-start.4 = (bf16[64,3456]{1,0:T(8,128)(2,1)S(1)}, bf16[64,3456]{1,0:T(8,128)(2,1)}, u32[]{:S(2)}) copy-start(bf16[64,3456]{1,0:T(8,128)(2,1)} %copy-done.3) | copy-start | bytes 1327108
  29.6 6.2 %collective-permute-start.5 = (f32[64,256]{1,0:T(8,128)S(1)}, f32[64,256]{1,0:T(8,128)S(1)}, u32[]{:S(2)}, u32[]{:S(2)}) collective-permute-start(f32[64,256]{1,0:T(8,128)S(1)} %get-tuple-element.51), channel_id=1, source_target_pairs={{0,1},{1,0},{2,3},{3,2},{4,5},{5,4},{6,7},{7,6},{8,9},{9,8},{10,11... | collective-permute-start | bytes 196616 | tf_op jit(solution)/shard_map/ppermute | solution.py:362
  30.2 8.6 %collective-permute-start.7 = (f32[64,256]{1,0:T(8,128)S(1)}, f32[64,256]{1,0:T(8,128)S(1)}, u32[]{:S(2)}, u32[]{:S(2)}) collective-permute-start(f32[64,256]{1,0:T(8,128)S(1)} %add.19), channel_id=1, source_target_pairs={{0,8},{8,16},{16,24},{24,32},{32,40},{40,48},{48,56},{56,64},{64,7... | collective-permute-start | bytes 196616 | tf_op jit(solution)/shard_map/ppermute | solution.py:345
  35.7 21.4 %collective-permute-start.8 = (bf16[64,3456]{1,0:T(8,128)(2,1)}, bf16[64,3456]{1,0:T(8,128)(2,1)S(1)}, u32[]{:S(2)}, u32[]{:S(2)}) collective-permute-start(bf16[64,3456]{1,0:T(8,128)(2,1)} %copy-done.9), channel_id=1, source_target_pairs={{0,4},{1,5},{2,6},{3,7},{4,0},{5,1},{6,2},{7,3},{8,12},{9,13},{10,... | collective-permute-start | bytes 1327112 | tf_op jit(solution)/shard_map/ppermute | solution.py:349
  40.4 15.1 %collective-permute-start.10 = (bf16[2,4,64,256]{3,2,1,0:T(8,128)(2,1)S(1)}, bf16[2,4,64,256]{3,2,1,0:T(8,128)(2,1)S(1)}, u32[]{:S(2)}, u32[]{:S(2)}) collective-permute-start(bf16[2,4,64,256]{3,2,1,0:T(8,128)(2,1)S(1)} %slice_bitcast_fusion), channel_id=1, source_target_pairs={{0,16},{8,24},{16,32},{24,40},{32,48},{40,56},{48,64},{56,72},{64,... | collective-permute-start | bytes 786440 | tf_op jit(solution)/shard_map/ppermute | solution.py:345
  44.3 11.2 %all-to-all-start.1 = ((bf16[8,64,256]{2,1,0:T(8,128)(2,1)}), bf16[8,64,256]{2,1,0:T(8,128)(2,1)S(1)}, u32[]{:S(2)}, u32[]{:S(2)}) async-start(bf16[8,64,256]{2,1,0:T(8,128)(2,1)} %get-tuple-element.58), calls=%async_computation.1 | async-start | bytes 524288 | tf_op jit(solution)/shard_map/all_to_all | solution.py:398
  47.7 9.4 %collective-permute-start.9 = (bf16[64,256]{1,0:T(8,128)(2,1)S(1)}, bf16[64,256]{1,0:T(8,128)(2,1)S(1)}, u32[]{:S(2)}, u32[]{:S(2)}) collective-permute-start(bf16[64,256]{1,0:T(8,128)(2,1)S(1)} %get-tuple-element.57), channel_id=1, source_target_pairs={{8,0},{16,8},{24,16},{32,24},{40,32},{48,40},{56,48},{64,56},{72,6... | collective-permute-start | bytes 98312 | tf_op jit(solution)/shard_map/ppermute | solution.py:345
  57.1 21.3 %all-to-all-start.2 = ((bf16[16,16,896]{2,1,0:T(8,128)(2,1)}), bf16[16,16,896]{2,1,0:T(8,128)(2,1)S(1)}, u32[]{:S(2)}, u32[]{:S(2)}) async-start(bf16[16,16,896]{2,1,0:T(8,128)(2,1)} %shard_map.82), calls=%async_computation.2 | async-start | bytes 917504 | tf_op jit(solution)/shard_map/all_to_all | solution.py:406
  64.8 13.6 %collective-permute-start.11 = (bf16[64,3456]{1,0:T(8,128)(2,1)}, bf16[64,3456]{1,0:T(8,128)(2,1)S(1)}, u32[]{:S(2)}, u32[]{:S(2)}) collective-permute-start(bf16[64,3456]{1,0:T(8,128)(2,1)} %copy-done.8), channel_id=1, source_target_pairs={{0,2},{1,3},{2,4},{3,5},{4,6},{5,7},{6,0},{7,1},{8,10},{9,11},{10,... | collective-permute-start | bytes 1327112 | tf_op jit(solution)/shard_map/ppermute | solution.py:349
  64.8 13.6 %collective-permute-start.12 = (bf16[64,3456]{1,0:T(8,128)(2,1)}, bf16[64,3456]{1,0:T(8,128)(2,1)S(1)}, u32[]{:S(2)}, u32[]{:S(2)}) collective-permute-start(bf16[64,3456]{1,0:T(8,128)(2,1)} %copy-done.7), channel_id=1, source_target_pairs={{0,6},{1,7},{2,0},{3,1},{4,2},{5,3},{6,4},{7,5},{8,14},{9,15},{10,... | collective-permute-start | bytes 1327112 | tf_op jit(solution)/shard_map/ppermute | solution.py:349
  79.4 21.3 %all-to-all-start.3 = ((bf16[8,2,16,896]{3,2,1,0:T(8,128)(2,1)}), bf16[8,2,16,896]{3,2,1,0:T(8,128)(2,1)S(1)}, u32[]{:S(2)}, u32[]{:S(2)}) async-start(bf16[8,2,16,896]{3,2,1,0:T(8,128)(2,1)} %shard_map.84), calls=%async_computation.3 | async-start | bytes 917504 | tf_op jit(solution)/shard_map/all_to_all | solution.py:421
  86.6 5.7 %collective-permute-start.15 = (bf16[2,64,256]{2,1,0:T(8,128)(2,1)S(1)}, bf16[2,64,256]{2,1,0:T(8,128)(2,1)S(1)}, u32[]{:S(2)}, u32[]{:S(2)}) collective-permute-start(bf16[2,64,256]{2,1,0:T(8,128)(2,1)S(1)} %pad_maximum_fusion.refs_4_), channel_id=1, source_target_pairs={{0,6},{1,7},{2,0},{3,1},{4,2},{5,3},{6,4},{7,5},{8,14},{9,15},{10,... | collective-permute-start | bytes 196616 | tf_op jit(solution)/shard_map/ppermute | solution.py:349
  89.8 5.9 %collective-permute-start.14 = (bf16[2,64,256]{2,1,0:T(8,128)(2,1)S(1)}, bf16[2,64,256]{2,1,0:T(8,128)(2,1)S(1)}, u32[]{:S(2)}, u32[]{:S(2)}) collective-permute-start(bf16[2,64,256]{2,1,0:T(8,128)(2,1)S(1)} %pad_maximum_fusion.refs_4_), channel_id=1, source_target_pairs={{0,4},{1,5},{2,6},{3,7},{4,0},{5,1},{6,2},{7,3},{8,12},{9,13},{10,... | collective-permute-start | bytes 196616 | tf_op jit(solution)/shard_map/ppermute | solution.py:349
  89.8 6.2 %collective-permute-start.13 = (bf16[2,64,256]{2,1,0:T(8,128)(2,1)S(1)}, bf16[2,64,256]{2,1,0:T(8,128)(2,1)S(1)}, u32[]{:S(2)}, u32[]{:S(2)}) collective-permute-start(bf16[2,64,256]{2,1,0:T(8,128)(2,1)S(1)} %pad_maximum_fusion.refs_4_), channel_id=1, source_target_pairs={{0,2},{1,3},{2,4},{3,5},{4,6},{5,7},{6,0},{7,1},{8,10},{9,11},{10,... | collective-permute-start | bytes 196616 | tf_op jit(solution)/shard_map/ppermute | solution.py:349
  97.0 2.0 %collective-permute-start.16 = (f32[2,4,64,256]{3,2,1,0:T(8,128)S(1)}, f32[2,4,64,256]{3,2,1,0:T(8,128)S(1)}, u32[]{:S(2)}, u32[]{:S(2)}) collective-permute-start(f32[2,4,64,256]{3,2,1,0:T(8,128)S(1)} %get-tuple-element.73), channel_id=1, source_target_pairs={{0,1},{1,0},{2,3},{3,2},{4,5},{5,4},{6,7},{7,6},{8,9},{9,8},{10,11... | collective-permute-start | bytes 1572872 | tf_op jit(solution)/shard_map/ppermute | solution.py:362
  100.8 8.1 %collective-permute-start.17 = (bf16[4,2,16,896]{3,2,1,0:T(8,128)(2,1)S(1)}, bf16[4,2,16,896]{3,2,1,0:T(8,128)(2,1)S(1)}, u32[]{:S(2)}, u32[]{:S(2)}) collective-permute-start(bf16[4,2,16,896]{3,2,1,0:T(8,128)(2,1)S(1)} %get-tuple-element.78.refs_0_), channel_id=1, source_target_pairs={{0,128},{8,136},{16,144},{24,152},{32,160},{40,168},{48,176},{56,1... | collective-permute-start | bytes 688136 | tf_op jit(solution)/shard_map/ppermute | solution.py:358
  101.1 9.6 %collective-permute-start.19 = (bf16[4,2,16,896]{3,2,1,0:T(8,128)(2,1)S(1)}, bf16[4,2,16,896]{3,2,1,0:T(8,128)(2,1)S(1)}, u32[]{:S(2)}, u32[]{:S(2)}) collective-permute-start(bf16[4,2,16,896]{3,2,1,0:T(8,128)(2,1)S(1)} %get-tuple-element.79.refs_1_), channel_id=1, source_target_pairs={{0,136},{8,128},{16,152},{24,144},{32,168},{40,160},{48,184},{56,1... | collective-permute-start | bytes 688136 | tf_op jit(solution)/shard_map/ppermute | solution.py:358
  104.1 13.6 %collective-permute-start.22 = (bf16[4,2,16,896]{3,2,1,0:T(8,128)(2,1)S(1)}, bf16[4,2,16,896]{3,2,1,0:T(8,128)(2,1)S(1)}, u32[]{:S(2)}, u32[]{:S(2)}) collective-permute-start(bf16[4,2,16,896]{3,2,1,0:T(8,128)(2,1)S(1)} %get-tuple-element.78.refs_0_), channel_id=1, source_target_pairs={{0,136},{8,128},{16,152},{24,144},{32,168},{40,160},{48,184},{56,1... | collective-permute-start | bytes 688136 | tf_op jit(solution)/shard_map/ppermute | solution.py:358
  106.0 11.7 %collective-permute-start.21 = (bf16[4,2,16,896]{3,2,1,0:T(8,128)(2,1)S(1)}, bf16[4,2,16,896]{3,2,1,0:T(8,128)(2,1)S(1)}, u32[]{:S(2)}, u32[]{:S(2)}) collective-permute-start(bf16[4,2,16,896]{3,2,1,0:T(8,128)(2,1)S(1)} %get-tuple-element.79.refs_1_), channel_id=1, source_target_pairs={{0,128},{8,136},{16,144},{24,152},{32,160},{40,168},{48,176},{56,1... | collective-permute-start | bytes 688136 | tf_op jit(solution)/shard_map/ppermute | solution.py:358
  108.8 10.8 %collective-permute-start.18 = (bf16[4,2,16,896]{3,2,1,0:T(8,128)(2,1)S(1)}, bf16[4,2,16,896]{3,2,1,0:T(8,128)(2,1)S(1)}, u32[]{:S(2)}, u32[]{:S(2)}) collective-permute-start(bf16[4,2,16,896]{3,2,1,0:T(8,128)(2,1)S(1)} %collective-permute-done.17.refs_0_), channel_id=1, source_target_pairs={{0,128},{8,136},{16,144},{24,152},{32,160},{40,168},{48,176},{56,1... | collective-permute-start | bytes 688136 | tf_op jit(solution)/shard_map/ppermute | solution.py:358
  110.7 8.9 %collective-permute-start.20 = (bf16[4,2,16,896]{3,2,1,0:T(8,128)(2,1)S(1)}, bf16[4,2,16,896]{3,2,1,0:T(8,128)(2,1)S(1)}, u32[]{:S(2)}, u32[]{:S(2)}) collective-permute-start(bf16[4,2,16,896]{3,2,1,0:T(8,128)(2,1)S(1)} %collective-permute-done.19.refs_3_), channel_id=1, source_target_pairs={{0,136},{8,128},{16,152},{24,144},{32,168},{40,160},{48,184},{56,1... | collective-permute-start | bytes 688136 | tf_op jit(solution)/shard_map/ppermute | solution.py:358

commit v6 on v5

--- a/solution.py
+++ b/solution.py
@@ -13,7 +13,7 @@
 DS = ("dp", "space")
 ALL = ("dp", "space", "chan")
 Y_GROUPS = [[dp * 16 + z * 2 + yh for yh in range(2) for dp in range(2)] for z in range(8)]
-Z_GROUPS = [[dp * 16 + z * 2 + yh for z in range(8)] for yh in range(2) for dp in range(2)]
+Z_GROUPS = [[dp * 16 + z * 2 + yh for z in range(7, -1, -1)] for yh in range(2) for dp in range(2)]
 YC_GROUPS = [
     [((dp * 16 + z * 2 + yh) * 8 + 2 * x + core) for yh in range(2) for dp in range(2) for core in range(2)]
     for z in range(8)
@@ -212,8 +212,9 @@
 
 
 def cut_kernel(r_ref, a_ref, b_ref):
-    a_ref[...] = r_ref[:4]
-    b_ref[...] = r_ref[4:]
+    for i in range(4):
+        a_ref[i] = r_ref[7 - i]
+        b_ref[i] = r_ref[3 - i]
 
 
 def place(first, second, store, bias):
@@ -401,12 +402,13 @@
     (terms,) = call(
         filter_grad_kernel, [((16, 16, 896), BF)], dy, ring, edge, scratch=[pltpu.VMEM((4, 192, 1024), BF)]
     )
-    far, dy_next, terms, *packed = lax.optimization_barrier((far, dy_next, terms, *packed))
-    far = [to_x(packed[1], 1), far, to_x(packed[3], 3)]
+    far, dy_next, terms = lax.optimization_barrier((far, dy_next, terms))
     terms = lax.all_to_all(terms, ALL, 0, 0, axis_index_groups=ZC_GROUPS)
     both = jnp.stack([dy_own, dy_next])
     grads = [both] + [to_x(both, d) for d in range(1, 4)]
-    *far, terms = lax.optimization_barrier((*far, terms))
+    *near, grads[1], grads[2], grads[3] = lax.optimization_barrier((packed[1], packed[3], *grads[1:]))
+    grads[1], terms = lax.optimization_barrier((grads[1], terms))
+    far = [to_x(near[0], 1), far, to_x(near[1], 3)]
     (terms,) = call(sum_z_kernel, [((8, 2, 16, 896), BF)], z_odd, terms, scalars=1)
     mine, theirs = call(
         input_grad_kernel,

time: 123 us -> 121 us (0.984)
  starting transfers between devices: 61.8 us -> 59.1 us
    ppermute x10, waiting for transfers between devices: 22.3 us -> 11.2 us  [to_x(): return lax.ppermute(a, 'chan', [(i, (i + 2 * d) % 8) for i in range(8)])]
    all_to_all x1, waiting for transfers between devices: 1.7 us -> 9.65 us  [per_device(): terms = lax.all_to_all(terms, DS, 0, 0, axis_index_groups=Z_GROUPS)]
    all_to_all x1, waiting for transfers between devices: 0.01 us -> 2.48 us  [per_device(): terms = lax.all_to_all(terms, ALL, 0, 0, axis_index_groups=ZC_GROUPS)]
    ppermute x10, starting transfers between devices: 14.1 us -> 12.1 us  [to_x(): return lax.ppermute(a, 'chan', [(i, (i + 2 * d) % 8) for i in range(8)])]
    ppermute x6, starting transfers between devices: 9.89 us -> 8.58 us  [over_y(): return lax.ppermute(a, DS, pairs)]
    ppermute x6, waiting for transfers between devices: 3.19 us -> 4.47 us  [over_y(): return lax.ppermute(a, DS, pairs)]
    unnamed x22 -> x20, local copies, waits for them, and re-layouts: 4.16 us -> 4.16 us
  transfers between devices with their start and end apart: 27 -> 27, of which waited for: 14 -> 14; matrix products, arithmetic and copies ran while one was open for 1% -> 1% of each run, Pallas kernels for 12% -> 14%
where the time goes in v6:
time: 121 us; the launch traced here: 120 us
  starting transfers between devices  59.1 us (49%)
  waiting for transfers between devices  36.3 us (30%)
  Pallas kernels  18.4 us (15%)
  local copies, waits for them, and re-layouts  4.3 us (4%)
    ppermute x3, starting transfers between devices, shift_space(): lax.ppermute(a, 'space', [(i, i + by) for i in range(16) if 0 <= i + by <...  14.2 us
    pallas_call x12, Pallas kernels, call(): pl.pallas_call(kernel, out_shape=shapes, in_specs=[SMEM] * scalars + [VME...  13.4 us
    ppermute x10, starting transfers between devices, to_x(): return lax.ppermute(a, 'chan', [(i, (i + 2 * d) % 8) for i in range(8)])  12.1 us
    ppermute x10, waiting for transfers between devices, to_x(): return lax.ppermute(a, 'chan', [(i, (i + 2 * d) % 8) for i in range(8)])  11.2 us
    all_to_all x1, waiting for transfers between devices, per_device(): terms = lax.all_to_all(terms, DS, 0, 0, axis_index_groups=Z_GROUPS)  9.65 us
    ppermute x6, starting transfers between devices, over_y(): return lax.ppermute(a, DS, pairs)  8.58 us
    all_to_all x1, starting transfers between devices, per_device(): terms = lax.all_to_all(terms, DS, 0, 0, axis_index_groups=Z_GROUPS)  7.76 us
    all_to_all x1, starting transfers between devices, per_device(): terms = lax.all_to_all(terms, ALL, 0, 0, axis_index_groups=ZC_GROUPS)  7.7 us
  transfers between devices with their start and end apart: 27, of which 14 were waited for; matrix products, arithmetic and copies ran while one was open for 1% of the time, Pallas kernels for 14%

profile of v6, /device:TPU:32, one launch (start us, length us, event | category | flops | bytes accessed | tf_op | source)
XLA Modules:
  0.0 119.8 jit_solution(14088379742021647618)
XLA Ops:
  0.6 0.9 copy-done.5
  1.6 0.6 shard_map.76.own_ref
  2.2 2.8 %collective-permute-start.1 = (bf16[2,4,64,256]{3,2,1,0:T(8,128)(2,1)S(1)}, bf16[2,4,64,256]{3,2,1,0:T(8,128)(2,1)S(1)}, u32[]{:S(2)}, u32[]{:S(2)}) collective-permute-start(bf16[2,4,64,256]{3,2,1,0:T(8,128)(2,1)S(1)} %shard_map.76.own_ref), channel_id=1, source_target_pairs={{0,6},{1,7},{2,0},{3,1},{4,2},{5,3},{6,4},{7,5},{8,14},{9,15},{10,... | collective-permute-start | bytes 786440 | tf_op jit(solution)/shard_map/ppermute | solution.py:350
  5.1 1.5 %copy-done = bf16[64,13824]{1,0:T(8,128)(2,1)S(1)} copy-done((bf16[64,13824]{1,0:T(8,128)(2,1)S(1)}, bf16[64,13824]{1,0:T(8,128)(2,1)}, u32[]{:S(2)}) %copy-start) | copy-done | bytes 1769496
  6.6 2.3 %shard_map.78 = (bf16[64,6912]{1,0:T(8,128)(2,1)S(1)}, bf16[64,6912]{1,0:T(8,128)(2,1)}) custom-call(s32[2]{0:T(128)S(1)} %pad_add_fusion.where_ref, bf16[64,13824]{1,0:T(8,128)(2,1)S(1)} %copy-done), custom_call_target="tpu_custom_call" | custom-call | tf_op jit(solution)/shard_map/pallas_call | solution.py:334
  8.9 1.7 %collective-permute-done.1.ahead_ref = bf16[2,4,64,256]{3,2,1,0:T(8,128)(2,1)S(1)} collective-permute-done((bf16[2,4,64,256]{3,2,1,0:T(8,128)(2,1)S(1)}, bf16[2,4,64,256]{3,2,1,0:T(8,128)(2,1)S(1)}, u32[]{:S(2)}, u32[]{:S(2)}) %collective-permute-start.1) | collective-permute-done | bytes 262176 | tf_op jit(solution)/shard_map/ppermute | solution.py:350
  10.6 3.8 %collective-permute-start.2 = (bf16[4,64,256]{2,1,0:T(8,128)(2,1)S(1)}, bf16[4,64,256]{2,1,0:T(8,128)(2,1)S(1)}, u32[]{:S(2)}, u32[]{:S(2)}) collective-permute-start(bf16[4,64,256]{2,1,0:T(8,128)(2,1)S(1)} %slice_bitcast_fusion.2), channel_id=1, source_target_pairs={{0,6},{1,7},{2,0},{3,1},{4,2},{5,3},{6,4},{7,5},{8,14},{9,15},{10,... | collective-permute-start | bytes 393224 | tf_op jit(solution)/shard_map/ppermute | solution.py:350
  14.5 1.1 shard_map.75
  15.6 0.8 copy-done.3
  16.4 0.5 collective-permute-done.2.across_0
  16.9 3.8 %collective-permute-done.3.across_1.across_ref = bf16[4,64,256]{2,1,0:T(8,128)(2,1)S(1)} collective-permute-done((bf16[4,64,256]{2,1,0:T(8,128)(2,1)S(1)}, bf16[4,64,256]{2,1,0:T(8,128)(2,1)S(1)}, u32[]{:S(2)}, u32[]{:S(2)}) %collective-permute-start.3) | collective-permute-done | bytes 131104 | tf_op jit(solution)/shard_map/ppermute | solution.py:350
  20.7 1.0 shard_map.77.all_ref
  21.7 4.6 %all-to-all-start = ((bf16[4,2,4,64,256]{4,3,2,1,0:T(8,128)(2,1)}), bf16[4,2,4,64,256]{4,3,2,1,0:T(8,128)(2,1)S(1)}, u32[]{:S(2)}, u32[]{:S(2)}) async-start(bf16[4,2,4,64,256]{4,3,2,1,0:T(8,128)(2,1)} %shard_map.77.all_ref), calls=%async_computation | async-start | bytes 2097152 | tf_op jit(solution)/shard_map/all_to_all | solution.py:387
  26.3 0.9 copy-done.2
  27.8 1.9 %shard_map.79 = (f32[64,256]{1,0:T(8,128)S(1)}, f32[64,256]{1,0:T(8,128)S(1)}) custom-call(s32[1]{0:T(128)} %bitcast.x_ref, bf16[4,2,4,64,256]{4,3,2,1,0:T(8,128)(2,1)} %shard_map.77.all_ref, bf16[64,6912]{1,0:T(8,128)(2,1)S(1)} %get-tuple-element.48.w_ref, bf16[64,6912]{1,0:T(8,128)(2,1)S(1)} %collective-permute-done.4.v_ref), custom_call_target="tpu_custom_call" | custom-call | tf_op jit(solution)/shard_map/pallas_call | solution.py:334
  29.7 0.6 collective-permute-start.5
  30.3 5.4 %collective-permute-start.7 = (f32[64,256]{1,0:T(8,128)S(1)}, f32[64,256]{1,0:T(8,128)S(1)}, u32[]{:S(2)}, u32[]{:S(2)}) collective-permute-start(f32[64,256]{1,0:T(8,128)S(1)} %add.19), channel_id=1, source_target_pairs={{0,8},{8,16},{16,24},{24,32},{32,40},{40,48},{48,56},{56,64},{64,7... | collective-permute-start | bytes 196616 | tf_op jit(solution)/shard_map/ppermute | solution.py:346
  35.9 2.9 %collective-permute-done.7.c_ref = f32[64,256]{1,0:T(8,128)S(1)} collective-permute-done((f32[64,256]{1,0:T(8,128)S(1)}, f32[64,256]{1,0:T(8,128)S(1)}, u32[]{:S(2)}, u32[]{:S(2)}) %collective-permute-start.7) | collective-permute-done | bytes 65568 | tf_op jit(solution)/shard_map/ppermute | solution.py:346
  38.9 0.8 shard_map.81
  39.7 0.8 all-to-all-done.x_ref
  40.5 3.8 %collective-permute-start.10 = (bf16[2,4,64,256]{3,2,1,0:T(8,128)(2,1)S(1)}, bf16[2,4,64,256]{3,2,1,0:T(8,128)(2,1)S(1)}, u32[]{:S(2)}, u32[]{:S(2)}) collective-permute-start(bf16[2,4,64,256]{3,2,1,0:T(8,128)(2,1)S(1)} %slice_bitcast_fusion), channel_id=1, source_target_pairs={{0,16},{8,24},{16,32},{24,40},{32,48},{40,56},{48,64},{56,72},{64,... | collective-permute-start | bytes 786440 | tf_op jit(solution)/shard_map/ppermute | solution.py:346
  44.4 3.4 %all-to-all-start.1 = ((bf16[8,64,256]{2,1,0:T(8,128)(2,1)}), bf16[8,64,256]{2,1,0:T(8,128)(2,1)S(1)}, u32[]{:S(2)}, u32[]{:S(2)}) async-start(bf16[8,64,256]{2,1,0:T(8,128)(2,1)} %get-tuple-element.61), calls=%async_computation.1 | async-start | bytes 524288 | tf_op jit(solution)/shard_map/all_to_all | solution.py:399
  47.8 4.9 %collective-permute-start.9 = (bf16[64,256]{1,0:T(8,128)(2,1)S(1)}, bf16[64,256]{1,0:T(8,128)(2,1)S(1)}, u32[]{:S(2)}, u32[]{:S(2)}) collective-permute-start(bf16[64,256]{1,0:T(8,128)(2,1)S(1)} %get-tuple-element.59), channel_id=1, source_target_pairs={{8,0},{16,8},{24,16},{32,24},{40,32},{48,40},{56,48},{64,56},{72,6... | collective-permute-start | bytes 98312 | tf_op jit(solution)/shard_map/ppermute | solution.py:346
  52.7 2.9 %all-to-all-done.1.dy_ref = bf16[8,64,256]{2,1,0:T(8,128)(2,1)S(1)} async-done(((bf16[8,64,256]{2,1,0:T(8,128)(2,1)}), bf16[8,64,256]{2,1,0:T(8,128)(2,1)S(1)}, u32[]{:S(2)}, u32[]{:S(2)}) %all-to-all-start.1) | async-done | bytes 262176 | tf_op jit(solution)/shard_map/all_to_all | solution.py:399
  55.6 1.6 %shard_map.82 = bf16[16,16,896]{2,1,0:T(8,128)(2,1)} custom-call(bf16[8,64,256]{2,1,0:T(8,128)(2,1)S(1)} %all-to-all-done.1.dy_ref, bf16[4,2,4,64,256]{4,3,2,1,0:T(8,128)(2,1)S(1)} %all-to-all-done.x_ref, bf16[2,4,64,256]{3,2,1,0:T(8,128)(2,1)S(1)} %collective-permute-done.10.e_ref), custom_call_target="tpu_custom_call" | custom-call | tf_op jit(solution)/shard_map/pallas_call | solution.py:334
  57.3 7.7 %all-to-all-start.2 = ((bf16[16,16,896]{2,1,0:T(8,128)(2,1)}), bf16[16,16,896]{2,1,0:T(8,128)(2,1)S(1)}, u32[]{:S(2)}, u32[]{:S(2)}) async-start(bf16[16,16,896]{2,1,0:T(8,128)(2,1)} %shard_map.82), calls=%async_computation.2 | async-start | bytes 917504 | tf_op jit(solution)/shard_map/all_to_all | solution.py:406
  65.2 1.0 collective-permute-start.12
  66.2 0.9 collective-permute-start.11
  67.1 2.8 %collective-permute-done.13.refs_7_ = bf16[2,64,256]{2,1,0:T(8,128)(2,1)S(1)} collective-permute-done((bf16[2,64,256]{2,1,0:T(8,128)(2,1)S(1)}, bf16[2,64,256]{2,1,0:T(8,128)(2,1)S(1)}, u32[]{:S(2)}, u32[]{:S(2)}) %collective-permute-start.13) | collective-permute-done | bytes 65568 | tf_op jit(solution)/shard_map/ppermute | solution.py:350
  69.9 1.2 %collective-permute-done.12.refs_6_ = bf16[2,64,256]{2,1,0:T(8,128)(2,1)S(1)} collective-permute-done((bf16[2,64,256]{2,1,0:T(8,128)(2,1)S(1)}, bf16[2,64,256]{2,1,0:T(8,128)(2,1)S(1)}, u32[]{:S(2)}, u32[]{:S(2)}) %collective-permute-start.12) | collective-permute-done | bytes 65568 | tf_op jit(solution)/shard_map/ppermute | solution.py:350
  71.1 1.2 collective-permute-done.11.refs_5_
  72.3 0.6 collective-permute-start.14
  72.8 2.7 %collective-permute-start.15 = (bf16[64,3456]{1,0:T(8,128)(2,1)}, bf16[64,3456]{1,0:T(8,128)(2,1)S(1)}, u32[]{:S(2)}, u32[]{:S(2)}) collective-permute-start(bf16[64,3456]{1,0:T(8,128)(2,1)} %copy-done.7), channel_id=1, source_target_pairs={{0,6},{1,7},{2,0},{3,1},{4,2},{5,3},{6,4},{7,5},{8,14},{9,15},{10,... | collective-permute-start | bytes 1327112 | tf_op jit(solution)/shard_map/ppermute | solution.py:350
  75.5 2.5 %all-to-all-done.2.r_ref = bf16[16,16,896]{2,1,0:T(8,128)(2,1)S(1)} async-done(((bf16[16,16,896]{2,1,0:T(8,128)(2,1)}), bf16[16,16,896]{2,1,0:T(8,128)(2,1)S(1)}, u32[]{:S(2)}, u32[]{:S(2)}) %all-to-all-start.2) | async-done | bytes 458784 | tf_op jit(solution)/shard_map/all_to_all | solution.py:406
  78.0 0.9 shard_map.84
  78.9 7.8 %all-to-all-start.3 = ((bf16[8,2,16,896]{3,2,1,0:T(8,128)(2,1)}), bf16[8,2,16,896]{3,2,1,0:T(8,128)(2,1)S(1)}, u32[]{:S(2)}, u32[]{:S(2)}) async-start(bf16[8,2,16,896]{3,2,1,0:T(8,128)(2,1)} %shard_map.84), calls=%async_computation.3 | async-start | bytes 917504 | tf_op jit(solution)/shard_map/all_to_all | solution.py:423
  86.7 1.0 shard_map.83
  87.8 1.9 %collective-permute-done.16.b_ref = f32[2,4,64,256]{3,2,1,0:T(8,128)S(1)} collective-permute-done((f32[2,4,64,256]{3,2,1,0:T(8,128)S(1)}, f32[2,4,64,256]{3,2,1,0:T(8,128)S(1)}, u32[]{:S(2)}, u32[]{:S(2)}) %collective-permute-start.16) | collective-permute-done | bytes 524320 | tf_op jit(solution)/shard_map/ppermute | solution.py:363
  89.7 9.7 %all-to-all-done.3.r_ref = bf16[8,2,16,896]{3,2,1,0:T(8,128)(2,1)S(1)} async-done(((bf16[8,2,16,896]{3,2,1,0:T(8,128)(2,1)}), bf16[8,2,16,896]{3,2,1,0:T(8,128)(2,1)S(1)}, u32[]{:S(2)}, u32[]{:S(2)}) %all-to-all-start.3) | async-done | bytes 458784 | tf_op jit(solution)/shard_map/all_to_all | solution.py:423
  99.7 3.0 %collective-permute-start.19 = (bf16[4,2,16,896]{3,2,1,0:T(8,128)(2,1)S(1)}, bf16[4,2,16,896]{3,2,1,0:T(8,128)(2,1)S(1)}, u32[]{:S(2)}, u32[]{:S(2)}) collective-permute-start(bf16[4,2,16,896]{3,2,1,0:T(8,128)(2,1)S(1)} %get-tuple-element.79.refs_1_), channel_id=1, source_target_pairs={{0,136},{8,128},{16,152},{24,144},{32,168},{40,160},{48,184},{56,1... | collective-permute-start | bytes 688136 | tf_op jit(solution)/shard_map/ppermute | solution.py:359
  102.7 1.9 %collective-permute-start.22 = (bf16[4,2,16,896]{3,2,1,0:T(8,128)(2,1)S(1)}, bf16[4,2,16,896]{3,2,1,0:T(8,128)(2,1)S(1)}, u32[]{:S(2)}, u32[]{:S(2)}) collective-permute-start(bf16[4,2,16,896]{3,2,1,0:T(8,128)(2,1)S(1)} %get-tuple-element.78.refs_0_), channel_id=1, source_target_pairs={{0,136},{8,128},{16,152},{24,144},{32,168},{40,160},{48,184},{56,1... | collective-permute-start | bytes 688136 | tf_op jit(solution)/shard_map/ppermute | solution.py:359
  104.8 4.0 %collective-permute-done.17.refs_0_ = bf16[4,2,16,896]{3,2,1,0:T(8,128)(2,1)S(1)} collective-permute-done((bf16[4,2,16,896]{3,2,1,0:T(8,128)(2,1)S(1)}, bf16[4,2,16,896]{3,2,1,0:T(8,128)(2,1)S(1)}, u32[]{:S(2)}, u32[]{:S(2)}) %collective-permute-start.17) | collective-permute-done | bytes 229408 | tf_op jit(solution)/shard_map/ppermute | solution.py:359
  109.3 3.2 %collective-permute-start.20 = (bf16[4,2,16,896]{3,2,1,0:T(8,128)(2,1)S(1)}, bf16[4,2,16,896]{3,2,1,0:T(8,128)(2,1)S(1)}, u32[]{:S(2)}, u32[]{:S(2)}) collective-permute-start(bf16[4,2,16,896]{3,2,1,0:T(8,128)(2,1)S(1)} %collective-permute-done.19.refs_3_), channel_id=1, source_target_pairs={{0,136},{8,128},{16,152},{24,144},{32,168},{40,160},{48,184},{56,1... | collective-permute-start | bytes 688136 | tf_op jit(solution)/shard_map/ppermute | solution.py:359
  112.5 1.6 %shard_map.87 = (f32[64,13824]{1,0:T(8,128)}, f32[64,1]{1,0:T(8,128)S(1)}) custom-call(s32[1]{0:T(128)} %bitcast.13.q_ref, bf16[4,2,16,896]{3,2,1,0:T(8,128)(2,1)S(1)} %get-tuple-element.78.refs_0_, bf16[4,2,16,896]{3,2,1,0:T(8,128)(2,1)S(1)} %get-tuple-element.79.refs_1_), custom_call_target="tpu_custom_call" | custom-call | tf_op jit(solution)/shard_map/pallas_call | solution.py:272
  114.1 1.5 %shard_map.85 = bf16[2,64,1024]{2,1,0:T(8,128)(2,1)} custom-call(f32[2,4,64,256]{3,2,1,0:T(8,128)S(1)} %get-tuple-element.75.a_ref, f32[2,4,64,256]{3,2,1,0:T(8,128)S(1)} %collective-permute-done.16.b_ref), custom_call_target="tpu_custom_call" | custom-call | tf_op jit(solution)/shard_map/pallas_call | solution.py:334
  115.6 0.6 reduce
  116.3 2.0 %shard_map.88.refs_2_ = f32[64,13824]{1,0:T(8,128)} custom-call(s32[1]{0:T(128)} %bitcast.13.q_ref, bf16[4,2,16,896]{3,2,1,0:T(8,128)(2,1)S(1)} %collective-permute-done.17.refs_0_, bf16[4,2,16,896]{3,2,1,0:T(8,128)(2,1)S(1)} %collective-permute-done.21.refs_1_, ...), custom_call_target="tpu_custom_call", output_to_operand_aliasing={{}: (5, {})} | custom-call | tf_op jit(solution)/shard_map/pallas_call | solution.py:272
  118.2 1.4 %shard_map.89 = f32[64,13824]{1,0:T(8,128)} custom-call(s32[1]{0:T(128)} %bitcast.13.q_ref, bf16[4,2,16,896]{3,2,1,0:T(8,128)(2,1)S(1)} %collective-permute-done.18.refs_0_, bf16[4,2,16,896]{3,2,1,0:T(8,128)(2,1)S(1)} %collective-permute-done.20.refs_1_, f32[64,13824]{1,0:T(8,128)} %shard_map.88.refs_2_), custom_call_target="tpu_custom_call", output_to_operand_aliasing={{}: (3, {})} | custom-call | tf_op jit(solution)/shard_map/pallas_call | solution.py:272
  (49 shorter events, 2.3 us)
Async XLA Ops:
  0.6 1.0 copy-start.5
  2.2 8.4 %collective-permute-start.1 = (bf16[2,4,64,256]{3,2,1,0:T(8,128)(2,1)S(1)}, bf16[2,4,64,256]{3,2,1,0:T(8,128)(2,1)S(1)}, u32[]{:S(2)}, u32[]{:S(2)}) collective-permute-start(bf16[2,4,64,256]{3,2,1,0:T(8,128)(2,1)S(1)} %shard_map.76.own_ref), channel_id=1, source_target_pairs={{0,6},{1,7},{2,0},{3,1},{4,2},{5,3},{6,4},{7,5},{8,14},{9,15},{10,... | collective-permute-start | bytes 786440 | tf_op jit(solution)/shard_map/ppermute | solution.py:350
  5.0 9.3 %collective-permute-start = (bf16[2,4,64,256]{3,2,1,0:T(8,128)(2,1)S(1)}, bf16[2,4,64,256]{3,2,1,0:T(8,128)(2,1)S(1)}, u32[]{:S(2)}, u32[]{:S(2)}) collective-permute-start(bf16[2,4,64,256]{3,2,1,0:T(8,128)(2,1)S(1)} %shard_map.76.own_ref), channel_id=1, source_target_pairs={{0,2},{1,3},{2,4},{3,5},{4,6},{5,7},{6,0},{7,1},{8,10},{9,11},{10,... | collective-permute-start | bytes 786440 | tf_op jit(solution)/shard_map/ppermute | solution.py:350
  5.1 1.5 %copy-start = (bf16[64,13824]{1,0:T(8,128)(2,1)S(1)}, bf16[64,13824]{1,0:T(8,128)(2,1)}, u32[]{:S(2)}) copy-start(bf16[64,13824]{1,0:T(8,128)(2,1)} %w_ref.3) | copy-start | bytes 5308420
  8.9 17.4 %collective-permute-start.4 = (bf16[64,6912]{1,0:T(8,128)(2,1)}, bf16[64,6912]{1,0:T(8,128)(2,1)S(1)}, u32[]{:S(2)}, u32[]{:S(2)}) collective-permute-start(bf16[64,6912]{1,0:T(8,128)(2,1)} %get-tuple-element.49), channel_id=1, source_target_pairs={{0,1},{1,0},{2,3},{3,2},{4,5},{5,4},{6,7},{7,6},{8,9},{9,8},{10,11... | collective-permute-start | bytes 2654216 | tf_op jit(solution)/shard_map/ppermute | solution.py:363
  10.6 6.3 %collective-permute-start.2 = (bf16[4,64,256]{2,1,0:T(8,128)(2,1)S(1)}, bf16[4,64,256]{2,1,0:T(8,128)(2,1)S(1)}, u32[]{:S(2)}, u32[]{:S(2)}) collective-permute-start(bf16[4,64,256]{2,1,0:T(8,128)(2,1)S(1)} %slice_bitcast_fusion.2), channel_id=1, source_target_pairs={{0,6},{1,7},{2,0},{3,1},{4,2},{5,3},{6,4},{7,5},{8,14},{9,15},{10,... | collective-permute-start | bytes 393224 | tf_op jit(solution)/shard_map/ppermute | solution.py:350
  14.4 7.3 %copy-start.1 = (bf16[2,4,64,256]{3,2,1,0:T(8,128)(2,1)}, bf16[2,4,64,256]{3,2,1,0:T(8,128)(2,1)S(1)}, u32[]{:S(2)}) copy-start(bf16[2,4,64,256]{3,2,1,0:T(8,128)(2,1)S(1)} %collective-permute-done.back_ref) | copy-start | bytes 786436
  14.4 6.3 %collective-permute-start.3 = (bf16[4,64,256]{2,1,0:T(8,128)(2,1)S(1)}, bf16[4,64,256]{2,1,0:T(8,128)(2,1)S(1)}, u32[]{:S(2)}, u32[]{:S(2)}) collective-permute-start(bf16[4,64,256]{2,1,0:T(8,128)(2,1)S(1)} %slice_bitcast_fusion.1), channel_id=1, source_target_pairs={{0,2},{1,3},{2,4},{3,5},{4,6},{5,7},{6,0},{7,1},{8,10},{9,11},{10,... | collective-permute-start | bytes 393224 | tf_op jit(solution)/shard_map/ppermute | solution.py:350
  15.6 0.8 copy-start.3
  16.4 5.3 %copy-start.8 = (bf16[64,3456]{1,0:T(8,128)(2,1)}, bf16[64,3456]{1,0:T(8,128)(2,1)S(1)}, u32[]{:S(2)}) copy-start(bf16[64,3456]{1,0:T(8,128)(2,1)S(1)} %get-tuple-element.60) | copy-start | bytes 1327108
  16.4 5.3 %copy-start.7 = (bf16[64,3456]{1,0:T(8,128)(2,1)}, bf16[64,3456]{1,0:T(8,128)(2,1)S(1)}, u32[]{:S(2)}) copy-start(bf16[64,3456]{1,0:T(8,128)(2,1)S(1)} %get-tuple-element.66) | copy-start | bytes 1327108
  21.7 14.1 %copy-start.9 = (f32[64]{0:T(128)S(1)}, f32[64]{0:T(128)}, u32[]{:S(2)}) copy-start(f32[64]{0:T(128)} %param.6) | copy-start | bytes 772
  21.7 17.2 %copy-start.6 = (bf16[1,1,64,256]{3,2,1,0:T(8,128)(2,1)S(1)}, bf16[1,1,64,256]{3,2,1,0:T(8,128)(2,1)}, u32[]{:S(2)}) copy-start(bf16[1,1,64,256]{3,2,1,0:T(8,128)(2,1)} %param.7) | copy-start | bytes 98308
  21.7 18.8 %all-to-all-start = ((bf16[4,2,4,64,256]{4,3,2,1,0:T(8,128)(2,1)}), bf16[4,2,4,64,256]{4,3,2,1,0:T(8,128)(2,1)S(1)}, u32[]{:S(2)}, u32[]{:S(2)}) async-start(bf16[4,2,4,64,256]{4,3,2,1,0:T(8,128)(2,1)} %shard_map.77.all_ref), calls=%async_computation | async-start | bytes 2097152 | tf_op jit(solution)/shard_map/all_to_all | solution.py:387
  26.3 1.0 copy-start.2
  27.7 2.6 %collective-permute-start.6 = (f32[64,256]{1,0:T(8,128)S(1)}, f32[64,256]{1,0:T(8,128)S(1)}, u32[]{:S(2)}, u32[]{:S(2)}) collective-permute-start(f32[64,256]{1,0:T(8,128)S(1)} %get-tuple-element.53), channel_id=1, source_target_pairs={{0,1},{1,0},{2,3},{3,2},{4,5},{5,4},{6,7},{7,6},{8,9},{9,8},{10,11... | collective-permute-start | bytes 196616 | tf_op jit(solution)/shard_map/ppermute | solution.py:363
  29.7 57.0 %copy-start.4 = (bf16[64,3456]{1,0:T(8,128)(2,1)S(1)}, bf16[64,3456]{1,0:T(8,128)(2,1)}, u32[]{:S(2)}) copy-start(bf16[64,3456]{1,0:T(8,128)(2,1)} %copy-done.3) | copy-start | bytes 1327108
  29.7 6.2 %collective-permute-start.5 = (f32[64,256]{1,0:T(8,128)S(1)}, f32[64,256]{1,0:T(8,128)S(1)}, u32[]{:S(2)}, u32[]{:S(2)}) collective-permute-start(f32[64,256]{1,0:T(8,128)S(1)} %get-tuple-element.51), channel_id=1, source_target_pairs={{0,1},{1,0},{2,3},{3,2},{4,5},{5,4},{6,7},{7,6},{8,9},{9,8},{10,11... | collective-permute-start | bytes 196616 | tf_op jit(solution)/shard_map/ppermute | solution.py:363
  30.3 8.6 %collective-permute-start.7 = (f32[64,256]{1,0:T(8,128)S(1)}, f32[64,256]{1,0:T(8,128)S(1)}, u32[]{:S(2)}, u32[]{:S(2)}) collective-permute-start(f32[64,256]{1,0:T(8,128)S(1)} %add.19), channel_id=1, source_target_pairs={{0,8},{8,16},{16,24},{24,32},{32,40},{40,48},{48,56},{56,64},{64,7... | collective-permute-start | bytes 196616 | tf_op jit(solution)/shard_map/ppermute | solution.py:346
  35.9 21.4 %collective-permute-start.8 = (bf16[64,3456]{1,0:T(8,128)(2,1)}, bf16[64,3456]{1,0:T(8,128)(2,1)S(1)}, u32[]{:S(2)}, u32[]{:S(2)}) collective-permute-start(bf16[64,3456]{1,0:T(8,128)(2,1)} %copy-done.8), channel_id=1, source_target_pairs={{0,4},{1,5},{2,6},{3,7},{4,0},{5,1},{6,2},{7,3},{8,12},{9,13},{10,... | collective-permute-start | bytes 1327112 | tf_op jit(solution)/shard_map/ppermute | solution.py:350
  40.5 15.1 %collective-permute-start.10 = (bf16[2,4,64,256]{3,2,1,0:T(8,128)(2,1)S(1)}, bf16[2,4,64,256]{3,2,1,0:T(8,128)(2,1)S(1)}, u32[]{:S(2)}, u32[]{:S(2)}) collective-permute-start(bf16[2,4,64,256]{3,2,1,0:T(8,128)(2,1)S(1)} %slice_bitcast_fusion), channel_id=1, source_target_pairs={{0,16},{8,24},{16,32},{24,40},{32,48},{40,56},{48,64},{56,72},{64,... | collective-permute-start | bytes 786440 | tf_op jit(solution)/shard_map/ppermute | solution.py:346
  44.4 11.2 %all-to-all-start.1 = ((bf16[8,64,256]{2,1,0:T(8,128)(2,1)}), bf16[8,64,256]{2,1,0:T(8,128)(2,1)S(1)}, u32[]{:S(2)}, u32[]{:S(2)}) async-start(bf16[8,64,256]{2,1,0:T(8,128)(2,1)} %get-tuple-element.61), calls=%async_computation.1 | async-start | bytes 524288 | tf_op jit(solution)/shard_map/all_to_all | solution.py:399
  47.8 9.4 %collective-permute-start.9 = (bf16[64,256]{1,0:T(8,128)(2,1)S(1)}, bf16[64,256]{1,0:T(8,128)(2,1)S(1)}, u32[]{:S(2)}, u32[]{:S(2)}) collective-permute-start(bf16[64,256]{1,0:T(8,128)(2,1)S(1)} %get-tuple-element.59), channel_id=1, source_target_pairs={{8,0},{16,8},{24,16},{32,24},{40,32},{48,40},{56,48},{64,56},{72,6... | collective-permute-start | bytes 98312 | tf_op jit(solution)/shard_map/ppermute | solution.py:346
  57.3 20.7 %all-to-all-start.2 = ((bf16[16,16,896]{2,1,0:T(8,128)(2,1)}), bf16[16,16,896]{2,1,0:T(8,128)(2,1)S(1)}, u32[]{:S(2)}, u32[]{:S(2)}) async-start(bf16[16,16,896]{2,1,0:T(8,128)(2,1)} %shard_map.82), calls=%async_computation.2 | async-start | bytes 917504 | tf_op jit(solution)/shard_map/all_to_all | solution.py:406
  65.0 4.9 %collective-permute-start.13 = (bf16[2,64,256]{2,1,0:T(8,128)(2,1)S(1)}, bf16[2,64,256]{2,1,0:T(8,128)(2,1)S(1)}, u32[]{:S(2)}, u32[]{:S(2)}) collective-permute-start(bf16[2,64,256]{2,1,0:T(8,128)(2,1)S(1)} %pad_maximum_fusion.refs_4_), channel_id=1, source_target_pairs={{0,6},{1,7},{2,0},{3,1},{4,2},{5,3},{6,4},{7,5},{8,14},{9,15},{10,... | collective-permute-start | bytes 196616 | tf_op jit(solution)/shard_map/ppermute | solution.py:350
  65.2 5.9 %collective-permute-start.12 = (bf16[2,64,256]{2,1,0:T(8,128)(2,1)S(1)}, bf16[2,64,256]{2,1,0:T(8,128)(2,1)S(1)}, u32[]{:S(2)}, u32[]{:S(2)}) collective-permute-start(bf16[2,64,256]{2,1,0:T(8,128)(2,1)S(1)} %pad_maximum_fusion.refs_4_), channel_id=1, source_target_pairs={{0,4},{1,5},{2,6},{3,7},{4,0},{5,1},{6,2},{7,3},{8,12},{9,13},{10,... | collective-permute-start | bytes 196616 | tf_op jit(solution)/shard_map/ppermute | solution.py:350
  66.2 6.1 %collective-permute-start.11 = (bf16[2,64,256]{2,1,0:T(8,128)(2,1)S(1)}, bf16[2,64,256]{2,1,0:T(8,128)(2,1)S(1)}, u32[]{:S(2)}, u32[]{:S(2)}) collective-permute-start(bf16[2,64,256]{2,1,0:T(8,128)(2,1)S(1)} %pad_maximum_fusion.refs_4_), channel_id=1, source_target_pairs={{0,2},{1,3},{2,4},{3,5},{4,6},{5,7},{6,0},{7,1},{8,10},{9,11},{10,... | collective-permute-start | bytes 196616 | tf_op jit(solution)/shard_map/ppermute | solution.py:350
  72.3 14.4 %collective-permute-start.14 = (bf16[64,3456]{1,0:T(8,128)(2,1)}, bf16[64,3456]{1,0:T(8,128)(2,1)S(1)}, u32[]{:S(2)}, u32[]{:S(2)}) collective-permute-start(bf16[64,3456]{1,0:T(8,128)(2,1)} %get-tuple-element.64), channel_id=1, source_target_pairs={{0,2},{1,3},{2,4},{3,5},{4,6},{5,7},{6,0},{7,1},{8,10},{9,11},{10,... | collective-permute-start | bytes 1327112 | tf_op jit(solution)/shard_map/ppermute | solution.py:350
  72.8 13.9 %collective-permute-start.15 = (bf16[64,3456]{1,0:T(8,128)(2,1)}, bf16[64,3456]{1,0:T(8,128)(2,1)S(1)}, u32[]{:S(2)}, u32[]{:S(2)}) collective-permute-start(bf16[64,3456]{1,0:T(8,128)(2,1)} %copy-done.7), channel_id=1, source_target_pairs={{0,6},{1,7},{2,0},{3,1},{4,2},{5,3},{6,4},{7,5},{8,14},{9,15},{10,... | collective-permute-start | bytes 1327112 | tf_op jit(solution)/shard_map/ppermute | solution.py:350
  78.9 20.4 %all-to-all-start.3 = ((bf16[8,2,16,896]{3,2,1,0:T(8,128)(2,1)}), bf16[8,2,16,896]{3,2,1,0:T(8,128)(2,1)S(1)}, u32[]{:S(2)}, u32[]{:S(2)}) async-start(bf16[8,2,16,896]{3,2,1,0:T(8,128)(2,1)} %shard_map.84), calls=%async_computation.3 | async-start | bytes 917504 | tf_op jit(solution)/shard_map/all_to_all | solution.py:423
  87.7 2.0 %collective-permute-start.16 = (f32[2,4,64,256]{3,2,1,0:T(8,128)S(1)}, f32[2,4,64,256]{3,2,1,0:T(8,128)S(1)}, u32[]{:S(2)}, u32[]{:S(2)}) collective-permute-start(f32[2,4,64,256]{3,2,1,0:T(8,128)S(1)} %get-tuple-element.73), channel_id=1, source_target_pairs={{0,1},{1,0},{2,3},{3,2},{4,5},{5,4},{6,7},{7,6},{8,9},{9,8},{10,11... | collective-permute-start | bytes 1572872 | tf_op jit(solution)/shard_map/ppermute | solution.py:363
  99.4 9.3 %collective-permute-start.17 = (bf16[4,2,16,896]{3,2,1,0:T(8,128)(2,1)S(1)}, bf16[4,2,16,896]{3,2,1,0:T(8,128)(2,1)S(1)}, u32[]{:S(2)}, u32[]{:S(2)}) collective-permute-start(bf16[4,2,16,896]{3,2,1,0:T(8,128)(2,1)S(1)} %get-tuple-element.78.refs_0_), channel_id=1, source_target_pairs={{0,128},{8,136},{16,144},{24,152},{32,160},{40,168},{48,176},{56,1... | collective-permute-start | bytes 688136 | tf_op jit(solution)/shard_map/ppermute | solution.py:359
  99.7 9.6 %collective-permute-start.19 = (bf16[4,2,16,896]{3,2,1,0:T(8,128)(2,1)S(1)}, bf16[4,2,16,896]{3,2,1,0:T(8,128)(2,1)S(1)}, u32[]{:S(2)}, u32[]{:S(2)}) collective-permute-start(bf16[4,2,16,896]{3,2,1,0:T(8,128)(2,1)S(1)} %get-tuple-element.79.refs_1_), channel_id=1, source_target_pairs={{0,136},{8,128},{16,152},{24,144},{32,168},{40,160},{48,184},{56,1... | collective-permute-start | bytes 688136 | tf_op jit(solution)/shard_map/ppermute | solution.py:359
  102.7 13.5 %collective-permute-start.22 = (bf16[4,2,16,896]{3,2,1,0:T(8,128)(2,1)S(1)}, bf16[4,2,16,896]{3,2,1,0:T(8,128)(2,1)S(1)}, u32[]{:S(2)}, u32[]{:S(2)}) collective-permute-start(bf16[4,2,16,896]{3,2,1,0:T(8,128)(2,1)S(1)} %get-tuple-element.78.refs_0_), channel_id=1, source_target_pairs={{0,136},{8,128},{16,152},{24,144},{32,168},{40,160},{48,184},{56,1... | collective-permute-start | bytes 688136 | tf_op jit(solution)/shard_map/ppermute | solution.py:359
  104.6 11.7 %collective-permute-start.21 = (bf16[4,2,16,896]{3,2,1,0:T(8,128)(2,1)S(1)}, bf16[4,2,16,896]{3,2,1,0:T(8,128)(2,1)S(1)}, u32[]{:S(2)}, u32[]{:S(2)}) collective-permute-start(bf16[4,2,16,896]{3,2,1,0:T(8,128)(2,1)S(1)} %get-tuple-element.79.refs_1_), channel_id=1, source_target_pairs={{0,128},{8,136},{16,144},{24,152},{32,160},{40,168},{48,176},{56,1... | collective-permute-start | bytes 688136 | tf_op jit(solution)/shard_map/ppermute | solution.py:359
  108.8 9.5 %collective-permute-start.18 = (bf16[4,2,16,896]{3,2,1,0:T(8,128)(2,1)S(1)}, bf16[4,2,16,896]{3,2,1,0:T(8,128)(2,1)S(1)}, u32[]{:S(2)}, u32[]{:S(2)}) collective-permute-start(bf16[4,2,16,896]{3,2,1,0:T(8,128)(2,1)S(1)} %collective-permute-done.17.refs_0_), channel_id=1, source_target_pairs={{0,128},{8,136},{16,144},{24,152},{32,160},{40,168},{48,176},{56,1... | collective-permute-start | bytes 688136 | tf_op jit(solution)/shard_map/ppermute | solution.py:359
  109.3 8.9 %collective-permute-start.20 = (bf16[4,2,16,896]{3,2,1,0:T(8,128)(2,1)S(1)}, bf16[4,2,16,896]{3,2,1,0:T(8,128)(2,1)S(1)}, u32[]{:S(2)}, u32[]{:S(2)}) collective-permute-start(bf16[4,2,16,896]{3,2,1,0:T(8,128)(2,1)S(1)} %collective-permute-done.19.refs_3_), channel_id=1, source_target_pairs={{0,136},{8,128},{16,152},{24,144},{32,168},{40,160},{48,184},{56,1... | collective-permute-start | bytes 688136 | tf_op jit(solution)/shard_map/ppermute | solution.py:359

commit v7 on v6

--- a/solution.py
+++ b/solution.py
@@ -20,7 +20,7 @@
     for x in range(4)
 ]
 ZC_GROUPS = [
-    [((dp * 16 + z * 2 + yh) * 8 + 2 * x + core) for z in range(8) for core in range(2)]
+    [((dp * 16 + (z + 7) % 8 * 2 + yh) * 8 + 2 * x + core) for z in range(8) for core in range(2)]
     for yh in range(2)
     for dp in range(2)
     for x in range(4)
@@ -179,7 +179,7 @@
         for core in range(2):
             for fb in range(4):
                 row = core * 64 + fb * 16
-                o_ref[4 * fb + 2 * h + core, :, at * 128 : at * 128 + 128] = block[row : row + 16]
+                o_ref[(2 * fb + h + 1) % 8 * 2 + core, :, at * 128 : at * 128 + 128] = block[row : row + 16]
 
     firsts = {}
     for c in range(4):

time: 121 us -> 121 us (level)
    all_to_all x1, starting transfers between devices: 7.7 us -> 9.76 us  [per_device(): terms = lax.all_to_all(terms, ALL, 0, 0, axis_index_groups=ZC_GROUPS)]
    all_to_all x1, starting transfers between devices: 7.76 us -> 6.39 us  [per_device(): terms = lax.all_to_all(terms, DS, 0, 0, axis_index_groups=Z_GROUPS)]
  transfers between devices with their start and end apart: 27 -> 27, of which waited for: 14 -> 15; matrix products, arithmetic and copies ran while one was open for 1% -> 1% of each run, Pallas kernels for 14% -> 14%
where the time goes in v7:
time: 121 us; the launch traced here: 120 us
  starting transfers between devices  59.8 us (49%)
  waiting for transfers between devices  35.5 us (29%)
  Pallas kernels  18.4 us (15%)
  local copies, waits for them, and re-layouts  4.3 us (4%)
    ppermute x3, starting transfers between devices, shift_space(): lax.ppermute(a, 'space', [(i, i + by) for i in range(16) if 0 <= i + by <...  14.2 us
    pallas_call x12, Pallas kernels, call(): pl.pallas_call(kernel, out_shape=shapes, in_specs=[SMEM] * scalars + [VME...  13.4 us
    ppermute x10, starting transfers between devices, to_x(): return lax.ppermute(a, 'chan', [(i, (i + 2 * d) % 8) for i in range(8)])  12.1 us
    ppermute x10, waiting for transfers between devices, to_x(): return lax.ppermute(a, 'chan', [(i, (i + 2 * d) % 8) for i in range(8)])  11.9 us
    all_to_all x1, starting transfers between devices, per_device(): terms = lax.all_to_all(terms, ALL, 0, 0, axis_index_groups=ZC_GROUPS)  9.76 us
    all_to_all x1, waiting for transfers between devices, per_device(): terms = lax.all_to_all(terms, DS, 0, 0, axis_index_groups=Z_GROUPS)  8.78 us
    ppermute x6, starting transfers between devices, over_y(): return lax.ppermute(a, DS, pairs)  8.66 us
    all_to_all x1, starting transfers between devices, per_device(): terms = lax.all_to_all(terms, DS, 0, 0, axis_index_groups=Z_GROUPS)  6.39 us
  transfers between devices with their start and end apart: 27, of which 15 were waited for; matrix products, arithmetic and copies ran while one was open for 1% of the time, Pallas kernels for 14%

profile of v7, /device:TPU:32, one launch (start us, length us, event | category | flops | bytes accessed | tf_op | source)
XLA Modules:
  0.0 119.8 jit_solution(13892357661241841047)
XLA Ops:
  0.6 0.9 copy-done.5
  1.6 0.6 shard_map.76.own_ref
  2.2 2.8 %collective-permute-start.1 = (bf16[2,4,64,256]{3,2,1,0:T(8,128)(2,1)S(1)}, bf16[2,4,64,256]{3,2,1,0:T(8,128)(2,1)S(1)}, u32[]{:S(2)}, u32[]{:S(2)}) collective-permute-start(bf16[2,4,64,256]{3,2,1,0:T(8,128)(2,1)S(1)} %shard_map.76.own_ref), channel_id=1, source_target_pairs={{0,6},{1,7},{2,0},{3,1},{4,2},{5,3},{6,4},{7,5},{8,14},{9,15},{10,... | collective-permute-start | bytes 786440 | tf_op jit(solution)/shard_map/ppermute | solution.py:350
  5.1 1.5 %copy-done = bf16[64,13824]{1,0:T(8,128)(2,1)S(1)} copy-done((bf16[64,13824]{1,0:T(8,128)(2,1)S(1)}, bf16[64,13824]{1,0:T(8,128)(2,1)}, u32[]{:S(2)}) %copy-start) | copy-done | bytes 1769496
  6.6 2.3 %shard_map.78 = (bf16[64,6912]{1,0:T(8,128)(2,1)S(1)}, bf16[64,6912]{1,0:T(8,128)(2,1)}) custom-call(s32[2]{0:T(128)S(1)} %pad_add_fusion.where_ref, bf16[64,13824]{1,0:T(8,128)(2,1)S(1)} %copy-done), custom_call_target="tpu_custom_call" | custom-call | tf_op jit(solution)/shard_map/pallas_call | solution.py:334
  8.9 1.7 %collective-permute-done.1.ahead_ref = bf16[2,4,64,256]{3,2,1,0:T(8,128)(2,1)S(1)} collective-permute-done((bf16[2,4,64,256]{3,2,1,0:T(8,128)(2,1)S(1)}, bf16[2,4,64,256]{3,2,1,0:T(8,128)(2,1)S(1)}, u32[]{:S(2)}, u32[]{:S(2)}) %collective-permute-start.1) | collective-permute-done | bytes 262176 | tf_op jit(solution)/shard_map/ppermute | solution.py:350
  10.6 3.8 %collective-permute-start.2 = (bf16[4,64,256]{2,1,0:T(8,128)(2,1)S(1)}, bf16[4,64,256]{2,1,0:T(8,128)(2,1)S(1)}, u32[]{:S(2)}, u32[]{:S(2)}) collective-permute-start(bf16[4,64,256]{2,1,0:T(8,128)(2,1)S(1)} %slice_bitcast_fusion.2), channel_id=1, source_target_pairs={{0,6},{1,7},{2,0},{3,1},{4,2},{5,3},{6,4},{7,5},{8,14},{9,15},{10,... | collective-permute-start | bytes 393224 | tf_op jit(solution)/shard_map/ppermute | solution.py:350
  14.5 1.1 shard_map.75
  15.6 0.8 copy-done.3
  16.9 3.8 %collective-permute-done.3.across_1.across_ref = bf16[4,64,256]{2,1,0:T(8,128)(2,1)S(1)} collective-permute-done((bf16[4,64,256]{2,1,0:T(8,128)(2,1)S(1)}, bf16[4,64,256]{2,1,0:T(8,128)(2,1)S(1)}, u32[]{:S(2)}, u32[]{:S(2)}) %collective-permute-start.3) | collective-permute-done | bytes 131104 | tf_op jit(solution)/shard_map/ppermute | solution.py:350
  20.7 1.0 shard_map.77.all_ref
  21.7 4.6 %all-to-all-start = ((bf16[4,2,4,64,256]{4,3,2,1,0:T(8,128)(2,1)}), bf16[4,2,4,64,256]{4,3,2,1,0:T(8,128)(2,1)S(1)}, u32[]{:S(2)}, u32[]{:S(2)}) async-start(bf16[4,2,4,64,256]{4,3,2,1,0:T(8,128)(2,1)} %shard_map.77.all_ref), calls=%async_computation | async-start | bytes 2097152 | tf_op jit(solution)/shard_map/all_to_all | solution.py:387
  26.3 0.9 copy-done.2
  27.8 1.9 %shard_map.79 = (f32[64,256]{1,0:T(8,128)S(1)}, f32[64,256]{1,0:T(8,128)S(1)}) custom-call(s32[1]{0:T(128)} %bitcast.x_ref, bf16[4,2,4,64,256]{4,3,2,1,0:T(8,128)(2,1)} %shard_map.77.all_ref, bf16[64,6912]{1,0:T(8,128)(2,1)S(1)} %get-tuple-element.48.w_ref, bf16[64,6912]{1,0:T(8,128)(2,1)S(1)} %collective-permute-done.4.v_ref), custom_call_target="tpu_custom_call" | custom-call | tf_op jit(solution)/shard_map/pallas_call | solution.py:334
  29.7 0.6 collective-permute-start.5
  30.3 5.4 %collective-permute-start.7 = (f32[64,256]{1,0:T(8,128)S(1)}, f32[64,256]{1,0:T(8,128)S(1)}, u32[]{:S(2)}, u32[]{:S(2)}) collective-permute-start(f32[64,256]{1,0:T(8,128)S(1)} %add.19), channel_id=1, source_target_pairs={{0,8},{8,16},{16,24},{24,32},{32,40},{40,48},{48,56},{56,64},{64,7... | collective-permute-start | bytes 196616 | tf_op jit(solution)/shard_map/ppermute | solution.py:346
  35.9 2.9 %collective-permute-done.7.c_ref = f32[64,256]{1,0:T(8,128)S(1)} collective-permute-done((f32[64,256]{1,0:T(8,128)S(1)}, f32[64,256]{1,0:T(8,128)S(1)}, u32[]{:S(2)}, u32[]{:S(2)}) %collective-permute-start.7) | collective-permute-done | bytes 65568 | tf_op jit(solution)/shard_map/ppermute | solution.py:346
  38.9 0.8 shard_map.81
  39.7 0.8 all-to-all-done.x_ref
  40.5 3.8 %collective-permute-start.10 = (bf16[2,4,64,256]{3,2,1,0:T(8,128)(2,1)S(1)}, bf16[2,4,64,256]{3,2,1,0:T(8,128)(2,1)S(1)}, u32[]{:S(2)}, u32[]{:S(2)}) collective-permute-start(bf16[2,4,64,256]{3,2,1,0:T(8,128)(2,1)S(1)} %slice_bitcast_fusion), channel_id=1, source_target_pairs={{0,16},{8,24},{16,32},{24,40},{32,48},{40,56},{48,64},{56,72},{64,... | collective-permute-start | bytes 786440 | tf_op jit(solution)/shard_map/ppermute | solution.py:346
  44.4 3.4 %all-to-all-start.1 = ((bf16[8,64,256]{2,1,0:T(8,128)(2,1)}), bf16[8,64,256]{2,1,0:T(8,128)(2,1)S(1)}, u32[]{:S(2)}, u32[]{:S(2)}) async-start(bf16[8,64,256]{2,1,0:T(8,128)(2,1)} %get-tuple-element.61), calls=%async_computation.1 | async-start | bytes 524288 | tf_op jit(solution)/shard_map/all_to_all | solution.py:399
  47.8 4.9 %collective-permute-start.9 = (bf16[64,256]{1,0:T(8,128)(2,1)S(1)}, bf16[64,256]{1,0:T(8,128)(2,1)S(1)}, u32[]{:S(2)}, u32[]{:S(2)}) collective-permute-start(bf16[64,256]{1,0:T(8,128)(2,1)S(1)} %get-tuple-element.59), channel_id=1, source_target_pairs={{8,0},{16,8},{24,16},{32,24},{40,32},{48,40},{56,48},{64,56},{72,6... | collective-permute-start | bytes 98312 | tf_op jit(solution)/shard_map/ppermute | solution.py:346
  52.7 2.9 %all-to-all-done.1.dy_ref = bf16[8,64,256]{2,1,0:T(8,128)(2,1)S(1)} async-done(((bf16[8,64,256]{2,1,0:T(8,128)(2,1)}), bf16[8,64,256]{2,1,0:T(8,128)(2,1)S(1)}, u32[]{:S(2)}, u32[]{:S(2)}) %all-to-all-start.1) | async-done | bytes 262176 | tf_op jit(solution)/shard_map/all_to_all | solution.py:399
  55.6 1.6 %shard_map.82 = bf16[16,16,896]{2,1,0:T(8,128)(2,1)} custom-call(bf16[8,64,256]{2,1,0:T(8,128)(2,1)S(1)} %all-to-all-done.1.dy_ref, bf16[4,2,4,64,256]{4,3,2,1,0:T(8,128)(2,1)S(1)} %all-to-all-done.x_ref, bf16[2,4,64,256]{3,2,1,0:T(8,128)(2,1)S(1)} %collective-permute-done.10.e_ref), custom_call_target="tpu_custom_call" | custom-call | tf_op jit(solution)/shard_map/pallas_call | solution.py:334
  57.3 9.8 %all-to-all-start.2 = ((bf16[16,16,896]{2,1,0:T(8,128)(2,1)}), bf16[16,16,896]{2,1,0:T(8,128)(2,1)S(1)}, u32[]{:S(2)}, u32[]{:S(2)}) async-start(bf16[16,16,896]{2,1,0:T(8,128)(2,1)} %shard_map.82), calls=%async_computation.2 | async-start | bytes 917504 | tf_op jit(solution)/shard_map/all_to_all | solution.py:406
  67.1 0.8 collective-permute-start.12
  68.0 1.2 collective-permute-start.11
  69.1 2.8 %collective-permute-done.13.refs_7_ = bf16[2,64,256]{2,1,0:T(8,128)(2,1)S(1)} collective-permute-done((bf16[2,64,256]{2,1,0:T(8,128)(2,1)S(1)}, bf16[2,64,256]{2,1,0:T(8,128)(2,1)S(1)}, u32[]{:S(2)}, u32[]{:S(2)}) %collective-permute-start.13) | collective-permute-done | bytes 65568 | tf_op jit(solution)/shard_map/ppermute | solution.py:350
  71.9 1.1 collective-permute-done.12.refs_6_
  73.1 1.3 %collective-permute-done.11.refs_5_ = bf16[2,64,256]{2,1,0:T(8,128)(2,1)S(1)} collective-permute-done((bf16[2,64,256]{2,1,0:T(8,128)(2,1)S(1)}, bf16[2,64,256]{2,1,0:T(8,128)(2,1)S(1)}, u32[]{:S(2)}, u32[]{:S(2)}) %collective-permute-start.11) | collective-permute-done | bytes 65568 | tf_op jit(solution)/shard_map/ppermute | solution.py:350
  74.3 0.6 collective-permute-start.14
  74.9 2.7 %collective-permute-start.15 = (bf16[64,3456]{1,0:T(8,128)(2,1)}, bf16[64,3456]{1,0:T(8,128)(2,1)S(1)}, u32[]{:S(2)}, u32[]{:S(2)}) collective-permute-start(bf16[64,3456]{1,0:T(8,128)(2,1)} %copy-done.7), channel_id=1, source_target_pairs={{0,6},{1,7},{2,0},{3,1},{4,2},{5,3},{6,4},{7,5},{8,14},{9,15},{10,... | collective-permute-start | bytes 1327112 | tf_op jit(solution)/shard_map/ppermute | solution.py:350
  77.6 1.8 %all-to-all-done.2.r_ref = bf16[16,16,896]{2,1,0:T(8,128)(2,1)S(1)} async-done(((bf16[16,16,896]{2,1,0:T(8,128)(2,1)}), bf16[16,16,896]{2,1,0:T(8,128)(2,1)S(1)}, u32[]{:S(2)}, u32[]{:S(2)}) %all-to-all-start.2) | async-done | bytes 458784 | tf_op jit(solution)/shard_map/all_to_all | solution.py:406
  79.4 0.9 shard_map.84
  80.4 6.4 %all-to-all-start.3 = ((bf16[8,2,16,896]{3,2,1,0:T(8,128)(2,1)}), bf16[8,2,16,896]{3,2,1,0:T(8,128)(2,1)S(1)}, u32[]{:S(2)}, u32[]{:S(2)}) async-start(bf16[8,2,16,896]{3,2,1,0:T(8,128)(2,1)} %shard_map.84), calls=%async_computation.3 | async-start | bytes 917504 | tf_op jit(solution)/shard_map/all_to_all | solution.py:423
  86.7 0.8 collective-permute-done.14.refs_1_
  87.5 1.0 shard_map.83
  88.7 1.9 %collective-permute-done.16.b_ref = f32[2,4,64,256]{3,2,1,0:T(8,128)S(1)} collective-permute-done((f32[2,4,64,256]{3,2,1,0:T(8,128)S(1)}, f32[2,4,64,256]{3,2,1,0:T(8,128)S(1)}, u32[]{:S(2)}, u32[]{:S(2)}) %collective-permute-start.16) | collective-permute-done | bytes 524320 | tf_op jit(solution)/shard_map/ppermute | solution.py:363
  90.6 8.8 %all-to-all-done.3.r_ref = bf16[8,2,16,896]{3,2,1,0:T(8,128)(2,1)S(1)} async-done(((bf16[8,2,16,896]{3,2,1,0:T(8,128)(2,1)}), bf16[8,2,16,896]{3,2,1,0:T(8,128)(2,1)S(1)}, u32[]{:S(2)}, u32[]{:S(2)}) %all-to-all-start.3) | async-done | bytes 458784 | tf_op jit(solution)/shard_map/all_to_all | solution.py:423
  99.7 3.0 %collective-permute-start.19 = (bf16[4,2,16,896]{3,2,1,0:T(8,128)(2,1)S(1)}, bf16[4,2,16,896]{3,2,1,0:T(8,128)(2,1)S(1)}, u32[]{:S(2)}, u32[]{:S(2)}) collective-permute-start(bf16[4,2,16,896]{3,2,1,0:T(8,128)(2,1)S(1)} %get-tuple-element.79.refs_1_), channel_id=1, source_target_pairs={{0,136},{8,128},{16,152},{24,144},{32,168},{40,160},{48,184},{56,1... | collective-permute-start | bytes 688136 | tf_op jit(solution)/shard_map/ppermute | solution.py:359
  102.7 1.9 %collective-permute-start.22 = (bf16[4,2,16,896]{3,2,1,0:T(8,128)(2,1)S(1)}, bf16[4,2,16,896]{3,2,1,0:T(8,128)(2,1)S(1)}, u32[]{:S(2)}, u32[]{:S(2)}) collective-permute-start(bf16[4,2,16,896]{3,2,1,0:T(8,128)(2,1)S(1)} %get-tuple-element.78.refs_0_), channel_id=1, source_target_pairs={{0,136},{8,128},{16,152},{24,144},{32,168},{40,160},{48,184},{56,1... | collective-permute-start | bytes 688136 | tf_op jit(solution)/shard_map/ppermute | solution.py:359
  104.7 3.9 %collective-permute-done.17.refs_0_ = bf16[4,2,16,896]{3,2,1,0:T(8,128)(2,1)S(1)} collective-permute-done((bf16[4,2,16,896]{3,2,1,0:T(8,128)(2,1)S(1)}, bf16[4,2,16,896]{3,2,1,0:T(8,128)(2,1)S(1)}, u32[]{:S(2)}, u32[]{:S(2)}) %collective-permute-start.17) | collective-permute-done | bytes 229408 | tf_op jit(solution)/shard_map/ppermute | solution.py:359
  109.3 3.1 %collective-permute-start.20 = (bf16[4,2,16,896]{3,2,1,0:T(8,128)(2,1)S(1)}, bf16[4,2,16,896]{3,2,1,0:T(8,128)(2,1)S(1)}, u32[]{:S(2)}, u32[]{:S(2)}) collective-permute-start(bf16[4,2,16,896]{3,2,1,0:T(8,128)(2,1)S(1)} %collective-permute-done.19.refs_3_), channel_id=1, source_target_pairs={{0,136},{8,128},{16,152},{24,144},{32,168},{40,160},{48,184},{56,1... | collective-permute-start | bytes 688136 | tf_op jit(solution)/shard_map/ppermute | solution.py:359
  112.4 1.6 %shard_map.87 = (f32[64,13824]{1,0:T(8,128)}, f32[64,1]{1,0:T(8,128)S(1)}) custom-call(s32[1]{0:T(128)} %bitcast.13.q_ref, bf16[4,2,16,896]{3,2,1,0:T(8,128)(2,1)S(1)} %get-tuple-element.78.refs_0_, bf16[4,2,16,896]{3,2,1,0:T(8,128)(2,1)S(1)} %get-tuple-element.79.refs_1_), custom_call_target="tpu_custom_call" | custom-call | tf_op jit(solution)/shard_map/pallas_call | solution.py:272
  114.1 1.5 %shard_map.85 = bf16[2,64,1024]{2,1,0:T(8,128)(2,1)} custom-call(f32[2,4,64,256]{3,2,1,0:T(8,128)S(1)} %get-tuple-element.75.a_ref, f32[2,4,64,256]{3,2,1,0:T(8,128)S(1)} %collective-permute-done.16.b_ref), custom_call_target="tpu_custom_call" | custom-call | tf_op jit(solution)/shard_map/pallas_call | solution.py:334
  115.6 0.6 reduce
  116.2 2.0 %shard_map.88.refs_2_ = f32[64,13824]{1,0:T(8,128)} custom-call(s32[1]{0:T(128)} %bitcast.13.q_ref, bf16[4,2,16,896]{3,2,1,0:T(8,128)(2,1)S(1)} %collective-permute-done.17.refs_0_, bf16[4,2,16,896]{3,2,1,0:T(8,128)(2,1)S(1)} %collective-permute-done.21.refs_1_, ...), custom_call_target="tpu_custom_call", output_to_operand_aliasing={{}: (5, {})} | custom-call | tf_op jit(solution)/shard_map/pallas_call | solution.py:272
  118.2 1.4 %shard_map.89 = f32[64,13824]{1,0:T(8,128)} custom-call(s32[1]{0:T(128)} %bitcast.13.q_ref, bf16[4,2,16,896]{3,2,1,0:T(8,128)(2,1)S(1)} %collective-permute-done.18.refs_0_, bf16[4,2,16,896]{3,2,1,0:T(8,128)(2,1)S(1)} %collective-permute-done.20.refs_1_, f32[64,13824]{1,0:T(8,128)} %shard_map.88.refs_2_), custom_call_target="tpu_custom_call", output_to_operand_aliasing={{}: (3, {})} | custom-call | tf_op jit(solution)/shard_map/pallas_call | solution.py:272
  (49 shorter events, 2.7 us)
Async XLA Ops:
  0.6 1.0 copy-start.5
  2.2 8.4 %collective-permute-start.1 = (bf16[2,4,64,256]{3,2,1,0:T(8,128)(2,1)S(1)}, bf16[2,4,64,256]{3,2,1,0:T(8,128)(2,1)S(1)}, u32[]{:S(2)}, u32[]{:S(2)}) collective-permute-start(bf16[2,4,64,256]{3,2,1,0:T(8,128)(2,1)S(1)} %shard_map.76.own_ref), channel_id=1, source_target_pairs={{0,6},{1,7},{2,0},{3,1},{4,2},{5,3},{6,4},{7,5},{8,14},{9,15},{10,... | collective-permute-start | bytes 786440 | tf_op jit(solution)/shard_map/ppermute | solution.py:350
  5.0 9.3 %collective-permute-start = (bf16[2,4,64,256]{3,2,1,0:T(8,128)(2,1)S(1)}, bf16[2,4,64,256]{3,2,1,0:T(8,128)(2,1)S(1)}, u32[]{:S(2)}, u32[]{:S(2)}) collective-permute-start(bf16[2,4,64,256]{3,2,1,0:T(8,128)(2,1)S(1)} %shard_map.76.own_ref), channel_id=1, source_target_pairs={{0,2},{1,3},{2,4},{3,5},{4,6},{5,7},{6,0},{7,1},{8,10},{9,11},{10,... | collective-permute-start | bytes 786440 | tf_op jit(solution)/shard_map/ppermute | solution.py:350
  5.1 1.5 %copy-start = (bf16[64,13824]{1,0:T(8,128)(2,1)S(1)}, bf16[64,13824]{1,0:T(8,128)(2,1)}, u32[]{:S(2)}) copy-start(bf16[64,13824]{1,0:T(8,128)(2,1)} %w_ref.3) | copy-start | bytes 5308420
  8.9 17.4 %collective-permute-start.4 = (bf16[64,6912]{1,0:T(8,128)(2,1)}, bf16[64,6912]{1,0:T(8,128)(2,1)S(1)}, u32[]{:S(2)}, u32[]{:S(2)}) collective-permute-start(bf16[64,6912]{1,0:T(8,128)(2,1)} %get-tuple-element.49), channel_id=1, source_target_pairs={{0,1},{1,0},{2,3},{3,2},{4,5},{5,4},{6,7},{7,6},{8,9},{9,8},{10,11... | collective-permute-start | bytes 2654216 | tf_op jit(solution)/shard_map/ppermute | solution.py:363
  10.6 6.3 %collective-permute-start.2 = (bf16[4,64,256]{2,1,0:T(8,128)(2,1)S(1)}, bf16[4,64,256]{2,1,0:T(8,128)(2,1)S(1)}, u32[]{:S(2)}, u32[]{:S(2)}) collective-permute-start(bf16[4,64,256]{2,1,0:T(8,128)(2,1)S(1)} %slice_bitcast_fusion.2), channel_id=1, source_target_pairs={{0,6},{1,7},{2,0},{3,1},{4,2},{5,3},{6,4},{7,5},{8,14},{9,15},{10,... | collective-permute-start | bytes 393224 | tf_op jit(solution)/shard_map/ppermute | solution.py:350
  14.4 7.3 %copy-start.1 = (bf16[2,4,64,256]{3,2,1,0:T(8,128)(2,1)}, bf16[2,4,64,256]{3,2,1,0:T(8,128)(2,1)S(1)}, u32[]{:S(2)}) copy-start(bf16[2,4,64,256]{3,2,1,0:T(8,128)(2,1)S(1)} %collective-permute-done.back_ref) | copy-start | bytes 786436
  14.4 6.3 %collective-permute-start.3 = (bf16[4,64,256]{2,1,0:T(8,128)(2,1)S(1)}, bf16[4,64,256]{2,1,0:T(8,128)(2,1)S(1)}, u32[]{:S(2)}, u32[]{:S(2)}) collective-permute-start(bf16[4,64,256]{2,1,0:T(8,128)(2,1)S(1)} %slice_bitcast_fusion.1), channel_id=1, source_target_pairs={{0,2},{1,3},{2,4},{3,5},{4,6},{5,7},{6,0},{7,1},{8,10},{9,11},{10,... | collective-permute-start | bytes 393224 | tf_op jit(solution)/shard_map/ppermute | solution.py:350
  15.6 0.8 copy-start.3
  16.4 5.3 %copy-start.8 = (bf16[64,3456]{1,0:T(8,128)(2,1)}, bf16[64,3456]{1,0:T(8,128)(2,1)S(1)}, u32[]{:S(2)}) copy-start(bf16[64,3456]{1,0:T(8,128)(2,1)S(1)} %get-tuple-element.60) | copy-start | bytes 1327108
  16.4 5.3 %copy-start.7 = (bf16[64,3456]{1,0:T(8,128)(2,1)}, bf16[64,3456]{1,0:T(8,128)(2,1)S(1)}, u32[]{:S(2)}) copy-start(bf16[64,3456]{1,0:T(8,128)(2,1)S(1)} %get-tuple-element.66) | copy-start | bytes 1327108
  21.7 14.1 %copy-start.9 = (f32[64]{0:T(128)S(1)}, f32[64]{0:T(128)}, u32[]{:S(2)}) copy-start(f32[64]{0:T(128)} %param.6) | copy-start | bytes 772
  21.7 17.2 %copy-start.6 = (bf16[1,1,64,256]{3,2,1,0:T(8,128)(2,1)S(1)}, bf16[1,1,64,256]{3,2,1,0:T(8,128)(2,1)}, u32[]{:S(2)}) copy-start(bf16[1,1,64,256]{3,2,1,0:T(8,128)(2,1)} %param.7) | copy-start | bytes 98308
  21.7 18.8 %all-to-all-start = ((bf16[4,2,4,64,256]{4,3,2,1,0:T(8,128)(2,1)}), bf16[4,2,4,64,256]{4,3,2,1,0:T(8,128)(2,1)S(1)}, u32[]{:S(2)}, u32[]{:S(2)}) async-start(bf16[4,2,4,64,256]{4,3,2,1,0:T(8,128)(2,1)} %shard_map.77.all_ref), calls=%async_computation | async-start | bytes 2097152 | tf_op jit(solution)/shard_map/all_to_all | solution.py:387
  26.3 1.0 copy-start.2
  27.7 2.6 %collective-permute-start.6 = (f32[64,256]{1,0:T(8,128)S(1)}, f32[64,256]{1,0:T(8,128)S(1)}, u32[]{:S(2)}, u32[]{:S(2)}) collective-permute-start(f32[64,256]{1,0:T(8,128)S(1)} %get-tuple-element.53), channel_id=1, source_target_pairs={{0,1},{1,0},{2,3},{3,2},{4,5},{5,4},{6,7},{7,6},{8,9},{9,8},{10,11... | collective-permute-start | bytes 196616 | tf_op jit(solution)/shard_map/ppermute | solution.py:363
  29.7 57.8 %copy-start.4 = (bf16[64,3456]{1,0:T(8,128)(2,1)S(1)}, bf16[64,3456]{1,0:T(8,128)(2,1)}, u32[]{:S(2)}) copy-start(bf16[64,3456]{1,0:T(8,128)(2,1)} %copy-done.3) | copy-start | bytes 1327108
  29.7 6.2 %collective-permute-start.5 = (f32[64,256]{1,0:T(8,128)S(1)}, f32[64,256]{1,0:T(8,128)S(1)}, u32[]{:S(2)}, u32[]{:S(2)}) collective-permute-start(f32[64,256]{1,0:T(8,128)S(1)} %get-tuple-element.51), channel_id=1, source_target_pairs={{0,1},{1,0},{2,3},{3,2},{4,5},{5,4},{6,7},{7,6},{8,9},{9,8},{10,11... | collective-permute-start | bytes 196616 | tf_op jit(solution)/shard_map/ppermute | solution.py:363
  30.3 8.6 %collective-permute-start.7 = (f32[64,256]{1,0:T(8,128)S(1)}, f32[64,256]{1,0:T(8,128)S(1)}, u32[]{:S(2)}, u32[]{:S(2)}) collective-permute-start(f32[64,256]{1,0:T(8,128)S(1)} %add.19), channel_id=1, source_target_pairs={{0,8},{8,16},{16,24},{24,32},{32,40},{40,48},{48,56},{56,64},{64,7... | collective-permute-start | bytes 196616 | tf_op jit(solution)/shard_map/ppermute | solution.py:346
  35.9 21.4 %collective-permute-start.8 = (bf16[64,3456]{1,0:T(8,128)(2,1)}, bf16[64,3456]{1,0:T(8,128)(2,1)S(1)}, u32[]{:S(2)}, u32[]{:S(2)}) collective-permute-start(bf16[64,3456]{1,0:T(8,128)(2,1)} %copy-done.8), channel_id=1, source_target_pairs={{0,4},{1,5},{2,6},{3,7},{4,0},{5,1},{6,2},{7,3},{8,12},{9,13},{10,... | collective-permute-start | bytes 1327112 | tf_op jit(solution)/shard_map/ppermute | solution.py:350
  40.5 15.1 %collective-permute-start.10 = (bf16[2,4,64,256]{3,2,1,0:T(8,128)(2,1)S(1)}, bf16[2,4,64,256]{3,2,1,0:T(8,128)(2,1)S(1)}, u32[]{:S(2)}, u32[]{:S(2)}) collective-permute-start(bf16[2,4,64,256]{3,2,1,0:T(8,128)(2,1)S(1)} %slice_bitcast_fusion), channel_id=1, source_target_pairs={{0,16},{8,24},{16,32},{24,40},{32,48},{40,56},{48,64},{56,72},{64,... | collective-permute-start | bytes 786440 | tf_op jit(solution)/shard_map/ppermute | solution.py:346
  44.4 11.2 %all-to-all-start.1 = ((bf16[8,64,256]{2,1,0:T(8,128)(2,1)}), bf16[8,64,256]{2,1,0:T(8,128)(2,1)S(1)}, u32[]{:S(2)}, u32[]{:S(2)}) async-start(bf16[8,64,256]{2,1,0:T(8,128)(2,1)} %get-tuple-element.61), calls=%async_computation.1 | async-start | bytes 524288 | tf_op jit(solution)/shard_map/all_to_all | solution.py:399
  47.8 9.4 %collective-permute-start.9 = (bf16[64,256]{1,0:T(8,128)(2,1)S(1)}, bf16[64,256]{1,0:T(8,128)(2,1)S(1)}, u32[]{:S(2)}, u32[]{:S(2)}) collective-permute-start(bf16[64,256]{1,0:T(8,128)(2,1)S(1)} %get-tuple-element.59), channel_id=1, source_target_pairs={{8,0},{16,8},{24,16},{32,24},{40,32},{48,40},{56,48},{64,56},{72,6... | collective-permute-start | bytes 98312 | tf_op jit(solution)/shard_map/ppermute | solution.py:346
  57.3 22.2 %all-to-all-start.2 = ((bf16[16,16,896]{2,1,0:T(8,128)(2,1)}), bf16[16,16,896]{2,1,0:T(8,128)(2,1)S(1)}, u32[]{:S(2)}, u32[]{:S(2)}) async-start(bf16[16,16,896]{2,1,0:T(8,128)(2,1)} %shard_map.82), calls=%async_computation.2 | async-start | bytes 917504 | tf_op jit(solution)/shard_map/all_to_all | solution.py:406
  67.0 4.9 %collective-permute-start.13 = (bf16[2,64,256]{2,1,0:T(8,128)(2,1)S(1)}, bf16[2,64,256]{2,1,0:T(8,128)(2,1)S(1)}, u32[]{:S(2)}, u32[]{:S(2)}) collective-permute-start(bf16[2,64,256]{2,1,0:T(8,128)(2,1)S(1)} %pad_maximum_fusion.refs_4_), channel_id=1, source_target_pairs={{0,6},{1,7},{2,0},{3,1},{4,2},{5,3},{6,4},{7,5},{8,14},{9,15},{10,... | collective-permute-start | bytes 196616 | tf_op jit(solution)/shard_map/ppermute | solution.py:350
  67.1 6.0 %collective-permute-start.12 = (bf16[2,64,256]{2,1,0:T(8,128)(2,1)S(1)}, bf16[2,64,256]{2,1,0:T(8,128)(2,1)S(1)}, u32[]{:S(2)}, u32[]{:S(2)}) collective-permute-start(bf16[2,64,256]{2,1,0:T(8,128)(2,1)S(1)} %pad_maximum_fusion.refs_4_), channel_id=1, source_target_pairs={{0,4},{1,5},{2,6},{3,7},{4,0},{5,1},{6,2},{7,3},{8,12},{9,13},{10,... | collective-permute-start | bytes 196616 | tf_op jit(solution)/shard_map/ppermute | solution.py:350
  68.0 6.4 %collective-permute-start.11 = (bf16[2,64,256]{2,1,0:T(8,128)(2,1)S(1)}, bf16[2,64,256]{2,1,0:T(8,128)(2,1)S(1)}, u32[]{:S(2)}, u32[]{:S(2)}) collective-permute-start(bf16[2,64,256]{2,1,0:T(8,128)(2,1)S(1)} %pad_maximum_fusion.refs_4_), channel_id=1, source_target_pairs={{0,2},{1,3},{2,4},{3,5},{4,6},{5,7},{6,0},{7,1},{8,10},{9,11},{10,... | collective-permute-start | bytes 196616 | tf_op jit(solution)/shard_map/ppermute | solution.py:350
  74.3 13.2 %collective-permute-start.14 = (bf16[64,3456]{1,0:T(8,128)(2,1)}, bf16[64,3456]{1,0:T(8,128)(2,1)S(1)}, u32[]{:S(2)}, u32[]{:S(2)}) collective-permute-start(bf16[64,3456]{1,0:T(8,128)(2,1)} %get-tuple-element.64), channel_id=1, source_target_pairs={{0,2},{1,3},{2,4},{3,5},{4,6},{5,7},{6,0},{7,1},{8,10},{9,11},{10,... | collective-permute-start | bytes 1327112 | tf_op jit(solution)/shard_map/ppermute | solution.py:350
  74.9 12.6 %collective-permute-start.15 = (bf16[64,3456]{1,0:T(8,128)(2,1)}, bf16[64,3456]{1,0:T(8,128)(2,1)S(1)}, u32[]{:S(2)}, u32[]{:S(2)}) collective-permute-start(bf16[64,3456]{1,0:T(8,128)(2,1)} %copy-done.7), channel_id=1, source_target_pairs={{0,6},{1,7},{2,0},{3,1},{4,2},{5,3},{6,4},{7,5},{8,14},{9,15},{10,... | collective-permute-start | bytes 1327112 | tf_op jit(solution)/shard_map/ppermute | solution.py:350
  80.4 19.0 %all-to-all-start.3 = ((bf16[8,2,16,896]{3,2,1,0:T(8,128)(2,1)}), bf16[8,2,16,896]{3,2,1,0:T(8,128)(2,1)S(1)}, u32[]{:S(2)}, u32[]{:S(2)}) async-start(bf16[8,2,16,896]{3,2,1,0:T(8,128)(2,1)} %shard_map.84), calls=%async_computation.3 | async-start | bytes 917504 | tf_op jit(solution)/shard_map/all_to_all | solution.py:423
  88.6 2.0 %collective-permute-start.16 = (f32[2,4,64,256]{3,2,1,0:T(8,128)S(1)}, f32[2,4,64,256]{3,2,1,0:T(8,128)S(1)}, u32[]{:S(2)}, u32[]{:S(2)}) collective-permute-start(f32[2,4,64,256]{3,2,1,0:T(8,128)S(1)} %get-tuple-element.73), channel_id=1, source_target_pairs={{0,1},{1,0},{2,3},{3,2},{4,5},{5,4},{6,7},{7,6},{8,9},{9,8},{10,11... | collective-permute-start | bytes 1572872 | tf_op jit(solution)/shard_map/ppermute | solution.py:363
  99.4 9.3 %collective-permute-start.17 = (bf16[4,2,16,896]{3,2,1,0:T(8,128)(2,1)S(1)}, bf16[4,2,16,896]{3,2,1,0:T(8,128)(2,1)S(1)}, u32[]{:S(2)}, u32[]{:S(2)}) collective-permute-start(bf16[4,2,16,896]{3,2,1,0:T(8,128)(2,1)S(1)} %get-tuple-element.78.refs_0_), channel_id=1, source_target_pairs={{0,128},{8,136},{16,144},{24,152},{32,160},{40,168},{48,176},{56,1... | collective-permute-start | bytes 688136 | tf_op jit(solution)/shard_map/ppermute | solution.py:359
  99.7 9.6 %collective-permute-start.19 = (bf16[4,2,16,896]{3,2,1,0:T(8,128)(2,1)S(1)}, bf16[4,2,16,896]{3,2,1,0:T(8,128)(2,1)S(1)}, u32[]{:S(2)}, u32[]{:S(2)}) collective-permute-start(bf16[4,2,16,896]{3,2,1,0:T(8,128)(2,1)S(1)} %get-tuple-element.79.refs_1_), channel_id=1, source_target_pairs={{0,136},{8,128},{16,152},{24,144},{32,168},{40,160},{48,184},{56,1... | collective-permute-start | bytes 688136 | tf_op jit(solution)/shard_map/ppermute | solution.py:359
  102.7 13.5 %collective-permute-start.22 = (bf16[4,2,16,896]{3,2,1,0:T(8,128)(2,1)S(1)}, bf16[4,2,16,896]{3,2,1,0:T(8,128)(2,1)S(1)}, u32[]{:S(2)}, u32[]{:S(2)}) collective-permute-start(bf16[4,2,16,896]{3,2,1,0:T(8,128)(2,1)S(1)} %get-tuple-element.78.refs_0_), channel_id=1, source_target_pairs={{0,136},{8,128},{16,152},{24,144},{32,168},{40,160},{48,184},{56,1... | collective-permute-start | bytes 688136 | tf_op jit(solution)/shard_map/ppermute | solution.py:359
  104.6 11.6 %collective-permute-start.21 = (bf16[4,2,16,896]{3,2,1,0:T(8,128)(2,1)S(1)}, bf16[4,2,16,896]{3,2,1,0:T(8,128)(2,1)S(1)}, u32[]{:S(2)}, u32[]{:S(2)}) collective-permute-start(bf16[4,2,16,896]{3,2,1,0:T(8,128)(2,1)S(1)} %get-tuple-element.79.refs_1_), channel_id=1, source_target_pairs={{0,128},{8,136},{16,144},{24,152},{32,160},{40,168},{48,176},{56,1... | collective-permute-start | bytes 688136 | tf_op jit(solution)/shard_map/ppermute | solution.py:359
  108.7 9.5 %collective-permute-start.18 = (bf16[4,2,16,896]{3,2,1,0:T(8,128)(2,1)S(1)}, bf16[4,2,16,896]{3,2,1,0:T(8,128)(2,1)S(1)}, u32[]{:S(2)}, u32[]{:S(2)}) collective-permute-start(bf16[4,2,16,896]{3,2,1,0:T(8,128)(2,1)S(1)} %collective-permute-done.17.refs_0_), channel_id=1, source_target_pairs={{0,128},{8,136},{16,144},{24,152},{32,160},{40,168},{48,176},{56,1... | collective-permute-start | bytes 688136 | tf_op jit(solution)/shard_map/ppermute | solution.py:359
  109.3 8.9 %collective-permute-start.20 = (bf16[4,2,16,896]{3,2,1,0:T(8,128)(2,1)S(1)}, bf16[4,2,16,896]{3,2,1,0:T(8,128)(2,1)S(1)}, u32[]{:S(2)}, u32[]{:S(2)}) collective-permute-start(bf16[4,2,16,896]{3,2,1,0:T(8,128)(2,1)S(1)} %collective-permute-done.19.refs_3_), channel_id=1, source_target_pairs={{0,136},{8,128},{16,152},{24,144},{32,168},{40,160},{48,184},{56,1... | collective-permute-start | bytes 688136 | tf_op jit(solution)/shard_map/ppermute | solution.py:359

commit v8 on v7

--- a/solution.py
+++ b/solution.py
@@ -15,7 +15,7 @@
 Y_GROUPS = [[dp * 16 + z * 2 + yh for yh in range(2) for dp in range(2)] for z in range(8)]
 Z_GROUPS = [[dp * 16 + z * 2 + yh for z in range(7, -1, -1)] for yh in range(2) for dp in range(2)]
 YC_GROUPS = [
-    [((dp * 16 + z * 2 + yh) * 8 + 2 * x + core) for yh in range(2) for dp in range(2) for core in range(2)]
+    [((dp * 16 + z * 2 + yh) * 8 + 2 * x + core) for yh in (1, 0) for dp in (1, 0) for core in (1, 0)]
     for z in range(8)
     for x in range(4)
 ]
@@ -170,7 +170,7 @@
             xs_ref[c, 64:128, cells] = x_ref[y, 1, c]
             xs_ref[c, 128:192, cells] = e_ref[y, c] if y < 2 else x_ref[y - 2, 1, c]
     grads = jnp.concatenate(
-        [jnp.concatenate([dy_ref[2 * y + core] for y in range(4)], 1) for core in range(2)], 0
+        [jnp.concatenate([dy_ref[7 - 2 * y - core] for y in range(4)], 1) for core in range(2)], 0
     ).astype(F32)
     shifted = {(sy, sz): earlier(grads, sy, sz).astype(BF) for sy in range(2) for sz in range(2)}
 

time: 121 us -> 121 us (level)
    ppermute x3, starting transfers between devices: 14.2 us -> 12.2 us  [shift_space(): lax.ppermute(a, 'space', [(i, i + by) for i in range(16) if 0 <= i + by <...]
    all_to_all x1, starting transfers between devices: 3.42 us -> 4.93 us  [per_device(): dy = lax.all_to_all(dy_copies, ALL, 0, 0, axis_index_groups=YC_GROUPS)]
  transfers between devices with their start and end apart: 27 -> 27, of which waited for: 15 -> 16; matrix products, arithmetic and copies ran while one was open for 1% -> 1% of each run, Pallas kernels for 14% -> 14%
where the time goes in v8:
time: 121 us; the launch traced here: 120 us
  starting transfers between devices  59.9 us (50%)
  waiting for transfers between devices  35.7 us (30%)
  Pallas kernels  18.4 us (15%)
  local copies, waits for them, and re-layouts  4.3 us (4%)
    pallas_call x12, Pallas kernels, call(): pl.pallas_call(kernel, out_shape=shapes, in_specs=[SMEM] * scalars + [VME...  13.4 us
    ppermute x3, starting transfers between devices, shift_space(): lax.ppermute(a, 'space', [(i, i + by) for i in range(16) if 0 <= i + by <...  12.2 us
    ppermute x10, starting transfers between devices, to_x(): return lax.ppermute(a, 'chan', [(i, (i + 2 * d) % 8) for i in range(8)])  12.1 us
    ppermute x10, waiting for transfers between devices, to_x(): return lax.ppermute(a, 'chan', [(i, (i + 2 * d) % 8) for i in range(8)])  11.9 us
    all_to_all x1, starting transfers between devices, per_device(): terms = lax.all_to_all(terms, ALL, 0, 0, axis_index_groups=ZC_GROUPS)  10.6 us
    all_to_all x1, waiting for transfers between devices, per_device(): terms = lax.all_to_all(terms, DS, 0, 0, axis_index_groups=Z_GROUPS)  8.78 us
    ppermute x6, starting transfers between devices, over_y(): return lax.ppermute(a, DS, pairs)  8.36 us
    all_to_all x1, starting transfers between devices, per_device(): terms = lax.all_to_all(terms, DS, 0, 0, axis_index_groups=Z_GROUPS)  6.39 us
  transfers between devices with their start and end apart: 27, of which 16 were waited for; matrix products, arithmetic and copies ran while one was open for 1% of the time, Pallas kernels for 14%

profile of v8, /device:TPU:32, one launch (start us, length us, event | category | flops | bytes accessed | tf_op | source)
XLA Modules:
  0.0 120.0 jit_solution(15836783370000442791)
XLA Ops:
  0.6 0.9 copy-done.5
  1.6 0.6 shard_map.76.own_ref
  2.2 2.8 %collective-permute-start.1 = (bf16[2,4,64,256]{3,2,1,0:T(8,128)(2,1)S(1)}, bf16[2,4,64,256]{3,2,1,0:T(8,128)(2,1)S(1)}, u32[]{:S(2)}, u32[]{:S(2)}) collective-permute-start(bf16[2,4,64,256]{3,2,1,0:T(8,128)(2,1)S(1)} %shard_map.76.own_ref), channel_id=1, source_target_pairs={{0,6},{1,7},{2,0},{3,1},{4,2},{5,3},{6,4},{7,5},{8,14},{9,15},{10,... | collective-permute-start | bytes 786440 | tf_op jit(solution)/shard_map/ppermute | solution.py:350
  5.1 1.5 %copy-done = bf16[64,13824]{1,0:T(8,128)(2,1)S(1)} copy-done((bf16[64,13824]{1,0:T(8,128)(2,1)S(1)}, bf16[64,13824]{1,0:T(8,128)(2,1)}, u32[]{:S(2)}) %copy-start) | copy-done | bytes 1769496
  6.6 2.3 %shard_map.78 = (bf16[64,6912]{1,0:T(8,128)(2,1)S(1)}, bf16[64,6912]{1,0:T(8,128)(2,1)}) custom-call(s32[2]{0:T(128)S(1)} %pad_add_fusion.where_ref, bf16[64,13824]{1,0:T(8,128)(2,1)S(1)} %copy-done), custom_call_target="tpu_custom_call" | custom-call | tf_op jit(solution)/shard_map/pallas_call | solution.py:334
  8.9 1.7 %collective-permute-done.1.ahead_ref = bf16[2,4,64,256]{3,2,1,0:T(8,128)(2,1)S(1)} collective-permute-done((bf16[2,4,64,256]{3,2,1,0:T(8,128)(2,1)S(1)}, bf16[2,4,64,256]{3,2,1,0:T(8,128)(2,1)S(1)}, u32[]{:S(2)}, u32[]{:S(2)}) %collective-permute-start.1) | collective-permute-done | bytes 262176 | tf_op jit(solution)/shard_map/ppermute | solution.py:350
  10.6 3.8 %collective-permute-start.2 = (bf16[4,64,256]{2,1,0:T(8,128)(2,1)S(1)}, bf16[4,64,256]{2,1,0:T(8,128)(2,1)S(1)}, u32[]{:S(2)}, u32[]{:S(2)}) collective-permute-start(bf16[4,64,256]{2,1,0:T(8,128)(2,1)S(1)} %slice_bitcast_fusion.2), channel_id=1, source_target_pairs={{0,6},{1,7},{2,0},{3,1},{4,2},{5,3},{6,4},{7,5},{8,14},{9,15},{10,... | collective-permute-start | bytes 393224 | tf_op jit(solution)/shard_map/ppermute | solution.py:350
  14.5 1.1 shard_map.75
  15.6 0.8 copy-done.3
  16.9 3.8 %collective-permute-done.3.across_1.across_ref = bf16[4,64,256]{2,1,0:T(8,128)(2,1)S(1)} collective-permute-done((bf16[4,64,256]{2,1,0:T(8,128)(2,1)S(1)}, bf16[4,64,256]{2,1,0:T(8,128)(2,1)S(1)}, u32[]{:S(2)}, u32[]{:S(2)}) %collective-permute-start.3) | collective-permute-done | bytes 131104 | tf_op jit(solution)/shard_map/ppermute | solution.py:350
  20.7 1.0 shard_map.77.all_ref
  21.7 4.6 %all-to-all-start = ((bf16[4,2,4,64,256]{4,3,2,1,0:T(8,128)(2,1)}), bf16[4,2,4,64,256]{4,3,2,1,0:T(8,128)(2,1)S(1)}, u32[]{:S(2)}, u32[]{:S(2)}) async-start(bf16[4,2,4,64,256]{4,3,2,1,0:T(8,128)(2,1)} %shard_map.77.all_ref), calls=%async_computation | async-start | bytes 2097152 | tf_op jit(solution)/shard_map/all_to_all | solution.py:387
  26.3 0.9 copy-done.2
  27.8 1.9 %shard_map.79 = (f32[64,256]{1,0:T(8,128)S(1)}, f32[64,256]{1,0:T(8,128)S(1)}) custom-call(s32[1]{0:T(128)} %bitcast.x_ref, bf16[4,2,4,64,256]{4,3,2,1,0:T(8,128)(2,1)} %shard_map.77.all_ref, bf16[64,6912]{1,0:T(8,128)(2,1)S(1)} %get-tuple-element.48.w_ref, bf16[64,6912]{1,0:T(8,128)(2,1)S(1)} %collective-permute-done.4.v_ref), custom_call_target="tpu_custom_call" | custom-call | tf_op jit(solution)/shard_map/pallas_call | solution.py:334
  30.3 5.4 %collective-permute-start.7 = (f32[64,256]{1,0:T(8,128)S(1)}, f32[64,256]{1,0:T(8,128)S(1)}, u32[]{:S(2)}, u32[]{:S(2)}) collective-permute-start(f32[64,256]{1,0:T(8,128)S(1)} %add.19), channel_id=1, source_target_pairs={{0,8},{8,16},{16,24},{24,32},{32,40},{40,48},{48,56},{56,64},{64,7... | collective-permute-start | bytes 196616 | tf_op jit(solution)/shard_map/ppermute | solution.py:346
  35.9 2.9 %collective-permute-done.7.c_ref = f32[64,256]{1,0:T(8,128)S(1)} collective-permute-done((f32[64,256]{1,0:T(8,128)S(1)}, f32[64,256]{1,0:T(8,128)S(1)}, u32[]{:S(2)}, u32[]{:S(2)}) %collective-permute-start.7) | collective-permute-done | bytes 65568 | tf_op jit(solution)/shard_map/ppermute | solution.py:346
  38.9 0.8 shard_map.81
  39.7 0.8 all-to-all-done.x_ref
  40.5 3.8 %collective-permute-start.10 = (bf16[2,4,64,256]{3,2,1,0:T(8,128)(2,1)S(1)}, bf16[2,4,64,256]{3,2,1,0:T(8,128)(2,1)S(1)}, u32[]{:S(2)}, u32[]{:S(2)}) collective-permute-start(bf16[2,4,64,256]{3,2,1,0:T(8,128)(2,1)S(1)} %slice_bitcast_fusion), channel_id=1, source_target_pairs={{0,16},{8,24},{16,32},{24,40},{32,48},{40,56},{48,64},{56,72},{64,... | collective-permute-start | bytes 786440 | tf_op jit(solution)/shard_map/ppermute | solution.py:346
  44.4 4.9 %all-to-all-start.1 = ((bf16[8,64,256]{2,1,0:T(8,128)(2,1)}), bf16[8,64,256]{2,1,0:T(8,128)(2,1)S(1)}, u32[]{:S(2)}, u32[]{:S(2)}) async-start(bf16[8,64,256]{2,1,0:T(8,128)(2,1)} %get-tuple-element.61), calls=%async_computation.1 | async-start | bytes 524288 | tf_op jit(solution)/shard_map/all_to_all | solution.py:399
  49.3 2.9 %collective-permute-start.9 = (bf16[64,256]{1,0:T(8,128)(2,1)S(1)}, bf16[64,256]{1,0:T(8,128)(2,1)S(1)}, u32[]{:S(2)}, u32[]{:S(2)}) collective-permute-start(bf16[64,256]{1,0:T(8,128)(2,1)S(1)} %get-tuple-element.59), channel_id=1, source_target_pairs={{8,0},{16,8},{24,16},{32,24},{40,32},{48,40},{56,48},{64,56},{72,6... | collective-permute-start | bytes 98312 | tf_op jit(solution)/shard_map/ppermute | solution.py:346
  52.2 2.5 %all-to-all-done.1.dy_ref = bf16[8,64,256]{2,1,0:T(8,128)(2,1)S(1)} async-done(((bf16[8,64,256]{2,1,0:T(8,128)(2,1)}), bf16[8,64,256]{2,1,0:T(8,128)(2,1)S(1)}, u32[]{:S(2)}, u32[]{:S(2)}) %all-to-all-start.1) | async-done | bytes 262176 | tf_op jit(solution)/shard_map/all_to_all | solution.py:399
  54.7 1.6 %shard_map.82 = bf16[16,16,896]{2,1,0:T(8,128)(2,1)} custom-call(bf16[8,64,256]{2,1,0:T(8,128)(2,1)S(1)} %all-to-all-done.1.dy_ref, bf16[4,2,4,64,256]{4,3,2,1,0:T(8,128)(2,1)S(1)} %all-to-all-done.x_ref, bf16[2,4,64,256]{3,2,1,0:T(8,128)(2,1)S(1)} %collective-permute-done.10.e_ref), custom_call_target="tpu_custom_call" | custom-call | tf_op jit(solution)/shard_map/pallas_call | solution.py:334
  56.6 10.6 %all-to-all-start.2 = ((bf16[16,16,896]{2,1,0:T(8,128)(2,1)}), bf16[16,16,896]{2,1,0:T(8,128)(2,1)S(1)}, u32[]{:S(2)}, u32[]{:S(2)}) async-start(bf16[16,16,896]{2,1,0:T(8,128)(2,1)} %shard_map.82), calls=%async_computation.2 | async-start | bytes 917504 | tf_op jit(solution)/shard_map/all_to_all | solution.py:406
  67.3 0.8 collective-permute-start.12
  68.1 1.2 collective-permute-start.11
  69.3 2.8 %collective-permute-done.13.refs_7_ = bf16[2,64,256]{2,1,0:T(8,128)(2,1)S(1)} collective-permute-done((bf16[2,64,256]{2,1,0:T(8,128)(2,1)S(1)}, bf16[2,64,256]{2,1,0:T(8,128)(2,1)S(1)}, u32[]{:S(2)}, u32[]{:S(2)}) %collective-permute-start.13) | collective-permute-done | bytes 65568 | tf_op jit(solution)/shard_map/ppermute | solution.py:350
  72.1 1.1 collective-permute-done.12.refs_6_
  73.2 1.3 %collective-permute-done.11.refs_5_ = bf16[2,64,256]{2,1,0:T(8,128)(2,1)S(1)} collective-permute-done((bf16[2,64,256]{2,1,0:T(8,128)(2,1)S(1)}, bf16[2,64,256]{2,1,0:T(8,128)(2,1)S(1)}, u32[]{:S(2)}, u32[]{:S(2)}) %collective-permute-start.11) | collective-permute-done | bytes 65568 | tf_op jit(solution)/shard_map/ppermute | solution.py:350
  75.1 2.7 %collective-permute-start.15 = (bf16[64,3456]{1,0:T(8,128)(2,1)}, bf16[64,3456]{1,0:T(8,128)(2,1)S(1)}, u32[]{:S(2)}, u32[]{:S(2)}) collective-permute-start(bf16[64,3456]{1,0:T(8,128)(2,1)} %copy-done.7), channel_id=1, source_target_pairs={{0,6},{1,7},{2,0},{3,1},{4,2},{5,3},{6,4},{7,5},{8,14},{9,15},{10,... | collective-permute-start | bytes 1327112 | tf_op jit(solution)/shard_map/ppermute | solution.py:350
  77.7 1.8 %all-to-all-done.2.r_ref = bf16[16,16,896]{2,1,0:T(8,128)(2,1)S(1)} async-done(((bf16[16,16,896]{2,1,0:T(8,128)(2,1)}), bf16[16,16,896]{2,1,0:T(8,128)(2,1)S(1)}, u32[]{:S(2)}, u32[]{:S(2)}) %all-to-all-start.2) | async-done | bytes 458784 | tf_op jit(solution)/shard_map/all_to_all | solution.py:406
  79.6 0.9 shard_map.84
  80.5 6.4 %all-to-all-start.3 = ((bf16[8,2,16,896]{3,2,1,0:T(8,128)(2,1)}), bf16[8,2,16,896]{3,2,1,0:T(8,128)(2,1)S(1)}, u32[]{:S(2)}, u32[]{:S(2)}) async-start(bf16[8,2,16,896]{3,2,1,0:T(8,128)(2,1)} %shard_map.84), calls=%async_computation.3 | async-start | bytes 917504 | tf_op jit(solution)/shard_map/all_to_all | solution.py:423
  86.9 0.8 collective-permute-done.14.refs_1_
  87.7 1.0 shard_map.83
  88.8 1.9 %collective-permute-done.16.b_ref = f32[2,4,64,256]{3,2,1,0:T(8,128)S(1)} collective-permute-done((f32[2,4,64,256]{3,2,1,0:T(8,128)S(1)}, f32[2,4,64,256]{3,2,1,0:T(8,128)S(1)}, u32[]{:S(2)}, u32[]{:S(2)}) %collective-permute-start.16) | collective-permute-done | bytes 524320 | tf_op jit(solution)/shard_map/ppermute | solution.py:363
  90.7 8.8 %all-to-all-done.3.r_ref = bf16[8,2,16,896]{3,2,1,0:T(8,128)(2,1)S(1)} async-done(((bf16[8,2,16,896]{3,2,1,0:T(8,128)(2,1)}), bf16[8,2,16,896]{3,2,1,0:T(8,128)(2,1)S(1)}, u32[]{:S(2)}, u32[]{:S(2)}) %all-to-all-start.3) | async-done | bytes 458784 | tf_op jit(solution)/shard_map/all_to_all | solution.py:423
  99.5 0.9 collective-permute-start.17
  100.5 2.4 %collective-permute-start.19 = (bf16[4,2,16,896]{3,2,1,0:T(8,128)(2,1)S(1)}, bf16[4,2,16,896]{3,2,1,0:T(8,128)(2,1)S(1)}, u32[]{:S(2)}, u32[]{:S(2)}) collective-permute-start(bf16[4,2,16,896]{3,2,1,0:T(8,128)(2,1)S(1)} %get-tuple-element.79.refs_1_), channel_id=1, source_target_pairs={{0,136},{8,128},{16,152},{24,144},{32,168},{40,160},{48,184},{56,1... | collective-permute-start | bytes 688136 | tf_op jit(solution)/shard_map/ppermute | solution.py:359
  102.8 1.3 %collective-permute-start.22 = (bf16[4,2,16,896]{3,2,1,0:T(8,128)(2,1)S(1)}, bf16[4,2,16,896]{3,2,1,0:T(8,128)(2,1)S(1)}, u32[]{:S(2)}, u32[]{:S(2)}) collective-permute-start(bf16[4,2,16,896]{3,2,1,0:T(8,128)(2,1)S(1)} %get-tuple-element.78.refs_0_), channel_id=1, source_target_pairs={{0,136},{8,128},{16,152},{24,144},{32,168},{40,160},{48,184},{56,1... | collective-permute-start | bytes 688136 | tf_op jit(solution)/shard_map/ppermute | solution.py:359
  104.1 0.8 collective-permute-start.21
  104.9 4.2 %collective-permute-done.17.refs_0_ = bf16[4,2,16,896]{3,2,1,0:T(8,128)(2,1)S(1)} collective-permute-done((bf16[4,2,16,896]{3,2,1,0:T(8,128)(2,1)S(1)}, bf16[4,2,16,896]{3,2,1,0:T(8,128)(2,1)S(1)}, u32[]{:S(2)}, u32[]{:S(2)}) %collective-permute-start.17) | collective-permute-done | bytes 229408 | tf_op jit(solution)/shard_map/ppermute | solution.py:359
  109.6 3.0 %collective-permute-start.20 = (bf16[4,2,16,896]{3,2,1,0:T(8,128)(2,1)S(1)}, bf16[4,2,16,896]{3,2,1,0:T(8,128)(2,1)S(1)}, u32[]{:S(2)}, u32[]{:S(2)}) collective-permute-start(bf16[4,2,16,896]{3,2,1,0:T(8,128)(2,1)S(1)} %collective-permute-done.19.refs_3_), channel_id=1, source_target_pairs={{0,136},{8,128},{16,152},{24,144},{32,168},{40,160},{48,184},{56,1... | collective-permute-start | bytes 688136 | tf_op jit(solution)/shard_map/ppermute | solution.py:359
  112.6 1.6 %shard_map.87 = (f32[64,13824]{1,0:T(8,128)}, f32[64,1]{1,0:T(8,128)S(1)}) custom-call(s32[1]{0:T(128)} %bitcast.13.q_ref, bf16[4,2,16,896]{3,2,1,0:T(8,128)(2,1)S(1)} %get-tuple-element.78.refs_0_, bf16[4,2,16,896]{3,2,1,0:T(8,128)(2,1)S(1)} %get-tuple-element.79.refs_1_), custom_call_target="tpu_custom_call" | custom-call | tf_op jit(solution)/shard_map/pallas_call | solution.py:272
  114.2 1.5 %shard_map.85 = bf16[2,64,1024]{2,1,0:T(8,128)(2,1)} custom-call(f32[2,4,64,256]{3,2,1,0:T(8,128)S(1)} %get-tuple-element.75.a_ref, f32[2,4,64,256]{3,2,1,0:T(8,128)S(1)} %collective-permute-done.16.b_ref), custom_call_target="tpu_custom_call" | custom-call | tf_op jit(solution)/shard_map/pallas_call | solution.py:334
  115.8 0.6 reduce
  116.4 2.0 %shard_map.88.refs_2_ = f32[64,13824]{1,0:T(8,128)} custom-call(s32[1]{0:T(128)} %bitcast.13.q_ref, bf16[4,2,16,896]{3,2,1,0:T(8,128)(2,1)S(1)} %collective-permute-done.17.refs_0_, bf16[4,2,16,896]{3,2,1,0:T(8,128)(2,1)S(1)} %collective-permute-done.21.refs_1_, ...), custom_call_target="tpu_custom_call", output_to_operand_aliasing={{}: (5, {})} | custom-call | tf_op jit(solution)/shard_map/pallas_call | solution.py:272
  118.4 1.4 %shard_map.89 = f32[64,13824]{1,0:T(8,128)} custom-call(s32[1]{0:T(128)} %bitcast.13.q_ref, bf16[4,2,16,896]{3,2,1,0:T(8,128)(2,1)S(1)} %collective-permute-done.18.refs_0_, bf16[4,2,16,896]{3,2,1,0:T(8,128)(2,1)S(1)} %collective-permute-done.20.refs_1_, f32[64,13824]{1,0:T(8,128)} %shard_map.88.refs_2_), custom_call_target="tpu_custom_call", output_to_operand_aliasing={{}: (3, {})} | custom-call | tf_op jit(solution)/shard_map/pallas_call | solution.py:272
  (49 shorter events, 3.6 us)
Async XLA Ops:
  0.6 1.0 copy-start.5
  2.2 8.4 %collective-permute-start.1 = (bf16[2,4,64,256]{3,2,1,0:T(8,128)(2,1)S(1)}, bf16[2,4,64,256]{3,2,1,0:T(8,128)(2,1)S(1)}, u32[]{:S(2)}, u32[]{:S(2)}) collective-permute-start(bf16[2,4,64,256]{3,2,1,0:T(8,128)(2,1)S(1)} %shard_map.76.own_ref), channel_id=1, source_target_pairs={{0,6},{1,7},{2,0},{3,1},{4,2},{5,3},{6,4},{7,5},{8,14},{9,15},{10,... | collective-permute-start | bytes 786440 | tf_op jit(solution)/shard_map/ppermute | solution.py:350
  5.0 9.3 %collective-permute-start = (bf16[2,4,64,256]{3,2,1,0:T(8,128)(2,1)S(1)}, bf16[2,4,64,256]{3,2,1,0:T(8,128)(2,1)S(1)}, u32[]{:S(2)}, u32[]{:S(2)}) collective-permute-start(bf16[2,4,64,256]{3,2,1,0:T(8,128)(2,1)S(1)} %shard_map.76.own_ref), channel_id=1, source_target_pairs={{0,2},{1,3},{2,4},{3,5},{4,6},{5,7},{6,0},{7,1},{8,10},{9,11},{10,... | collective-permute-start | bytes 786440 | tf_op jit(solution)/shard_map/ppermute | solution.py:350
  5.1 1.5 %copy-start = (bf16[64,13824]{1,0:T(8,128)(2,1)S(1)}, bf16[64,13824]{1,0:T(8,128)(2,1)}, u32[]{:S(2)}) copy-start(bf16[64,13824]{1,0:T(8,128)(2,1)} %w_ref.3) | copy-start | bytes 5308420
  8.9 17.4 %collective-permute-start.4 = (bf16[64,6912]{1,0:T(8,128)(2,1)}, bf16[64,6912]{1,0:T(8,128)(2,1)S(1)}, u32[]{:S(2)}, u32[]{:S(2)}) collective-permute-start(bf16[64,6912]{1,0:T(8,128)(2,1)} %get-tuple-element.49), channel_id=1, source_target_pairs={{0,1},{1,0},{2,3},{3,2},{4,5},{5,4},{6,7},{7,6},{8,9},{9,8},{10,11... | collective-permute-start | bytes 2654216 | tf_op jit(solution)/shard_map/ppermute | solution.py:363
  10.6 6.3 %collective-permute-start.2 = (bf16[4,64,256]{2,1,0:T(8,128)(2,1)S(1)}, bf16[4,64,256]{2,1,0:T(8,128)(2,1)S(1)}, u32[]{:S(2)}, u32[]{:S(2)}) collective-permute-start(bf16[4,64,256]{2,1,0:T(8,128)(2,1)S(1)} %slice_bitcast_fusion.2), channel_id=1, source_target_pairs={{0,6},{1,7},{2,0},{3,1},{4,2},{5,3},{6,4},{7,5},{8,14},{9,15},{10,... | collective-permute-start | bytes 393224 | tf_op jit(solution)/shard_map/ppermute | solution.py:350
  14.4 7.3 %copy-start.1 = (bf16[2,4,64,256]{3,2,1,0:T(8,128)(2,1)}, bf16[2,4,64,256]{3,2,1,0:T(8,128)(2,1)S(1)}, u32[]{:S(2)}) copy-start(bf16[2,4,64,256]{3,2,1,0:T(8,128)(2,1)S(1)} %collective-permute-done.back_ref) | copy-start | bytes 786436
  14.4 6.3 %collective-permute-start.3 = (bf16[4,64,256]{2,1,0:T(8,128)(2,1)S(1)}, bf16[4,64,256]{2,1,0:T(8,128)(2,1)S(1)}, u32[]{:S(2)}, u32[]{:S(2)}) collective-permute-start(bf16[4,64,256]{2,1,0:T(8,128)(2,1)S(1)} %slice_bitcast_fusion.1), channel_id=1, source_target_pairs={{0,2},{1,3},{2,4},{3,5},{4,6},{5,7},{6,0},{7,1},{8,10},{9,11},{10,... | collective-permute-start | bytes 393224 | tf_op jit(solution)/shard_map/ppermute | solution.py:350
  15.6 0.8 copy-start.3
  16.4 5.3 %copy-start.8 = (bf16[64,3456]{1,0:T(8,128)(2,1)}, bf16[64,3456]{1,0:T(8,128)(2,1)S(1)}, u32[]{:S(2)}) copy-start(bf16[64,3456]{1,0:T(8,128)(2,1)S(1)} %get-tuple-element.60) | copy-start | bytes 1327108
  16.4 5.3 %copy-start.7 = (bf16[64,3456]{1,0:T(8,128)(2,1)}, bf16[64,3456]{1,0:T(8,128)(2,1)S(1)}, u32[]{:S(2)}) copy-start(bf16[64,3456]{1,0:T(8,128)(2,1)S(1)} %get-tuple-element.66) | copy-start | bytes 1327108
  21.7 14.1 %copy-start.9 = (f32[64]{0:T(128)S(1)}, f32[64]{0:T(128)}, u32[]{:S(2)}) copy-start(f32[64]{0:T(128)} %param.6) | copy-start | bytes 772
  21.7 17.2 %copy-start.6 = (bf16[1,1,64,256]{3,2,1,0:T(8,128)(2,1)S(1)}, bf16[1,1,64,256]{3,2,1,0:T(8,128)(2,1)}, u32[]{:S(2)}) copy-start(bf16[1,1,64,256]{3,2,1,0:T(8,128)(2,1)} %param.7) | copy-start | bytes 98308
  21.7 18.8 %all-to-all-start = ((bf16[4,2,4,64,256]{4,3,2,1,0:T(8,128)(2,1)}), bf16[4,2,4,64,256]{4,3,2,1,0:T(8,128)(2,1)S(1)}, u32[]{:S(2)}, u32[]{:S(2)}) async-start(bf16[4,2,4,64,256]{4,3,2,1,0:T(8,128)(2,1)} %shard_map.77.all_ref), calls=%async_computation | async-start | bytes 2097152 | tf_op jit(solution)/shard_map/all_to_all | solution.py:387
  26.3 1.0 copy-start.2
  27.7 2.6 %collective-permute-start.6 = (f32[64,256]{1,0:T(8,128)S(1)}, f32[64,256]{1,0:T(8,128)S(1)}, u32[]{:S(2)}, u32[]{:S(2)}) collective-permute-start(f32[64,256]{1,0:T(8,128)S(1)} %get-tuple-element.53), channel_id=1, source_target_pairs={{0,1},{1,0},{2,3},{3,2},{4,5},{5,4},{6,7},{7,6},{8,9},{9,8},{10,11... | collective-permute-start | bytes 196616 | tf_op jit(solution)/shard_map/ppermute | solution.py:363
  29.7 58.0 %copy-start.4 = (bf16[64,3456]{1,0:T(8,128)(2,1)S(1)}, bf16[64,3456]{1,0:T(8,128)(2,1)}, u32[]{:S(2)}) copy-start(bf16[64,3456]{1,0:T(8,128)(2,1)} %copy-done.3) | copy-start | bytes 1327108
  29.7 6.2 %collective-permute-start.5 = (f32[64,256]{1,0:T(8,128)S(1)}, f32[64,256]{1,0:T(8,128)S(1)}, u32[]{:S(2)}, u32[]{:S(2)}) collective-permute-start(f32[64,256]{1,0:T(8,128)S(1)} %get-tuple-element.51), channel_id=1, source_target_pairs={{0,1},{1,0},{2,3},{3,2},{4,5},{5,4},{6,7},{7,6},{8,9},{9,8},{10,11... | collective-permute-start | bytes 196616 | tf_op jit(solution)/shard_map/ppermute | solution.py:363
  30.3 8.6 %collective-permute-start.7 = (f32[64,256]{1,0:T(8,128)S(1)}, f32[64,256]{1,0:T(8,128)S(1)}, u32[]{:S(2)}, u32[]{:S(2)}) collective-permute-start(f32[64,256]{1,0:T(8,128)S(1)} %add.19), channel_id=1, source_target_pairs={{0,8},{8,16},{16,24},{24,32},{32,40},{40,48},{48,56},{56,64},{64,7... | collective-permute-start | bytes 196616 | tf_op jit(solution)/shard_map/ppermute | solution.py:346
  35.9 20.5 %collective-permute-start.8 = (bf16[64,3456]{1,0:T(8,128)(2,1)}, bf16[64,3456]{1,0:T(8,128)(2,1)S(1)}, u32[]{:S(2)}, u32[]{:S(2)}) collective-permute-start(bf16[64,3456]{1,0:T(8,128)(2,1)} %copy-done.8), channel_id=1, source_target_pairs={{0,4},{1,5},{2,6},{3,7},{4,0},{5,1},{6,2},{7,3},{8,12},{9,13},{10,... | collective-permute-start | bytes 1327112 | tf_op jit(solution)/shard_map/ppermute | solution.py:350
  40.5 14.2 %collective-permute-start.10 = (bf16[2,4,64,256]{3,2,1,0:T(8,128)(2,1)S(1)}, bf16[2,4,64,256]{3,2,1,0:T(8,128)(2,1)S(1)}, u32[]{:S(2)}, u32[]{:S(2)}) collective-permute-start(bf16[2,4,64,256]{3,2,1,0:T(8,128)(2,1)S(1)} %slice_bitcast_fusion), channel_id=1, source_target_pairs={{0,16},{8,24},{16,32},{24,40},{32,48},{40,56},{48,64},{56,72},{64,... | collective-permute-start | bytes 786440 | tf_op jit(solution)/shard_map/ppermute | solution.py:346
  44.4 10.3 %all-to-all-start.1 = ((bf16[8,64,256]{2,1,0:T(8,128)(2,1)}), bf16[8,64,256]{2,1,0:T(8,128)(2,1)S(1)}, u32[]{:S(2)}, u32[]{:S(2)}) async-start(bf16[8,64,256]{2,1,0:T(8,128)(2,1)} %get-tuple-element.61), calls=%async_computation.1 | async-start | bytes 524288 | tf_op jit(solution)/shard_map/all_to_all | solution.py:399
  49.3 7.3 %collective-permute-start.9 = (bf16[64,256]{1,0:T(8,128)(2,1)S(1)}, bf16[64,256]{1,0:T(8,128)(2,1)S(1)}, u32[]{:S(2)}, u32[]{:S(2)}) collective-permute-start(bf16[64,256]{1,0:T(8,128)(2,1)S(1)} %get-tuple-element.59), channel_id=1, source_target_pairs={{8,0},{16,8},{24,16},{32,24},{40,32},{48,40},{56,48},{64,56},{72,6... | collective-permute-start | bytes 98312 | tf_op jit(solution)/shard_map/ppermute | solution.py:346
  56.6 23.0 %all-to-all-start.2 = ((bf16[16,16,896]{2,1,0:T(8,128)(2,1)}), bf16[16,16,896]{2,1,0:T(8,128)(2,1)S(1)}, u32[]{:S(2)}, u32[]{:S(2)}) async-start(bf16[16,16,896]{2,1,0:T(8,128)(2,1)} %shard_map.82), calls=%async_computation.2 | async-start | bytes 917504 | tf_op jit(solution)/shard_map/all_to_all | solution.py:406
  67.2 4.9 %collective-permute-start.13 = (bf16[2,64,256]{2,1,0:T(8,128)(2,1)S(1)}, bf16[2,64,256]{2,1,0:T(8,128)(2,1)S(1)}, u32[]{:S(2)}, u32[]{:S(2)}) collective-permute-start(bf16[2,64,256]{2,1,0:T(8,128)(2,1)S(1)} %pad_maximum_fusion.refs_4_), channel_id=1, source_target_pairs={{0,6},{1,7},{2,0},{3,1},{4,2},{5,3},{6,4},{7,5},{8,14},{9,15},{10,... | collective-permute-start | bytes 196616 | tf_op jit(solution)/shard_map/ppermute | solution.py:350
  67.3 6.0 %collective-permute-start.12 = (bf16[2,64,256]{2,1,0:T(8,128)(2,1)S(1)}, bf16[2,64,256]{2,1,0:T(8,128)(2,1)S(1)}, u32[]{:S(2)}, u32[]{:S(2)}) collective-permute-start(bf16[2,64,256]{2,1,0:T(8,128)(2,1)S(1)} %pad_maximum_fusion.refs_4_), channel_id=1, source_target_pairs={{0,4},{1,5},{2,6},{3,7},{4,0},{5,1},{6,2},{7,3},{8,12},{9,13},{10,... | collective-permute-start | bytes 196616 | tf_op jit(solution)/shard_map/ppermute | solution.py:350
  68.1 6.4 %collective-permute-start.11 = (bf16[2,64,256]{2,1,0:T(8,128)(2,1)S(1)}, bf16[2,64,256]{2,1,0:T(8,128)(2,1)S(1)}, u32[]{:S(2)}, u32[]{:S(2)}) collective-permute-start(bf16[2,64,256]{2,1,0:T(8,128)(2,1)S(1)} %pad_maximum_fusion.refs_4_), channel_id=1, source_target_pairs={{0,2},{1,3},{2,4},{3,5},{4,6},{5,7},{6,0},{7,1},{8,10},{9,11},{10,... | collective-permute-start | bytes 196616 | tf_op jit(solution)/shard_map/ppermute | solution.py:350
  74.5 13.2 %collective-permute-start.14 = (bf16[64,3456]{1,0:T(8,128)(2,1)}, bf16[64,3456]{1,0:T(8,128)(2,1)S(1)}, u32[]{:S(2)}, u32[]{:S(2)}) collective-permute-start(bf16[64,3456]{1,0:T(8,128)(2,1)} %get-tuple-element.64), channel_id=1, source_target_pairs={{0,2},{1,3},{2,4},{3,5},{4,6},{5,7},{6,0},{7,1},{8,10},{9,11},{10,... | collective-permute-start | bytes 1327112 | tf_op jit(solution)/shard_map/ppermute | solution.py:350
  75.1 12.6 %collective-permute-start.15 = (bf16[64,3456]{1,0:T(8,128)(2,1)}, bf16[64,3456]{1,0:T(8,128)(2,1)S(1)}, u32[]{:S(2)}, u32[]{:S(2)}) collective-permute-start(bf16[64,3456]{1,0:T(8,128)(2,1)} %copy-done.7), channel_id=1, source_target_pairs={{0,6},{1,7},{2,0},{3,1},{4,2},{5,3},{6,4},{7,5},{8,14},{9,15},{10,... | collective-permute-start | bytes 1327112 | tf_op jit(solution)/shard_map/ppermute | solution.py:350
  80.5 19.0 %all-to-all-start.3 = ((bf16[8,2,16,896]{3,2,1,0:T(8,128)(2,1)}), bf16[8,2,16,896]{3,2,1,0:T(8,128)(2,1)S(1)}, u32[]{:S(2)}, u32[]{:S(2)}) async-start(bf16[8,2,16,896]{3,2,1,0:T(8,128)(2,1)} %shard_map.84), calls=%async_computation.3 | async-start | bytes 917504 | tf_op jit(solution)/shard_map/all_to_all | solution.py:423
  88.7 2.0 %collective-permute-start.16 = (f32[2,4,64,256]{3,2,1,0:T(8,128)S(1)}, f32[2,4,64,256]{3,2,1,0:T(8,128)S(1)}, u32[]{:S(2)}, u32[]{:S(2)}) collective-permute-start(f32[2,4,64,256]{3,2,1,0:T(8,128)S(1)} %get-tuple-element.73), channel_id=1, source_target_pairs={{0,1},{1,0},{2,3},{3,2},{4,5},{5,4},{6,7},{7,6},{8,9},{9,8},{10,11... | collective-permute-start | bytes 1572872 | tf_op jit(solution)/shard_map/ppermute | solution.py:363
  99.5 9.6 %collective-permute-start.17 = (bf16[4,2,16,896]{3,2,1,0:T(8,128)(2,1)S(1)}, bf16[4,2,16,896]{3,2,1,0:T(8,128)(2,1)S(1)}, u32[]{:S(2)}, u32[]{:S(2)}) collective-permute-start(bf16[4,2,16,896]{3,2,1,0:T(8,128)(2,1)S(1)} %get-tuple-element.78.refs_0_), channel_id=1, source_target_pairs={{0,128},{8,136},{16,144},{24,152},{32,160},{40,168},{48,176},{56,1... | collective-permute-start | bytes 688136 | tf_op jit(solution)/shard_map/ppermute | solution.py:359
  100.5 9.2 %collective-permute-start.19 = (bf16[4,2,16,896]{3,2,1,0:T(8,128)(2,1)S(1)}, bf16[4,2,16,896]{3,2,1,0:T(8,128)(2,1)S(1)}, u32[]{:S(2)}, u32[]{:S(2)}) collective-permute-start(bf16[4,2,16,896]{3,2,1,0:T(8,128)(2,1)S(1)} %get-tuple-element.79.refs_1_), channel_id=1, source_target_pairs={{0,136},{8,128},{16,152},{24,144},{32,168},{40,160},{48,184},{56,1... | collective-permute-start | bytes 688136 | tf_op jit(solution)/shard_map/ppermute | solution.py:359
  102.8 13.6 %collective-permute-start.22 = (bf16[4,2,16,896]{3,2,1,0:T(8,128)(2,1)S(1)}, bf16[4,2,16,896]{3,2,1,0:T(8,128)(2,1)S(1)}, u32[]{:S(2)}, u32[]{:S(2)}) collective-permute-start(bf16[4,2,16,896]{3,2,1,0:T(8,128)(2,1)S(1)} %get-tuple-element.78.refs_0_), channel_id=1, source_target_pairs={{0,136},{8,128},{16,152},{24,144},{32,168},{40,160},{48,184},{56,1... | collective-permute-start | bytes 688136 | tf_op jit(solution)/shard_map/ppermute | solution.py:359
  104.1 12.3 %collective-permute-start.21 = (bf16[4,2,16,896]{3,2,1,0:T(8,128)(2,1)S(1)}, bf16[4,2,16,896]{3,2,1,0:T(8,128)(2,1)S(1)}, u32[]{:S(2)}, u32[]{:S(2)}) collective-permute-start(bf16[4,2,16,896]{3,2,1,0:T(8,128)(2,1)S(1)} %get-tuple-element.79.refs_1_), channel_id=1, source_target_pairs={{0,128},{8,136},{16,144},{24,152},{32,160},{40,168},{48,176},{56,1... | collective-permute-start | bytes 688136 | tf_op jit(solution)/shard_map/ppermute | solution.py:359
  109.1 9.2 %collective-permute-start.18 = (bf16[4,2,16,896]{3,2,1,0:T(8,128)(2,1)S(1)}, bf16[4,2,16,896]{3,2,1,0:T(8,128)(2,1)S(1)}, u32[]{:S(2)}, u32[]{:S(2)}) collective-permute-start(bf16[4,2,16,896]{3,2,1,0:T(8,128)(2,1)S(1)} %collective-permute-done.17.refs_0_), channel_id=1, source_target_pairs={{0,128},{8,136},{16,144},{24,152},{32,160},{40,168},{48,176},{56,1... | collective-permute-start | bytes 688136 | tf_op jit(solution)/shard_map/ppermute | solution.py:359
  109.6 8.7 %collective-permute-start.20 = (bf16[4,2,16,896]{3,2,1,0:T(8,128)(2,1)S(1)}, bf16[4,2,16,896]{3,2,1,0:T(8,128)(2,1)S(1)}, u32[]{:S(2)}, u32[]{:S(2)}) collective-permute-start(bf16[4,2,16,896]{3,2,1,0:T(8,128)(2,1)S(1)} %collective-permute-done.19.refs_3_), channel_id=1, source_target_pairs={{0,136},{8,128},{16,152},{24,144},{32,168},{40,160},{48,184},{56,1... | collective-permute-start | bytes 688136 | tf_op jit(solution)/shard_map/ppermute | solution.py:359
